TPU v7x, 32 devices: a whole 2x2x4 slice. The times are simulated.
32 devices in a mesh: grp: 2 (over y), ctx: 4 (over x, core), exp: 4 (over z).
Axes of the slice: x: 2, y: 2, z: 4, core: 2. Of those that a mesh axis runs over, the one named last changes fastest.
Arguments:
- queries: bfloat16 [2048, 8192], P(('grp', 'ctx'), 'exp'), parts along dimension 0, may hold values from -6.5 to 6.5
- keys: bfloat16 [2048, 512], P(('grp', 'ctx')), parts along dimension 0, may hold values from -4 to 4
- values: bfloat16 [2048, 512], P(('grp', 'ctx')), parts along dimension 0, may hold values from -6 to 6
- doc_lengths: int32 [48], P('grp'), parts along dimension 0, may hold values from 1 to 512, 1024 in all
- residual_in: bfloat16 [2048, 4096], P(('grp', 'ctx', 'exp')), parts along dimension 0, may hold values from -3 to 3
- out_weight: bfloat16 [8192, 4096], P('exp', 'ctx'), may hold values from -0.125 to 0.125
- norm_gain: float32 [4096], replicated, may hold values from 0.5 to 2
- routes: int32 [2048, 8], P(('grp', 'ctx', 'exp')), parts along dimension 0, may hold values from 0 to 127, as said below
- route_weights: float32 [2048, 8], P(('grp', 'ctx', 'exp')), parts along dimension 0, may hold values from 0.05 to 1
- gate_weight: bfloat16 [4, 4096, 1536], P('exp', None, 'ctx'), may hold values from -0.09375 to 0.09375
- up_weight: bfloat16 [4, 4096, 1536], P('exp', None, 'ctx'), may hold values from -0.09375 to 0.09375
- down_weight: bfloat16 [4, 1536, 4096], P('exp', None, 'ctx'), may hold values from -0.3125 to 0.3125
Outputs:
- attended: bfloat16 [2048, 4096], P(('grp', 'ctx', 'exp')), parts along dimension 0
- expert_sum: bfloat16 [2048, 4096], P(('grp', 'ctx', 'exp')), parts along dimension 0
There are 2 independent parts, one for each index of `grp`. A program takes and returns all parts, laid end to end along the dimension named above; an argument that names none is the same for every part. Nothing has to cross between parts.
Inputs may be any that keep to these rules, and one draw needn't show every extreme that they name: `routes`: each row names 8 different experts. In each aligned block of 64 rows, each of the experts below 4 is named by at most 2 rows, and one of them by exactly 2 rows in every block.
All inputs are finite; a program needn't handle non-finite values.
Results may differ from a plain program's by a relative error of at most 0.018.
Values may be sent and summed in bfloat16 or wider, within the bound.
No kernel may reach another device: no remote copies, remote signals or barrier semaphores. Data moves between devices by JAX's collectives and lax.ppermute only.
A program may use at most 128 MiB of HBM per device.

v0:
```python
import jax
import jax.numpy as jnp
from jax import lax
from jax.sharding import PartitionSpec as P

QH = 64
KVH = 4
HD = 128
CAP = 2


def doc_starts(doc_lengths, positions):
    bounds = jnp.cumsum(doc_lengths) - doc_lengths
    picked = jnp.where(bounds[None, :] <= positions[:, None], bounds[None, :], 0)
    return jnp.max(picked, axis=1)


def slot_tables(route_rows, weight_rows, flight, capacity):
    count = route_rows.shape[0]
    top = route_rows.shape[1]
    flat = route_rows.reshape(-1)
    experts = jnp.arange(flight, dtype=jnp.int32)
    onehot = (flat[:, None] == experts[None, :]).astype(jnp.int32)
    earlier = jnp.cumsum(onehot, axis=0) - onehot
    rank = jnp.sum(earlier * onehot, axis=1)
    target = jnp.where(flat < flight, flat * capacity + rank, flight * capacity)
    slots = jnp.arange(flight * capacity, dtype=jnp.int32)
    chosen = (target[None, :] == slots[:, None]).reshape(flight * capacity, count, top)
    picks = jnp.sum(chosen.astype(jnp.float32), axis=2)
    weights = jnp.sum(jnp.where(chosen, weight_rows[None, :, :], jnp.float32(0.0)), axis=2)
    return (picks, weights)


def shards(
    queries,
    keys,
    values,
    doc_lengths,
    residual_in,
    out_weight,
    norm_gain,
    routes,
    route_weights,
    gate_weight,
    up_weight,
    down_weight,
):
    tok_count = queries.shape[0]
    local_heads = queries.shape[1] // HD
    ctx_index = lax.axis_index("ctx")
    exp_index = lax.axis_index("exp")
    first_row = ctx_index * tok_count
    positions = first_row + jnp.arange(tok_count, dtype=jnp.int32)
    starts = doc_starts(doc_lengths, positions)
    kv_head = exp_index * local_heads // (QH // KVH)
    own_keys = lax.dynamic_slice_in_dim(keys, kv_head * HD, HD, 1)
    own_values = lax.dynamic_slice_in_dim(values, kv_head * HD, HD, 1)
    stacked = jnp.stack([own_keys, own_values])
    query_heads = queries.reshape(tok_count, local_heads, HD)
    scale = 1.0 / HD**0.5
    initial = (
        jnp.full((local_heads, tok_count), -1e30, jnp.float32),
        jnp.zeros((local_heads, tok_count), jnp.float32),
        jnp.zeros((local_heads, tok_count, HD), jnp.float32),
    )
    piece = lax.all_gather(stacked, "ctx", axis=1, tiled=True)
    start = jnp.int32(0)
    width = piece.shape[1]

    def update(state):
        best, total, accum = state
        key_pos = jnp.arange(width, dtype=jnp.int32)
        scores = (
            jnp.einsum("qhd,kd->hqk", query_heads, piece[0], preferred_element_type=jnp.float32)
            * scale
        )
        allowed = (key_pos[None, :] <= positions[:, None]) & (key_pos[None, :] >= starts[:, None])
        scores = jnp.where(allowed[None], scores, jnp.float32(-1e30))
        fresh = jnp.maximum(best, jnp.max(scores, axis=2))
        probs = jnp.where(allowed[None], jnp.exp(scores - fresh[:, :, None]), jnp.float32(0.0))
        total = jnp.sum(probs, axis=2)
        mixed = jnp.einsum(
            "hqk,kd->hqd", probs.astype(jnp.bfloat16), piece[1], preferred_element_type=jnp.float32
        )
        accum = mixed
        return (fresh, total, accum)

    live = (start < first_row + tok_count) & (start + width > starts[0])
    state = lax.cond(live, update, lambda state: state, initial)
    best, total, accum = state
    heads_out = (accum / total[:, :, None]).astype(jnp.bfloat16)
    heads_out = jnp.transpose(heads_out, (1, 0, 2)).reshape(tok_count, local_heads * HD)
    partial_sum = jnp.dot(
        heads_out,
        lax.all_gather(out_weight, "ctx", axis=1, tiled=True),
        preferred_element_type=jnp.float32,
    )
    head_sum = lax.psum_scatter(
        partial_sum.astype(jnp.bfloat16), "exp", scatter_dimension=0, tiled=True
    ).astype(jnp.float32)
    stream = residual_in.astype(jnp.float32) + head_sum
    attended = stream.astype(jnp.bfloat16)
    normed = (
        stream
        * lax.rsqrt(jnp.mean(stream * stream, axis=1, keepdims=True) + 1e-06)
        * norm_gain[None, :]
    ).astype(jnp.bfloat16)
    width_model = normed.shape[1]
    flight = gate_weight.shape[0] * lax.axis_size("exp")
    shares = route_weights / jnp.sum(route_weights, axis=1, keepdims=True)
    picks, weights = slot_tables(routes, shares, flight, CAP)
    outgoing = jnp.dot(
        picks.astype(jnp.bfloat16), normed, preferred_element_type=jnp.float32
    ).astype(jnp.bfloat16)
    outgoing = outgoing.reshape(flight, CAP, width_model)
    gate_local = gate_weight[0]
    up_local = up_weight[0]
    down_local = down_weight[0]
    arrived = lax.all_to_all(outgoing, "exp", split_axis=0, concat_axis=0, tiled=True)
    expand_piece = lax.all_gather(arrived.reshape(-1, width_model), "ctx", axis=0, tiled=True)
    gate = jnp.dot(expand_piece, gate_local, preferred_element_type=jnp.float32)
    up = jnp.dot(expand_piece, up_local, preferred_element_type=jnp.float32)
    hidden_part = (jax.nn.silu(gate) * up).astype(jnp.bfloat16)
    produced = jnp.dot(
        lax.all_gather(hidden_part, "ctx", axis=1, tiled=True),
        down_local,
        preferred_element_type=jnp.float32,
    )
    returned_local = produced.astype(jnp.bfloat16).reshape(
        lax.axis_size("ctx"), lax.axis_size("exp"), CAP, down_local.shape[1]
    )
    arrived_back = lax.all_to_all(
        lax.all_to_all(returned_local, "ctx", split_axis=0, concat_axis=3, tiled=True),
        "exp",
        split_axis=1,
        concat_axis=0,
        tiled=True,
    )
    combined = jnp.dot(
        weights.T,
        arrived_back.reshape(flight * CAP, width_model).astype(jnp.float32),
        precision=lax.Precision.HIGHEST,
    )
    return (attended, combined.astype(jnp.bfloat16))


def solution(mesh):
    placed = (
        P(("grp", "ctx"), "exp"),
        P(("grp", "ctx"), None),
        P(("grp", "ctx"), None),
        P("grp"),
        P(("grp", "ctx", "exp"), None),
        P("exp", "ctx"),
        P(),
        P(("grp", "ctx", "exp"), None),
        P(("grp", "ctx", "exp"), None),
        P("exp", None, "ctx"),
        P("exp", None, "ctx"),
        P("exp", None, "ctx"),
    )
    return jax.shard_map(
        shards,
        mesh=mesh,
        in_specs=placed,
        out_specs=(P(("grp", "ctx", "exp"), None), P(("grp", "ctx", "exp"), None)),
        check_vma=False,
    )
```

profile of v0, /device:TPU:0, one launch (start us, length us, event | category | flops | bytes accessed | tf_op | source)
XLA Modules:
  0.0 226.6 jit_solution(3199461654648628209)
XLA Ops:
  7.2 0.0 copy-start
  7.2 0.0 all-gather.2.cloned.1.call-start
  7.2 0.7 all-gather.2.cloned.1.call-update
  7.9 0.0 reduce-scatter.2.cloned.1.call-start
  8.0 0.9 copy.60
  8.9 0.1 reduce
  9.0 0.7 sub.18
  9.7 0.1 select_reduce_fusion.1
  9.8 0.5 slice.15
  10.9 0.9 dynamic-slice_bitcast_fusion
  11.9 8.6 %all_gather.12 = bf16[2,1024,128]{2,1,0:T(8,128)(2,1)S(1)} all-gather(bf16[2,256,128]{2,1,0:T(8,128)(2,1)S(1)} %pad_maximum_fusion), channel_id=1, replica_groups=mesh['grp'=2,'ctx'=4,'exp'=4] {'ctx'}, dimensions={1}, use_global_device_ids=true | all-gather | bytes 655360 | tf_op jit(solution)/shard_map/all_gather | solution.py:66
  20.5 12.3 %conditional.1 = (f32[16,256]{1,0:T(8,128)S(1)}, f32[16,256,128]{1,2,0:T(8,128)S(1)}) conditional(s32[]{:T(128)} %convert_element_type.51, () %tuple.16, (s32[]{:T(128)}, s32[256]{0:T(256)S(1)}, s32[256]{0:T(256)S(1)}, bf16[2,1024,128]{2,1,0:T(8,128)(2,1)S(1)}, bf16[256,2048]{1,0:T(8,128)(2,1)}) %tuple.17), branch_computations={%region_2.3_spmd, %region_3.6_spmd} | conditional | flops 2202792192 | bytes 55152660 | solution.py:89
  20.5 0.2 fusion.9
  20.8 3.9 %fusion = (f32[16,256]{1,0:T(8,128)S(1)}, f32[1024,256,16]{1,0,2:T(8,128)S(1)}) fusion(pred[256,1024]{0,1:T(8,128)(4,1)S(1)} %fusion.9, bf16[2,1024,128]{2,1,0:T(8,128)(2,1)S(1)} %get-tuple-element.16, bf16[256,2048]{1,0:T(8,128)(2,1)} %get-tuple-element.25), kind=kOutput, calls=%fused_computation.2 | convolution fusion | flops 1086320640 | bytes 18366464 | tf_op jit(solution)/shard_map/cond/branch_1_fun/qhd,kd->hqk/dot_general | solution.py:74
  24.6 4.0 %fusion.3 = f32[16,256,128]{1,2,0:T(8,128)S(1)} fusion(f32[1024,256,16]{1,0,2:T(8,128)S(1)} %get-tuple-element.30, f32[16,256]{1,0:T(8,128)S(1)} %broadcast_maximum_fusion, pred[256,1024]{0,1:T(8,128)(4,1)S(1)} %fusion.9, bf16[2,1024,128]{2,1,0:T(8,128)(2,1)S(1)} %get-tuple-element.16), kind=kOutput, calls=%fused_computation.5 | convolution fusion | flops 1094713344 | bytes 19415040 | tf_op jit(solution)/shard_map/cond | solution.py:89
  28.6 4.0 %fusion.2 = f32[16,256]{1,0:T(8,128)S(1)} fusion(f32[1024,256,16]{1,0,2:T(8,128)S(1)} %get-tuple-element.30, f32[16,256]{1,0:T(8,128)S(1)} %broadcast_maximum_fusion, pred[256,1024]{0,1:T(8,128)(4,1)S(1)} %fusion.9), kind=kLoop, calls=%fused_computation.4 | loop fusion | flops 20967424 | bytes 17072128 | tf_op jit(solution)/shard_map/cond/branch_1_fun/reduce_sum | solution.py:81
  32.8 0.0 copy-start.1
  32.8 0.0 copy-start.2
  32.8 0.0 copy-start.3
  32.9 1.2 divide_convert_fusion
  34.0 84.2 %all-gather.2.cloned.1.call-done = bf16[2048,4096]{1,0:T(8,128)(2,1)} async-done(((bf16[2048,1024]{1,0:T(8,128)(2,1)}), bf16[2048,4096]{1,0:T(8,128)(2,1)}) %all-gather.2.cloned.1.call-update) | async-done | bytes 16777232 | tf_op jit(solution)/shard_map/all_gather | solution.py:95
  118.2 12.0 %convolution_convert_fusion = bf16[256,4096]{1,0:T(8,128)(2,1)} fusion(bf16[256,2048]{0,1:T(8,128)(2,1)} %bitcast.90, bf16[2048,4096]{1,0:T(8,128)(2,1)} %all-gather.2.cloned.1.call-done), kind=kOutput, calls=%fused_computation.22 | convolution fusion | flops 4296015872 | bytes 19922944 | tf_op jit(solution)/shard_map/dot_general | solution.py:93
  130.3 0.0 reduce-scatter.2.cloned.1.call-update
  130.3 0.0 copy-done.1
  130.3 0.1 copy.62
  130.4 0.1 eq.43
  130.5 0.1 eq.39
  130.6 1.2 reduce-window.20
  131.8 0.2 slice_reduce_fusion
  132.0 0.2 reduce-window.21
  132.2 0.1 add_bitcast_fusion
  132.3 0.1 reduce_sum.57
  132.4 0.1 copy.64
  132.5 0.0 copy-done.2
  132.6 41.8 %reduce-scatter.2.cloned.1.call-done = bf16[64,4096]{1,0:T(8,128)(2,1)} async-done(((bf16[256,4096]{1,0:T(8,128)(2,1)}), bf16[64,4096]{1,0:T(8,128)(2,1)}) %reduce-scatter.2.cloned.1.call-update) | async-done | bytes 524304 | tf_op jit(solution)/shard_map/reduce_scatter | solution.py:98
  174.3 2.3 %multiply_reduce_fusion = (f32[64]{0:T(128)S(1)}, bf16[64,4096]{1,0:T(8,128)(2,1)}) fusion(bf16[64,4096]{1,0:T(8,128)(2,1)} %reduce-scatter.2.cloned.1.call-done, bf16[64,4096]{1,0:T(8,128)(2,1)} %param.18), kind=kLoop, calls=%fused_computation.36 | loop fusion | flops 1572800 | bytes 1573120 | tf_op jit(solution)/shard_map/reduce_sum | solution.py:105
  176.6 0.0 copy-done.3
  176.6 1.5 convolution_convert_fusion.2
  178.1 0.1 reshape.155
  178.2 8.5 %all_to_all.32 = bf16[4,2,4096]{2,1,0:T(2,128)(2,1)S(1)} all-to-all(bf16[4,2,4096]{2,1,0:T(2,128)(2,1)S(1)} %reshape.155), channel_id=1, replica_groups=mesh['grp'=2,'ctx'=4,'exp'=4] {'exp'}, dimensions={0} | all-to-all | bytes 131072 | tf_op jit(solution)/shard_map/all_to_all | solution.py:119
  186.8 5.8 %all_gather.14 = bf16[32,4096]{1,0:T(8,128)(2,1)S(1)} all-gather(bf16[8,4096]{1,0:T(8,128)(2,1)S(1)} %reshape.156), channel_id=1, replica_groups=mesh['grp'=2,'ctx'=4,'exp'=4] {'ctx'}, dimensions={0}, use_global_device_ids=true | all-gather | bytes 327680 | tf_op jit(solution)/shard_map/all_gather | solution.py:120
  192.6 2.4 %fusion.21 = f32[32,384]{1,0:T(8,128)S(1)} fusion(bf16[32,4096]{1,0:T(8,128)(2,1)S(1)} %all_gather.14, bf16[1,4096,384]{2,1,0:T(8,128)(2,1)} %param.23), kind=kOutput, calls=%fused_computation.29 | convolution fusion | flops 100663296 | bytes 3457024 | tf_op jit(solution)/shard_map/dot_general | solution.py:121
  195.0 2.4 %fusion.29 = bf16[32,384]{1,0:T(8,128)(2,1)S(1)} fusion(bf16[32,4096]{1,0:T(8,128)(2,1)S(1)} %all_gather.14, bf16[1,4096,384]{2,1,0:T(8,128)(2,1)} %param.24, f32[32,384]{1,0:T(8,128)S(1)} %fusion.21), kind=kOutput, calls=%fused_computation.34 | convolution fusion | flops 100737024 | bytes 3481600 | tf_op jit(solution)/shard_map/dot_general | solution.py:122
  197.5 5.3 %all_gather.15 = bf16[32,1536]{1,0:T(8,128)(2,1)S(1)} all-gather(bf16[32,384]{1,0:T(8,128)(2,1)S(1)} %fusion.29), channel_id=1, replica_groups=mesh['grp'=2,'ctx'=4,'exp'=4] {'ctx'}, dimensions={1}, use_global_device_ids=true | all-gather | bytes 122880 | tf_op jit(solution)/shard_map/all_gather | solution.py:125
  202.8 0.6 fusion.23
  203.5 6.6 %all_to_all.33 = bf16[4,4,2,1024]{3,2,1,0:T(2,128)(2,1)S(1)} all-to-all(bf16[4,4,2,1024]{3,2,1,0:T(2,128)(2,1)S(1)} %reshape.157), channel_id=1, replica_groups=mesh['grp'=2,'ctx'=4,'exp'=4] {'ctx'}, dimensions={0} | all-to-all | bytes 131072 | tf_op jit(solution)/shard_map/all_to_all | solution.py:133
  210.2 8.1 %all_to_all.34 = bf16[1,4,2,4096]{3,2,0,1:T(2,128)(2,1)S(1)} all-to-all(bf16[1,4,2,4096]{3,2,0,1:T(2,128)(2,1)S(1)} %bitcast.92), channel_id=1, replica_groups=mesh['grp'=2,'ctx'=4,'exp'=4] {'exp'}, dimensions={1} | all-to-all | bytes 131072 | tf_op jit(solution)/shard_map/all_to_all | solution.py:132
  218.3 1.4 convolution_convert_fusion.1
  (18 shorter events, 0.3 us)
Async XLA Ops:
  7.2 195.6 %copy-start = (bf16[1,1536,1024]{2,1,0:T(8,128)(2,1)S(1)}, bf16[1,1536,1024]{2,1,0:T(8,128)(2,1)}, u32[]{:S(2)}) copy-start(bf16[1,1536,1024]{2,1,0:T(8,128)(2,1)} %param.25) | copy-start | bytes 9437188
  7.2 111.0 %all-gather.2.cloned.1.call-start = ((), (), s32[]{:S(2)}) async-start(), calls=%async_computation.4 | async-start | bytes 20971520 | tf_op jit(solution)/shard_map/all_gather | solution.py:95
  7.9 166.4 %reduce-scatter.2.cloned.1.call-start = ((), (), s32[]{:S(2)}) async-start(), calls=%async_computation.5 | async-start | bytes 2621440 | tf_op jit(solution)/shard_map/reduce_scatter | solution.py:98
  32.8 97.5 %copy-start.1 = (s32[64,8]{0,1:T(8,128)S(1)}, s32[64,8]{0,1:T(8,128)}, u32[]{:S(2)}) copy-start(s32[64,8]{0,1:T(8,128)} %param.21) | copy-start | bytes 6148
  32.8 99.6 %copy-start.2 = (f32[64,8]{0,1:T(8,128)S(1)}, f32[64,8]{0,1:T(8,128)}, u32[]{:S(2)}) copy-start(f32[64,8]{0,1:T(8,128)} %param.22) | copy-start | bytes 6148
  32.8 143.8 %copy-start.3 = (f32[4096]{0:T(1024)S(1)}, f32[4096]{0:T(1024)}, u32[]{:S(2)}) copy-start(f32[4096]{0:T(1024)} %param.20) | copy-start | bytes 49156
Sparse Core Ops, SparseCore 0:
  9.6 108.6 all-gather.1
  130.4 43.8 reduce-scatter.1
where the time goes:
time: 227 us
  waiting for transfers between devices  127 us (56%)
  blocking collectives  43 us (19%)
  matrix products  28.3 us (12%)
  between operations  14.9 us (7%)
  other arithmetic  10.3 us (5%)
  local copies, waits for them, and re-layouts  3.15 us (1%)
    all_gather x1, waiting for transfers between devices, shards(): lax.all_gather(out_weight, 'ctx', axis=1, tiled=True)  84.2 us
    reduce_scatter x1, waiting for transfers between devices, shards(): lax.psum_scatter(partial_sum.astype(jnp.bfloat16), 'exp', scatter_dimensi...  41.8 us
    dot_general x1, matrix products, shards(): jnp.dot(heads_out, lax.all_gather(out_weight, 'ctx', axis=1, tiled=True),...  12 us
    all_gather x1, blocking collectives, shards(): piece = lax.all_gather(stacked, 'ctx', axis=1, tiled=True)  8.62 us
    all_to_all x1, blocking collectives, shards(): lax.all_to_all(outgoing, 'exp', split_axis=0, concat_axis=0, tiled=True)  8.55 us
    all_to_all x1, blocking collectives, shards(): lax.all_to_all(lax.all_to_all(returned_local, 'ctx', split_axis=0, concat...  8.11 us
    all_to_all x1, blocking collectives, shards(): lax.all_to_all(returned_local, 'ctx', split_axis=0, concat_axis=3, tiled=...  6.65 us
    all_gather x1, blocking collectives, shards(): lax.all_gather(arrived.reshape(-1, width_model), 'ctx', axis=0, tiled=True)  5.79 us
  transfers between devices with their start and end apart: 2, of which 2 were waited for; matrix products, arithmetic and copies ran while one was open for 8% of the time, Pallas kernels for 0%

commit v1 on v0

v1 whole, which is shorter than its diff:
```python
import functools

import jax
import jax.numpy as jnp
from jax import lax
from jax.experimental import pallas as pl
from jax.experimental.pallas import tpu as pltpu
from jax.sharding import PartitionSpec as P

QH = 64
KVH = 4
HD = 128
CAP = 2
DOCMAX = 512
KEY_TILE = 128
MIB = 1024 * 1024
LOG2E = 1.4426950408889634


def swap(x, axis, mask):
    count = lax.axis_size(axis)
    return lax.ppermute(x, axis, [(i, i ^ mask) for i in range(count)])


def shift(x, axis, by):
    count = lax.axis_size(axis)
    return lax.ppermute(x, axis, [(i, i + by) for i in range(count - by)])


def reversed_bits(count):
    order = [0]
    step = 1
    while step < count:
        order = [2 * i for i in order]
        order = order + [i + 1 for i in order]
        step *= 2
    return order


def vmem(limit_mib):
    return pltpu.CompilerParams(vmem_limit_bytes=limit_mib * MIB)


def whole_vmem(count):
    return [pl.BlockSpec(memory_space=pltpu.VMEM)] * count


def slot_ranks(routes_t, flight):
    tokens = routes_t.shape[1]
    rows = [jnp.max((routes_t == j).astype(jnp.float32), axis=0, keepdims=True) for j in range(flight)]
    named = jnp.concatenate(rows, axis=0)
    before = lax.broadcasted_iota(jnp.int32, (tokens, tokens), 0) < lax.broadcasted_iota(
        jnp.int32, (tokens, tokens), 1
    )
    ranks = jnp.dot(
        named.astype(jnp.bfloat16), before.astype(jnp.bfloat16), preferred_element_type=jnp.float32
    )
    return named, ranks


def spread(rows, count, source_of):
    have = rows.shape[0]
    out_row = lax.broadcasted_iota(jnp.int32, (count, have), 0)
    col = lax.broadcasted_iota(jnp.int32, (count, have), 1)
    onehot = (col == source_of(out_row)).astype(jnp.bfloat16)
    return jnp.dot(onehot, rows.astype(jnp.bfloat16), preferred_element_type=jnp.float32)


def prep_kernel(routes_ref, weights_ref, residual_ref, rows_ref, combine_ref, *, flight):
    routes_t = routes_ref[...]
    named, ranks = slot_ranks(routes_t, flight)
    slots = flight * CAP
    slot_row = lax.broadcasted_iota(jnp.int32, (slots, 1), 0)
    named_s = spread(named, slots, lambda i: i // CAP)
    ranks_s = spread(ranks, slots, lambda i: i // CAP)
    want = (slot_row % CAP).astype(jnp.float32)
    hit = (named_s > 0.5) & (ranks_s == want)
    picks = jnp.where(hit, 1.0, 0.0).astype(jnp.bfloat16)
    rows_ref[...] = jnp.dot(picks, residual_ref[...], preferred_element_type=jnp.float32).astype(
        jnp.bfloat16
    )
    scores = weights_ref[...]
    shares = scores / jnp.sum(scores, axis=0, keepdims=True)
    parts = [
        jnp.sum(jnp.where(routes_t == j, shares, 0.0), axis=0, keepdims=True) for j in range(flight)
    ]
    for j in range(flight):
        for r in range(CAP):
            line = j * CAP + r
            combine_ref[line : line + 1, :] = jnp.where(hit[line : line + 1, :], parts[j], 0.0)


def prep(routes_t, weights_t, residual, flight):
    tokens = residual.shape[0]
    width = residual.shape[1]
    return pl.pallas_call(
        functools.partial(prep_kernel, flight=flight),
        out_shape=(
            jax.ShapeDtypeStruct((flight * CAP, width), jnp.bfloat16),
            jax.ShapeDtypeStruct((flight * CAP, tokens), jnp.float32),
        ),
        in_specs=whole_vmem(3),
        out_specs=whole_vmem(2),
        compiler_params=vmem(16),
        name="prep",
    )(routes_t, weights_t, residual)


def attention_kernel(
    lengths_ref,
    q_ref,
    kv_far_ref,
    kv_near_ref,
    kv_own_ref,
    routes_ref,
    *refs,
    heads,
    homes,
    halves,
    reach,
):
    out_refs = refs[:halves]
    routed_ref = refs[halves]
    k_all, v_all = refs[halves + 1 :]
    tokens = q_ref.shape[0]
    top = routes_ref.shape[1]
    block_tokens = tokens // homes
    sub = block_tokens // halves
    ctx_index = lax.axis_index("ctx")
    exp_index = lax.axis_index("exp")
    first = ctx_index * tokens
    for place, ref in enumerate((kv_far_ref, kv_near_ref, kv_own_ref)):
        k_all[place * tokens : (place + 1) * tokens, :] = ref[0]
        v_all[place * tokens : (place + 1) * tokens, :] = ref[1]
    order = reversed_bits(homes)
    window = reach + KEY_TILE
    docs = lengths_ref.shape[0]
    scale = LOG2E / HD**0.5

    for half in range(halves):

        @pl.loop(0, homes)
        def one_home(home):
            row0 = home * block_tokens + half * sub
            row0 = pl.multiple_of(row0, sub)
            key0 = pl.multiple_of(row0 // KEY_TILE * KEY_TILE, KEY_TILE)
            query_pos = first + row0 + lax.broadcasted_iota(jnp.int32, (sub, 1), 0)
            starts = jnp.zeros((sub, 1), jnp.int32)
            bound = jnp.int32(0)
            for i in range(docs):
                starts = jnp.where(query_pos >= bound, bound, starts)
                bound = bound + lengths_ref[i]
            key_pos = first + key0 - reach + lax.broadcasted_iota(jnp.int32, (sub, window), 1)
            allowed = (key_pos <= query_pos) & (key_pos >= starts)
            bias = jnp.where(allowed, 0.0, -1e30)
            queries = jnp.concatenate(
                [q_ref[pl.ds(row0, sub), h * HD : (h + 1) * HD] for h in range(heads)], axis=0
            )
            k = k_all[pl.ds(key0, window), :]
            v = v_all[pl.ds(key0, window), :]
            scores = lax.dot_general(
                queries, k, (((1,), (1,)), ((), ())), preferred_element_type=jnp.float32
            )
            scores = scores.reshape(heads, sub, window) * scale + bias[None]
            best = jnp.max(scores, axis=2, keepdims=True)
            probs = jnp.exp2(scores - best)
            total = jnp.sum(probs, axis=2, keepdims=True)
            mixed = jnp.dot(
                probs.reshape(heads * sub, window).astype(jnp.bfloat16),
                v,
                preferred_element_type=jnp.float32,
            )
            result = (mixed / total.reshape(heads * sub, 1)).astype(jnp.bfloat16)
            other = home ^ exp_index
            place = jnp.int32(0)
            for position in range(homes):
                place = jnp.where(other == order[position], position, place)
            at = pl.multiple_of(place * sub, sub)
            for h in range(heads):
                out_refs[half][pl.ds(at, sub), h * HD : (h + 1) * HD] = result[
                    h * sub : (h + 1) * sub
                ]

    flight = homes
    lines = flight * homes * CAP
    line = lax.broadcasted_iota(jnp.int32, (lines, 1), 0)
    line_home = line // CAP % homes
    line_slot = line % CAP
    line_place = line // (CAP * homes)
    line_expert = jnp.zeros((lines, 1), jnp.int32)
    for position in range(flight):
        line_expert = jnp.where(line_place == position, order[position] ^ exp_index, line_expert)
    routed = jnp.zeros((lines, heads * HD), jnp.float32)
    for position in range(homes):
        mask = order[position]
        named, ranks = slot_ranks(routes_ref[mask], flight)
        col = lax.broadcasted_iota(jnp.int32, (lines, flight), 1)
        onehot = (col == line_expert).astype(jnp.bfloat16)
        named_l = jnp.dot(onehot, named.astype(jnp.bfloat16), preferred_element_type=jnp.float32)
        ranks_l = jnp.dot(onehot, ranks.astype(jnp.bfloat16), preferred_element_type=jnp.float32)
        hit = (
            (named_l > 0.5)
            & (ranks_l == line_slot.astype(jnp.float32))
            & (line_home == (mask ^ exp_index))
        )
        picks = jnp.where(hit, 1.0, 0.0)
        for half in range(halves):
            routed = routed + jnp.dot(
                picks[:, half * sub : (half + 1) * sub].astype(jnp.bfloat16),
                out_refs[half][position * sub : (position + 1) * sub, :],
                preferred_element_type=jnp.float32,
            )
    routed_ref[...] = routed.astype(jnp.bfloat16)


def attention(lengths, queries, kv_far, kv_near, kv_own, routes_all, homes, halves, reach):
    tokens, width = queries.shape
    heads = width // HD
    rows = tokens // halves
    flops = 4 * heads * HD * tokens * (reach + KEY_TILE)
    return pl.pallas_call(
        functools.partial(
            attention_kernel, heads=heads, homes=homes, halves=halves, reach=reach
        ),
        out_shape=tuple(jax.ShapeDtypeStruct((rows, width), jnp.bfloat16) for _ in range(halves))
        + (jax.ShapeDtypeStruct((homes * homes * CAP, width), jnp.bfloat16),),
        in_specs=[pl.BlockSpec(memory_space=pltpu.SMEM)] + whole_vmem(5),
        out_specs=tuple(whole_vmem(halves + 1)),
        scratch_shapes=[pltpu.VMEM((3 * tokens, HD), jnp.bfloat16)] * 2,
        compiler_params=vmem(40),
        cost_estimate=pl.CostEstimate(
            flops=flops,
            bytes_accessed=4 * tokens * width,
            transcendentals=heads * tokens * (reach + KEY_TILE),
        ),
        name="attention",
    )(lengths, queries, kv_far, kv_near, kv_own, routes_all)


def hidden_kernel(*refs, count):
    row_refs = refs[:count]
    gain_ref, gate_ref, up_ref, out_ref = refs[count:]
    ctx_index = lax.axis_index("ctx")
    cols = row_refs[0].shape[1]
    rows = [ref[...].astype(jnp.float32) for ref in row_refs]
    square = sum(jnp.sum(row * row, axis=1, keepdims=True) for row in rows)
    inverse = lax.rsqrt(square / (cols * count) + 1e-06)
    gate = None
    up = None
    for place in range(count):
        at = pl.multiple_of((ctx_index ^ place) * cols, cols)
        normed = (rows[place] * inverse * gain_ref[:, pl.ds(at, cols)]).astype(jnp.bfloat16)
        gate_part = jnp.dot(normed, gate_ref[0, pl.ds(at, cols), :], preferred_element_type=jnp.float32)
        up_part = jnp.dot(normed, up_ref[0, pl.ds(at, cols), :], preferred_element_type=jnp.float32)
        gate = gate_part if gate is None else gate + gate_part
        up = up_part if up is None else up + up_part
    out_ref[...] = (gate / (1.0 + jnp.exp(-gate)) * up).astype(jnp.bfloat16)


def hidden_units(pieces, gain, gate_weight, up_weight):
    count = len(pieces)
    rows = pieces[0].shape[0]
    units = gate_weight.shape[2]
    return pl.pallas_call(
        functools.partial(hidden_kernel, count=count),
        out_shape=jax.ShapeDtypeStruct((rows, units), jnp.bfloat16),
        in_specs=whole_vmem(count + 3),
        out_specs=pl.BlockSpec(memory_space=pltpu.VMEM),
        compiler_params=vmem(20),
        name="hidden_units",
    )(*pieces, gain, gate_weight, up_weight)


def down_kernel(*refs, count):
    piece_refs = refs[:count]
    down_ref, out_ref = refs[count:]
    ctx_index = lax.axis_index("ctx")
    units = piece_refs[0].shape[1]
    total = None
    for place in range(count):
        at = pl.multiple_of((ctx_index ^ place) * units, units)
        part = jnp.dot(
            piece_refs[place][...], down_ref[0, pl.ds(at, units), :], preferred_element_type=jnp.float32
        )
        total = part if total is None else total + part
    out_ref[...] = total.astype(jnp.bfloat16)


def down_product(pieces, down_weight):
    count = len(pieces)
    rows = pieces[0].shape[0]
    return pl.pallas_call(
        functools.partial(down_kernel, count=count),
        out_shape=jax.ShapeDtypeStruct((rows, down_weight.shape[2]), jnp.bfloat16),
        in_specs=whole_vmem(count + 1),
        out_specs=pl.BlockSpec(memory_space=pltpu.VMEM),
        compiler_params=vmem(20),
        name="down_product",
    )(*pieces, down_weight)


def attended_kernel(*refs, count):
    piece_refs = refs[:count]
    residual_ref, out_ref = refs[count:]
    ctx_index = lax.axis_index("ctx")
    cols = piece_refs[0].shape[1]
    for place in range(count):
        at = pl.multiple_of((ctx_index ^ place) * cols, cols)
        total = residual_ref[:, pl.ds(at, cols)].astype(jnp.float32) + piece_refs[place][...].astype(
            jnp.float32
        )
        out_ref[:, pl.ds(at, cols)] = total.astype(jnp.bfloat16)


def attended_rows(pieces, residual):
    count = len(pieces)
    return pl.pallas_call(
        functools.partial(attended_kernel, count=count),
        out_shape=jax.ShapeDtypeStruct(residual.shape, jnp.bfloat16),
        in_specs=whole_vmem(count + 1),
        out_specs=pl.BlockSpec(memory_space=pltpu.VMEM),
        compiler_params=vmem(20),
        name="attended_rows",
    )(*pieces, residual)


def gather_pieces(x, axis):
    count = lax.axis_size(axis)
    found = {0: x}
    step = count // 2
    while step >= 1:
        keys = sorted(found)
        if len(keys) == 1:
            moved = [swap(found[0], axis, step)]
        else:
            packed = swap(jnp.stack([found[k] for k in keys]), axis, step)
            moved = [packed[i] for i in range(len(keys))]
        for k, piece in zip(keys, moved):
            found[k ^ step] = piece
        step //= 2
    return [found[k] for k in range(count)]


def sum_over_exp(part):
    step = 1
    total = part
    while total.shape[0] > 1:
        half = total.shape[0] // 2
        arrived = swap(total[half:].astype(jnp.bfloat16), "exp", step)
        total = total[:half].astype(jnp.float32) + arrived.astype(jnp.float32)
        step *= 2
    return total[0]


def shards(
    queries,
    keys,
    values,
    doc_lengths,
    residual_in,
    out_weight,
    norm_gain,
    routes,
    route_weights,
    gate_weight,
    up_weight,
    down_weight,
):
    tokens = queries.shape[0]
    local_heads = queries.shape[1] // HD
    n_ctx = lax.axis_size("ctx")
    homes = lax.axis_size("exp")
    flight = gate_weight.shape[0] * homes
    ctx_index = lax.axis_index("ctx")
    exp_index = lax.axis_index("exp")
    block_tokens = residual_in.shape[0]
    width = residual_in.shape[1]
    cols = out_weight.shape[1]
    halves = 2 if block_tokens % 32 == 0 else 1
    sub = block_tokens // halves
    reach = DOCMAX

    kv_head = exp_index * local_heads // (QH // KVH)
    kv_own = jnp.stack(
        [
            lax.dynamic_slice_in_dim(keys, kv_head * HD, HD, 1),
            lax.dynamic_slice_in_dim(values, kv_head * HD, HD, 1),
        ]
    )
    kv_near = shift(kv_own, "ctx", 1)
    kv_far = shift(kv_own, "ctx", 2)
    routes_t = routes.T
    routes_all = jnp.stack(gather_pieces(routes_t, "exp"))
    rows_own, combine = prep(routes_t, route_weights.T, residual_in, flight)
    residual_rows = gather_pieces(rows_own, "ctx")

    *heads_out, routed = attention(
        doc_lengths, queries, kv_far, kv_near, kv_own, routes_all, homes, halves, reach
    )

    def project(rows):
        return jnp.dot(rows, out_weight, preferred_element_type=jnp.float32).astype(jnp.bfloat16)

    routed_pieces = gather_pieces(routed, "ctx")
    order = reversed_bits(homes)
    lines = flight * homes * CAP
    line = jnp.arange(lines, dtype=jnp.int32)
    expert = jnp.asarray(order, jnp.int32)[line // (CAP * homes)] ^ exp_index
    source = jnp.where(line // CAP % homes == exp_index, expert * CAP + line % CAP, -1)
    place_rows = (source[:, None] == jnp.arange(flight * CAP, dtype=jnp.int32)[None, :]).astype(
        jnp.bfloat16
    )
    routed_all = jnp.stack(routed_pieces)
    own_cols = [
        lax.dynamic_slice_in_dim(rows, ctx_index * cols, cols, 1) for rows in residual_rows
    ]
    extra = jnp.einsum(
        "ls,csd->cld", place_rows, jnp.stack(own_cols), preferred_element_type=jnp.float32
    )
    routed_part = (
        jnp.einsum("cld,dn->cln", routed_all, out_weight, preferred_element_type=jnp.float32) + extra
    ).astype(jnp.bfloat16)
    routed_part = jnp.transpose(
        routed_part.reshape(n_ctx, flight, homes * CAP, cols), (1, 0, 2, 3)
    )
    routed_sum = sum_over_exp(routed_part).astype(jnp.bfloat16)
    absolute = jnp.stack(
        [lax.dynamic_index_in_dim(routed_sum, ctx_index ^ k, 0, keepdims=False) for k in range(n_ctx)]
    )
    stream_rows = gather_pieces(absolute.reshape(-1, cols), "ctx")
    hidden = hidden_units(stream_rows, norm_gain[None, :], gate_weight, up_weight)
    produced = down_product(gather_pieces(hidden, "ctx"), down_weight)
    back = lax.all_to_all(
        produced.reshape(n_ctx * homes, CAP, cols),
        ("ctx", "exp"),
        split_axis=0,
        concat_axis=0,
        tiled=True,
    )
    back = jnp.transpose(back.reshape(n_ctx, flight * CAP, cols), (1, 0, 2)).reshape(
        flight * CAP, width
    )
    combined = jnp.dot(combine.T, back.astype(jnp.float32), precision=lax.Precision.HIGHEST)

    near = [swap(rows, "ctx", 1) for rows in heads_out]
    far = []
    for rows in heads_out:
        found = {0: rows}
        step = n_ctx // 2
        while step >= 2:
            for k in sorted(found):
                found[k ^ step] = swap(found[k], "ctx", step)
            step //= 2
        for k in sorted(found):
            found[k ^ 1] = swap(found[k], "ctx", 1) if k else None
        far.append(found)

    def reduced(blocks):
        part = project(jnp.concatenate(blocks, axis=0))
        part = part.reshape(len(blocks), homes, sub, cols)
        return sum_over_exp(jnp.transpose(part, (1, 0, 2, 3)))

    first = reduced(heads_out + near).astype(jnp.bfloat16)
    pieces = {0: list(first[:halves]), 1: list(first[halves:])}
    for half in range(halves):
        keys_far = [k for k in sorted(far[half]) if k > 1]
        got = reduced([far[half][k] for k in keys_far]).astype(jnp.bfloat16)
        for i, k in enumerate(keys_far):
            pieces.setdefault(k, []).append(got[i])
    returned = [jnp.concatenate(pieces[0], axis=0)]
    for k in range(1, n_ctx):
        returned.append(
            jnp.concatenate([swap(piece, "ctx", k) for piece in pieces[k]], axis=0)
        )
    attended = attended_rows(returned, residual_in)
    return (attended, combined.astype(jnp.bfloat16))


def solution(mesh):
    placed = (
        P(("grp", "ctx"), "exp"),
        P(("grp", "ctx"), None),
        P(("grp", "ctx"), None),
        P("grp"),
        P(("grp", "ctx", "exp"), None),
        P("exp", "ctx"),
        P(),
        P(("grp", "ctx", "exp"), None),
        P(("grp", "ctx", "exp"), None),
        P("exp", None, "ctx"),
        P("exp", None, "ctx"),
        P("exp", None, "ctx"),
    )
    return jax.shard_map(
        shards,
        mesh=mesh,
        in_specs=placed,
        out_specs=(P(("grp", "ctx", "exp"), None), P(("grp", "ctx", "exp"), None)),
        check_vma=False,
    )
```

time: 227 us -> 131 us (0.58)
  waiting for transfers between devices: 127 us -> 52.1 us
  blocking collectives: 43 us -> 0 us
  starting transfers between devices: 0.08 us -> 40.9 us
  matrix products: 28.3 us -> 12.3 us
  between operations: 14.9 us -> 1.22 us
  Pallas kernels: 0 us -> 12.6 us
  other arithmetic: 10.3 us -> 2.84 us
  local copies, waits for them, and re-layouts: 3.15 us -> 8.41 us
    all_gather x1 -> x0, waiting for transfers between devices: 84.2 us -> none  [shards(): lax.all_gather(out_weight, 'ctx', axis=1, tiled=True)]
    ppermute x0 -> x32, waiting for transfers between devices: none -> 52.1 us  [the longest x30 52 us: swap(): return lax.ppermute(x, axis, [(i, i ^ mask) for i in range(count)])]
    reduce_scatter x1 -> x0, waiting for transfers between devices: 41.8 us -> none  [shards(): lax.psum_scatter(partial_sum.astype(jnp.bfloat16), 'exp', scatter_dimensi...]
    ppermute x0 -> x32, starting transfers between devices: none -> 36 us  [the longest x30 29.7 us: swap(): return lax.ppermute(x, axis, [(i, i ^ mask) for i in range(count)])]
    all_to_all x3 -> x0, blocking collectives: 23.3 us -> none  [the longest x1 8.55 us: shards(): lax.all_to_all(outgoing, 'exp', split_axis=0, concat_axis=0, tiled=True)]
    all_gather x3 -> x0, blocking collectives: 19.7 us -> none  [the longest x1 8.62 us: shards(): piece = lax.all_gather(stacked, 'ctx', axis=1, tiled=True)]
    pallas_call x0 -> x5, Pallas kernels: none -> 12.6 us  [the longest x1 9.49 us: attention(): pl.pallas_call(functools.partial(attention_kernel, heads=heads, homes=hom...]
    dot_general x7 -> x6, matrix products: 24.3 us -> 12.3 us  [the longest x3 9.87 us: project(): jnp.dot(rows, out_weight, preferred_element_type=jnp.float32)]
  transfers between devices with their start and end apart: 2 -> 33, of which waited for: 2 -> 17; matrix products, arithmetic and copies ran while one was open for 8% -> 11% of each run, Pallas kernels for 0% -> 9%
where the time goes in v1:
time: 131 us; the launch traced here: 130 us
  waiting for transfers between devices  52.1 us (40%)
  starting transfers between devices  40.9 us (31%)
  Pallas kernels  12.6 us (10%)
  matrix products  12.3 us (9%)
  local copies, waits for them, and re-layouts  8.41 us (6%)
  other arithmetic  2.84 us (2%)
    ppermute x30, waiting for transfers between devices, swap(): return lax.ppermute(x, axis, [(i, i ^ mask) for i in range(count)])  52 us
    ppermute x30, starting transfers between devices, swap(): return lax.ppermute(x, axis, [(i, i ^ mask) for i in range(count)])  29.7 us
    dot_general x3, matrix products, project(): jnp.dot(rows, out_weight, preferred_element_type=jnp.float32)  9.87 us
    pallas_call x1, Pallas kernels, attention(): pl.pallas_call(functools.partial(attention_kernel, heads=heads, homes=hom...  9.49 us
    unnamed x26, local copies, waits for them, and re-layouts  6.35 us
    ppermute x2, starting transfers between devices, shift(): return lax.ppermute(x, axis, [(i, i + by) for i in range(count - by)])  6.32 us
    all_to_all x1, starting transfers between devices, shards(): lax.all_to_all(produced.reshape(n_ctx * homes, CAP, cols), ('ctx', 'exp')...  4.81 us
  transfers between devices with their start and end apart: 33, of which 17 were waited for; matrix products, arithmetic and copies ran while one was open for 11% of the time, Pallas kernels for 9%

profile of v1, /device:TPU:0, one launch (start us, length us, event | category | flops | bytes accessed | tf_op | source)
XLA Modules:
  0.0 130.3 jit_solution(8141004782245011393)
XLA Ops:
  0.7 0.9 dynamic-slice_bitcast_fusion
  1.6 4.8 %collective-permute-start = (bf16[2,256,128]{2,1,0:T(8,128)(2,1)S(1)}, bf16[2,256,128]{2,1,0:T(8,128)(2,1)S(1)}, u32[]{:S(2)}, u32[]{:S(2)}) collective-permute-start(bf16[2,256,128]{2,1,0:T(8,128)(2,1)S(1)} %pad_maximum_fusion.1.kv_own_ref), channel_id=1, source_target_pairs={{0,8},{4,12},{1,9},{5,13},{2,10},{6,14},{3,11},{7,15},{16,24},{20,... | collective-permute-start | bytes 393224 | tf_op jit(solution)/shard_map/ppermute | solution.py:27
  6.4 1.5 %collective-permute-start.1 = (bf16[2,256,128]{2,1,0:T(8,128)(2,1)S(1)}, bf16[2,256,128]{2,1,0:T(8,128)(2,1)S(1)}, u32[]{:S(2)}, u32[]{:S(2)}) collective-permute-start(bf16[2,256,128]{2,1,0:T(8,128)(2,1)S(1)} %pad_maximum_fusion.1.kv_own_ref), channel_id=1, source_target_pairs={{0,4},{4,8},{8,12},{1,5},{5,9},{9,13},{2,6},{6,10},{10,14},{3,7},{... | collective-permute-start | bytes 393224 | tf_op jit(solution)/shard_map/ppermute | solution.py:27
  7.9 2.7 %collective-permute-start.2 = (s32[8,64]{1,0:T(8,128)}, s32[8,64]{1,0:T(8,128)S(1)}, u32[]{:S(2)}, u32[]{:S(2)}) collective-permute-start(s32[8,64]{1,0:T(8,128)} %bitcast.105), channel_id=1, source_target_pairs={{0,2},{1,3},{2,0},{3,1},{4,6},{5,7},{6,4},{7,5},{8,10},{9,11},{10,... | collective-permute-start | bytes 6152 | tf_op jit(solution)/shard_map/ppermute | solution.py:22
  10.6 1.0 copy-done.3
  11.6 0.7 copy-done.5
  13.5 0.7 pad_add_fusion.1
  14.2 1.6 %collective-permute-start.3 = (s32[2,8,64]{2,1,0:T(8,128)S(1)}, s32[2,8,64]{2,1,0:T(8,128)S(1)}, u32[]{:S(2)}, u32[]{:S(2)}) collective-permute-start(s32[2,8,64]{2,1,0:T(8,128)S(1)} %pad_add_fusion.1), channel_id=1, source_target_pairs={{0,1},{1,0},{2,3},{3,2},{4,5},{5,4},{6,7},{7,6},{8,9},{9,8},{10,11... | collective-permute-start | bytes 12296 | tf_op jit(solution)/shard_map/ppermute | solution.py:22
  15.8 2.1 %collective-permute-done.3 = s32[2,8,64]{2,1,0:T(8,128)S(1)} collective-permute-done((s32[2,8,64]{2,1,0:T(8,128)S(1)}, s32[2,8,64]{2,1,0:T(8,128)S(1)}, u32[]{:S(2)}, u32[]{:S(2)}) %collective-permute-start.3) | collective-permute-done | bytes 4128 | tf_op jit(solution)/shard_map/ppermute | solution.py:22
  17.8 0.7 pad_add_fusion.routes_ref
  18.7 1.2 copy-done.8
  20.6 9.5 %attention.1 = (bf16[128,2048]{1,0:T(8,128)(2,1)}, bf16[128,2048]{1,0:T(8,128)(2,1)}, bf16[32,2048]{1,0:T(8,128)(2,1)S(1)}) custom-call(s32[24]{0:T(128)S(1)} %copy-done.9, bf16[256,2048]{1,0:T(8,128)(2,1)S(1)} %copy-done.8, bf16[2,256,128]{2,1,0:T(8,128)(2,1)S(1)} %collective-permute-done.kv_far_ref, ...), custom_call_target="tpu_custom_call" | custom-call | flops 1342177280 | bytes 2097152 | tf_op jit(solution)/shard_map/attention/pallas_call | solution.py:221
  30.1 2.1 %collective-permute-start.22 = (bf16[32,2048]{1,0:T(8,128)(2,1)S(1)}, bf16[32,2048]{1,0:T(8,128)(2,1)S(1)}, u32[]{:S(2)}, u32[]{:S(2)}) collective-permute-start(bf16[32,2048]{1,0:T(8,128)(2,1)S(1)} %get-tuple-element.10), channel_id=1, source_target_pairs={{0,8},{4,12},{8,0},{12,4},{1,9},{5,13},{9,1},{13,5},{2,10},{6,14},... | collective-permute-start | bytes 393224 | tf_op jit(solution)/shard_map/ppermute | solution.py:22
  32.1 4.1 %collective-permute-done.22 = bf16[32,2048]{1,0:T(8,128)(2,1)S(1)} collective-permute-done((bf16[32,2048]{1,0:T(8,128)(2,1)S(1)}, bf16[32,2048]{1,0:T(8,128)(2,1)S(1)}, u32[]{:S(2)}, u32[]{:S(2)}) %collective-permute-start.22) | collective-permute-done | bytes 131104 | tf_op jit(solution)/shard_map/ppermute | solution.py:22
  36.6 1.2 collective-permute-done.23
  37.9 0.7 fusion.19
  38.7 1.6 %collective-permute-start.26 = (bf16[2,4,8,1024]{3,2,0,1:T(8,128)(2,1)S(1)}, bf16[2,4,8,1024]{3,2,0,1:T(8,128)(2,1)S(1)}, u32[]{:S(2)}, u32[]{:S(2)}) collective-permute-start(bf16[2,4,8,1024]{3,2,0,1:T(8,128)(2,1)S(1)} %slice.166), channel_id=1, source_target_pairs={{0,1},{1,0},{2,3},{3,2},{4,5},{5,4},{6,7},{7,6},{8,9},{9,8},{10,11... | collective-permute-start | bytes 393224 | tf_op jit(solution)/shard_map/ppermute | solution.py:22
  40.3 4.0 %collective-permute-done.26 = bf16[2,4,8,1024]{3,2,0,1:T(8,128)(2,1)S(1)} collective-permute-done((bf16[2,4,8,1024]{3,2,0,1:T(8,128)(2,1)S(1)}, bf16[2,4,8,1024]{3,2,0,1:T(8,128)(2,1)S(1)}, u32[]{:S(2)}, u32[]{:S(2)}) %collective-permute-start.26) | collective-permute-done | bytes 131104 | tf_op jit(solution)/shard_map/ppermute | solution.py:22
  44.3 1.6 %collective-permute-start.27 = (bf16[1,4,8,1024]{3,2,0,1:T(8,128)(2,1)S(1)}, bf16[1,4,8,1024]{3,2,0,1:T(8,128)(2,1)}, u32[]{:S(2)}, u32[]{:S(2)}) collective-permute-start(bf16[1,4,8,1024]{3,2,0,1:T(8,128)(2,1)S(1)} %slice.204), channel_id=1, source_target_pairs={{0,2},{1,3},{2,0},{3,1},{4,6},{5,7},{6,4},{7,5},{8,10},{9,11},{10,... | collective-permute-start | bytes 196616 | tf_op jit(solution)/shard_map/ppermute | solution.py:22
  45.9 3.8 %collective-permute-done.27 = bf16[1,4,8,1024]{3,2,0,1:T(8,128)(2,1)} collective-permute-done((bf16[1,4,8,1024]{3,2,0,1:T(8,128)(2,1)S(1)}, bf16[1,4,8,1024]{3,2,0,1:T(8,128)(2,1)}, u32[]{:S(2)}, u32[]{:S(2)}) %collective-permute-start.27) | collective-permute-done | bytes 65568 | tf_op jit(solution)/shard_map/ppermute | solution.py:22
  49.7 0.9 fusion.38
  50.6 1.8 %collective-permute-start.28 = (bf16[32,1024]{1,0:T(8,128)(2,1)S(1)}, bf16[32,1024]{1,0:T(8,128)(2,1)S(1)}, u32[]{:S(2)}, u32[]{:S(2)}) collective-permute-start(bf16[32,1024]{1,0:T(8,128)(2,1)S(1)} %get-tuple-element.27.refs_0_), channel_id=1, source_target_pairs={{0,8},{4,12},{8,0},{12,4},{1,9},{5,13},{9,1},{13,5},{2,10},{6,14},... | collective-permute-start | bytes 196616 | tf_op jit(solution)/shard_map/ppermute | solution.py:22
  53.0 2.0 %collective-permute-done.28.refs_2_ = bf16[32,1024]{1,0:T(8,128)(2,1)S(1)} collective-permute-done((bf16[32,1024]{1,0:T(8,128)(2,1)S(1)}, bf16[32,1024]{1,0:T(8,128)(2,1)S(1)}, u32[]{:S(2)}, u32[]{:S(2)}) %collective-permute-start.28) | collective-permute-done | bytes 65568 | tf_op jit(solution)/shard_map/ppermute | solution.py:22
  55.1 1.3 %collective-permute-done.29 = bf16[2,32,1024]{2,1,0:T(8,128)(2,1)S(1)} collective-permute-done((bf16[2,32,1024]{2,1,0:T(8,128)(2,1)S(1)}, bf16[2,32,1024]{2,1,0:T(8,128)(2,1)S(1)}, u32[]{:S(2)}, u32[]{:S(2)}) %collective-permute-start.29) | collective-permute-done | bytes 131104 | tf_op jit(solution)/shard_map/ppermute | solution.py:22
  56.5 1.9 %copy-done.1 = bf16[1,4096,384]{2,1,0:T(8,128)(2,1)S(1)} copy-done((bf16[1,4096,384]{2,1,0:T(8,128)(2,1)S(1)}, bf16[1,4096,384]{2,1,0:T(8,128)(2,1)}, u32[]{:S(2)}) %copy-start.1) | copy-done | bytes 3145752
  58.3 1.1 hidden_units.1.refs_0_
  59.4 1.8 %collective-permute-start.30 = (bf16[32,384]{1,0:T(8,128)(2,1)S(1)}, bf16[32,384]{1,0:T(8,128)(2,1)S(1)}, u32[]{:S(2)}, u32[]{:S(2)}) collective-permute-start(bf16[32,384]{1,0:T(8,128)(2,1)S(1)} %hidden_units.1.refs_0_), channel_id=1, source_target_pairs={{0,8},{4,12},{8,0},{12,4},{1,9},{5,13},{9,1},{13,5},{2,10},{6,14},... | collective-permute-start | bytes 73736 | tf_op jit(solution)/shard_map/ppermute | solution.py:22
  61.5 1.7 %collective-permute-start.10 = (bf16[128,2048]{1,0:T(8,128)(2,1)}, bf16[128,2048]{1,0:T(8,128)(2,1)S(1)}, u32[]{:S(2)}, u32[]{:S(2)}) collective-permute-start(bf16[128,2048]{1,0:T(8,128)(2,1)} %get-tuple-element.7), channel_id=1, source_target_pairs={{0,8},{4,12},{8,0},{12,4},{1,9},{5,13},{9,1},{13,5},{2,10},{6,14},... | collective-permute-start | bytes 1572872 | tf_op jit(solution)/shard_map/ppermute | solution.py:22
  63.4 3.6 %fusion.10 = bf16[512,1024]{1,0:T(8,128)(2,1)S(1)} fusion(bf16[2048,1024]{1,0:T(8,128)(2,1)S(1)} %copy-done.11, bf16[128,2048]{1,0:T(8,128)(2,1)S(1)} %collective-permute-done.5, bf16[128,2048]{1,0:T(8,128)(2,1)S(1)} %collective-permute-done.4, bf16[128,2048]{1,0:T(8,128)(2,1)} %get-tuple-element.8, bf16[128,2048]{1,0:T(8,128)(2,1)} %get-tuple-element.7), kind=kOutput, calls=%fused_computation.11 | convolution fusion | flops 2156396544 | bytes 7340032 | tf_op jit(solution)/shard_map/dot_general | solution.py:402
  67.2 1.6 %collective-permute-start.6 = (bf16[2,4,32,1024]{3,2,1,0:T(8,128)(2,1)S(1)}, bf16[2,4,32,1024]{3,2,1,0:T(8,128)(2,1)S(1)}, u32[]{:S(2)}, u32[]{:S(2)}) collective-permute-start(bf16[2,4,32,1024]{3,2,1,0:T(8,128)(2,1)S(1)} %slice.146), channel_id=1, source_target_pairs={{0,1},{1,0},{2,3},{3,2},{4,5},{5,4},{6,7},{7,6},{8,9},{9,8},{10,11... | collective-permute-start | bytes 1572872 | tf_op jit(solution)/shard_map/ppermute | solution.py:22
  70.2 4.8 %all-to-all-start = ((bf16[16,2,1024]{2,1,0:T(2,128)(2,1)}), bf16[16,2,1024]{2,1,0:T(2,128)(2,1)S(1)}, u32[]{:S(2)}, u32[]{:S(2)}) async-start(bf16[16,2,1024]{2,1,0:T(2,128)(2,1)} %reshape.139), calls=%async_computation | async-start | bytes 131072 | tf_op jit(solution)/shard_map/all_to_all | solution.py:433
  75.1 1.2 collective-permute-done.15
  76.3 10.7 %collective-permute-done.10 = bf16[128,2048]{1,0:T(8,128)(2,1)S(1)} collective-permute-done((bf16[128,2048]{1,0:T(8,128)(2,1)}, bf16[128,2048]{1,0:T(8,128)(2,1)S(1)}, u32[]{:S(2)}, u32[]{:S(2)}) %collective-permute-start.10) | collective-permute-done | bytes 524320 | tf_op jit(solution)/shard_map/ppermute | solution.py:22
  87.1 1.4 %convolution_convert_fusion = bf16[64,4096]{1,0:T(8,128)(2,1)} fusion(f32[8,64]{1,0:T(8,128)S(1)} %get-tuple-element.9, bf16[8,4096]{1,0:T(8,128)(2,1)S(1)} %bitcast.120), kind=kOutput, calls=%fused_computation | convolution fusion | flops 25427968 | bytes 591872 | tf_op jit(solution)/shard_map/dot_general | solution.py:443
  89.4 4.0 %convolution_convert_fusion.1 = bf16[256,1024]{1,0:T(8,128)(2,1)S(1)} fusion(bf16[2048,1024]{1,0:T(8,128)(2,1)} %param.18, bf16[128,2048]{1,0:T(8,128)(2,1)} %collective-permute-done.16, bf16[128,2048]{1,0:T(8,128)(2,1)S(1)} %collective-permute-done.15), kind=kOutput, calls=%fused_computation.12 | convolution fusion | flops 1076101120 | bytes 5767168 | tf_op jit(solution)/shard_map/dot_general | solution.py:402
  93.5 1.8 %collective-permute-start.17 = (bf16[2,2,32,1024]{3,2,1,0:T(8,128)(2,1)S(1)}, bf16[2,2,32,1024]{3,2,1,0:T(8,128)(2,1)S(1)}, u32[]{:S(2)}, u32[]{:S(2)}) collective-permute-start(bf16[2,2,32,1024]{3,2,1,0:T(8,128)(2,1)S(1)} %slice.155), channel_id=1, source_target_pairs={{0,1},{1,0},{2,3},{3,2},{4,5},{5,4},{6,7},{7,6},{8,9},{9,8},{10,11... | collective-permute-start | bytes 786440 | tf_op jit(solution)/shard_map/ppermute | solution.py:22
  95.3 2.3 %convolution_convert_fusion.2 = bf16[256,1024]{1,0:T(8,128)(2,1)S(1)} fusion(bf16[2048,1024]{1,0:T(8,128)(2,1)S(1)} %copy-done.12, bf16[128,2048]{1,0:T(8,128)(2,1)} %collective-permute-done.11, bf16[128,2048]{1,0:T(8,128)(2,1)S(1)} %collective-permute-done.10), kind=kOutput, calls=%fused_computation.13 | convolution fusion | flops 1076101120 | bytes 5767168 | tf_op jit(solution)/shard_map/dot_general | solution.py:402
  98.1 6.0 %collective-permute-done.7 = bf16[1,4,32,1024]{3,2,1,0:T(8,128)(2,1)S(1)} collective-permute-done((bf16[1,4,32,1024]{3,2,1,0:T(8,128)(2,1)S(1)}, bf16[1,4,32,1024]{3,2,1,0:T(8,128)(2,1)S(1)}, u32[]{:S(2)}, u32[]{:S(2)}) %collective-permute-start.7) | collective-permute-done | bytes 262176 | tf_op jit(solution)/shard_map/ppermute | solution.py:22
  104.8 2.4 %collective-permute-done.17 = bf16[2,2,32,1024]{3,2,1,0:T(8,128)(2,1)S(1)} collective-permute-done((bf16[2,2,32,1024]{3,2,1,0:T(8,128)(2,1)S(1)}, bf16[2,2,32,1024]{3,2,1,0:T(8,128)(2,1)S(1)}, u32[]{:S(2)}, u32[]{:S(2)}) %collective-permute-start.17) | collective-permute-done | bytes 262176 | tf_op jit(solution)/shard_map/ppermute | solution.py:22
  107.3 2.1 %collective-permute-start.18 = (bf16[1,2,32,1024]{3,2,1,0:T(8,128)(2,1)S(1)}, bf16[1,2,32,1024]{3,2,1,0:T(8,128)(2,1)S(1)}, u32[]{:S(2)}, u32[]{:S(2)}) collective-permute-start(bf16[1,2,32,1024]{3,2,1,0:T(8,128)(2,1)S(1)} %slice.202), channel_id=1, source_target_pairs={{0,2},{1,3},{2,0},{3,1},{4,6},{5,7},{6,4},{7,5},{8,10},{9,11},{10,... | collective-permute-start | bytes 393224 | tf_op jit(solution)/shard_map/ppermute | solution.py:22
  109.4 4.4 %collective-permute-done.12 = bf16[2,2,32,1024]{3,2,1,0:T(8,128)(2,1)S(1)} collective-permute-done((bf16[2,2,32,1024]{3,2,1,0:T(8,128)(2,1)S(1)}, bf16[2,2,32,1024]{3,2,1,0:T(8,128)(2,1)S(1)}, u32[]{:S(2)}, u32[]{:S(2)}) %collective-permute-start.12) | collective-permute-done | bytes 262176 | tf_op jit(solution)/shard_map/ppermute | solution.py:22
  113.9 3.2 %collective-permute-start.13 = (bf16[1,2,32,1024]{3,2,1,0:T(8,128)(2,1)S(1)}, bf16[1,2,32,1024]{3,2,1,0:T(8,128)(2,1)S(1)}, u32[]{:S(2)}, u32[]{:S(2)}) collective-permute-start(bf16[1,2,32,1024]{3,2,1,0:T(8,128)(2,1)S(1)} %slice.203), channel_id=1, source_target_pairs={{0,2},{1,3},{2,0},{3,1},{4,6},{5,7},{6,4},{7,5},{8,10},{9,11},{10,... | collective-permute-start | bytes 393224 | tf_op jit(solution)/shard_map/ppermute | solution.py:22
  117.1 1.0 collective-permute-start.19
  118.1 4.6 %collective-permute-done.13 = bf16[1,2,32,1024]{3,2,1,0:T(8,128)(2,1)S(1)} collective-permute-done((bf16[1,2,32,1024]{3,2,1,0:T(8,128)(2,1)S(1)}, bf16[1,2,32,1024]{3,2,1,0:T(8,128)(2,1)S(1)}, u32[]{:S(2)}, u32[]{:S(2)}) %collective-permute-start.13) | collective-permute-done | bytes 131104 | tf_op jit(solution)/shard_map/ppermute | solution.py:22
  124.0 1.3 collective-permute-start.20
  125.3 2.5 %collective-permute-done.14 = bf16[32,1024]{1,0:T(8,128)(2,1)S(1)} collective-permute-done((bf16[32,1024]{1,0:T(8,128)(2,1)S(1)}, bf16[32,1024]{1,0:T(8,128)(2,1)S(1)}, u32[]{:S(2)}, u32[]{:S(2)}) %collective-permute-start.14) | collective-permute-done | bytes 65568 | tf_op jit(solution)/shard_map/ppermute | solution.py:22
  127.9 1.4 %collective-permute-done.20 = bf16[32,1024]{1,0:T(8,128)(2,1)S(1)} collective-permute-done((bf16[32,1024]{1,0:T(8,128)(2,1)S(1)}, bf16[32,1024]{1,0:T(8,128)(2,1)S(1)}, u32[]{:S(2)}, u32[]{:S(2)}) %collective-permute-start.20) | collective-permute-done | bytes 65568 | tf_op jit(solution)/shard_map/ppermute | solution.py:22
  129.3 0.9 attended_rows.1
  (102 shorter events, 8.8 us)
Async XLA Ops:
  1.6 17.1 %collective-permute-start = (bf16[2,256,128]{2,1,0:T(8,128)(2,1)S(1)}, bf16[2,256,128]{2,1,0:T(8,128)(2,1)S(1)}, u32[]{:S(2)}, u32[]{:S(2)}) collective-permute-start(bf16[2,256,128]{2,1,0:T(8,128)(2,1)S(1)} %pad_maximum_fusion.1.kv_own_ref), channel_id=1, source_target_pairs={{0,8},{4,12},{1,9},{5,13},{2,10},{6,14},{3,11},{7,15},{16,24},{20,... | collective-permute-start | bytes 393224 | tf_op jit(solution)/shard_map/ppermute | solution.py:27
  6.4 12.2 %collective-permute-start.1 = (bf16[2,256,128]{2,1,0:T(8,128)(2,1)S(1)}, bf16[2,256,128]{2,1,0:T(8,128)(2,1)S(1)}, u32[]{:S(2)}, u32[]{:S(2)}) collective-permute-start(bf16[2,256,128]{2,1,0:T(8,128)(2,1)S(1)} %pad_maximum_fusion.1.kv_own_ref), channel_id=1, source_target_pairs={{0,4},{4,8},{8,12},{1,5},{5,9},{9,13},{2,6},{6,10},{10,14},{3,7},{... | collective-permute-start | bytes 393224 | tf_op jit(solution)/shard_map/ppermute | solution.py:27
  7.9 5.6 %collective-permute-start.2 = (s32[8,64]{1,0:T(8,128)}, s32[8,64]{1,0:T(8,128)S(1)}, u32[]{:S(2)}, u32[]{:S(2)}) collective-permute-start(s32[8,64]{1,0:T(8,128)} %bitcast.105), channel_id=1, source_target_pairs={{0,2},{1,3},{2,0},{3,1},{4,6},{5,7},{6,4},{7,5},{8,10},{9,11},{10,... | collective-permute-start | bytes 6152 | tf_op jit(solution)/shard_map/ppermute | solution.py:22
  10.6 1.0 copy-start.3
  11.6 0.7 copy-start.5
  12.3 0.7 copy-start.7
  13.4 5.2 %collective-permute-start.24 = (bf16[8,4096]{1,0:T(8,128)(2,1)S(1)}, bf16[8,4096]{1,0:T(8,128)(2,1)S(1)}, u32[]{:S(2)}, u32[]{:S(2)}) collective-permute-start(bf16[8,4096]{1,0:T(8,128)(2,1)S(1)} %get-tuple-element.11), channel_id=1, source_target_pairs={{0,8},{4,12},{8,0},{12,4},{1,9},{5,13},{9,1},{13,5},{2,10},{6,14},... | collective-permute-start | bytes 196616 | tf_op jit(solution)/shard_map/ppermute | solution.py:22
  14.2 3.7 %collective-permute-start.3 = (s32[2,8,64]{2,1,0:T(8,128)S(1)}, s32[2,8,64]{2,1,0:T(8,128)S(1)}, u32[]{:S(2)}, u32[]{:S(2)}) collective-permute-start(s32[2,8,64]{2,1,0:T(8,128)S(1)} %pad_add_fusion.1), channel_id=1, source_target_pairs={{0,1},{1,0},{2,3},{3,2},{4,5},{5,4},{6,7},{7,6},{8,9},{9,8},{10,11... | collective-permute-start | bytes 12296 | tf_op jit(solution)/shard_map/ppermute | solution.py:22
  18.6 13.6 %collective-permute-start.25 = (bf16[2,8,4096]{2,1,0:T(8,128)(2,1)S(1)}, bf16[2,8,4096]{2,1,0:T(8,128)(2,1)S(1)}, u32[]{:S(2)}, u32[]{:S(2)}) collective-permute-start(bf16[2,8,4096]{2,1,0:T(8,128)(2,1)S(1)} %pad_maximum_fusion.6), channel_id=1, source_target_pairs={{0,4},{4,0},{8,12},{12,8},{1,5},{5,1},{9,13},{13,9},{2,6},{6,2},{1... | collective-permute-start | bytes 393224 | tf_op jit(solution)/shard_map/ppermute | solution.py:22
  18.7 1.2 copy-start.8
  19.9 0.7 copy-start.9
  20.6 17.3 %copy-start.10 = (bf16[2048,1024]{1,0:T(8,128)(2,1)S(1)}, bf16[2048,1024]{1,0:T(8,128)(2,1)}, u32[]{:S(2)}) copy-start(bf16[2048,1024]{1,0:T(8,128)(2,1)} %param.18) | copy-start | bytes 12582916
  30.1 6.2 %collective-permute-start.22 = (bf16[32,2048]{1,0:T(8,128)(2,1)S(1)}, bf16[32,2048]{1,0:T(8,128)(2,1)S(1)}, u32[]{:S(2)}, u32[]{:S(2)}) collective-permute-start(bf16[32,2048]{1,0:T(8,128)(2,1)S(1)} %get-tuple-element.10), channel_id=1, source_target_pairs={{0,8},{4,12},{8,0},{12,4},{1,9},{5,13},{9,1},{13,5},{2,10},{6,14},... | collective-permute-start | bytes 393224 | tf_op jit(solution)/shard_map/ppermute | solution.py:22
  36.3 1.6 %collective-permute-start.23 = (bf16[2,32,2048]{2,1,0:T(8,128)(2,1)S(1)}, bf16[2,32,2048]{2,1,0:T(8,128)(2,1)S(1)}, u32[]{:S(2)}, u32[]{:S(2)}) collective-permute-start(bf16[2,32,2048]{2,1,0:T(8,128)(2,1)S(1)} %pad_maximum_fusion), channel_id=1, source_target_pairs={{0,4},{4,0},{8,12},{12,8},{1,5},{5,1},{9,13},{13,9},{2,6},{6,2},{1... | collective-permute-start | bytes 786440 | tf_op jit(solution)/shard_map/ppermute | solution.py:22
  37.9 18.5 %copy-start = (bf16[1,4096,384]{2,1,0:T(8,128)(2,1)S(1)}, bf16[1,4096,384]{2,1,0:T(8,128)(2,1)}, u32[]{:S(2)}) copy-start(bf16[1,4096,384]{2,1,0:T(8,128)(2,1)} %refs_5_.1) | copy-start | bytes 9437188
  37.9 18.5 %copy-start.6 = (f32[4096]{0:T(1024)S(1)}, f32[4096]{0:T(1024)}, u32[]{:S(2)}) copy-start(f32[4096]{0:T(1024)} %param.19) | copy-start | bytes 49156
  38.7 5.6 %collective-permute-start.26 = (bf16[2,4,8,1024]{3,2,0,1:T(8,128)(2,1)S(1)}, bf16[2,4,8,1024]{3,2,0,1:T(8,128)(2,1)S(1)}, u32[]{:S(2)}, u32[]{:S(2)}) collective-permute-start(bf16[2,4,8,1024]{3,2,0,1:T(8,128)(2,1)S(1)} %slice.166), channel_id=1, source_target_pairs={{0,1},{1,0},{2,3},{3,2},{4,5},{5,4},{6,7},{7,6},{8,9},{9,8},{10,11... | collective-permute-start | bytes 393224 | tf_op jit(solution)/shard_map/ppermute | solution.py:22
  44.3 5.4 %collective-permute-start.27 = (bf16[1,4,8,1024]{3,2,0,1:T(8,128)(2,1)S(1)}, bf16[1,4,8,1024]{3,2,0,1:T(8,128)(2,1)}, u32[]{:S(2)}, u32[]{:S(2)}) collective-permute-start(bf16[1,4,8,1024]{3,2,0,1:T(8,128)(2,1)S(1)} %slice.204), channel_id=1, source_target_pairs={{0,2},{1,3},{2,0},{3,1},{4,6},{5,7},{6,4},{7,5},{8,10},{9,11},{10,... | collective-permute-start | bytes 196616 | tf_op jit(solution)/shard_map/ppermute | solution.py:22
  50.6 4.3 %collective-permute-start.28 = (bf16[32,1024]{1,0:T(8,128)(2,1)S(1)}, bf16[32,1024]{1,0:T(8,128)(2,1)S(1)}, u32[]{:S(2)}, u32[]{:S(2)}) collective-permute-start(bf16[32,1024]{1,0:T(8,128)(2,1)S(1)} %get-tuple-element.27.refs_0_), channel_id=1, source_target_pairs={{0,8},{4,12},{8,0},{12,4},{1,9},{5,13},{9,1},{13,5},{2,10},{6,14},... | collective-permute-start | bytes 196616 | tf_op jit(solution)/shard_map/ppermute | solution.py:22
  52.5 11.0 %collective-permute-start.5 = (bf16[128,2048]{1,0:T(8,128)(2,1)}, bf16[128,2048]{1,0:T(8,128)(2,1)S(1)}, u32[]{:S(2)}, u32[]{:S(2)}) collective-permute-start(bf16[128,2048]{1,0:T(8,128)(2,1)} %get-tuple-element.8), channel_id=1, source_target_pairs={{0,4},{4,0},{8,12},{12,8},{1,5},{5,1},{9,13},{13,9},{2,6},{6,2},{1... | collective-permute-start | bytes 1572872 | tf_op jit(solution)/shard_map/ppermute | solution.py:22
  52.5 11.0 %collective-permute-start.4 = (bf16[128,2048]{1,0:T(8,128)(2,1)}, bf16[128,2048]{1,0:T(8,128)(2,1)S(1)}, u32[]{:S(2)}, u32[]{:S(2)}) collective-permute-start(bf16[128,2048]{1,0:T(8,128)(2,1)} %get-tuple-element.7), channel_id=1, source_target_pairs={{0,4},{4,0},{8,12},{12,8},{1,5},{5,1},{9,13},{13,9},{2,6},{6,2},{1... | collective-permute-start | bytes 1572872 | tf_op jit(solution)/shard_map/ppermute | solution.py:22
  55.0 1.4 %collective-permute-start.29 = (bf16[2,32,1024]{2,1,0:T(8,128)(2,1)S(1)}, bf16[2,32,1024]{2,1,0:T(8,128)(2,1)S(1)}, u32[]{:S(2)}, u32[]{:S(2)}) collective-permute-start(bf16[2,32,1024]{2,1,0:T(8,128)(2,1)S(1)} %pad_maximum_fusion.7), channel_id=1, source_target_pairs={{0,4},{4,0},{8,12},{12,8},{1,5},{5,1},{9,13},{13,9},{2,6},{6,2},{1... | collective-permute-start | bytes 393224 | tf_op jit(solution)/shard_map/ppermute | solution.py:22
  56.4 1.9 %copy-start.1 = (bf16[1,4096,384]{2,1,0:T(8,128)(2,1)S(1)}, bf16[1,4096,384]{2,1,0:T(8,128)(2,1)}, u32[]{:S(2)}) copy-start(bf16[1,4096,384]{2,1,0:T(8,128)(2,1)} %refs_6_.1) | copy-start | bytes 9437188
  58.3 5.1 %copy-start.11 = (bf16[2048,1024]{1,0:T(8,128)(2,1)S(1)}, bf16[2048,1024]{1,0:T(8,128)(2,1)}, u32[]{:S(2)}) copy-start(bf16[2048,1024]{1,0:T(8,128)(2,1)} %param.18) | copy-start | bytes 12582916
  59.4 3.9 %collective-permute-start.30 = (bf16[32,384]{1,0:T(8,128)(2,1)S(1)}, bf16[32,384]{1,0:T(8,128)(2,1)S(1)}, u32[]{:S(2)}, u32[]{:S(2)}) collective-permute-start(bf16[32,384]{1,0:T(8,128)(2,1)S(1)} %hidden_units.1.refs_0_), channel_id=1, source_target_pairs={{0,8},{4,12},{8,0},{12,4},{1,9},{5,13},{9,1},{13,5},{2,10},{6,14},... | collective-permute-start | bytes 73736 | tf_op jit(solution)/shard_map/ppermute | solution.py:22
  61.2 15.0 %collective-permute-start.15 = (bf16[128,2048]{1,0:T(8,128)(2,1)}, bf16[128,2048]{1,0:T(8,128)(2,1)S(1)}, u32[]{:S(2)}, u32[]{:S(2)}) collective-permute-start(bf16[128,2048]{1,0:T(8,128)(2,1)} %get-tuple-element.8), channel_id=1, source_target_pairs={{0,8},{4,12},{8,0},{12,4},{1,9},{5,13},{9,1},{13,5},{2,10},{6,14},... | collective-permute-start | bytes 1572872 | tf_op jit(solution)/shard_map/ppermute | solution.py:22
  61.5 25.5 %collective-permute-start.10 = (bf16[128,2048]{1,0:T(8,128)(2,1)}, bf16[128,2048]{1,0:T(8,128)(2,1)S(1)}, u32[]{:S(2)}, u32[]{:S(2)}) collective-permute-start(bf16[128,2048]{1,0:T(8,128)(2,1)} %get-tuple-element.7), channel_id=1, source_target_pairs={{0,8},{4,12},{8,0},{12,4},{1,9},{5,13},{9,1},{13,5},{2,10},{6,14},... | collective-permute-start | bytes 1572872 | tf_op jit(solution)/shard_map/ppermute | solution.py:22
  63.3 5.4 %collective-permute-start.31 = (bf16[2,32,384]{2,1,0:T(8,128)(2,1)S(1)}, bf16[2,32,384]{2,1,0:T(8,128)(2,1)S(1)}, u32[]{:S(2)}, u32[]{:S(2)}) collective-permute-start(bf16[2,32,384]{2,1,0:T(8,128)(2,1)S(1)} %pad_maximum_fusion.9), channel_id=1, source_target_pairs={{0,4},{4,0},{8,12},{12,8},{1,5},{5,1},{9,13},{13,9},{2,6},{6,2},{1... | collective-permute-start | bytes 147464 | tf_op jit(solution)/shard_map/ppermute | solution.py:22
  67.0 1.9 %copy-start.2 = (bf16[1,1536,1024]{2,1,0:T(8,128)(2,1)S(1)}, bf16[1,1536,1024]{2,1,0:T(8,128)(2,1)}, u32[]{:S(2)}) copy-start(bf16[1,1536,1024]{2,1,0:T(8,128)(2,1)} %refs_4_.3) | copy-start | bytes 9437188
  67.2 21.3 %collective-permute-start.6 = (bf16[2,4,32,1024]{3,2,1,0:T(8,128)(2,1)S(1)}, bf16[2,4,32,1024]{3,2,1,0:T(8,128)(2,1)S(1)}, u32[]{:S(2)}, u32[]{:S(2)}) collective-permute-start(bf16[2,4,32,1024]{3,2,1,0:T(8,128)(2,1)S(1)} %slice.146), channel_id=1, source_target_pairs={{0,1},{1,0},{2,3},{3,2},{4,5},{5,4},{6,7},{7,6},{8,9},{9,8},{10,11... | collective-permute-start | bytes 1572872 | tf_op jit(solution)/shard_map/ppermute | solution.py:22
  70.2 16.8 %all-to-all-start = ((bf16[16,2,1024]{2,1,0:T(2,128)(2,1)}), bf16[16,2,1024]{2,1,0:T(2,128)(2,1)S(1)}, u32[]{:S(2)}, u32[]{:S(2)}) async-start(bf16[16,2,1024]{2,1,0:T(2,128)(2,1)} %reshape.139), calls=%async_computation | async-start | bytes 131072 | tf_op jit(solution)/shard_map/all_to_all | solution.py:433
  76.3 13.2 %collective-permute-start.16 = (bf16[128,2048]{1,0:T(8,128)(2,1)S(1)}, bf16[128,2048]{1,0:T(8,128)(2,1)}, u32[]{:S(2)}, u32[]{:S(2)}) collective-permute-start(bf16[128,2048]{1,0:T(8,128)(2,1)S(1)} %collective-permute-done.15), channel_id=1, source_target_pairs={{0,4},{4,0},{8,12},{12,8},{1,5},{5,1},{9,13},{13,9},{2,6},{6,2},{1... | collective-permute-start | bytes 1572872 | tf_op jit(solution)/shard_map/ppermute | solution.py:22
  87.0 8.3 %collective-permute-start.11 = (bf16[128,2048]{1,0:T(8,128)(2,1)S(1)}, bf16[128,2048]{1,0:T(8,128)(2,1)}, u32[]{:S(2)}, u32[]{:S(2)}) collective-permute-start(bf16[128,2048]{1,0:T(8,128)(2,1)S(1)} %collective-permute-done.10), channel_id=1, source_target_pairs={{0,4},{4,0},{8,12},{12,8},{1,5},{5,1},{9,13},{13,9},{2,6},{6,2},{1... | collective-permute-start | bytes 1572872 | tf_op jit(solution)/shard_map/ppermute | solution.py:22
  88.7 6.6 %copy-start.12 = (bf16[2048,1024]{1,0:T(8,128)(2,1)S(1)}, bf16[2048,1024]{1,0:T(8,128)(2,1)}, u32[]{:S(2)}) copy-start(bf16[2048,1024]{1,0:T(8,128)(2,1)} %param.18) | copy-start | bytes 12582916
  88.7 15.4 %collective-permute-start.7 = (bf16[1,4,32,1024]{3,2,1,0:T(8,128)(2,1)S(1)}, bf16[1,4,32,1024]{3,2,1,0:T(8,128)(2,1)S(1)}, u32[]{:S(2)}, u32[]{:S(2)}) collective-permute-start(bf16[1,4,32,1024]{3,2,1,0:T(8,128)(2,1)S(1)} %slice.201), channel_id=1, source_target_pairs={{0,2},{1,3},{2,0},{3,1},{4,6},{5,7},{6,4},{7,5},{8,10},{9,11},{10,... | collective-permute-start | bytes 786440 | tf_op jit(solution)/shard_map/ppermute | solution.py:22
  93.5 13.7 %collective-permute-start.17 = (bf16[2,2,32,1024]{3,2,1,0:T(8,128)(2,1)S(1)}, bf16[2,2,32,1024]{3,2,1,0:T(8,128)(2,1)S(1)}, u32[]{:S(2)}, u32[]{:S(2)}) collective-permute-start(bf16[2,2,32,1024]{3,2,1,0:T(8,128)(2,1)S(1)} %slice.155), channel_id=1, source_target_pairs={{0,1},{1,0},{2,3},{3,2},{4,5},{5,4},{6,7},{7,6},{8,9},{9,8},{10,11... | collective-permute-start | bytes 786440 | tf_op jit(solution)/shard_map/ppermute | solution.py:22
  97.6 31.7 %copy-start.4 = (bf16[64,4096]{1,0:T(8,128)(2,1)S(1)}, bf16[64,4096]{1,0:T(8,128)(2,1)}, u32[]{:S(2)}) copy-start(bf16[64,4096]{1,0:T(8,128)(2,1)} %residual_ref.1) | copy-start | bytes 1572868
  97.7 16.1 %collective-permute-start.12 = (bf16[2,2,32,1024]{3,2,1,0:T(8,128)(2,1)S(1)}, bf16[2,2,32,1024]{3,2,1,0:T(8,128)(2,1)S(1)}, u32[]{:S(2)}, u32[]{:S(2)}) collective-permute-start(bf16[2,2,32,1024]{3,2,1,0:T(8,128)(2,1)S(1)} %slice.150), channel_id=1, source_target_pairs={{0,1},{1,0},{2,3},{3,2},{4,5},{5,4},{6,7},{7,6},{8,9},{9,8},{10,11... | collective-permute-start | bytes 786440 | tf_op jit(solution)/shard_map/ppermute | solution.py:22
  104.2 19.2 %collective-permute-start.9 = (bf16[32,1024]{1,0:T(8,128)(2,1)S(1)}, bf16[32,1024]{1,0:T(8,128)(2,1)S(1)}, u32[]{:S(2)}, u32[]{:S(2)}) collective-permute-start(bf16[32,1024]{1,0:T(8,128)(2,1)S(1)} %get-tuple-element.15), channel_id=1, source_target_pairs={{0,4},{4,0},{8,12},{12,8},{1,5},{5,1},{9,13},{13,9},{2,6},{6,2},{1... | collective-permute-start | bytes 196616 | tf_op jit(solution)/shard_map/ppermute | solution.py:22
  104.3 19.2 %collective-permute-start.8 = (bf16[32,1024]{1,0:T(8,128)(2,1)S(1)}, bf16[32,1024]{1,0:T(8,128)(2,1)S(1)}, u32[]{:S(2)}, u32[]{:S(2)}) collective-permute-start(bf16[32,1024]{1,0:T(8,128)(2,1)S(1)} %get-tuple-element.14), channel_id=1, source_target_pairs={{0,4},{4,0},{8,12},{12,8},{1,5},{5,1},{9,13},{13,9},{2,6},{6,2},{1... | collective-permute-start | bytes 196616 | tf_op jit(solution)/shard_map/ppermute | solution.py:22
  107.3 9.8 %collective-permute-start.18 = (bf16[1,2,32,1024]{3,2,1,0:T(8,128)(2,1)S(1)}, bf16[1,2,32,1024]{3,2,1,0:T(8,128)(2,1)S(1)}, u32[]{:S(2)}, u32[]{:S(2)}) collective-permute-start(bf16[1,2,32,1024]{3,2,1,0:T(8,128)(2,1)S(1)} %slice.202), channel_id=1, source_target_pairs={{0,2},{1,3},{2,0},{3,1},{4,6},{5,7},{6,4},{7,5},{8,10},{9,11},{10,... | collective-permute-start | bytes 393224 | tf_op jit(solution)/shard_map/ppermute | solution.py:22
  113.9 8.9 %collective-permute-start.13 = (bf16[1,2,32,1024]{3,2,1,0:T(8,128)(2,1)S(1)}, bf16[1,2,32,1024]{3,2,1,0:T(8,128)(2,1)S(1)}, u32[]{:S(2)}, u32[]{:S(2)}) collective-permute-start(bf16[1,2,32,1024]{3,2,1,0:T(8,128)(2,1)S(1)} %slice.203), channel_id=1, source_target_pairs={{0,2},{1,3},{2,0},{3,1},{4,6},{5,7},{6,4},{7,5},{8,10},{9,11},{10,... | collective-permute-start | bytes 393224 | tf_op jit(solution)/shard_map/ppermute | solution.py:22
  117.1 8.1 %collective-permute-start.19 = (bf16[32,1024]{1,0:T(8,128)(2,1)S(1)}, bf16[32,1024]{1,0:T(8,128)(2,1)S(1)}, u32[]{:S(2)}, u32[]{:S(2)}) collective-permute-start(bf16[32,1024]{1,0:T(8,128)(2,1)S(1)} %get-tuple-element.25), channel_id=1, source_target_pairs={{0,8},{4,12},{8,0},{12,4},{1,9},{5,13},{9,1},{13,5},{2,10},{6,14},... | collective-permute-start | bytes 196616 | tf_op jit(solution)/shard_map/ppermute | solution.py:22
  122.8 5.0 %collective-permute-start.14 = (bf16[32,1024]{1,0:T(8,128)(2,1)S(1)}, bf16[32,1024]{1,0:T(8,128)(2,1)S(1)}, u32[]{:S(2)}, u32[]{:S(2)}) collective-permute-start(bf16[32,1024]{1,0:T(8,128)(2,1)S(1)} %get-tuple-element.23), channel_id=1, source_target_pairs={{0,8},{4,12},{8,0},{12,4},{1,9},{5,13},{9,1},{13,5},{2,10},{6,14},... | collective-permute-start | bytes 196616 | tf_op jit(solution)/shard_map/ppermute | solution.py:22
  123.5 4.5 %collective-permute-start.21 = (bf16[32,1024]{1,0:T(8,128)(2,1)S(1)}, bf16[32,1024]{1,0:T(8,128)(2,1)S(1)}, u32[]{:S(2)}, u32[]{:S(2)}) collective-permute-start(bf16[32,1024]{1,0:T(8,128)(2,1)S(1)} %get-tuple-element.24), channel_id=1, source_target_pairs={{0,12},{4,8},{8,4},{12,0},{1,13},{5,9},{9,5},{13,1},{2,14},{6,10},... | collective-permute-start | bytes 196616 | tf_op jit(solution)/shard_map/ppermute | solution.py:22
  124.0 5.3 %collective-permute-start.20 = (bf16[32,1024]{1,0:T(8,128)(2,1)S(1)}, bf16[32,1024]{1,0:T(8,128)(2,1)S(1)}, u32[]{:S(2)}, u32[]{:S(2)}) collective-permute-start(bf16[32,1024]{1,0:T(8,128)(2,1)S(1)} %get-tuple-element.22), channel_id=1, source_target_pairs={{0,12},{4,8},{8,4},{12,0},{1,13},{5,9},{9,5},{13,1},{2,14},{6,10},... | collective-permute-start | bytes 196616 | tf_op jit(solution)/shard_map/ppermute | solution.py:22

commit v2 on v1

v2 whole, which is shorter than its diff:
```python
import functools

import jax
import jax.numpy as jnp
from jax import lax
from jax.experimental import pallas as pl
from jax.experimental.pallas import tpu as pltpu
from jax.sharding import PartitionSpec as P

QH = 64
KVH = 4
HD = 128
CAP = 2
DOCMAX = 512
KEY_TILE = 128
MIB = 1024 * 1024
LOG2E = 1.4426950408889634


def swap(x, axis, mask):
    count = lax.axis_size(axis)
    return lax.ppermute(x, axis, [(i, i ^ mask) for i in range(count)])


def shift(x, axis, by):
    count = lax.axis_size(axis)
    return lax.ppermute(x, axis, [(i, i + by) for i in range(count - by)])


def reversed_bits(count):
    order = [0]
    step = 1
    while step < count:
        order = [2 * i for i in order]
        order = order + [i + 1 for i in order]
        step *= 2
    return order


def vmem(limit_mib):
    return pltpu.CompilerParams(vmem_limit_bytes=limit_mib * MIB)


def whole_vmem(count):
    return [pl.BlockSpec(memory_space=pltpu.VMEM)] * count


def anywhere(count):
    return [pl.BlockSpec(memory_space=pl.ANY)] * count


FREE = pl.CostEstimate(flops=0, bytes_accessed=0, transcendentals=0)


def slot_ranks(routes_t, flight):
    tokens = routes_t.shape[1]
    rows = [jnp.max((routes_t == j).astype(jnp.float32), axis=0, keepdims=True) for j in range(flight)]
    named = jnp.concatenate(rows, axis=0)
    before = lax.broadcasted_iota(jnp.int32, (tokens, tokens), 0) < lax.broadcasted_iota(
        jnp.int32, (tokens, tokens), 1
    )
    ranks = jnp.dot(
        named.astype(jnp.bfloat16), before.astype(jnp.bfloat16), preferred_element_type=jnp.float32
    )
    return named, ranks


def spread(rows, count, source_of):
    have = rows.shape[0]
    out_row = lax.broadcasted_iota(jnp.int32, (count, have), 0)
    col = lax.broadcasted_iota(jnp.int32, (count, have), 1)
    onehot = (col == source_of(out_row)).astype(jnp.bfloat16)
    return jnp.dot(onehot, rows.astype(jnp.bfloat16), preferred_element_type=jnp.float32)


def attention_kernel(
    lengths_ref,
    q_ref,
    kv_far_ref,
    kv_near_ref,
    kv_own_ref,
    out_ref,
    k_all,
    v_all,
    *,
    heads,
    homes,
    half,
    sub,
):
    tokens = q_ref.shape[0]
    block_tokens = tokens // homes
    first = lax.axis_index("ctx") * tokens
    exp_index = lax.axis_index("exp")
    for place, ref in enumerate((kv_far_ref, kv_near_ref, kv_own_ref)):
        k_all[place * tokens : (place + 1) * tokens, :] = ref[0]
        v_all[place * tokens : (place + 1) * tokens, :] = ref[1]
    order = reversed_bits(homes)
    reach = DOCMAX
    window = reach + KEY_TILE
    docs = lengths_ref.shape[0]
    scale = LOG2E / HD**0.5

    @pl.loop(0, homes)
    def one_home(home):
        row0 = pl.multiple_of(home * block_tokens + half * sub, sub)
        key0 = pl.multiple_of(row0 // KEY_TILE * KEY_TILE, KEY_TILE)
        query_pos = first + row0 + lax.broadcasted_iota(jnp.int32, (sub, 1), 0)
        starts = jnp.zeros((sub, 1), jnp.int32)
        bound = jnp.int32(0)
        for i in range(docs):
            starts = jnp.where(query_pos >= bound, bound, starts)
            bound = bound + lengths_ref[i]
        key_pos = first + key0 - reach + lax.broadcasted_iota(jnp.int32, (sub, window), 1)
        allowed = (key_pos <= query_pos) & (key_pos >= starts)
        bias = jnp.where(allowed, 0.0, -1e30)
        queries = jnp.concatenate(
            [q_ref[pl.ds(row0, sub), h * HD : (h + 1) * HD] for h in range(heads)], axis=0
        )
        k = k_all[pl.ds(key0, window), :]
        v = v_all[pl.ds(key0, window), :]
        scores = lax.dot_general(
            queries, k, (((1,), (1,)), ((), ())), preferred_element_type=jnp.float32
        )
        scores = scores.reshape(heads, sub, window) * scale + bias[None]
        best = jnp.max(scores, axis=2, keepdims=True)
        probs = jnp.exp2(scores - best)
        total = jnp.sum(probs, axis=2, keepdims=True)
        mixed = jnp.dot(
            probs.reshape(heads * sub, window).astype(jnp.bfloat16),
            v,
            preferred_element_type=jnp.float32,
        )
        result = (mixed / total.reshape(heads * sub, 1)).astype(jnp.bfloat16)
        other = home ^ exp_index
        place = jnp.int32(0)
        for position in range(homes):
            place = jnp.where(other == order[position], position, place)
        at = pl.multiple_of(place * sub, sub)
        for h in range(heads):
            out_ref[pl.ds(at, sub), h * HD : (h + 1) * HD] = result[h * sub : (h + 1) * sub]


def attention(lengths, queries, kv_far, kv_near, kv_own, homes, half, sub):
    tokens, width = queries.shape
    return pl.pallas_call(
        functools.partial(
            attention_kernel, heads=width // HD, homes=homes, half=half, sub=sub
        ),
        out_shape=jax.ShapeDtypeStruct((homes * sub, width), jnp.bfloat16),
        in_specs=[pl.BlockSpec(memory_space=pltpu.SMEM)] + whole_vmem(4),
        out_specs=pl.BlockSpec(memory_space=pltpu.VMEM),
        scratch_shapes=[pltpu.VMEM((3 * tokens, HD), jnp.bfloat16)] * 2,
        compiler_params=vmem(24),
        cost_estimate=FREE,
        name="attention_" + str(half),
    )(lengths, queries, kv_far, kv_near, kv_own)


def pick_kernel(residual_ref, *refs, homes, halves, sub):
    routes_refs = refs[:homes]
    heads_refs = refs[homes : homes + halves]
    out_ref = refs[-1]
    exp_index = lax.axis_index("exp")
    order = reversed_bits(homes)
    width = heads_refs[0].shape[1]
    flight = homes
    lines = flight * homes * CAP
    line = lax.broadcasted_iota(jnp.int32, (lines, 1), 0)
    line_home = line // CAP % homes
    line_slot = (line % CAP).astype(jnp.float32)
    line_place = line // (CAP * homes)
    line_expert = jnp.zeros((lines, 1), jnp.int32)
    for position in range(flight):
        line_expert = jnp.where(line_place == position, order[position] ^ exp_index, line_expert)
    col = lax.broadcasted_iota(jnp.int32, (lines, flight), 1)
    onehot = (col == line_expert).astype(jnp.bfloat16)
    routed = jnp.zeros((lines, width), jnp.float32)
    for position in range(homes):
        mask = order[position]
        named, ranks = slot_ranks(routes_refs[mask][...], flight)
        named_l = jnp.dot(onehot, named.astype(jnp.bfloat16), preferred_element_type=jnp.float32)
        ranks_l = jnp.dot(onehot, ranks.astype(jnp.bfloat16), preferred_element_type=jnp.float32)
        hit = (named_l > 0.5) & (ranks_l == line_slot) & (line_home == (mask ^ exp_index))
        picks = jnp.where(hit, 1.0, 0.0)
        for half in range(halves):
            routed = routed + jnp.dot(
                picks[:, half * sub : (half + 1) * sub].astype(jnp.bfloat16),
                heads_refs[half][position * sub : (position + 1) * sub, :],
                preferred_element_type=jnp.float32,
            )
    out_ref[:lines, :] = routed.astype(jnp.bfloat16)
    slots = flight * CAP
    named, ranks = slot_ranks(routes_refs[0][...], flight)
    slot = lax.broadcasted_iota(jnp.int32, (slots, 1), 0)
    named_s = spread(named, slots, lambda i: i // CAP)
    ranks_s = spread(ranks, slots, lambda i: i // CAP)
    hit = (named_s > 0.5) & (ranks_s == (slot % CAP).astype(jnp.float32))
    rows = jnp.dot(
        jnp.where(hit, 1.0, 0.0).astype(jnp.bfloat16),
        residual_ref[...],
        preferred_element_type=jnp.float32,
    )
    parts = residual_ref.shape[1] // width
    rows = jnp.concatenate([rows[:, i * width : (i + 1) * width] for i in range(parts)], axis=0)
    out_ref[lines:, :] = rows.astype(jnp.bfloat16)


def pick(residual, routes_pieces, heads_out, sub):
    homes = len(routes_pieces)
    width = heads_out[0].shape[1]
    rows = homes * homes * CAP + homes * CAP * (residual.shape[1] // width)
    return pl.pallas_call(
        functools.partial(pick_kernel, homes=homes, halves=len(heads_out), sub=sub),
        out_shape=jax.ShapeDtypeStruct((rows, width), jnp.bfloat16),
        in_specs=whole_vmem(1 + homes + len(heads_out)),
        out_specs=pl.BlockSpec(memory_space=pltpu.VMEM),
        compiler_params=vmem(16),
        cost_estimate=FREE,
        name="pick",
    )(residual, *routes_pieces, *heads_out)


def routed_kernel(*refs, count, homes, after):
    piece_refs = refs[:count]
    weight_ref = refs[count]
    keep_ref, send_ref = refs[count + 1 + after :]
    ctx_index = lax.axis_index("ctx")
    exp_index = lax.axis_index("exp")
    order = reversed_bits(homes)
    cols = weight_ref.shape[1]
    depth = weight_ref.shape[0]
    flight = homes
    slots = flight * CAP
    lines = flight * homes * CAP
    half = lines // 2
    line = lax.broadcasted_iota(jnp.int32, (lines, slots), 0)
    line_place = line // (CAP * homes)
    expert = jnp.zeros((lines, slots), jnp.int32)
    for position in range(flight):
        expert = jnp.where(line_place == position, order[position] ^ exp_index, expert)
    source = jnp.where(line // CAP % homes == exp_index, expert * CAP + line % CAP, -1)
    onehot = (source == lax.broadcasted_iota(jnp.int32, (lines, slots), 1)).astype(jnp.bfloat16)
    heads = jnp.concatenate([ref[:lines, :] for ref in piece_refs], axis=0)
    product = jnp.dot(heads, weight_ref[...], preferred_element_type=jnp.float32)
    first_col = ctx_index * cols
    column = pl.multiple_of(first_col % depth, HD)
    row = pl.multiple_of(lines + first_col // depth * slots, slots)
    for place in range(count):
        extra = jnp.dot(
            onehot,
            piece_refs[place][pl.ds(row, slots), pl.ds(column, cols)],
            preferred_element_type=jnp.float32,
        )
        total = product[place * lines : (place + 1) * lines] + extra
        keep_ref[ctx_index ^ place] = total[:half].astype(jnp.bfloat16)
        send_ref[ctx_index ^ place] = total[half:].astype(jnp.bfloat16)


def routed_product(pieces, out_weight, homes, after=()):
    count = len(pieces)
    cols = out_weight.shape[1]
    shape = jax.ShapeDtypeStruct((count, homes * homes * CAP // 2, cols), jnp.bfloat16)
    return pl.pallas_call(
        functools.partial(routed_kernel, count=count, homes=homes, after=len(after)),
        out_shape=(shape, shape),
        in_specs=whole_vmem(count + 1) + anywhere(len(after)),
        out_specs=tuple(whole_vmem(2)),
        compiler_params=vmem(32),
        cost_estimate=FREE,
        name="routed_product",
    )(*pieces, out_weight, *after)


def add_middle_kernel(keep_ref, arrived_ref, *refs, last):
    total = keep_ref[...].astype(jnp.float32) + arrived_ref[...].astype(jnp.float32)
    count, rows, cols = total.shape
    if last:
        refs[0][...] = total.reshape(count * rows, cols).astype(refs[0].dtype)
    else:
        refs[0][...] = total[:, : rows // 2].astype(refs[0].dtype)
        refs[1][...] = total[:, rows // 2 :].astype(refs[1].dtype)


def add_middle(keep, arrived, last):
    count, rows, cols = keep.shape
    if last:
        out = jax.ShapeDtypeStruct((count * rows, cols), jnp.bfloat16)
    else:
        out = (
            jax.ShapeDtypeStruct((count, rows // 2, cols), jnp.float32),
            jax.ShapeDtypeStruct((count, rows // 2, cols), jnp.bfloat16),
        )
    return pl.pallas_call(
        functools.partial(add_middle_kernel, last=last),
        out_shape=out,
        in_specs=whole_vmem(2),
        out_specs=whole_vmem(1)[0] if last else tuple(whole_vmem(2)),
        compiler_params=vmem(16),
        cost_estimate=FREE,
        name="routed_sum",
    )(keep, arrived)


def project_kernel(*refs, count, homes, sub, upper, after):
    piece_refs = refs[:count]
    weight_ref = refs[count]
    out_ref = refs[-1]
    half = homes // 2
    begin = half * sub if upper else 0
    weight = weight_ref[...]
    for i in range(0, count, 2):
        pair = piece_refs[i : i + 2]
        rows = jnp.concatenate([ref[begin : begin + half * sub, :] for ref in pair], axis=0)
        product = jnp.dot(rows, weight, preferred_element_type=jnp.float32).astype(jnp.bfloat16)
        for k in range(len(pair)):
            for place in range(half):
                at = (place * count + i + k) * sub
                source = (k * half + place) * sub
                out_ref[at : at + sub, :] = product[source : source + sub]


def project(pieces, out_weight, homes, sub, upper, after=()):
    count = len(pieces)
    return pl.pallas_call(
        functools.partial(
            project_kernel, count=count, homes=homes, sub=sub, upper=upper, after=len(after)
        ),
        out_shape=jax.ShapeDtypeStruct(
            (homes // 2 * count * sub, out_weight.shape[1]), jnp.bfloat16
        ),
        in_specs=whole_vmem(count + 1) + anywhere(len(after)),
        out_specs=pl.BlockSpec(memory_space=pltpu.VMEM),
        compiler_params=vmem(32),
        cost_estimate=FREE,
        name="project_leave" if upper else "project_stay",
    )(*pieces, out_weight, *after)


def add_kernel(keep_ref, arrived_ref, *refs):
    rows = keep_ref.shape[0] // len(refs)
    for i, ref in enumerate(refs):
        part = slice(i * rows, (i + 1) * rows)
        total = keep_ref[part, :].astype(jnp.float32) + arrived_ref[part, :].astype(jnp.float32)
        ref[...] = total.astype(ref.dtype)


def add(keep, arrived, dtypes):
    rows, cols = keep.shape
    count = len(dtypes)
    out = tuple(jax.ShapeDtypeStruct((rows // count, cols), dtype) for dtype in dtypes)
    return pl.pallas_call(
        add_kernel,
        out_shape=out,
        in_specs=whole_vmem(2),
        out_specs=tuple(whole_vmem(count)),
        compiler_params=vmem(16),
        cost_estimate=FREE,
        name="add",
    )(keep, arrived)


def hidden_kernel(*refs, count):
    row_refs = refs[:count]
    gain_ref, gate_ref, up_ref = refs[count : count + 3]
    out_ref = refs[-1]
    ctx_index = lax.axis_index("ctx")
    cols = row_refs[0].shape[1]
    rows = [ref[...].astype(jnp.float32) for ref in row_refs]
    square = sum(jnp.sum(row * row, axis=1, keepdims=True) for row in rows)
    inverse = lax.rsqrt(square / (cols * count) + 1e-06)
    gate = None
    up = None
    for place in range(count):
        at = pl.multiple_of((ctx_index ^ place) * cols, cols)
        normed = (rows[place] * inverse * gain_ref[:, pl.ds(at, cols)]).astype(jnp.bfloat16)
        gate_part = jnp.dot(normed, gate_ref[0, pl.ds(at, cols), :], preferred_element_type=jnp.float32)
        up_part = jnp.dot(normed, up_ref[0, pl.ds(at, cols), :], preferred_element_type=jnp.float32)
        gate = gate_part if gate is None else gate + gate_part
        up = up_part if up is None else up + up_part
    out_ref[...] = (gate / (1.0 + jnp.exp(-gate)) * up).astype(jnp.bfloat16)


def hidden_units(pieces, gain, gate_weight, up_weight, after=()):
    count = len(pieces)
    rows = pieces[0].shape[0]
    units = gate_weight.shape[2]
    return pl.pallas_call(
        functools.partial(hidden_kernel, count=count),
        out_shape=jax.ShapeDtypeStruct((rows, units), jnp.bfloat16),
        in_specs=whole_vmem(count + 3) + anywhere(len(after)),
        out_specs=pl.BlockSpec(memory_space=pltpu.VMEM),
        compiler_params=vmem(20),
        cost_estimate=FREE,
        name="hidden_units",
    )(*pieces, gain, gate_weight, up_weight, *after)


def down_kernel(*refs, count):
    piece_refs = refs[:count]
    down_ref = refs[count]
    out_ref = refs[-1]
    ctx_index = lax.axis_index("ctx")
    units = piece_refs[0].shape[1]
    total = None
    for place in range(count):
        at = pl.multiple_of((ctx_index ^ place) * units, units)
        part = jnp.dot(
            piece_refs[place][...], down_ref[0, pl.ds(at, units), :], preferred_element_type=jnp.float32
        )
        total = part if total is None else total + part
    out_ref[...] = total.astype(jnp.bfloat16)


def down_product(pieces, down_weight, after=()):
    count = len(pieces)
    rows = pieces[0].shape[0]
    return pl.pallas_call(
        functools.partial(down_kernel, count=count),
        out_shape=jax.ShapeDtypeStruct((rows, down_weight.shape[2]), jnp.bfloat16),
        in_specs=whole_vmem(count + 1) + anywhere(len(after)),
        out_specs=pl.BlockSpec(memory_space=pltpu.VMEM),
        compiler_params=vmem(20),
        cost_estimate=FREE,
        name="down_product",
    )(*pieces, down_weight, *after)


def attended_kernel(*refs, places):
    residual_ref = refs[len(places)]
    out_ref = refs[-1]
    ctx_index = lax.axis_index("ctx")
    for (place, row0), ref in zip(places, refs):
        rows, cols = ref.shape
        at = pl.multiple_of((ctx_index ^ place) * cols, cols)
        total = residual_ref[row0 : row0 + rows, pl.ds(at, cols)].astype(jnp.float32)
        total = total + ref[...].astype(jnp.float32)
        out_ref[row0 : row0 + rows, pl.ds(at, cols)] = total.astype(jnp.bfloat16)


def attended_rows(pieces, places, residual):
    return pl.pallas_call(
        functools.partial(attended_kernel, places=places),
        out_shape=jax.ShapeDtypeStruct(residual.shape, jnp.bfloat16),
        in_specs=whole_vmem(len(pieces) + 1),
        out_specs=pl.BlockSpec(memory_space=pltpu.VMEM),
        compiler_params=vmem(20),
        cost_estimate=FREE,
        name="attended_rows",
    )(*pieces, residual)


def combine_kernel(routes_ref, weights_ref, *refs, flight, count):
    back_refs = refs[:count]
    out_ref = refs[-1]
    routes_t = routes_ref[...]
    scores = weights_ref[...]
    shares = scores / jnp.sum(scores, axis=0, keepdims=True)
    named, ranks = slot_ranks(routes_t, flight)
    lines = []
    for j in range(flight):
        share = jnp.sum(jnp.where(routes_t == j, shares, 0.0), axis=0, keepdims=True)
        for r in range(CAP):
            lines.append(jnp.where(ranks[j : j + 1] == r, share, 0.0))
    lines = jnp.concatenate(lines, axis=0)
    cols = back_refs[0].shape[1]
    for place, ref in enumerate(back_refs):
        out_ref[:, place * cols : (place + 1) * cols] = lax.dot_general(
            lines,
            ref[...].astype(jnp.float32),
            (((0,), (0,)), ((), ())),
            precision=lax.Precision.HIGHEST,
            preferred_element_type=jnp.float32,
        ).astype(jnp.bfloat16)


def gather_pieces(x, axis):
    count = lax.axis_size(axis)
    found = {0: x}
    step = count // 2
    while step >= 1:
        keys = sorted(found)
        if len(keys) == 1:
            moved = [swap(found[0], axis, step)]
        else:
            packed = swap(jnp.stack([found[k] for k in keys]), axis, step)
            moved = [packed[i] for i in range(len(keys))]
        for k, piece in zip(keys, moved):
            found[k ^ step] = piece
        step //= 2
    return [found[k] for k in range(count)]


def gather_direct(x, axis):
    return [x] + [swap(x, axis, k) for k in range(1, lax.axis_size(axis))]


def sum_over_exp(keep, send, kinds):
    count = lax.axis_size("exp")
    step = 1
    while True:
        arrived = swap(send, "exp", step)
        step *= 2
        if step >= count:
            return add(keep, arrived, kinds)
        keep, send = add(keep, arrived, (jnp.float32, jnp.bfloat16))


def routed_over_exp(keep, send):
    count = lax.axis_size("exp")
    step = 1
    while True:
        arrived = swap(send, "exp", step)
        step *= 2
        if step >= count:
            return add_middle(keep, arrived, True)
        keep, send = add_middle(keep, arrived, False)


def shards(
    queries,
    keys,
    values,
    doc_lengths,
    residual_in,
    out_weight,
    norm_gain,
    routes,
    route_weights,
    gate_weight,
    up_weight,
    down_weight,
):
    tokens = queries.shape[0]
    local_heads = queries.shape[1] // HD
    n_ctx = lax.axis_size("ctx")
    homes = lax.axis_size("exp")
    flight = gate_weight.shape[0] * homes
    ctx_index = lax.axis_index("ctx")
    exp_index = lax.axis_index("exp")
    block_tokens = residual_in.shape[0]
    width = residual_in.shape[1]
    cols = out_weight.shape[1]
    halves = 2 if block_tokens % 32 == 0 else 1
    sub = block_tokens // halves
    kinds = jnp.bfloat16

    routes_t = routes.T
    routes_pieces = gather_pieces(routes_t, "exp")
    kv_head = exp_index * local_heads // (QH // KVH)
    kv_own = jnp.stack(
        [
            lax.dynamic_slice_in_dim(keys, kv_head * HD, HD, 1),
            lax.dynamic_slice_in_dim(values, kv_head * HD, HD, 1),
        ]
    )
    kv_near = shift(kv_own, "ctx", 1)
    kv_far = shift(kv_own, "ctx", 2)
    heads_out = [
        attention(doc_lengths, queries, kv_far, kv_near, kv_own, homes, half, sub)
        for half in range(halves)
    ]
    near = [swap(rows, "ctx", 1) for rows in heads_out]
    routed = pick(residual_in, routes_pieces, heads_out, sub)
    routed_pieces = gather_pieces(routed, "ctx")

    far = []
    for rows in heads_out:
        found = {0: rows}
        step = n_ctx // 2
        while step >= 2:
            for k in sorted(found):
                found[k ^ step] = swap(found[k], "ctx", step)
            step //= 2
        for k in sorted(found):
            if k:
                found[k ^ 1] = swap(found[k], "ctx", 1)
        far.append({k: found[k] for k in sorted(found) if k})

    both = heads_out + near
    send = project(both, out_weight, homes, sub, True)
    keep = project(both, out_weight, homes, sub, False)
    own_sum, near_sum = sum_over_exp(keep, send, (kinds, kinds))
    parts = [own_sum, swap(near_sum, "ctx", 1)]
    places = [(0, 0), (1, 0)]

    keep, send = routed_product(routed_pieces, out_weight, homes)
    routed_rows = routed_over_exp(keep, send)
    stream_rows = gather_direct(routed_rows, "ctx")
    hidden = hidden_units(stream_rows, norm_gain[None, :], gate_weight, up_weight)

    for half in range(halves):
        names = sorted(far[half])
        blocks = [far[half][k] for k in names]
        send = project(blocks, out_weight, homes, sub, True)
        keep = project(blocks, out_weight, homes, sub, False)
        sums = sum_over_exp(keep, send, (kinds,) * len(names))
        for k, piece in zip(names, sums):
            parts.append(swap(piece, "ctx", k))
            places.append((k, half * sub))

    produced = down_product(gather_direct(hidden, "ctx"), down_weight)
    back = lax.all_to_all(
        produced.reshape(n_ctx * homes, CAP, cols),
        ("ctx", "exp"),
        split_axis=0,
        concat_axis=0,
        tiled=True,
    ).reshape(n_ctx, flight * CAP, cols)
    combined = pl.pallas_call(
        functools.partial(combine_kernel, flight=flight, count=n_ctx),
        out_shape=jax.ShapeDtypeStruct((block_tokens, width), jnp.bfloat16),
        in_specs=whole_vmem(2 + n_ctx),
        out_specs=pl.BlockSpec(memory_space=pltpu.VMEM),
        compiler_params=vmem(20),
        cost_estimate=FREE,
        name="combine",
    )(routes_t, route_weights.T, *[back[i] for i in range(n_ctx)])
    attended = attended_rows(parts, places, residual_in)
    return (attended, combined)


def solution(mesh):
    placed = (
        P(("grp", "ctx"), "exp"),
        P(("grp", "ctx"), None),
        P(("grp", "ctx"), None),
        P("grp"),
        P(("grp", "ctx", "exp"), None),
        P("exp", "ctx"),
        P(),
        P(("grp", "ctx", "exp"), None),
        P(("grp", "ctx", "exp"), None),
        P("exp", None, "ctx"),
        P("exp", None, "ctx"),
        P("exp", None, "ctx"),
    )
    return jax.shard_map(
        shards,
        mesh=mesh,
        in_specs=placed,
        out_specs=(P(("grp", "ctx", "exp"), None), P(("grp", "ctx", "exp"), None)),
        check_vma=False,
    )
```

time: 131 us -> 112 us (0.85)
  matrix products: 12.3 us -> 0 us
  Pallas kernels: 12.6 us -> 21.5 us
  waiting for transfers between devices: 52.1 us -> 44.8 us
  local copies, waits for them, and re-layouts: 8.41 us -> 3.64 us
  other arithmetic: 2.84 us -> 0.74 us
    dot_general x6 -> x0, matrix products: 12.3 us -> none  [the longest x3 9.87 us: project(): jnp.dot(rows, out_weight, preferred_element_type=jnp.float32)]
    ppermute x30 -> x29, waiting for transfers between devices: 52 us -> 42.5 us  [swap(): return lax.ppermute(x, axis, [(i, i ^ mask) for i in range(count)])]
    pallas_call x3 -> x20, Pallas kernels: 10.8 us -> 19.7 us  [the longest x2 8.48 us: attention(): pl.pallas_call(functools.partial(attention_kernel, heads=width // HD, hom...]
    unnamed x26 -> x20, local copies, waits for them, and re-layouts: 6.35 us -> 1.93 us
    ppermute x2, waiting for transfers between devices: 0.01 us -> 1.84 us  [shift(): return lax.ppermute(x, axis, [(i, i + by) for i in range(count - by)])]
    ppermute x2, starting transfers between devices: 6.32 us -> 4.7 us  [shift(): return lax.ppermute(x, axis, [(i, i + by) for i in range(count - by)])]
    ppermute x30 -> x29, starting transfers between devices: 29.7 us -> 30.1 us  [swap(): return lax.ppermute(x, axis, [(i, i ^ mask) for i in range(count)])]
  transfers between devices with their start and end apart: 33 -> 32, of which waited for: 17 -> 14; matrix products, arithmetic and copies ran while one was open for 11% -> 2% of each run, Pallas kernels for 9% -> 9%
where the time goes in v2:
time: 112 us
  waiting for transfers between devices  44.8 us (40%)
  starting transfers between devices  40.3 us (36%)
  Pallas kernels  21.5 us (19%)
  local copies, waits for them, and re-layouts  3.64 us (3%)
    ppermute x29, waiting for transfers between devices, swap(): return lax.ppermute(x, axis, [(i, i ^ mask) for i in range(count)])  42.5 us
    ppermute x29, starting transfers between devices, swap(): return lax.ppermute(x, axis, [(i, i ^ mask) for i in range(count)])  30.1 us
    pallas_call x2, Pallas kernels, attention(): pl.pallas_call(functools.partial(attention_kernel, heads=width // HD, hom...  8.48 us
    all_to_all x1, starting transfers between devices, shards(): lax.all_to_all(produced.reshape(n_ctx * homes, CAP, cols), ('ctx', 'exp')...  5.46 us
    pallas_call x6, Pallas kernels, project(): pl.pallas_call(functools.partial(project_kernel, count=count, homes=homes...  5.4 us
    ppermute x2, starting transfers between devices, shift(): return lax.ppermute(x, axis, [(i, i + by) for i in range(count - by)])  4.7 us
  transfers between devices with their start and end apart: 32, of which 14 were waited for; matrix products, arithmetic and copies ran while one was open for 2% of the time, Pallas kernels for 9%

profile of v2, /device:TPU:0, one launch (start us, length us, event | category | flops | bytes accessed | tf_op | source)
XLA Modules:
  0.0 112.0 jit_solution(11744188277686364962)
XLA Ops:
  0.7 4.1 %collective-permute-start.19 = (s32[8,64]{1,0:T(8,128)}, s32[8,64]{1,0:T(8,128)S(1)}, u32[]{:S(2)}, u32[]{:S(2)}) collective-permute-start(s32[8,64]{1,0:T(8,128)} %bitcast.22), channel_id=1, source_target_pairs={{0,2},{1,3},{2,0},{3,1},{4,6},{5,7},{6,4},{7,5},{8,10},{9,11},{10,... | collective-permute-start | bytes 6152 | tf_op jit(solution)/shard_map/ppermute | solution.py:22
  4.8 0.9 dynamic-slice_bitcast_fusion
  5.6 0.9 collective-permute-done.19.refs_2_
  6.6 0.7 pad_add_fusion
  7.2 1.9 %collective-permute-start.20 = (s32[2,8,64]{2,1,0:T(8,128)S(1)}, s32[2,8,64]{2,1,0:T(8,128)S(1)}, u32[]{:S(2)}, u32[]{:S(2)}) collective-permute-start(s32[2,8,64]{2,1,0:T(8,128)S(1)} %pad_add_fusion), channel_id=1, source_target_pairs={{0,1},{1,0},{2,3},{3,2},{4,5},{5,4},{6,7},{7,6},{8,9},{9,8},{10,11... | collective-permute-start | bytes 12296 | tf_op jit(solution)/shard_map/ppermute | solution.py:22
  9.2 3.4 %collective-permute-start = (bf16[2,256,128]{2,1,0:T(8,128)(2,1)S(1)}, bf16[2,256,128]{2,1,0:T(8,128)(2,1)S(1)}, u32[]{:S(2)}, u32[]{:S(2)}) collective-permute-start(bf16[2,256,128]{2,1,0:T(8,128)(2,1)S(1)} %pad_maximum_fusion.1.kv_own_ref), channel_id=1, source_target_pairs={{0,8},{4,12},{1,9},{5,13},{2,10},{6,14},{3,11},{7,15},{16,24},{20,... | collective-permute-start | bytes 393224 | tf_op jit(solution)/shard_map/ppermute | solution.py:27
  12.6 1.3 %collective-permute-start.1 = (bf16[2,256,128]{2,1,0:T(8,128)(2,1)S(1)}, bf16[2,256,128]{2,1,0:T(8,128)(2,1)S(1)}, u32[]{:S(2)}, u32[]{:S(2)}) collective-permute-start(bf16[2,256,128]{2,1,0:T(8,128)(2,1)S(1)} %pad_maximum_fusion.1.kv_own_ref), channel_id=1, source_target_pairs={{0,4},{4,8},{8,12},{1,5},{5,9},{9,13},{2,6},{6,10},{10,14},{3,7},{... | collective-permute-start | bytes 393224 | tf_op jit(solution)/shard_map/ppermute | solution.py:27
  13.9 1.8 %collective-permute-done.kv_far_ref = bf16[2,256,128]{2,1,0:T(8,128)(2,1)S(1)} collective-permute-done((bf16[2,256,128]{2,1,0:T(8,128)(2,1)S(1)}, bf16[2,256,128]{2,1,0:T(8,128)(2,1)S(1)}, u32[]{:S(2)}, u32[]{:S(2)}) %collective-permute-start) | collective-permute-done | bytes 131104 | tf_op jit(solution)/shard_map/ppermute | solution.py:27
  15.8 1.2 %copy-done.1 = bf16[256,2048]{1,0:T(8,128)(2,1)S(1)} copy-done((bf16[256,2048]{1,0:T(8,128)(2,1)S(1)}, bf16[256,2048]{1,0:T(8,128)(2,1)}, u32[]{:S(2)}) %copy-start.1) | copy-done | bytes 1048600
  17.0 0.7 copy-done.9
  17.6 4.2 %attention_0.1.refs_0_.refs_4_ = bf16[128,2048]{1,0:T(8,128)(2,1)S(1)} custom-call(s32[24]{0:T(128)S(1)} %copy-done.9, bf16[256,2048]{1,0:T(8,128)(2,1)S(1)} %copy-done.1, bf16[2,256,128]{2,1,0:T(8,128)(2,1)S(1)} %collective-permute-done.kv_far_ref, bf16[2,256,128]{2,1,0:T(8,128)(2,1)S(1)} %collective-permute-done.1.kv_near_ref, ...), custom_call_target="tpu_custom_call" | custom-call | tf_op jit(solution)/shard_map/attention_0/pallas_call | solution.py:146
  21.9 4.2 %attention_1.1.refs_1_.refs_5_ = bf16[128,2048]{1,0:T(8,128)(2,1)S(1)} custom-call(s32[24]{0:T(128)S(1)} %copy-done.9, bf16[256,2048]{1,0:T(8,128)(2,1)S(1)} %copy-done.1, bf16[2,256,128]{2,1,0:T(8,128)(2,1)S(1)} %collective-permute-done.kv_far_ref, bf16[2,256,128]{2,1,0:T(8,128)(2,1)S(1)} %collective-permute-done.1.kv_near_ref, ...), custom_call_target="tpu_custom_call" | custom-call | tf_op jit(solution)/shard_map/attention_1/pallas_call | solution.py:146
  26.1 1.8 %pick.1.refs_0_ = bf16[48,2048]{1,0:T(8,128)(2,1)S(1)} custom-call(bf16[64,4096]{1,0:T(8,128)(2,1)S(1)} %copy-done.5, s32[8,64]{1,0:T(8,128)S(1)} %bitcast.24, s32[8,64]{1,0:T(8,128)S(1)} %get-tuple-element.41.refs_1_, s32[8,64]{1,0:T(8,128)S(1)} %collective-permute-done.19.refs_2_, s32[8,64]{1,0:T(8,128)S(1)} %get-tuple-element.40.refs_3_, ...), custom_call_target="tpu_custom_call" | custom-call | tf_op jit(solution)/shard_map/pick/pallas_call | solution.py:213
  28.0 3.2 %collective-permute-start.21 = (bf16[48,2048]{1,0:T(8,128)(2,1)S(1)}, bf16[48,2048]{1,0:T(8,128)(2,1)S(1)}, u32[]{:S(2)}, u32[]{:S(2)}) collective-permute-start(bf16[48,2048]{1,0:T(8,128)(2,1)S(1)} %pick.1.refs_0_), channel_id=1, source_target_pairs={{0,8},{4,12},{8,0},{12,4},{1,9},{5,13},{9,1},{13,5},{2,10},{6,14},... | collective-permute-start | bytes 589832 | tf_op jit(solution)/shard_map/ppermute | solution.py:22
  31.8 1.9 %collective-permute-start.13 = (bf16[128,2048]{1,0:T(8,128)(2,1)S(1)}, bf16[128,2048]{1,0:T(8,128)(2,1)S(1)}, u32[]{:S(2)}, u32[]{:S(2)}) collective-permute-start(bf16[128,2048]{1,0:T(8,128)(2,1)S(1)} %attention_1.1.refs_1_.refs_5_), channel_id=1, source_target_pairs={{0,8},{4,12},{8,0},{12,4},{1,9},{5,13},{9,1},{13,5},{2,10},{6,14},... | collective-permute-start | bytes 1572872 | tf_op jit(solution)/shard_map/ppermute | solution.py:22
  33.8 3.2 %collective-permute-done.21.refs_2_ = bf16[48,2048]{1,0:T(8,128)(2,1)S(1)} collective-permute-done((bf16[48,2048]{1,0:T(8,128)(2,1)S(1)}, bf16[48,2048]{1,0:T(8,128)(2,1)S(1)}, u32[]{:S(2)}, u32[]{:S(2)}) %collective-permute-start.21) | collective-permute-done | bytes 196640 | tf_op jit(solution)/shard_map/ppermute | solution.py:22
  37.1 1.3 %project_leave.3 = bf16[256,1024]{1,0:T(8,128)(2,1)S(1)} custom-call(bf16[128,2048]{1,0:T(8,128)(2,1)S(1)} %attention_0.1.refs_0_.refs_4_, bf16[128,2048]{1,0:T(8,128)(2,1)S(1)} %attention_1.1.refs_1_.refs_5_, bf16[128,2048]{1,0:T(8,128)(2,1)S(1)} %collective-permute-done.2.refs_2_, bf16[128,2048]{1,0:T(8,128)(2,1)S(1)} %collective-permute-done.3.refs_3_, ...), custom_call_target="tpu_custom_call" | custom-call | tf_op jit(solution)/shard_map/project_leave/pallas_call | solution.py:325
  38.9 9.3 %collective-permute-done.7.refs_0_ = bf16[128,2048]{1,0:T(8,128)(2,1)S(1)} collective-permute-done((bf16[128,2048]{1,0:T(8,128)(2,1)S(1)}, bf16[128,2048]{1,0:T(8,128)(2,1)S(1)}, u32[]{:S(2)}, u32[]{:S(2)}) %collective-permute-start.7) | collective-permute-done | bytes 524320 | tf_op jit(solution)/shard_map/ppermute | solution.py:22
  48.2 10.0 %collective-permute-done.13.refs_0_ = bf16[128,2048]{1,0:T(8,128)(2,1)S(1)} collective-permute-done((bf16[128,2048]{1,0:T(8,128)(2,1)S(1)}, bf16[128,2048]{1,0:T(8,128)(2,1)S(1)}, u32[]{:S(2)}, u32[]{:S(2)}) %collective-permute-start.13) | collective-permute-done | bytes 524320 | tf_op jit(solution)/shard_map/ppermute | solution.py:22
  58.2 0.8 routed_product.1
  59.5 0.7 project_leave.4
  60.2 1.6 %collective-permute-start.9 = (bf16[128,1024]{1,0:T(8,128)(2,1)S(1)}, bf16[128,1024]{1,0:T(8,128)(2,1)S(1)}, u32[]{:S(2)}, u32[]{:S(2)}) collective-permute-start(bf16[128,1024]{1,0:T(8,128)(2,1)S(1)} %project_leave.4), channel_id=1, source_target_pairs={{0,1},{1,0},{2,3},{3,2},{4,5},{5,4},{6,7},{7,6},{8,9},{9,8},{10,11... | collective-permute-start | bytes 786440 | tf_op jit(solution)/shard_map/ppermute | solution.py:22
  61.9 0.7 project_leave.5
  62.6 0.5 collective-permute-start.15
  63.1 2.2 %collective-permute-done.23.arrived_ref = bf16[4,16,1024]{2,1,0:T(8,128)(2,1)S(1)} collective-permute-done((bf16[4,16,1024]{2,1,0:T(8,128)(2,1)S(1)}, bf16[4,16,1024]{2,1,0:T(8,128)(2,1)S(1)}, u32[]{:S(2)}, u32[]{:S(2)}) %collective-permute-start.23) | collective-permute-done | bytes 131104 | tf_op jit(solution)/shard_map/ppermute | solution.py:22
  65.4 2.6 %collective-permute-start.24 = (bf16[4,8,1024]{2,1,0:T(8,128)(2,1)S(1)}, bf16[4,8,1024]{2,1,0:T(8,128)(2,1)S(1)}, u32[]{:S(2)}, u32[]{:S(2)}) collective-permute-start(bf16[4,8,1024]{2,1,0:T(8,128)(2,1)S(1)} %get-tuple-element.33), channel_id=1, source_target_pairs={{0,2},{1,3},{2,0},{3,1},{4,6},{5,7},{6,4},{7,5},{8,10},{9,11},{10,... | collective-permute-start | bytes 196616 | tf_op jit(solution)/shard_map/ppermute | solution.py:22
  68.0 7.5 %collective-permute-done.24.arrived_ref = bf16[4,8,1024]{2,1,0:T(8,128)(2,1)S(1)} collective-permute-done((bf16[4,8,1024]{2,1,0:T(8,128)(2,1)S(1)}, bf16[4,8,1024]{2,1,0:T(8,128)(2,1)S(1)}, u32[]{:S(2)}, u32[]{:S(2)}) %collective-permute-start.24) | collective-permute-done | bytes 65568 | tf_op jit(solution)/shard_map/ppermute | solution.py:22
  75.7 1.3 %project_stay.3.keep_ref = bf16[256,1024]{1,0:T(8,128)(2,1)S(1)} custom-call(bf16[128,2048]{1,0:T(8,128)(2,1)S(1)} %attention_0.1.refs_0_.refs_4_, bf16[128,2048]{1,0:T(8,128)(2,1)S(1)} %attention_1.1.refs_1_.refs_5_, bf16[128,2048]{1,0:T(8,128)(2,1)S(1)} %collective-permute-done.2.refs_2_, bf16[128,2048]{1,0:T(8,128)(2,1)S(1)} %collective-permute-done.3.refs_3_, ...), custom_call_target="tpu_custom_call" | custom-call | tf_op jit(solution)/shard_map/project_stay/pallas_call | solution.py:325
  77.1 3.4 %collective-permute-start.5 = (bf16[128,1024]{1,0:T(8,128)(2,1)S(1)}, bf16[128,1024]{1,0:T(8,128)(2,1)S(1)}, u32[]{:S(2)}, u32[]{:S(2)}) collective-permute-start(bf16[128,1024]{1,0:T(8,128)(2,1)S(1)} %get-tuple-element.19), channel_id=1, source_target_pairs={{0,2},{1,3},{2,0},{3,1},{4,6},{5,7},{6,4},{7,5},{8,10},{9,11},{10,... | collective-permute-start | bytes 786440 | tf_op jit(solution)/shard_map/ppermute | solution.py:22
  80.5 1.1 collective-permute-start.26
  81.6 0.5 collective-permute-start.27
  82.1 3.0 %collective-permute-done.26.refs_2_ = bf16[32,1024]{1,0:T(8,128)(2,1)S(1)} collective-permute-done((bf16[32,1024]{1,0:T(8,128)(2,1)S(1)}, bf16[32,1024]{1,0:T(8,128)(2,1)S(1)}, u32[]{:S(2)}, u32[]{:S(2)}) %collective-permute-start.26) | collective-permute-done | bytes 65568 | tf_op jit(solution)/shard_map/ppermute | solution.py:22
  85.1 0.8 collective-permute-done.27.refs_3_
  85.9 1.1 hidden_units.1.refs_0_
  87.5 1.1 collective-permute-start.29
  88.9 0.7 project_stay.4.keep_ref
  90.1 0.7 project_stay.5.keep_ref
  90.9 2.7 %collective-permute-start.16 = (bf16[64,1024]{1,0:T(8,128)(2,1)S(1)}, bf16[64,1024]{1,0:T(8,128)(2,1)S(1)}, u32[]{:S(2)}, u32[]{:S(2)}) collective-permute-start(bf16[64,1024]{1,0:T(8,128)(2,1)S(1)} %get-tuple-element.27), channel_id=1, source_target_pairs={{0,2},{1,3},{2,0},{3,1},{4,6},{5,7},{6,4},{7,5},{8,10},{9,11},{10,... | collective-permute-start | bytes 393224 | tf_op jit(solution)/shard_map/ppermute | solution.py:22
  93.6 0.6 down_product.1
  94.3 0.7 reshape.16
  95.0 5.5 %all-to-all-start = ((bf16[16,2,1024]{2,1,0:T(2,128)(2,1)}), bf16[16,2,1024]{2,1,0:T(2,128)(2,1)S(1)}, u32[]{:S(2)}, u32[]{:S(2)}) async-start(bf16[16,2,1024]{2,1,0:T(2,128)(2,1)} %reshape.16), calls=%async_computation | async-start | bytes 131072 | tf_op jit(solution)/shard_map/all_to_all | solution.py:603
  101.0 1.7 %collective-permute-done.10.arrived_ref = bf16[64,1024]{1,0:T(8,128)(2,1)S(1)} collective-permute-done((bf16[64,1024]{1,0:T(8,128)(2,1)S(1)}, bf16[64,1024]{1,0:T(8,128)(2,1)S(1)}, u32[]{:S(2)}, u32[]{:S(2)}) %collective-permute-start.10) | collective-permute-done | bytes 131104 | tf_op jit(solution)/shard_map/ppermute | solution.py:22
  102.7 1.1 collective-permute-start.11
  103.8 2.0 %collective-permute-done.16.arrived_ref = bf16[64,1024]{1,0:T(8,128)(2,1)S(1)} collective-permute-done((bf16[64,1024]{1,0:T(8,128)(2,1)S(1)}, bf16[64,1024]{1,0:T(8,128)(2,1)S(1)}, u32[]{:S(2)}, u32[]{:S(2)}) %collective-permute-start.16) | collective-permute-done | bytes 131104 | tf_op jit(solution)/shard_map/ppermute | solution.py:22
  105.9 0.8 collective-permute-start.17
  107.2 1.9 %combine.1 = bf16[64,4096]{1,0:T(8,128)(2,1)} custom-call(s32[8,64]{1,0:T(8,128)S(1)} %bitcast.25, f32[8,64]{1,0:T(8,128)S(1)} %bitcast.28, bf16[8,1024]{1,0:T(8,128)(2,1)S(1)} %squeeze.28.refs_0_, bf16[8,1024]{1,0:T(8,128)(2,1)S(1)} %squeeze.29.refs_1_, bf16[8,1024]{1,0:T(8,128)(2,1)S(1)} %squeeze.30.refs_2_, bf16[8,1024]{1,0:T(8,128)(2,1)S(1)} %squeeze.31.refs_3_), custom_call_target="tpu_custom_call" | custom-call | tf_op jit(solution)/shard_map/combine/pallas_call | solution.py:610
  109.2 1.6 %collective-permute-done.17.refs_4_ = bf16[32,1024]{1,0:T(8,128)(2,1)S(1)} collective-permute-done((bf16[32,1024]{1,0:T(8,128)(2,1)S(1)}, bf16[32,1024]{1,0:T(8,128)(2,1)S(1)}, u32[]{:S(2)}, u32[]{:S(2)}) %collective-permute-start.17) | collective-permute-done | bytes 65568 | tf_op jit(solution)/shard_map/ppermute | solution.py:22
  111.0 0.9 attended_rows.1
  (70 shorter events, 4.8 us)
Async XLA Ops:
  0.6 25.5 %copy-start.6 = (s32[64,8]{0,1:T(8,128)S(1)}, s32[64,8]{0,1:T(8,128)}, u32[]{:S(2)}) copy-start(s32[64,8]{0,1:T(8,128)} %param.19) | copy-start | bytes 6148
  0.6 25.5 %copy-start.5 = (bf16[64,4096]{1,0:T(8,128)(2,1)S(1)}, bf16[64,4096]{1,0:T(8,128)(2,1)}, u32[]{:S(2)}) copy-start(bf16[64,4096]{1,0:T(8,128)(2,1)} %residual_ref.1) | copy-start | bytes 1572868
  0.7 5.9 %collective-permute-start.19 = (s32[8,64]{1,0:T(8,128)}, s32[8,64]{1,0:T(8,128)S(1)}, u32[]{:S(2)}, u32[]{:S(2)}) collective-permute-start(s32[8,64]{1,0:T(8,128)} %bitcast.22), channel_id=1, source_target_pairs={{0,2},{1,3},{2,0},{3,1},{4,6},{5,7},{6,4},{7,5},{8,10},{9,11},{10,... | collective-permute-start | bytes 6152 | tf_op jit(solution)/shard_map/ppermute | solution.py:22
  7.2 6.6 %collective-permute-start.20 = (s32[2,8,64]{2,1,0:T(8,128)S(1)}, s32[2,8,64]{2,1,0:T(8,128)S(1)}, u32[]{:S(2)}, u32[]{:S(2)}) collective-permute-start(s32[2,8,64]{2,1,0:T(8,128)S(1)} %pad_add_fusion), channel_id=1, source_target_pairs={{0,1},{1,0},{2,3},{3,2},{4,5},{5,4},{6,7},{7,6},{8,9},{9,8},{10,11... | collective-permute-start | bytes 12296 | tf_op jit(solution)/shard_map/ppermute | solution.py:22
  9.2 6.6 %collective-permute-start = (bf16[2,256,128]{2,1,0:T(8,128)(2,1)S(1)}, bf16[2,256,128]{2,1,0:T(8,128)(2,1)S(1)}, u32[]{:S(2)}, u32[]{:S(2)}) collective-permute-start(bf16[2,256,128]{2,1,0:T(8,128)(2,1)S(1)} %pad_maximum_fusion.1.kv_own_ref), channel_id=1, source_target_pairs={{0,8},{4,12},{1,9},{5,13},{2,10},{6,14},{3,11},{7,15},{16,24},{20,... | collective-permute-start | bytes 393224 | tf_op jit(solution)/shard_map/ppermute | solution.py:27
  12.6 3.2 %collective-permute-start.1 = (bf16[2,256,128]{2,1,0:T(8,128)(2,1)S(1)}, bf16[2,256,128]{2,1,0:T(8,128)(2,1)S(1)}, u32[]{:S(2)}, u32[]{:S(2)}) collective-permute-start(bf16[2,256,128]{2,1,0:T(8,128)(2,1)S(1)} %pad_maximum_fusion.1.kv_own_ref), channel_id=1, source_target_pairs={{0,4},{4,8},{8,12},{1,5},{5,9},{9,13},{2,6},{6,10},{10,14},{3,7},{... | collective-permute-start | bytes 393224 | tf_op jit(solution)/shard_map/ppermute | solution.py:27
  13.9 23.2 %copy-start = (bf16[2048,1024]{1,0:T(8,128)(2,1)S(1)}, bf16[2048,1024]{1,0:T(8,128)(2,1)}, u32[]{:S(2)}) copy-start(bf16[2048,1024]{1,0:T(8,128)(2,1)} %refs_4_.6) | copy-start | bytes 12582916
  15.8 1.2 %copy-start.1 = (bf16[256,2048]{1,0:T(8,128)(2,1)S(1)}, bf16[256,2048]{1,0:T(8,128)(2,1)}, u32[]{:S(2)}) copy-start(bf16[256,2048]{1,0:T(8,128)(2,1)} %q_ref.3) | copy-start | bytes 3145732
  17.0 0.7 copy-start.9
  28.0 8.9 %collective-permute-start.21 = (bf16[48,2048]{1,0:T(8,128)(2,1)S(1)}, bf16[48,2048]{1,0:T(8,128)(2,1)S(1)}, u32[]{:S(2)}, u32[]{:S(2)}) collective-permute-start(bf16[48,2048]{1,0:T(8,128)(2,1)S(1)} %pick.1.refs_0_), channel_id=1, source_target_pairs={{0,8},{4,12},{8,0},{12,4},{1,9},{5,13},{9,1},{13,5},{2,10},{6,14},... | collective-permute-start | bytes 589832 | tf_op jit(solution)/shard_map/ppermute | solution.py:22
  31.2 5.8 %collective-permute-start.2 = (bf16[128,2048]{1,0:T(8,128)(2,1)S(1)}, bf16[128,2048]{1,0:T(8,128)(2,1)S(1)}, u32[]{:S(2)}, u32[]{:S(2)}) collective-permute-start(bf16[128,2048]{1,0:T(8,128)(2,1)S(1)} %attention_0.1.refs_0_.refs_4_), channel_id=1, source_target_pairs={{0,4},{4,0},{8,12},{12,8},{1,5},{5,1},{9,13},{13,9},{2,6},{6,2},{1... | collective-permute-start | bytes 1572872 | tf_op jit(solution)/shard_map/ppermute | solution.py:22
  31.2 5.8 %collective-permute-start.3 = (bf16[128,2048]{1,0:T(8,128)(2,1)S(1)}, bf16[128,2048]{1,0:T(8,128)(2,1)S(1)}, u32[]{:S(2)}, u32[]{:S(2)}) collective-permute-start(bf16[128,2048]{1,0:T(8,128)(2,1)S(1)} %attention_1.1.refs_1_.refs_5_), channel_id=1, source_target_pairs={{0,4},{4,0},{8,12},{12,8},{1,5},{5,1},{9,13},{13,9},{2,6},{6,2},{1... | collective-permute-start | bytes 1572872 | tf_op jit(solution)/shard_map/ppermute | solution.py:22
  31.7 16.4 %collective-permute-start.7 = (bf16[128,2048]{1,0:T(8,128)(2,1)S(1)}, bf16[128,2048]{1,0:T(8,128)(2,1)S(1)}, u32[]{:S(2)}, u32[]{:S(2)}) collective-permute-start(bf16[128,2048]{1,0:T(8,128)(2,1)S(1)} %attention_0.1.refs_0_.refs_4_), channel_id=1, source_target_pairs={{0,8},{4,12},{8,0},{12,4},{1,9},{5,13},{9,1},{13,5},{2,10},{6,14},... | collective-permute-start | bytes 1572872 | tf_op jit(solution)/shard_map/ppermute | solution.py:22
  31.8 26.3 %collective-permute-start.13 = (bf16[128,2048]{1,0:T(8,128)(2,1)S(1)}, bf16[128,2048]{1,0:T(8,128)(2,1)S(1)}, u32[]{:S(2)}, u32[]{:S(2)}) collective-permute-start(bf16[128,2048]{1,0:T(8,128)(2,1)S(1)} %attention_1.1.refs_1_.refs_5_), channel_id=1, source_target_pairs={{0,8},{4,12},{8,0},{12,4},{1,9},{5,13},{9,1},{13,5},{2,10},{6,14},... | collective-permute-start | bytes 1572872 | tf_op jit(solution)/shard_map/ppermute | solution.py:22
  37.0 21.2 %collective-permute-start.22 = (bf16[2,48,2048]{2,1,0:T(8,128)(2,1)S(1)}, bf16[2,48,2048]{2,1,0:T(8,128)(2,1)S(1)}, u32[]{:S(2)}, u32[]{:S(2)}) collective-permute-start(bf16[2,48,2048]{2,1,0:T(8,128)(2,1)S(1)} %pad_maximum_fusion), channel_id=1, source_target_pairs={{0,4},{4,0},{8,12},{12,8},{1,5},{5,1},{9,13},{13,9},{2,6},{6,2},{1... | collective-permute-start | bytes 1179656 | tf_op jit(solution)/shard_map/ppermute | solution.py:22
  38.4 38.6 %collective-permute-start.4 = (bf16[256,1024]{1,0:T(8,128)(2,1)S(1)}, bf16[256,1024]{1,0:T(8,128)(2,1)S(1)}, u32[]{:S(2)}, u32[]{:S(2)}) collective-permute-start(bf16[256,1024]{1,0:T(8,128)(2,1)S(1)} %project_leave.3), channel_id=1, source_target_pairs={{0,1},{1,0},{2,3},{3,2},{4,5},{5,4},{6,7},{7,6},{8,9},{9,8},{10,11... | collective-permute-start | bytes 1572872 | tf_op jit(solution)/shard_map/ppermute | solution.py:22
  48.2 11.3 %collective-permute-start.8 = (bf16[128,2048]{1,0:T(8,128)(2,1)S(1)}, bf16[128,2048]{1,0:T(8,128)(2,1)S(1)}, u32[]{:S(2)}, u32[]{:S(2)}) collective-permute-start(bf16[128,2048]{1,0:T(8,128)(2,1)S(1)} %collective-permute-done.7.refs_0_), channel_id=1, source_target_pairs={{0,4},{4,0},{8,12},{12,8},{1,5},{5,1},{9,13},{13,9},{2,6},{6,2},{1... | collective-permute-start | bytes 1572872 | tf_op jit(solution)/shard_map/ppermute | solution.py:22
  58.1 3.7 %collective-permute-start.14 = (bf16[128,2048]{1,0:T(8,128)(2,1)S(1)}, bf16[128,2048]{1,0:T(8,128)(2,1)S(1)}, u32[]{:S(2)}, u32[]{:S(2)}) collective-permute-start(bf16[128,2048]{1,0:T(8,128)(2,1)S(1)} %collective-permute-done.13.refs_0_), channel_id=1, source_target_pairs={{0,4},{4,0},{8,12},{12,8},{1,5},{5,1},{9,13},{13,9},{2,6},{6,2},{1... | collective-permute-start | bytes 1572872 | tf_op jit(solution)/shard_map/ppermute | solution.py:22
  59.0 6.4 %collective-permute-start.23 = (bf16[4,16,1024]{2,1,0:T(8,128)(2,1)S(1)}, bf16[4,16,1024]{2,1,0:T(8,128)(2,1)S(1)}, u32[]{:S(2)}, u32[]{:S(2)}) collective-permute-start(bf16[4,16,1024]{2,1,0:T(8,128)(2,1)S(1)} %get-tuple-element.31), channel_id=1, source_target_pairs={{0,1},{1,0},{2,3},{3,2},{4,5},{5,4},{6,7},{7,6},{8,9},{9,8},{10,11... | collective-permute-start | bytes 393224 | tf_op jit(solution)/shard_map/ppermute | solution.py:22
  60.2 28.3 %collective-permute-start.9 = (bf16[128,1024]{1,0:T(8,128)(2,1)S(1)}, bf16[128,1024]{1,0:T(8,128)(2,1)S(1)}, u32[]{:S(2)}, u32[]{:S(2)}) collective-permute-start(bf16[128,1024]{1,0:T(8,128)(2,1)S(1)} %project_leave.4), channel_id=1, source_target_pairs={{0,1},{1,0},{2,3},{3,2},{4,5},{5,4},{6,7},{7,6},{8,9},{9,8},{10,11... | collective-permute-start | bytes 786440 | tf_op jit(solution)/shard_map/ppermute | solution.py:22
  62.6 27.2 %collective-permute-start.15 = (bf16[128,1024]{1,0:T(8,128)(2,1)S(1)}, bf16[128,1024]{1,0:T(8,128)(2,1)S(1)}, u32[]{:S(2)}, u32[]{:S(2)}) collective-permute-start(bf16[128,1024]{1,0:T(8,128)(2,1)S(1)} %project_leave.5), channel_id=1, source_target_pairs={{0,1},{1,0},{2,3},{3,2},{4,5},{5,4},{6,7},{7,6},{8,9},{9,8},{10,11... | collective-permute-start | bytes 786440 | tf_op jit(solution)/shard_map/ppermute | solution.py:22
  65.4 10.2 %collective-permute-start.24 = (bf16[4,8,1024]{2,1,0:T(8,128)(2,1)S(1)}, bf16[4,8,1024]{2,1,0:T(8,128)(2,1)S(1)}, u32[]{:S(2)}, u32[]{:S(2)}) collective-permute-start(bf16[4,8,1024]{2,1,0:T(8,128)(2,1)S(1)} %get-tuple-element.33), channel_id=1, source_target_pairs={{0,2},{1,3},{2,0},{3,1},{4,6},{5,7},{6,4},{7,5},{8,10},{9,11},{10,... | collective-permute-start | bytes 196616 | tf_op jit(solution)/shard_map/ppermute | solution.py:22
  75.6 10.3 %copy-start.2 = (bf16[1,4096,384]{2,1,0:T(8,128)(2,1)S(1)}, bf16[1,4096,384]{2,1,0:T(8,128)(2,1)}, u32[]{:S(2)}) copy-start(bf16[1,4096,384]{2,1,0:T(8,128)(2,1)} %refs_5_.1) | copy-start | bytes 9437188
  75.6 10.3 %copy-start.3 = (bf16[1,4096,384]{2,1,0:T(8,128)(2,1)S(1)}, bf16[1,4096,384]{2,1,0:T(8,128)(2,1)}, u32[]{:S(2)}) copy-start(bf16[1,4096,384]{2,1,0:T(8,128)(2,1)} %refs_6_.3) | copy-start | bytes 9437188
  75.6 10.3 %copy-start.7 = (f32[4096]{0:T(1024)S(1)}, f32[4096]{0:T(1024)}, u32[]{:S(2)}) copy-start(f32[4096]{0:T(1024)} %param.18) | copy-start | bytes 49156
  75.6 6.0 %collective-permute-start.25 = (bf16[32,1024]{1,0:T(8,128)(2,1)S(1)}, bf16[32,1024]{1,0:T(8,128)(2,1)S(1)}, u32[]{:S(2)}, u32[]{:S(2)}) collective-permute-start(bf16[32,1024]{1,0:T(8,128)(2,1)S(1)} %routed_sum.3.refs_0_), channel_id=1, source_target_pairs={{0,4},{4,0},{8,12},{12,8},{1,5},{5,1},{9,13},{13,9},{2,6},{6,2},{1... | collective-permute-start | bytes 196616 | tf_op jit(solution)/shard_map/ppermute | solution.py:22
  77.1 23.3 %collective-permute-start.5 = (bf16[128,1024]{1,0:T(8,128)(2,1)S(1)}, bf16[128,1024]{1,0:T(8,128)(2,1)S(1)}, u32[]{:S(2)}, u32[]{:S(2)}) collective-permute-start(bf16[128,1024]{1,0:T(8,128)(2,1)S(1)} %get-tuple-element.19), channel_id=1, source_target_pairs={{0,2},{1,3},{2,0},{3,1},{4,6},{5,7},{6,4},{7,5},{8,10},{9,11},{10,... | collective-permute-start | bytes 786440 | tf_op jit(solution)/shard_map/ppermute | solution.py:22
  80.5 4.6 %collective-permute-start.26 = (bf16[32,1024]{1,0:T(8,128)(2,1)S(1)}, bf16[32,1024]{1,0:T(8,128)(2,1)S(1)}, u32[]{:S(2)}, u32[]{:S(2)}) collective-permute-start(bf16[32,1024]{1,0:T(8,128)(2,1)S(1)} %routed_sum.3.refs_0_), channel_id=1, source_target_pairs={{0,8},{4,12},{8,0},{12,4},{1,9},{5,13},{9,1},{13,5},{2,10},{6,14},... | collective-permute-start | bytes 196616 | tf_op jit(solution)/shard_map/ppermute | solution.py:22
  81.6 4.3 %collective-permute-start.27 = (bf16[32,1024]{1,0:T(8,128)(2,1)S(1)}, bf16[32,1024]{1,0:T(8,128)(2,1)S(1)}, u32[]{:S(2)}, u32[]{:S(2)}) collective-permute-start(bf16[32,1024]{1,0:T(8,128)(2,1)S(1)} %routed_sum.3.refs_0_), channel_id=1, source_target_pairs={{0,12},{4,8},{8,4},{12,0},{1,13},{5,9},{9,5},{13,1},{2,14},{6,10},... | collective-permute-start | bytes 196616 | tf_op jit(solution)/shard_map/ppermute | solution.py:22
  87.0 3.9 %collective-permute-start.28 = (bf16[32,384]{1,0:T(8,128)(2,1)S(1)}, bf16[32,384]{1,0:T(8,128)(2,1)S(1)}, u32[]{:S(2)}, u32[]{:S(2)}) collective-permute-start(bf16[32,384]{1,0:T(8,128)(2,1)S(1)} %hidden_units.1.refs_0_), channel_id=1, source_target_pairs={{0,4},{4,0},{8,12},{12,8},{1,5},{5,1},{9,13},{13,9},{2,6},{6,2},{1... | collective-permute-start | bytes 73736 | tf_op jit(solution)/shard_map/ppermute | solution.py:22
  87.5 6.1 %collective-permute-start.29 = (bf16[32,384]{1,0:T(8,128)(2,1)S(1)}, bf16[32,384]{1,0:T(8,128)(2,1)S(1)}, u32[]{:S(2)}, u32[]{:S(2)}) collective-permute-start(bf16[32,384]{1,0:T(8,128)(2,1)S(1)} %hidden_units.1.refs_0_), channel_id=1, source_target_pairs={{0,8},{4,12},{8,0},{12,4},{1,9},{5,13},{9,1},{13,5},{2,10},{6,14},... | collective-permute-start | bytes 73736 | tf_op jit(solution)/shard_map/ppermute | solution.py:22
  88.5 5.1 %collective-permute-start.30 = (bf16[32,384]{1,0:T(8,128)(2,1)S(1)}, bf16[32,384]{1,0:T(8,128)(2,1)S(1)}, u32[]{:S(2)}, u32[]{:S(2)}) collective-permute-start(bf16[32,384]{1,0:T(8,128)(2,1)S(1)} %hidden_units.1.refs_0_), channel_id=1, source_target_pairs={{0,12},{4,8},{8,4},{12,0},{1,13},{5,9},{9,5},{13,1},{2,14},{6,10},... | collective-permute-start | bytes 73736 | tf_op jit(solution)/shard_map/ppermute | solution.py:22
  89.7 3.9 %copy-start.4 = (bf16[1,1536,1024]{2,1,0:T(8,128)(2,1)S(1)}, bf16[1,1536,1024]{2,1,0:T(8,128)(2,1)}, u32[]{:S(2)}) copy-start(bf16[1,1536,1024]{2,1,0:T(8,128)(2,1)} %refs_4_.7) | copy-start | bytes 9437188
  89.8 12.9 %collective-permute-start.10 = (bf16[64,1024]{1,0:T(8,128)(2,1)S(1)}, bf16[64,1024]{1,0:T(8,128)(2,1)S(1)}, u32[]{:S(2)}, u32[]{:S(2)}) collective-permute-start(bf16[64,1024]{1,0:T(8,128)(2,1)S(1)} %get-tuple-element.23), channel_id=1, source_target_pairs={{0,2},{1,3},{2,0},{3,1},{4,6},{5,7},{6,4},{7,5},{8,10},{9,11},{10,... | collective-permute-start | bytes 393224 | tf_op jit(solution)/shard_map/ppermute | solution.py:22
  90.8 16.4 %copy-start.8 = (f32[64,8]{0,1:T(8,128)S(1)}, f32[64,8]{0,1:T(8,128)}, u32[]{:S(2)}) copy-start(f32[64,8]{0,1:T(8,128)} %param.20) | copy-start | bytes 6148
  90.9 14.9 %collective-permute-start.16 = (bf16[64,1024]{1,0:T(8,128)(2,1)S(1)}, bf16[64,1024]{1,0:T(8,128)(2,1)S(1)}, u32[]{:S(2)}, u32[]{:S(2)}) collective-permute-start(bf16[64,1024]{1,0:T(8,128)(2,1)S(1)} %get-tuple-element.27), channel_id=1, source_target_pairs={{0,2},{1,3},{2,0},{3,1},{4,6},{5,7},{6,4},{7,5},{8,10},{9,11},{10,... | collective-permute-start | bytes 393224 | tf_op jit(solution)/shard_map/ppermute | solution.py:22
  95.0 12.1 %all-to-all-start = ((bf16[16,2,1024]{2,1,0:T(2,128)(2,1)}), bf16[16,2,1024]{2,1,0:T(2,128)(2,1)S(1)}, u32[]{:S(2)}, u32[]{:S(2)}) async-start(bf16[16,2,1024]{2,1,0:T(2,128)(2,1)} %reshape.16), calls=%async_computation | async-start | bytes 131072 | tf_op jit(solution)/shard_map/all_to_all | solution.py:603
  100.5 8.7 %collective-permute-start.6 = (bf16[64,1024]{1,0:T(8,128)(2,1)S(1)}, bf16[64,1024]{1,0:T(8,128)(2,1)S(1)}, u32[]{:S(2)}, u32[]{:S(2)}) collective-permute-start(bf16[64,1024]{1,0:T(8,128)(2,1)S(1)} %get-tuple-element.21), channel_id=1, source_target_pairs={{0,4},{4,0},{8,12},{12,8},{1,5},{5,1},{9,13},{13,9},{2,6},{6,2},{1... | collective-permute-start | bytes 393224 | tf_op jit(solution)/shard_map/ppermute | solution.py:22
  102.7 6.4 %collective-permute-start.11 = (bf16[32,1024]{1,0:T(8,128)(2,1)S(1)}, bf16[32,1024]{1,0:T(8,128)(2,1)S(1)}, u32[]{:S(2)}, u32[]{:S(2)}) collective-permute-start(bf16[32,1024]{1,0:T(8,128)(2,1)S(1)} %get-tuple-element.24), channel_id=1, source_target_pairs={{0,8},{4,12},{8,0},{12,4},{1,9},{5,13},{9,1},{13,5},{2,10},{6,14},... | collective-permute-start | bytes 196616 | tf_op jit(solution)/shard_map/ppermute | solution.py:22
  103.8 5.3 %collective-permute-start.12 = (bf16[32,1024]{1,0:T(8,128)(2,1)S(1)}, bf16[32,1024]{1,0:T(8,128)(2,1)S(1)}, u32[]{:S(2)}, u32[]{:S(2)}) collective-permute-start(bf16[32,1024]{1,0:T(8,128)(2,1)S(1)} %get-tuple-element.25), channel_id=1, source_target_pairs={{0,12},{4,8},{8,4},{12,0},{1,13},{5,9},{9,5},{13,1},{2,14},{6,10},... | collective-permute-start | bytes 196616 | tf_op jit(solution)/shard_map/ppermute | solution.py:22
  105.9 4.9 %collective-permute-start.17 = (bf16[32,1024]{1,0:T(8,128)(2,1)S(1)}, bf16[32,1024]{1,0:T(8,128)(2,1)S(1)}, u32[]{:S(2)}, u32[]{:S(2)}) collective-permute-start(bf16[32,1024]{1,0:T(8,128)(2,1)S(1)} %get-tuple-element.28), channel_id=1, source_target_pairs={{0,8},{4,12},{8,0},{12,4},{1,9},{5,13},{9,1},{13,5},{2,10},{6,14},... | collective-permute-start | bytes 196616 | tf_op jit(solution)/shard_map/ppermute | solution.py:22
  106.6 4.4 %collective-permute-start.18 = (bf16[32,1024]{1,0:T(8,128)(2,1)S(1)}, bf16[32,1024]{1,0:T(8,128)(2,1)S(1)}, u32[]{:S(2)}, u32[]{:S(2)}) collective-permute-start(bf16[32,1024]{1,0:T(8,128)(2,1)S(1)} %get-tuple-element.29), channel_id=1, source_target_pairs={{0,12},{4,8},{8,4},{12,0},{1,13},{5,9},{9,5},{13,1},{2,14},{6,10},... | collective-permute-start | bytes 196616 | tf_op jit(solution)/shard_map/ppermute | solution.py:22

commit v3 on v2

--- a/solution.py
+++ b/solution.py
@@ -24,7 +24,7 @@
 
 def shift(x, axis, by):
     count = lax.axis_size(axis)
-    return lax.ppermute(x, axis, [(i, i + by) for i in range(count - by)])
+    return lax.ppermute(x, axis, [(i, (i + by) % count) for i in range(count)])
 
 
 def reversed_bits(count):
@@ -73,56 +73,81 @@
     return jnp.dot(onehot, rows.astype(jnp.bfloat16), preferred_element_type=jnp.float32)
 
 
+def ready_kernel(
+    lengths_hbm, q_hbm, q_ref, bias_ref, lengths_ref, q_sem, lengths_sem
+):
+    q_copy = pltpu.make_async_copy(q_hbm, q_ref, q_sem)
+    lengths_copy = pltpu.make_async_copy(lengths_hbm, lengths_ref, lengths_sem)
+    lengths_copy.start()
+    q_copy.start()
+    tokens = q_ref.shape[0]
+    window = DOCMAX + KEY_TILE
+    lengths_copy.wait()
+    first = lax.axis_index("ctx") * tokens
+    bounds = [jnp.int32(0)]
+    for i in range(lengths_ref.shape[0] - 1):
+        bounds.append(bounds[-1] + lengths_ref[i])
+    for row0 in range(0, tokens, KEY_TILE):
+        query_pos = first + row0 + lax.broadcasted_iota(jnp.int32, (KEY_TILE, 1), 0)
+        starts = jnp.zeros((KEY_TILE, 1), jnp.int32)
+        for bound in bounds:
+            starts = jnp.where(query_pos >= bound, bound, starts)
+        key_pos = first + row0 - DOCMAX + lax.broadcasted_iota(jnp.int32, (KEY_TILE, window), 1)
+        allowed = (key_pos <= query_pos) & (key_pos >= starts)
+        bias_ref[row0 : row0 + KEY_TILE, :] = jnp.where(allowed, 0.0, -1e30)
+    q_copy.wait()
+
+
+def ready(lengths, queries):
+    tokens = queries.shape[0]
+    return pl.pallas_call(
+        ready_kernel,
+        out_shape=(
+            jax.ShapeDtypeStruct(queries.shape, queries.dtype),
+            jax.ShapeDtypeStruct((tokens, DOCMAX + KEY_TILE), jnp.float32),
+        ),
+        in_specs=[pl.BlockSpec(memory_space=pltpu.HBM)] * 2,
+        out_specs=tuple(whole_vmem(2)),
+        scratch_shapes=[
+            pltpu.SMEM(lengths.shape, jnp.int32),
+            pltpu.SemaphoreType.DMA,
+            pltpu.SemaphoreType.DMA,
+        ],
+        compiler_params=vmem(16),
+        cost_estimate=FREE,
+        name="ready",
+    )(lengths, queries)
+
+
 def attention_kernel(
-    lengths_ref,
-    q_ref,
-    kv_far_ref,
-    kv_near_ref,
-    kv_own_ref,
-    out_ref,
-    k_all,
-    v_all,
-    *,
-    heads,
-    homes,
-    half,
-    sub,
+    q_ref, bias_ref, kv_far_ref, kv_near_ref, kv_own_ref, out_ref, k_all, v_all, *, heads, homes, half, sub
 ):
     tokens = q_ref.shape[0]
     block_tokens = tokens // homes
-    first = lax.axis_index("ctx") * tokens
     exp_index = lax.axis_index("exp")
     for place, ref in enumerate((kv_far_ref, kv_near_ref, kv_own_ref)):
         k_all[place * tokens : (place + 1) * tokens, :] = ref[0]
         v_all[place * tokens : (place + 1) * tokens, :] = ref[1]
     order = reversed_bits(homes)
-    reach = DOCMAX
-    window = reach + KEY_TILE
-    docs = lengths_ref.shape[0]
+    window = DOCMAX + KEY_TILE
     scale = LOG2E / HD**0.5
-
-    @pl.loop(0, homes)
-    def one_home(home):
-        row0 = pl.multiple_of(home * block_tokens + half * sub, sub)
-        key0 = pl.multiple_of(row0 // KEY_TILE * KEY_TILE, KEY_TILE)
-        query_pos = first + row0 + lax.broadcasted_iota(jnp.int32, (sub, 1), 0)
-        starts = jnp.zeros((sub, 1), jnp.int32)
-        bound = jnp.int32(0)
-        for i in range(docs):
-            starts = jnp.where(query_pos >= bound, bound, starts)
-            bound = bound + lengths_ref[i]
-        key_pos = first + key0 - reach + lax.broadcasted_iota(jnp.int32, (sub, window), 1)
-        allowed = (key_pos <= query_pos) & (key_pos >= starts)
-        bias = jnp.where(allowed, 0.0, -1e30)
+    for home in range(homes):
+        row0 = home * block_tokens + half * sub
+        key0 = row0 // KEY_TILE * KEY_TILE
+        k = k_all[key0 : key0 + window, :]
+        v = v_all[key0 : key0 + window, :]
+        other = home ^ exp_index
+        place = jnp.int32(0)
+        for position in range(homes):
+            place = jnp.where(other == order[position], position, place)
+        at = pl.multiple_of(place * sub, sub)
         queries = jnp.concatenate(
-            [q_ref[pl.ds(row0, sub), h * HD : (h + 1) * HD] for h in range(heads)], axis=0
+            [q_ref[row0 : row0 + sub, h * HD : (h + 1) * HD] for h in range(heads)], axis=0
         )
-        k = k_all[pl.ds(key0, window), :]
-        v = v_all[pl.ds(key0, window), :]
         scores = lax.dot_general(
             queries, k, (((1,), (1,)), ((), ())), preferred_element_type=jnp.float32
         )
-        scores = scores.reshape(heads, sub, window) * scale + bias[None]
+        scores = scores.reshape(heads, sub, window) * scale + bias_ref[row0 : row0 + sub, :][None]
         best = jnp.max(scores, axis=2, keepdims=True)
         probs = jnp.exp2(scores - best)
         total = jnp.sum(probs, axis=2, keepdims=True)
@@ -132,29 +157,24 @@
             preferred_element_type=jnp.float32,
         )
         result = (mixed / total.reshape(heads * sub, 1)).astype(jnp.bfloat16)
-        other = home ^ exp_index
-        place = jnp.int32(0)
-        for position in range(homes):
-            place = jnp.where(other == order[position], position, place)
-        at = pl.multiple_of(place * sub, sub)
         for h in range(heads):
             out_ref[pl.ds(at, sub), h * HD : (h + 1) * HD] = result[h * sub : (h + 1) * sub]
 
 
-def attention(lengths, queries, kv_far, kv_near, kv_own, homes, half, sub):
+def attention(queries, bias, kv_far, kv_near, kv_own, homes, half, sub):
     tokens, width = queries.shape
     return pl.pallas_call(
         functools.partial(
             attention_kernel, heads=width // HD, homes=homes, half=half, sub=sub
         ),
         out_shape=jax.ShapeDtypeStruct((homes * sub, width), jnp.bfloat16),
-        in_specs=[pl.BlockSpec(memory_space=pltpu.SMEM)] + whole_vmem(4),
+        in_specs=whole_vmem(5),
         out_specs=pl.BlockSpec(memory_space=pltpu.VMEM),
         scratch_shapes=[pltpu.VMEM((3 * tokens, HD), jnp.bfloat16)] * 2,
         compiler_params=vmem(24),
         cost_estimate=FREE,
         name="attention_" + str(half),
-    )(lengths, queries, kv_far, kv_near, kv_own)
+    )(queries, bias, kv_far, kv_near, kv_own)
 
 
 def pick_kernel(residual_ref, *refs, homes, halves, sub):
@@ -206,8 +226,8 @@
     out_ref[lines:, :] = rows.astype(jnp.bfloat16)
 
 
-def pick(residual, routes_pieces, heads_out, sub):
-    homes = len(routes_pieces)
+def pick(residual, routes_all, heads_out, sub):
+    homes = len(routes_all)
     width = heads_out[0].shape[1]
     rows = homes * homes * CAP + homes * CAP * (residual.shape[1] // width)
     return pl.pallas_call(
@@ -218,7 +238,7 @@
         compiler_params=vmem(16),
         cost_estimate=FREE,
         name="pick",
-    )(residual, *routes_pieces, *heads_out)
+    )(residual, *routes_all, *heads_out)
 
 
 def routed_kernel(*refs, count, homes, after):
@@ -495,26 +515,75 @@
     return [x] + [swap(x, axis, k) for k in range(1, lax.axis_size(axis))]
 
 
-def sum_over_exp(keep, send, kinds):
-    count = lax.axis_size("exp")
-    step = 1
-    while True:
-        arrived = swap(send, "exp", step)
-        step *= 2
-        if step >= count:
-            return add(keep, arrived, kinds)
-        keep, send = add(keep, arrived, (jnp.float32, jnp.bfloat16))
-
-
-def routed_over_exp(keep, send):
-    count = lax.axis_size("exp")
-    step = 1
-    while True:
-        arrived = swap(send, "exp", step)
-        step *= 2
-        if step >= count:
-            return add_middle(keep, arrived, True)
-        keep, send = add_middle(keep, arrived, False)
+def after(x, *others):
+    return lax.optimization_barrier((x,) + others)[0]
+
+
+class Sequence:
+    def __init__(self):
+        self.last = None
+
+    def tie(self, *xs):
+        if self.last is None:
+            return xs
+        return lax.optimization_barrier(xs + (self.last,))[:-1]
+
+    def run(self, step, xs, *rest):
+        out = step(*self.tie(*xs), *rest)
+        self.last = out[-1] if isinstance(out, (tuple, list)) else out
+        return out
+
+
+class Gather:
+    def __init__(self, sequence, x):
+        self.sequence = sequence
+        self.found = {0: x}
+        self.step = lax.axis_size("ctx") // 2
+
+    def hop(self):
+        names = sorted(self.found)
+        pieces = self.sequence.tie(*[self.found[k] for k in names])
+        for k, piece in zip(names, pieces):
+            self.found[k ^ self.step] = swap(piece, "ctx", self.step)
+        self.step //= 2
+
+    def hops_to(self, step):
+        while self.step >= step:
+            self.hop()
+
+    def pieces(self, names):
+        return tuple(self.found[k] for k in names)
+
+
+class Halving:
+    def __init__(self, sequence, send, add_step):
+        self.sequence = sequence
+        self.keep = None
+        self.result = None
+        self.step = 1
+        self.add_step = add_step
+        self.count = lax.axis_size("exp")
+        self.arrived = swap(send, "exp", 1)
+
+    def advance(self, hold=False):
+        self.step *= 2
+        last = self.step >= self.count
+        out = self.sequence.run(lambda k, a: self.add_step(k, a, last), (self.keep, self.arrived))
+        if last:
+            self.result = out
+        else:
+            self.keep, self.send = out
+            if not hold:
+                self.release()
+
+    def release(self):
+        (send,) = self.sequence.tie(self.send)
+        self.arrived = swap(send, "exp", self.step)
+
+    def finish(self):
+        while self.step < self.count:
+            self.advance()
+        return self.result
 
 
 def shards(
@@ -543,10 +612,14 @@
     cols = out_weight.shape[1]
     halves = 2 if block_tokens % 32 == 0 else 1
     sub = block_tokens // halves
-    kinds = jnp.bfloat16
-
-    routes_t = routes.T
-    routes_pieces = gather_pieces(routes_t, "exp")
+    sequence = Sequence()
+
+    def plain_add(kinds):
+        def step(keep, arrived, last):
+            return add(keep, arrived, kinds if last else (jnp.float32, jnp.bfloat16))
+
+        return step
+
     kv_head = exp_index * local_heads // (QH // KVH)
     kv_own = jnp.stack(
         [
@@ -556,50 +629,74 @@
     )
     kv_near = shift(kv_own, "ctx", 1)
     kv_far = shift(kv_own, "ctx", 2)
-    heads_out = [
-        attention(doc_lengths, queries, kv_far, kv_near, kv_own, homes, half, sub)
-        for half in range(halves)
-    ]
-    near = [swap(rows, "ctx", 1) for rows in heads_out]
-    routed = pick(residual_in, routes_pieces, heads_out, sub)
-    routed_pieces = gather_pieces(routed, "ctx")
-
+    q_ready, bias = ready(doc_lengths, after(queries, kv_own))
+
+    routes_all = gather_direct(after(routes.T, kv_own), "exp")
+    heads_out = []
+    near = []
     far = []
-    for rows in heads_out:
-        found = {0: rows}
-        step = n_ctx // 2
-        while step >= 2:
-            for k in sorted(found):
-                found[k ^ step] = swap(found[k], "ctx", step)
-            step //= 2
-        for k in sorted(found):
-            if k:
-                found[k ^ 1] = swap(found[k], "ctx", 1)
-        far.append({k: found[k] for k in sorted(found) if k})
-
-    both = heads_out + near
-    send = project(both, out_weight, homes, sub, True)
-    keep = project(both, out_weight, homes, sub, False)
-    own_sum, near_sum = sum_over_exp(keep, send, (kinds, kinds))
-    parts = [own_sum, swap(near_sum, "ctx", 1)]
-    places = [(0, 0), (1, 0)]
-
-    keep, send = routed_product(routed_pieces, out_weight, homes)
-    routed_rows = routed_over_exp(keep, send)
-    stream_rows = gather_direct(routed_rows, "ctx")
-    hidden = hidden_units(stream_rows, norm_gain[None, :], gate_weight, up_weight)
-
     for half in range(halves):
-        names = sorted(far[half])
-        blocks = [far[half][k] for k in names]
-        send = project(blocks, out_weight, homes, sub, True)
-        keep = project(blocks, out_weight, homes, sub, False)
-        sums = sum_over_exp(keep, send, (kinds,) * len(names))
-        for k, piece in zip(names, sums):
-            parts.append(swap(piece, "ctx", k))
-            places.append((k, half * sub))
-
-    produced = down_product(gather_direct(hidden, "ctx"), down_weight)
+        if half == halves - 1:
+            routes_all = list(sequence.tie(*routes_all))
+            (q_ready,) = lax.optimization_barrier((q_ready,) + tuple(routes_all))[:1]
+        rows = sequence.run(
+            lambda q: attention(q, bias, kv_far, kv_near, kv_own, homes, half, sub), (q_ready,)
+        )
+        heads_out.append(rows)
+        near.append(swap(rows, "ctx", 1))
+        far.append(Gather(sequence, rows))
+
+    def leaving(blocks):
+        return sequence.run(lambda *xs: project(xs, out_weight, homes, sub, True), blocks)
+
+    def staying(blocks):
+        return sequence.run(lambda *xs: project(xs, out_weight, homes, sub, False), blocks)
+
+    names = [k for k in range(n_ctx) if k > 1]
+    one = (jnp.bfloat16,)
+    mine = tuple(heads_out)
+    near = tuple(near)
+    own = Halving(sequence, leaving(mine), plain_add(one))
+    routed = sequence.run(lambda r: pick(r, routes_all, heads_out, sub), (residual_in,))
+    routed_all = Gather(sequence, routed)
+    routed_all.hops_to(2)
+    beside = Halving(sequence, leaving(near), plain_add(one))
+    own.keep = staying(mine)
+    beside.keep = staying(near)
+    own.advance()
+    routed_all.hop()
+    for gather in far:
+        gather.found[0] = after(gather.found[0], routed_all.found[n_ctx // 2])
+        gather.hops_to(2)
+    keep, send = sequence.run(
+        lambda *xs: routed_product(xs, out_weight, homes), routed_all.pieces(range(n_ctx))
+    )
+    routed_sum = Halving(sequence, send, add_middle)
+    routed_sum.keep = keep
+    beside.advance()
+    (own_sum,) = own.finish()
+    routed_sum.advance()
+    far[0].hop()
+    first = far[0].pieces(names)
+    sums = [Halving(sequence, leaving(first), plain_add(one * len(names)))]
+    sums[0].keep = staying(first)
+    (near_sum,) = beside.finish()
+    routed_sum.finish()
+    stream_rows = gather_direct(routed_sum.result, "ctx")
+    sums[0].advance()
+    if halves > 1:
+        far[1].hop()
+        second = far[1].pieces(names)
+        sums.append(Halving(sequence, leaving(second), plain_add(one * len(names))))
+        sums[1].keep = staying(second)
+    hidden = sequence.run(
+        lambda *xs: hidden_units(xs, norm_gain[None, :], gate_weight, up_weight), tuple(stream_rows)
+    )
+    hidden_pieces = gather_direct(hidden, "ctx")
+    sums[0].finish()
+    if halves > 1:
+        sums[1].advance()
+    produced = sequence.run(lambda *xs: down_product(xs, down_weight), tuple(hidden_pieces))
     back = lax.all_to_all(
         produced.reshape(n_ctx * homes, CAP, cols),
         ("ctx", "exp"),
@@ -607,16 +704,28 @@
         concat_axis=0,
         tiled=True,
     ).reshape(n_ctx, flight * CAP, cols)
-    combined = pl.pallas_call(
-        functools.partial(combine_kernel, flight=flight, count=n_ctx),
-        out_shape=jax.ShapeDtypeStruct((block_tokens, width), jnp.bfloat16),
-        in_specs=whole_vmem(2 + n_ctx),
-        out_specs=pl.BlockSpec(memory_space=pltpu.VMEM),
-        compiler_params=vmem(20),
-        cost_estimate=FREE,
-        name="combine",
-    )(routes_t, route_weights.T, *[back[i] for i in range(n_ctx)])
-    attended = attended_rows(parts, places, residual_in)
+    for total in sums:
+        total.finish()
+    parts = [own_sum, swap(near_sum, "ctx", 1)]
+    places = [(0, 0), (1, 0)]
+
+    def combine(*back):
+        return pl.pallas_call(
+            functools.partial(combine_kernel, flight=flight, count=n_ctx),
+            out_shape=jax.ShapeDtypeStruct((block_tokens, width), jnp.bfloat16),
+            in_specs=whole_vmem(2 + n_ctx),
+            out_specs=pl.BlockSpec(memory_space=pltpu.VMEM),
+            compiler_params=vmem(20),
+            cost_estimate=FREE,
+            name="combine",
+        )(routes.T, route_weights.T, *back)
+
+    combined = sequence.run(combine, tuple(back[i] for i in range(n_ctx)))
+    for half in range(halves):
+        for k, piece in zip(names, sums[half].result):
+            parts.append(swap(piece, "ctx", k))
+            places.append((k, half * sub))
+    attended = sequence.run(lambda *xs: attended_rows(xs, places, residual_in), tuple(parts))
     return (attended, combined)
 
 

time: 112 us -> 95.5 us (0.85)
  waiting for transfers between devices: 44.8 us -> 29.7 us
  Pallas kernels: 21.5 us -> 19.7 us
    ppermute x29 -> x33, waiting for transfers between devices: 42.5 us -> 27.1 us  [swap(): return lax.ppermute(x, axis, [(i, i ^ mask) for i in range(count)])]
    ppermute x29 -> x33, starting transfers between devices: 30.1 us -> 34.6 us  [swap(): return lax.ppermute(x, axis, [(i, i ^ mask) for i in range(count)])]
    pallas_call x2, Pallas kernels: 8.48 us -> 5.27 us  [attention(): pl.pallas_call(functools.partial(attention_kernel, heads=width // HD, hom...]
    all_to_all x1, waiting for transfers between devices: 0.42 us -> 2.58 us  [shards(): lax.all_to_all(produced.reshape(n_ctx * homes, CAP, cols), ('ctx', 'exp')...]
    all_to_all x1, starting transfers between devices: 5.46 us -> 3.5 us  [shards(): lax.all_to_all(produced.reshape(n_ctx * homes, CAP, cols), ('ctx', 'exp')...]
    ppermute x2, waiting for transfers between devices: 1.84 us -> 0.01 us  [shift(): return lax.ppermute(x, axis, [(i, (i + by) % count) for i in range(count)])]
    ppermute x2, starting transfers between devices: 4.7 us -> 3.01 us  [shift(): return lax.ppermute(x, axis, [(i, (i + by) % count) for i in range(count)])]
    pallas_call x1 -> x2, Pallas kernels: 1.95 us -> 2.81 us  [the longest x1 1.95 us: combine(): pl.pallas_call(functools.partial(combine_kernel, flight=flight, count=n_c...]
  transfers between devices with their start and end apart: 32 -> 36, of which waited for: 14 -> 14; matrix products, arithmetic and copies ran while one was open for 2% -> 1% of each run, Pallas kernels for 9% -> 19%
where the time goes in v3:
time: 95.5 us; the launch traced here: 95.2 us
  starting transfers between devices  41.1 us (43%)
  waiting for transfers between devices  29.7 us (31%)
  Pallas kernels  19.7 us (21%)
  local copies, waits for them, and re-layouts  3.61 us (4%)
  between operations  1.05 us (1%)
    ppermute x33, starting transfers between devices, swap(): return lax.ppermute(x, axis, [(i, i ^ mask) for i in range(count)])  34.6 us
    ppermute x33, waiting for transfers between devices, swap(): return lax.ppermute(x, axis, [(i, i ^ mask) for i in range(count)])  27.1 us
    pallas_call x8, Pallas kernels, project(): pl.pallas_call(functools.partial(project_kernel, count=count, homes=homes...  5.95 us
    pallas_call x2, Pallas kernels, attention(): pl.pallas_call(functools.partial(attention_kernel, heads=width // HD, hom...  5.27 us
    all_to_all x1, starting transfers between devices, shards(): lax.all_to_all(produced.reshape(n_ctx * homes, CAP, cols), ('ctx', 'exp')...  3.5 us
    ppermute x2, starting transfers between devices, shift(): return lax.ppermute(x, axis, [(i, (i + by) % count) for i in range(count)])  3.01 us
    all_to_all x1, waiting for transfers between devices, shards(): lax.all_to_all(produced.reshape(n_ctx * homes, CAP, cols), ('ctx', 'exp')...  2.58 us
    pallas_call x1, Pallas kernels, combine(): pl.pallas_call(functools.partial(combine_kernel, flight=flight, count=n_c...  1.95 us
  transfers between devices with their start and end apart: 36, of which 14 were waited for; matrix products, arithmetic and copies ran while one was open for 1% of the time, Pallas kernels for 19%

profile of v3, /device:TPU:0, one launch (start us, length us, event | category | flops | bytes accessed | tf_op | source)
XLA Modules:
  0.0 95.2 jit_solution(3546659486051015679)
XLA Ops:
  0.6 0.9 dynamic-slice_bitcast_fusion
  1.6 3.0 %collective-permute-start = (bf16[2,256,128]{2,1,0:T(8,128)(2,1)S(1)}, bf16[2,256,128]{2,1,0:T(8,128)(2,1)S(1)}, u32[]{:S(2)}, u32[]{:S(2)}) collective-permute-start(bf16[2,256,128]{2,1,0:T(8,128)(2,1)S(1)} %pad_maximum_fusion.kv_own_ref), channel_id=1, source_target_pairs={{0,8},{4,12},{8,0},{12,4},{1,9},{5,13},{9,1},{13,5},{2,10},{6,14},... | collective-permute-start | bytes 393224 | tf_op jit(solution)/shard_map/ppermute | solution.py:27
  4.6 1.6 %collective-permute-start.2 = (s32[8,64]{1,0:T(8,128)}, s32[8,64]{1,0:T(8,128)S(1)}, u32[]{:S(2)}, u32[]{:S(2)}) collective-permute-start(s32[8,64]{1,0:T(8,128)} %bitcast.8), channel_id=1, source_target_pairs={{0,1},{1,0},{2,3},{3,2},{4,5},{5,4},{6,7},{7,6},{8,9},{9,8},{10,11... | collective-permute-start | bytes 6152 | tf_op jit(solution)/shard_map/ppermute | solution.py:22
  6.2 2.6 %collective-permute-start.3 = (s32[8,64]{1,0:T(8,128)}, s32[8,64]{1,0:T(8,128)S(1)}, u32[]{:S(2)}, u32[]{:S(2)}) collective-permute-start(s32[8,64]{1,0:T(8,128)} %bitcast.9), channel_id=1, source_target_pairs={{0,2},{1,3},{2,0},{3,1},{4,6},{5,7},{6,4},{7,5},{8,10},{9,11},{10,... | collective-permute-start | bytes 6152 | tf_op jit(solution)/shard_map/ppermute | solution.py:22
  9.0 1.2 %copy-done.5 = bf16[256,2048]{1,0:T(8,128)(2,1)S(1)} copy-done((bf16[256,2048]{1,0:T(8,128)(2,1)S(1)}, bf16[256,2048]{1,0:T(8,128)(2,1)}, u32[]{:S(2)}) %copy-start.5) | copy-done | bytes 1048600
  10.8 0.9 ready.1
  11.7 2.6 %attention_0.1.refs_0_.refs_4_ = bf16[128,2048]{1,0:T(8,128)(2,1)S(1)} custom-call(bf16[256,2048]{1,0:T(8,128)(2,1)S(1)} %get-tuple-element.110.q_ref, f32[256,640]{1,0:T(8,128)S(1)} %get-tuple-element.103.bias_ref, bf16[2,256,128]{2,1,0:T(8,128)(2,1)S(1)} %collective-permute-done.kv_far_ref, bf16[2,256,128]{2,1,0:T(8,128)(2,1)S(1)} %collective-permute-done.1.kv_near_ref, ...), custom_call_target="tpu_custom_call" | custom-call | tf_op jit(solution)/shard_map/attention_0/pallas_call | solution.py:166
  14.5 2.6 %attention_1.1.refs_1_.refs_5_ = bf16[128,2048]{1,0:T(8,128)(2,1)S(1)} custom-call(bf16[256,2048]{1,0:T(8,128)(2,1)S(1)} %get-tuple-element.110.q_ref, f32[256,640]{1,0:T(8,128)S(1)} %get-tuple-element.103.bias_ref, bf16[2,256,128]{2,1,0:T(8,128)(2,1)S(1)} %collective-permute-done.kv_far_ref, bf16[2,256,128]{2,1,0:T(8,128)(2,1)S(1)} %collective-permute-done.1.kv_near_ref, ...), custom_call_target="tpu_custom_call" | custom-call | tf_op jit(solution)/shard_map/attention_1/pallas_call | solution.py:166
  17.7 0.7 project_leave.4
  18.4 0.8 collective-permute-start.7
  19.2 1.8 %pick.1.refs_0_ = bf16[48,2048]{1,0:T(8,128)(2,1)S(1)} custom-call(bf16[64,4096]{1,0:T(8,128)(2,1)S(1)} %copy-done.4, s32[8,64]{1,0:T(8,128)S(1)} %bitcast.11, s32[8,64]{1,0:T(8,128)S(1)} %collective-permute-done.2.refs_1_, s32[8,64]{1,0:T(8,128)S(1)} %collective-permute-done.3.refs_2_, s32[8,64]{1,0:T(8,128)S(1)} %collective-permute-done.4.refs_3_, ...), custom_call_target="tpu_custom_call" | custom-call | tf_op jit(solution)/shard_map/pick/pallas_call | solution.py:233
  21.0 0.9 collective-permute-start.10
  21.9 5.7 %collective-permute-done.10.refs_2_ = bf16[48,2048]{1,0:T(8,128)(2,1)S(1)} collective-permute-done((bf16[48,2048]{1,0:T(8,128)(2,1)S(1)}, bf16[48,2048]{1,0:T(8,128)(2,1)S(1)}, u32[]{:S(2)}, u32[]{:S(2)}) %collective-permute-start.10) | collective-permute-done | bytes 196640 | tf_op jit(solution)/shard_map/ppermute | solution.py:22
  27.6 0.7 project_leave.5
  28.4 0.7 project_stay.4.keep_ref
  29.1 0.7 project_stay.5.keep_ref
  29.9 1.3 %collective-permute-start.14 = (bf16[128,2048]{1,0:T(8,128)(2,1)S(1)}, bf16[128,2048]{1,0:T(8,128)(2,1)S(1)}, u32[]{:S(2)}, u32[]{:S(2)}) collective-permute-start(bf16[128,2048]{1,0:T(8,128)(2,1)S(1)} %attention_0.1.refs_0_.refs_4_), channel_id=1, source_target_pairs={{0,8},{4,12},{8,0},{12,4},{1,9},{5,13},{9,1},{13,5},{2,10},{6,14},... | collective-permute-start | bytes 1572872 | tf_op jit(solution)/shard_map/ppermute | solution.py:22
  31.7 1.4 %collective-permute-start.9 = (bf16[128,1024]{1,0:T(8,128)(2,1)S(1)}, bf16[128,1024]{1,0:T(8,128)(2,1)S(1)}, u32[]{:S(2)}, u32[]{:S(2)}) collective-permute-start(bf16[128,1024]{1,0:T(8,128)(2,1)S(1)} %project_leave.5), channel_id=1, source_target_pairs={{0,1},{1,0},{2,3},{3,2},{4,5},{5,4},{6,7},{7,6},{8,9},{9,8},{10,11... | collective-permute-start | bytes 786440 | tf_op jit(solution)/shard_map/ppermute | solution.py:22
  33.1 2.4 %collective-permute-start.8 = (bf16[64,1024]{1,0:T(8,128)(2,1)S(1)}, bf16[64,1024]{1,0:T(8,128)(2,1)S(1)}, u32[]{:S(2)}, u32[]{:S(2)}) collective-permute-start(bf16[64,1024]{1,0:T(8,128)(2,1)S(1)} %get-tuple-element.124), channel_id=1, source_target_pairs={{0,2},{1,3},{2,0},{3,1},{4,6},{5,7},{6,4},{7,5},{8,10},{9,11},{10,... | collective-permute-start | bytes 393224 | tf_op jit(solution)/shard_map/ppermute | solution.py:22
  35.5 0.8 routed_product.1
  36.3 1.8 %collective-permute-start.15 = (bf16[4,16,1024]{2,1,0:T(8,128)(2,1)S(1)}, bf16[4,16,1024]{2,1,0:T(8,128)(2,1)S(1)}, u32[]{:S(2)}, u32[]{:S(2)}) collective-permute-start(bf16[4,16,1024]{2,1,0:T(8,128)(2,1)S(1)} %get-tuple-element.132), channel_id=1, source_target_pairs={{0,1},{1,0},{2,3},{3,2},{4,5},{5,4},{6,7},{7,6},{8,9},{9,8},{10,11... | collective-permute-start | bytes 393224 | tf_op jit(solution)/shard_map/ppermute | solution.py:22
  38.1 5.6 %collective-permute-done.9.arrived_ref = bf16[128,1024]{1,0:T(8,128)(2,1)S(1)} collective-permute-done((bf16[128,1024]{1,0:T(8,128)(2,1)S(1)}, bf16[128,1024]{1,0:T(8,128)(2,1)S(1)}, u32[]{:S(2)}, u32[]{:S(2)}) %collective-permute-start.9) | collective-permute-done | bytes 262176 | tf_op jit(solution)/shard_map/ppermute | solution.py:22
  43.8 1.7 %collective-permute-done.15.arrived_ref = bf16[4,16,1024]{2,1,0:T(8,128)(2,1)S(1)} collective-permute-done((bf16[4,16,1024]{2,1,0:T(8,128)(2,1)S(1)}, bf16[4,16,1024]{2,1,0:T(8,128)(2,1)S(1)}, u32[]{:S(2)}, u32[]{:S(2)}) %collective-permute-start.15) | collective-permute-done | bytes 131104 | tf_op jit(solution)/shard_map/ppermute | solution.py:22
  45.7 0.8 collective-permute-start.24
  46.5 1.1 %collective-permute-done.16.refs_1_ = bf16[128,2048]{1,0:T(8,128)(2,1)S(1)} collective-permute-done((bf16[128,2048]{1,0:T(8,128)(2,1)S(1)}, bf16[128,2048]{1,0:T(8,128)(2,1)S(1)}, u32[]{:S(2)}, u32[]{:S(2)}) %collective-permute-start.16) | collective-permute-done | bytes 524320 | tf_op jit(solution)/shard_map/ppermute | solution.py:22
  47.6 0.7 project_leave.6
  48.3 1.7 %collective-permute-start.18 = (bf16[128,1024]{1,0:T(8,128)(2,1)S(1)}, bf16[128,1024]{1,0:T(8,128)(2,1)S(1)}, u32[]{:S(2)}, u32[]{:S(2)}) collective-permute-start(bf16[128,1024]{1,0:T(8,128)(2,1)S(1)} %project_leave.6), channel_id=1, source_target_pairs={{0,1},{1,0},{2,3},{3,2},{4,5},{5,4},{6,7},{7,6},{8,9},{9,8},{10,11... | collective-permute-start | bytes 786440 | tf_op jit(solution)/shard_map/ppermute | solution.py:22
  50.1 2.1 %collective-permute-start.13 = (bf16[64,1024]{1,0:T(8,128)(2,1)S(1)}, bf16[64,1024]{1,0:T(8,128)(2,1)S(1)}, u32[]{:S(2)}, u32[]{:S(2)}) collective-permute-start(bf16[64,1024]{1,0:T(8,128)(2,1)S(1)} %get-tuple-element.139), channel_id=1, source_target_pairs={{0,2},{1,3},{2,0},{3,1},{4,6},{5,7},{6,4},{7,5},{8,10},{9,11},{10,... | collective-permute-start | bytes 393224 | tf_op jit(solution)/shard_map/ppermute | solution.py:22
  52.2 0.8 collective-permute-start.19
  53.7 5.8 %collective-permute-done.13.arrived_ref = bf16[64,1024]{1,0:T(8,128)(2,1)S(1)} collective-permute-done((bf16[64,1024]{1,0:T(8,128)(2,1)S(1)}, bf16[64,1024]{1,0:T(8,128)(2,1)S(1)}, u32[]{:S(2)}, u32[]{:S(2)}) %collective-permute-start.13) | collective-permute-done | bytes 131104 | tf_op jit(solution)/shard_map/ppermute | solution.py:22
  60.2 0.7 collective-permute-done.18.arrived_ref
  61.1 1.9 %collective-permute-done.25.refs_1_ = bf16[128,2048]{1,0:T(8,128)(2,1)S(1)} collective-permute-done((bf16[128,2048]{1,0:T(8,128)(2,1)S(1)}, bf16[128,2048]{1,0:T(8,128)(2,1)S(1)}, u32[]{:S(2)}, u32[]{:S(2)}) %collective-permute-start.25) | collective-permute-done | bytes 524320 | tf_op jit(solution)/shard_map/ppermute | solution.py:22
  63.0 0.9 project_leave.7
  63.9 3.6 %collective-permute-start.28 = (bf16[128,1024]{1,0:T(8,128)(2,1)S(1)}, bf16[128,1024]{1,0:T(8,128)(2,1)S(1)}, u32[]{:S(2)}, u32[]{:S(2)}) collective-permute-start(bf16[128,1024]{1,0:T(8,128)(2,1)S(1)} %project_leave.7), channel_id=1, source_target_pairs={{0,1},{1,0},{2,3},{3,2},{4,5},{5,4},{6,7},{7,6},{8,9},{9,8},{10,11... | collective-permute-start | bytes 786440 | tf_op jit(solution)/shard_map/ppermute | solution.py:22
  67.5 1.3 %collective-permute-start.20 = (bf16[64,1024]{1,0:T(8,128)(2,1)S(1)}, bf16[64,1024]{1,0:T(8,128)(2,1)S(1)}, u32[]{:S(2)}, u32[]{:S(2)}) collective-permute-start(bf16[64,1024]{1,0:T(8,128)(2,1)S(1)} %get-tuple-element.161), channel_id=1, source_target_pairs={{0,2},{1,3},{2,0},{3,1},{4,6},{5,7},{6,4},{7,5},{8,10},{9,11},{10,... | collective-permute-start | bytes 393224 | tf_op jit(solution)/shard_map/ppermute | solution.py:22
  68.8 0.8 collective-permute-start.22
  69.6 1.1 %collective-permute-start.23 = (bf16[32,1024]{1,0:T(8,128)(2,1)S(1)}, bf16[32,1024]{1,0:T(8,128)(2,1)S(1)}, u32[]{:S(2)}, u32[]{:S(2)}) collective-permute-start(bf16[32,1024]{1,0:T(8,128)(2,1)S(1)} %routed_sum.3.refs_0_), channel_id=1, source_target_pairs={{0,12},{4,8},{8,4},{12,0},{1,13},{5,9},{9,5},{13,1},{2,14},{6,10},... | collective-permute-start | bytes 196616 | tf_op jit(solution)/shard_map/ppermute | solution.py:22
  70.7 0.7 project_stay.7.keep_ref
  71.4 2.3 %collective-permute-done.22.refs_2_ = bf16[32,1024]{1,0:T(8,128)(2,1)S(1)} collective-permute-done((bf16[32,1024]{1,0:T(8,128)(2,1)S(1)}, bf16[32,1024]{1,0:T(8,128)(2,1)S(1)}, u32[]{:S(2)}, u32[]{:S(2)}) %collective-permute-start.22) | collective-permute-done | bytes 65568 | tf_op jit(solution)/shard_map/ppermute | solution.py:22
  74.4 1.1 %hidden_units.1.refs_0_ = bf16[32,384]{1,0:T(8,128)(2,1)S(1)} custom-call(bf16[32,1024]{1,0:T(8,128)(2,1)S(1)} %routed_sum.3.refs_0_, bf16[32,1024]{1,0:T(8,128)(2,1)S(1)} %collective-permute-done.21.refs_1_, bf16[32,1024]{1,0:T(8,128)(2,1)S(1)} %collective-permute-done.22.refs_2_, bf16[32,1024]{1,0:T(8,128)(2,1)S(1)} %collective-permute-done.23.refs_3_, ...), custom_call_target="tpu_custom_call" | custom-call | tf_op jit(solution)/shard_map/hidden_units/pallas_call | solution.py:408
  76.0 0.8 collective-permute-start.31
  77.6 2.2 %collective-permute-start.29 = (bf16[64,1024]{1,0:T(8,128)(2,1)S(1)}, bf16[64,1024]{1,0:T(8,128)(2,1)S(1)}, u32[]{:S(2)}, u32[]{:S(2)}) collective-permute-start(bf16[64,1024]{1,0:T(8,128)(2,1)S(1)} %get-tuple-element.181), channel_id=1, source_target_pairs={{0,2},{1,3},{2,0},{3,1},{4,6},{5,7},{6,4},{7,5},{8,10},{9,11},{10,... | collective-permute-start | bytes 393224 | tf_op jit(solution)/shard_map/ppermute | solution.py:22
  81.6 3.5 %all-to-all-start = ((bf16[16,2,1024]{2,1,0:T(2,128)(2,1)}), bf16[16,2,1024]{2,1,0:T(2,128)(2,1)S(1)}, u32[]{:S(2)}, u32[]{:S(2)}) async-start(bf16[16,2,1024]{2,1,0:T(2,128)(2,1)} %reshape.16), calls=%async_computation | async-start | bytes 131072 | tf_op jit(solution)/shard_map/all_to_all | solution.py:700
  85.5 1.7 %collective-permute-start.27 = (bf16[32,1024]{1,0:T(8,128)(2,1)S(1)}, bf16[32,1024]{1,0:T(8,128)(2,1)S(1)}, u32[]{:S(2)}, u32[]{:S(2)}) collective-permute-start(bf16[32,1024]{1,0:T(8,128)(2,1)S(1)} %get-tuple-element.176), channel_id=1, source_target_pairs={{0,12},{4,8},{8,4},{12,0},{1,13},{5,9},{9,5},{13,1},{2,14},{6,10},... | collective-permute-start | bytes 196616 | tf_op jit(solution)/shard_map/ppermute | solution.py:22
  87.4 1.9 %collective-permute-start.33 = (bf16[32,1024]{1,0:T(8,128)(2,1)S(1)}, bf16[32,1024]{1,0:T(8,128)(2,1)S(1)}, u32[]{:S(2)}, u32[]{:S(2)}) collective-permute-start(bf16[32,1024]{1,0:T(8,128)(2,1)S(1)} %get-tuple-element.188), channel_id=1, source_target_pairs={{0,8},{4,12},{8,0},{12,4},{1,9},{5,13},{9,1},{13,5},{2,10},{6,14},... | collective-permute-start | bytes 196616 | tf_op jit(solution)/shard_map/ppermute | solution.py:22
  89.2 2.6 %all-to-all-done = bf16[16,2,1024]{2,1,0:T(2,128)(2,1)S(1)} async-done(((bf16[16,2,1024]{2,1,0:T(2,128)(2,1)}), bf16[16,2,1024]{2,1,0:T(2,128)(2,1)S(1)}, u32[]{:S(2)}, u32[]{:S(2)}) %all-to-all-start) | async-done | bytes 65568 | tf_op jit(solution)/shard_map/all_to_all | solution.py:700
  92.0 1.9 %combine.1 = bf16[64,4096]{1,0:T(8,128)(2,1)} custom-call(s32[8,64]{1,0:T(8,128)S(1)} %bitcast.12, f32[8,64]{1,0:T(8,128)S(1)} %bitcast.13, bf16[8,1024]{1,0:T(8,128)(2,1)S(1)} %squeeze.12.refs_0_, bf16[8,1024]{1,0:T(8,128)(2,1)S(1)} %squeeze.13.refs_1_, bf16[8,1024]{1,0:T(8,128)(2,1)S(1)} %squeeze.14.refs_2_, bf16[8,1024]{1,0:T(8,128)(2,1)S(1)} %squeeze.15.refs_3_), custom_call_target="tpu_custom_call" | custom-call | tf_op jit(solution)/shard_map/combine/pallas_call | solution.py:713
  94.3 0.9 attended_rows.1
  (79 shorter events, 8.8 us)
Async XLA Ops:
  1.6 10.1 %collective-permute-start = (bf16[2,256,128]{2,1,0:T(8,128)(2,1)S(1)}, bf16[2,256,128]{2,1,0:T(8,128)(2,1)S(1)}, u32[]{:S(2)}, u32[]{:S(2)}) collective-permute-start(bf16[2,256,128]{2,1,0:T(8,128)(2,1)S(1)} %pad_maximum_fusion.kv_own_ref), channel_id=1, source_target_pairs={{0,8},{4,12},{8,0},{12,4},{1,9},{5,13},{9,1},{13,5},{2,10},{6,14},... | collective-permute-start | bytes 393224 | tf_op jit(solution)/shard_map/ppermute | solution.py:27
  4.6 7.2 %collective-permute-start.1 = (bf16[2,256,128]{2,1,0:T(8,128)(2,1)S(1)}, bf16[2,256,128]{2,1,0:T(8,128)(2,1)S(1)}, u32[]{:S(2)}, u32[]{:S(2)}) collective-permute-start(bf16[2,256,128]{2,1,0:T(8,128)(2,1)S(1)} %pad_maximum_fusion.kv_own_ref), channel_id=1, source_target_pairs={{0,4},{4,8},{8,12},{12,0},{1,5},{5,9},{9,13},{13,1},{2,6},{6,10},{... | collective-permute-start | bytes 393224 | tf_op jit(solution)/shard_map/ppermute | solution.py:27
  4.6 13.1 %copy-start = (bf16[2048,1024]{1,0:T(8,128)(2,1)S(1)}, bf16[2048,1024]{1,0:T(8,128)(2,1)}, u32[]{:S(2)}) copy-start(bf16[2048,1024]{1,0:T(8,128)(2,1)} %refs_2_.15) | copy-start | bytes 12582916
  4.6 9.9 %collective-permute-start.2 = (s32[8,64]{1,0:T(8,128)}, s32[8,64]{1,0:T(8,128)S(1)}, u32[]{:S(2)}, u32[]{:S(2)}) collective-permute-start(s32[8,64]{1,0:T(8,128)} %bitcast.8), channel_id=1, source_target_pairs={{0,1},{1,0},{2,3},{3,2},{4,5},{5,4},{6,7},{7,6},{8,9},{9,8},{10,11... | collective-permute-start | bytes 6152 | tf_op jit(solution)/shard_map/ppermute | solution.py:22
  6.2 8.3 %collective-permute-start.3 = (s32[8,64]{1,0:T(8,128)}, s32[8,64]{1,0:T(8,128)S(1)}, u32[]{:S(2)}, u32[]{:S(2)}) collective-permute-start(s32[8,64]{1,0:T(8,128)} %bitcast.9), channel_id=1, source_target_pairs={{0,2},{1,3},{2,0},{3,1},{4,6},{5,7},{6,4},{7,5},{8,10},{9,11},{10,... | collective-permute-start | bytes 6152 | tf_op jit(solution)/shard_map/ppermute | solution.py:22
  8.8 5.7 %collective-permute-start.4 = (s32[8,64]{1,0:T(8,128)}, s32[8,64]{1,0:T(8,128)S(1)}, u32[]{:S(2)}, u32[]{:S(2)}) collective-permute-start(s32[8,64]{1,0:T(8,128)} %bitcast.10), channel_id=1, source_target_pairs={{0,3},{1,2},{2,1},{3,0},{4,7},{5,6},{6,5},{7,4},{8,11},{9,10},{10,... | collective-permute-start | bytes 6152 | tf_op jit(solution)/shard_map/ppermute | solution.py:22
  9.0 1.2 %copy-start.5 = (bf16[256,2048]{1,0:T(8,128)(2,1)S(1)}, bf16[256,2048]{1,0:T(8,128)(2,1)}, u32[]{:S(2)}) copy-start(bf16[256,2048]{1,0:T(8,128)(2,1)} %q_hbm) | copy-start | bytes 3145732
  10.2 0.7 copy-start.9
  14.4 13.3 %collective-permute-start.5 = (bf16[128,2048]{1,0:T(8,128)(2,1)S(1)}, bf16[128,2048]{1,0:T(8,128)(2,1)S(1)}, u32[]{:S(2)}, u32[]{:S(2)}) collective-permute-start(bf16[128,2048]{1,0:T(8,128)(2,1)S(1)} %attention_0.1.refs_0_.refs_4_), channel_id=1, source_target_pairs={{0,4},{4,0},{8,12},{12,8},{1,5},{5,1},{9,13},{13,9},{2,6},{6,2},{1... | collective-permute-start | bytes 1572872 | tf_op jit(solution)/shard_map/ppermute | solution.py:22
  17.1 2.0 %copy-start.4 = (bf16[64,4096]{1,0:T(8,128)(2,1)S(1)}, bf16[64,4096]{1,0:T(8,128)(2,1)}, u32[]{:S(2)}) copy-start(bf16[64,4096]{1,0:T(8,128)(2,1)} %refs_6_.3) | copy-start | bytes 1572868
  17.1 2.0 %copy-start.7 = (s32[64,8]{0,1:T(8,128)S(1)}, s32[64,8]{0,1:T(8,128)}, u32[]{:S(2)}) copy-start(s32[64,8]{0,1:T(8,128)} %param.19) | copy-start | bytes 6148
  17.1 10.5 %collective-permute-start.6 = (bf16[128,2048]{1,0:T(8,128)(2,1)S(1)}, bf16[128,2048]{1,0:T(8,128)(2,1)S(1)}, u32[]{:S(2)}, u32[]{:S(2)}) collective-permute-start(bf16[128,2048]{1,0:T(8,128)(2,1)S(1)} %attention_1.1.refs_1_.refs_5_), channel_id=1, source_target_pairs={{0,4},{4,0},{8,12},{12,8},{1,5},{5,1},{9,13},{13,9},{2,6},{6,2},{1... | collective-permute-start | bytes 1572872 | tf_op jit(solution)/shard_map/ppermute | solution.py:22
  18.4 11.4 %collective-permute-start.7 = (bf16[128,1024]{1,0:T(8,128)(2,1)S(1)}, bf16[128,1024]{1,0:T(8,128)(2,1)S(1)}, u32[]{:S(2)}, u32[]{:S(2)}) collective-permute-start(bf16[128,1024]{1,0:T(8,128)(2,1)S(1)} %project_leave.4), channel_id=1, source_target_pairs={{0,1},{1,0},{2,3},{3,2},{4,5},{5,4},{6,7},{7,6},{8,9},{9,8},{10,11... | collective-permute-start | bytes 786440 | tf_op jit(solution)/shard_map/ppermute | solution.py:22
  21.0 6.6 %collective-permute-start.10 = (bf16[48,2048]{1,0:T(8,128)(2,1)S(1)}, bf16[48,2048]{1,0:T(8,128)(2,1)S(1)}, u32[]{:S(2)}, u32[]{:S(2)}) collective-permute-start(bf16[48,2048]{1,0:T(8,128)(2,1)S(1)} %pick.1.refs_0_), channel_id=1, source_target_pairs={{0,8},{4,12},{8,0},{12,4},{1,9},{5,13},{9,1},{13,5},{2,10},{6,14},... | collective-permute-start | bytes 589832 | tf_op jit(solution)/shard_map/ppermute | solution.py:22
  29.9 15.7 %collective-permute-start.14 = (bf16[128,2048]{1,0:T(8,128)(2,1)S(1)}, bf16[128,2048]{1,0:T(8,128)(2,1)S(1)}, u32[]{:S(2)}, u32[]{:S(2)}) collective-permute-start(bf16[128,2048]{1,0:T(8,128)(2,1)S(1)} %attention_0.1.refs_0_.refs_4_), channel_id=1, source_target_pairs={{0,8},{4,12},{8,0},{12,4},{1,9},{5,13},{9,1},{13,5},{2,10},{6,14},... | collective-permute-start | bytes 1572872 | tf_op jit(solution)/shard_map/ppermute | solution.py:22
  31.2 4.3 %collective-permute-start.11 = (bf16[48,2048]{1,0:T(8,128)(2,1)S(1)}, bf16[48,2048]{1,0:T(8,128)(2,1)S(1)}, u32[]{:S(2)}, u32[]{:S(2)}) collective-permute-start(bf16[48,2048]{1,0:T(8,128)(2,1)S(1)} %pick.1.refs_0_), channel_id=1, source_target_pairs={{0,4},{4,0},{8,12},{12,8},{1,5},{5,1},{9,13},{13,9},{2,6},{6,2},{1... | collective-permute-start | bytes 589832 | tf_op jit(solution)/shard_map/ppermute | solution.py:22
  31.2 4.3 %collective-permute-start.12 = (bf16[48,2048]{1,0:T(8,128)(2,1)S(1)}, bf16[48,2048]{1,0:T(8,128)(2,1)S(1)}, u32[]{:S(2)}, u32[]{:S(2)}) collective-permute-start(bf16[48,2048]{1,0:T(8,128)(2,1)S(1)} %collective-permute-done.10.refs_2_), channel_id=1, source_target_pairs={{0,4},{4,0},{8,12},{12,8},{1,5},{5,1},{9,13},{13,9},{2,6},{6,2},{1... | collective-permute-start | bytes 589832 | tf_op jit(solution)/shard_map/ppermute | solution.py:22
  31.7 12.0 %collective-permute-start.9 = (bf16[128,1024]{1,0:T(8,128)(2,1)S(1)}, bf16[128,1024]{1,0:T(8,128)(2,1)S(1)}, u32[]{:S(2)}, u32[]{:S(2)}) collective-permute-start(bf16[128,1024]{1,0:T(8,128)(2,1)S(1)} %project_leave.5), channel_id=1, source_target_pairs={{0,1},{1,0},{2,3},{3,2},{4,5},{5,4},{6,7},{7,6},{8,9},{9,8},{10,11... | collective-permute-start | bytes 786440 | tf_op jit(solution)/shard_map/ppermute | solution.py:22
  33.1 10.6 %collective-permute-start.8 = (bf16[64,1024]{1,0:T(8,128)(2,1)S(1)}, bf16[64,1024]{1,0:T(8,128)(2,1)S(1)}, u32[]{:S(2)}, u32[]{:S(2)}) collective-permute-start(bf16[64,1024]{1,0:T(8,128)(2,1)S(1)} %get-tuple-element.124), channel_id=1, source_target_pairs={{0,2},{1,3},{2,0},{3,1},{4,6},{5,7},{6,4},{7,5},{8,10},{9,11},{10,... | collective-permute-start | bytes 393224 | tf_op jit(solution)/shard_map/ppermute | solution.py:22
  36.3 9.2 %collective-permute-start.15 = (bf16[4,16,1024]{2,1,0:T(8,128)(2,1)S(1)}, bf16[4,16,1024]{2,1,0:T(8,128)(2,1)S(1)}, u32[]{:S(2)}, u32[]{:S(2)}) collective-permute-start(bf16[4,16,1024]{2,1,0:T(8,128)(2,1)S(1)} %get-tuple-element.132), channel_id=1, source_target_pairs={{0,1},{1,0},{2,3},{3,2},{4,5},{5,4},{6,7},{7,6},{8,9},{9,8},{10,11... | collective-permute-start | bytes 393224 | tf_op jit(solution)/shard_map/ppermute | solution.py:22
  45.6 2.0 %collective-permute-start.16 = (bf16[128,2048]{1,0:T(8,128)(2,1)S(1)}, bf16[128,2048]{1,0:T(8,128)(2,1)S(1)}, u32[]{:S(2)}, u32[]{:S(2)}) collective-permute-start(bf16[128,2048]{1,0:T(8,128)(2,1)S(1)} %collective-permute-done.14.refs_0_), channel_id=1, source_target_pairs={{0,4},{4,0},{8,12},{12,8},{1,5},{5,1},{9,13},{13,9},{2,6},{6,2},{1... | collective-permute-start | bytes 1572872 | tf_op jit(solution)/shard_map/ppermute | solution.py:22
  45.7 15.3 %collective-permute-start.24 = (bf16[128,2048]{1,0:T(8,128)(2,1)S(1)}, bf16[128,2048]{1,0:T(8,128)(2,1)S(1)}, u32[]{:S(2)}, u32[]{:S(2)}) collective-permute-start(bf16[128,2048]{1,0:T(8,128)(2,1)S(1)} %attention_1.1.refs_1_.refs_5_), channel_id=1, source_target_pairs={{0,8},{4,12},{8,0},{12,4},{1,9},{5,13},{9,1},{13,5},{2,10},{6,14},... | collective-permute-start | bytes 1572872 | tf_op jit(solution)/shard_map/ppermute | solution.py:22
  48.3 12.6 %collective-permute-start.18 = (bf16[128,1024]{1,0:T(8,128)(2,1)S(1)}, bf16[128,1024]{1,0:T(8,128)(2,1)S(1)}, u32[]{:S(2)}, u32[]{:S(2)}) collective-permute-start(bf16[128,1024]{1,0:T(8,128)(2,1)S(1)} %project_leave.6), channel_id=1, source_target_pairs={{0,1},{1,0},{2,3},{3,2},{4,5},{5,4},{6,7},{7,6},{8,9},{9,8},{10,11... | collective-permute-start | bytes 786440 | tf_op jit(solution)/shard_map/ppermute | solution.py:22
  50.1 9.4 %collective-permute-start.13 = (bf16[64,1024]{1,0:T(8,128)(2,1)S(1)}, bf16[64,1024]{1,0:T(8,128)(2,1)S(1)}, u32[]{:S(2)}, u32[]{:S(2)}) collective-permute-start(bf16[64,1024]{1,0:T(8,128)(2,1)S(1)} %get-tuple-element.139), channel_id=1, source_target_pairs={{0,2},{1,3},{2,0},{3,1},{4,6},{5,7},{6,4},{7,5},{8,10},{9,11},{10,... | collective-permute-start | bytes 393224 | tf_op jit(solution)/shard_map/ppermute | solution.py:22
  52.2 8.0 %collective-permute-start.19 = (bf16[4,8,1024]{2,1,0:T(8,128)(2,1)S(1)}, bf16[4,8,1024]{2,1,0:T(8,128)(2,1)S(1)}, u32[]{:S(2)}, u32[]{:S(2)}) collective-permute-start(bf16[4,8,1024]{2,1,0:T(8,128)(2,1)S(1)} %get-tuple-element.154), channel_id=1, source_target_pairs={{0,2},{1,3},{2,0},{3,1},{4,6},{5,7},{6,4},{7,5},{8,10},{9,11},{10,... | collective-permute-start | bytes 196616 | tf_op jit(solution)/shard_map/ppermute | solution.py:22
  61.0 2.0 %collective-permute-start.25 = (bf16[128,2048]{1,0:T(8,128)(2,1)S(1)}, bf16[128,2048]{1,0:T(8,128)(2,1)S(1)}, u32[]{:S(2)}, u32[]{:S(2)}) collective-permute-start(bf16[128,2048]{1,0:T(8,128)(2,1)S(1)} %collective-permute-done.24.refs_0_), channel_id=1, source_target_pairs={{0,4},{4,0},{8,12},{12,8},{1,5},{5,1},{9,13},{13,9},{2,6},{6,2},{1... | collective-permute-start | bytes 1572872 | tf_op jit(solution)/shard_map/ppermute | solution.py:22
  63.0 11.4 %copy-start.2 = (bf16[1,4096,384]{2,1,0:T(8,128)(2,1)S(1)}, bf16[1,4096,384]{2,1,0:T(8,128)(2,1)}, u32[]{:S(2)}) copy-start(bf16[1,4096,384]{2,1,0:T(8,128)(2,1)} %refs_6_.2) | copy-start | bytes 9437188
  63.9 10.4 %copy-start.1 = (bf16[1,4096,384]{2,1,0:T(8,128)(2,1)S(1)}, bf16[1,4096,384]{2,1,0:T(8,128)(2,1)}, u32[]{:S(2)}) copy-start(bf16[1,4096,384]{2,1,0:T(8,128)(2,1)} %refs_5_.1) | copy-start | bytes 9437188
  63.9 10.4 %copy-start.6 = (f32[4096]{0:T(1024)S(1)}, f32[4096]{0:T(1024)}, u32[]{:S(2)}) copy-start(f32[4096]{0:T(1024)} %param.18) | copy-start | bytes 49156
  63.9 13.6 %collective-permute-start.28 = (bf16[128,1024]{1,0:T(8,128)(2,1)S(1)}, bf16[128,1024]{1,0:T(8,128)(2,1)S(1)}, u32[]{:S(2)}, u32[]{:S(2)}) collective-permute-start(bf16[128,1024]{1,0:T(8,128)(2,1)S(1)} %project_leave.7), channel_id=1, source_target_pairs={{0,1},{1,0},{2,3},{3,2},{4,5},{5,4},{6,7},{7,6},{8,9},{9,8},{10,11... | collective-permute-start | bytes 786440 | tf_op jit(solution)/shard_map/ppermute | solution.py:22
  67.5 10.0 %collective-permute-start.20 = (bf16[64,1024]{1,0:T(8,128)(2,1)S(1)}, bf16[64,1024]{1,0:T(8,128)(2,1)S(1)}, u32[]{:S(2)}, u32[]{:S(2)}) collective-permute-start(bf16[64,1024]{1,0:T(8,128)(2,1)S(1)} %get-tuple-element.161), channel_id=1, source_target_pairs={{0,2},{1,3},{2,0},{3,1},{4,6},{5,7},{6,4},{7,5},{8,10},{9,11},{10,... | collective-permute-start | bytes 393224 | tf_op jit(solution)/shard_map/ppermute | solution.py:22
  68.8 2.6 %collective-permute-start.21 = (bf16[32,1024]{1,0:T(8,128)(2,1)S(1)}, bf16[32,1024]{1,0:T(8,128)(2,1)S(1)}, u32[]{:S(2)}, u32[]{:S(2)}) collective-permute-start(bf16[32,1024]{1,0:T(8,128)(2,1)S(1)} %routed_sum.3.refs_0_), channel_id=1, source_target_pairs={{0,4},{4,0},{8,12},{12,8},{1,5},{5,1},{9,13},{13,9},{2,6},{6,2},{1... | collective-permute-start | bytes 196616 | tf_op jit(solution)/shard_map/ppermute | solution.py:22
  68.8 4.9 %collective-permute-start.22 = (bf16[32,1024]{1,0:T(8,128)(2,1)S(1)}, bf16[32,1024]{1,0:T(8,128)(2,1)S(1)}, u32[]{:S(2)}, u32[]{:S(2)}) collective-permute-start(bf16[32,1024]{1,0:T(8,128)(2,1)S(1)} %routed_sum.3.refs_0_), channel_id=1, source_target_pairs={{0,8},{4,12},{8,0},{12,4},{1,9},{5,13},{9,1},{13,5},{2,10},{6,14},... | collective-permute-start | bytes 196616 | tf_op jit(solution)/shard_map/ppermute | solution.py:22
  69.6 4.8 %collective-permute-start.23 = (bf16[32,1024]{1,0:T(8,128)(2,1)S(1)}, bf16[32,1024]{1,0:T(8,128)(2,1)S(1)}, u32[]{:S(2)}, u32[]{:S(2)}) collective-permute-start(bf16[32,1024]{1,0:T(8,128)(2,1)S(1)} %routed_sum.3.refs_0_), channel_id=1, source_target_pairs={{0,12},{4,8},{8,4},{12,0},{1,13},{5,9},{9,5},{13,1},{2,14},{6,10},... | collective-permute-start | bytes 196616 | tf_op jit(solution)/shard_map/ppermute | solution.py:22
  74.4 6.0 %copy-start.3 = (bf16[1,1536,1024]{2,1,0:T(8,128)(2,1)S(1)}, bf16[1,1536,1024]{2,1,0:T(8,128)(2,1)}, u32[]{:S(2)}) copy-start(bf16[1,1536,1024]{2,1,0:T(8,128)(2,1)} %refs_4_.3) | copy-start | bytes 9437188
  75.5 16.5 %copy-start.8 = (f32[64,8]{0,1:T(8,128)S(1)}, f32[64,8]{0,1:T(8,128)}, u32[]{:S(2)}) copy-start(f32[64,8]{0,1:T(8,128)} %param.20) | copy-start | bytes 6148
  75.5 4.3 %collective-permute-start.30 = (bf16[32,384]{1,0:T(8,128)(2,1)S(1)}, bf16[32,384]{1,0:T(8,128)(2,1)S(1)}, u32[]{:S(2)}, u32[]{:S(2)}) collective-permute-start(bf16[32,384]{1,0:T(8,128)(2,1)S(1)} %hidden_units.1.refs_0_), channel_id=1, source_target_pairs={{0,4},{4,0},{8,12},{12,8},{1,5},{5,1},{9,13},{13,9},{2,6},{6,2},{1... | collective-permute-start | bytes 73736 | tf_op jit(solution)/shard_map/ppermute | solution.py:22
  76.0 3.9 %collective-permute-start.31 = (bf16[32,384]{1,0:T(8,128)(2,1)S(1)}, bf16[32,384]{1,0:T(8,128)(2,1)S(1)}, u32[]{:S(2)}, u32[]{:S(2)}) collective-permute-start(bf16[32,384]{1,0:T(8,128)(2,1)S(1)} %hidden_units.1.refs_0_), channel_id=1, source_target_pairs={{0,8},{4,12},{8,0},{12,4},{1,9},{5,13},{9,1},{13,5},{2,10},{6,14},... | collective-permute-start | bytes 73736 | tf_op jit(solution)/shard_map/ppermute | solution.py:22
  76.8 3.5 %collective-permute-start.32 = (bf16[32,384]{1,0:T(8,128)(2,1)S(1)}, bf16[32,384]{1,0:T(8,128)(2,1)S(1)}, u32[]{:S(2)}, u32[]{:S(2)}) collective-permute-start(bf16[32,384]{1,0:T(8,128)(2,1)S(1)} %hidden_units.1.refs_0_), channel_id=1, source_target_pairs={{0,12},{4,8},{8,4},{12,0},{1,13},{5,9},{9,5},{13,1},{2,14},{6,10},... | collective-permute-start | bytes 73736 | tf_op jit(solution)/shard_map/ppermute | solution.py:22
  77.6 9.8 %collective-permute-start.29 = (bf16[64,1024]{1,0:T(8,128)(2,1)S(1)}, bf16[64,1024]{1,0:T(8,128)(2,1)S(1)}, u32[]{:S(2)}, u32[]{:S(2)}) collective-permute-start(bf16[64,1024]{1,0:T(8,128)(2,1)S(1)} %get-tuple-element.181), channel_id=1, source_target_pairs={{0,2},{1,3},{2,0},{3,1},{4,6},{5,7},{6,4},{7,5},{8,10},{9,11},{10,... | collective-permute-start | bytes 393224 | tf_op jit(solution)/shard_map/ppermute | solution.py:22
  81.6 10.2 %all-to-all-start = ((bf16[16,2,1024]{2,1,0:T(2,128)(2,1)}), bf16[16,2,1024]{2,1,0:T(2,128)(2,1)S(1)}, u32[]{:S(2)}, u32[]{:S(2)}) async-start(bf16[16,2,1024]{2,1,0:T(2,128)(2,1)} %reshape.16), calls=%async_computation | async-start | bytes 131072 | tf_op jit(solution)/shard_map/all_to_all | solution.py:700
  85.1 8.8 %collective-permute-start.17 = (bf16[64,1024]{1,0:T(8,128)(2,1)S(1)}, bf16[64,1024]{1,0:T(8,128)(2,1)S(1)}, u32[]{:S(2)}, u32[]{:S(2)}) collective-permute-start(bf16[64,1024]{1,0:T(8,128)(2,1)S(1)} %add.17), channel_id=1, source_target_pairs={{0,4},{4,0},{8,12},{12,8},{1,5},{5,1},{9,13},{13,9},{2,6},{6,2},{1... | collective-permute-start | bytes 393224 | tf_op jit(solution)/shard_map/ppermute | solution.py:22
  85.5 8.5 %collective-permute-start.27 = (bf16[32,1024]{1,0:T(8,128)(2,1)S(1)}, bf16[32,1024]{1,0:T(8,128)(2,1)S(1)}, u32[]{:S(2)}, u32[]{:S(2)}) collective-permute-start(bf16[32,1024]{1,0:T(8,128)(2,1)S(1)} %get-tuple-element.176), channel_id=1, source_target_pairs={{0,12},{4,8},{8,4},{12,0},{1,13},{5,9},{9,5},{13,1},{2,14},{6,10},... | collective-permute-start | bytes 196616 | tf_op jit(solution)/shard_map/ppermute | solution.py:22
  87.1 6.8 %collective-permute-start.26 = (bf16[32,1024]{1,0:T(8,128)(2,1)S(1)}, bf16[32,1024]{1,0:T(8,128)(2,1)S(1)}, u32[]{:S(2)}, u32[]{:S(2)}) collective-permute-start(bf16[32,1024]{1,0:T(8,128)(2,1)S(1)} %get-tuple-element.175), channel_id=1, source_target_pairs={{0,8},{4,12},{8,0},{12,4},{1,9},{5,13},{9,1},{13,5},{2,10},{6,14},... | collective-permute-start | bytes 196616 | tf_op jit(solution)/shard_map/ppermute | solution.py:22
  87.4 6.5 %collective-permute-start.33 = (bf16[32,1024]{1,0:T(8,128)(2,1)S(1)}, bf16[32,1024]{1,0:T(8,128)(2,1)S(1)}, u32[]{:S(2)}, u32[]{:S(2)}) collective-permute-start(bf16[32,1024]{1,0:T(8,128)(2,1)S(1)} %get-tuple-element.188), channel_id=1, source_target_pairs={{0,8},{4,12},{8,0},{12,4},{1,9},{5,13},{9,1},{13,5},{2,10},{6,14},... | collective-permute-start | bytes 196616 | tf_op jit(solution)/shard_map/ppermute | solution.py:22
  89.2 5.1 %collective-permute-start.34 = (bf16[32,1024]{1,0:T(8,128)(2,1)S(1)}, bf16[32,1024]{1,0:T(8,128)(2,1)S(1)}, u32[]{:S(2)}, u32[]{:S(2)}) collective-permute-start(bf16[32,1024]{1,0:T(8,128)(2,1)S(1)} %get-tuple-element.189), channel_id=1, source_target_pairs={{0,12},{4,8},{8,4},{12,0},{1,13},{5,9},{9,5},{13,1},{2,14},{6,10},... | collective-permute-start | bytes 196616 | tf_op jit(solution)/shard_map/ppermute | solution.py:22

commit v4 on v3

--- a/solution.py
+++ b/solution.py
@@ -50,6 +50,41 @@
 
 
 FREE = pl.CostEstimate(flops=0, bytes_accessed=0, transcendentals=0)
+
+
+class Step:
+    def __init__(self, body, operands, results):
+        self.body = body
+        self.operands = tuple(operands)
+        self.results = tuple(results)
+
+
+def together(name, steps, *operands):
+    counts = [(len(step.operands), len(step.results)) for step in steps]
+    total = sum(ins for ins, _ in counts)
+
+    def kernel(*refs):
+        at, out_at = 0, total
+        for step, (ins, outs) in zip(steps, counts):
+            step.body(*refs[at : at + ins], *refs[out_at : out_at + outs])
+            at += ins
+            out_at += outs
+
+    shapes = tuple(shape for step in steps for shape in step.results)
+    flat = pl.pallas_call(
+        kernel,
+        out_shape=shapes,
+        in_specs=whole_vmem(total),
+        out_specs=tuple(whole_vmem(len(shapes))),
+        compiler_params=vmem(40),
+        cost_estimate=FREE,
+        name=name,
+    )(*operands)
+    results = []
+    for _, outs in counts:
+        results.append(tuple(flat[:outs]))
+        flat = flat[outs:]
+    return results
 
 
 def slot_ranks(routes_t, flight):
@@ -190,9 +225,7 @@
     line_home = line // CAP % homes
     line_slot = (line % CAP).astype(jnp.float32)
     line_place = line // (CAP * homes)
-    line_expert = jnp.zeros((lines, 1), jnp.int32)
-    for position in range(flight):
-        line_expert = jnp.where(line_place == position, order[position] ^ exp_index, line_expert)
+    line_expert = line_place ^ exp_index
     col = lax.broadcasted_iota(jnp.int32, (lines, flight), 1)
     onehot = (col == line_expert).astype(jnp.bfloat16)
     routed = jnp.zeros((lines, width), jnp.float32)
@@ -230,35 +263,27 @@
     homes = len(routes_all)
     width = heads_out[0].shape[1]
     rows = homes * homes * CAP + homes * CAP * (residual.shape[1] // width)
-    return pl.pallas_call(
+    return Step(
         functools.partial(pick_kernel, homes=homes, halves=len(heads_out), sub=sub),
-        out_shape=jax.ShapeDtypeStruct((rows, width), jnp.bfloat16),
-        in_specs=whole_vmem(1 + homes + len(heads_out)),
-        out_specs=pl.BlockSpec(memory_space=pltpu.VMEM),
-        compiler_params=vmem(16),
-        cost_estimate=FREE,
-        name="pick",
-    )(residual, *routes_all, *heads_out)
-
-
-def routed_kernel(*refs, count, homes, after):
+        (residual, *routes_all, *heads_out),
+        (jax.ShapeDtypeStruct((rows, width), jnp.bfloat16),),
+    )
+
+
+def routed_kernel(*refs, count, homes):
     piece_refs = refs[:count]
     weight_ref = refs[count]
-    keep_ref, send_ref = refs[count + 1 + after :]
+    out_refs = refs[count + 1 :]
     ctx_index = lax.axis_index("ctx")
     exp_index = lax.axis_index("exp")
-    order = reversed_bits(homes)
     cols = weight_ref.shape[1]
     depth = weight_ref.shape[0]
     flight = homes
     slots = flight * CAP
-    lines = flight * homes * CAP
-    half = lines // 2
+    block = homes * CAP
+    lines = flight * block
     line = lax.broadcasted_iota(jnp.int32, (lines, slots), 0)
-    line_place = line // (CAP * homes)
-    expert = jnp.zeros((lines, slots), jnp.int32)
-    for position in range(flight):
-        expert = jnp.where(line_place == position, order[position] ^ exp_index, expert)
+    expert = line // block ^ exp_index
     source = jnp.where(line // CAP % homes == exp_index, expert * CAP + line % CAP, -1)
     onehot = (source == lax.broadcasted_iota(jnp.int32, (lines, slots), 1)).astype(jnp.bfloat16)
     heads = jnp.concatenate([ref[:lines, :] for ref in piece_refs], axis=0)
@@ -273,56 +298,42 @@
             preferred_element_type=jnp.float32,
         )
         total = product[place * lines : (place + 1) * lines] + extra
-        keep_ref[ctx_index ^ place] = total[:half].astype(jnp.bfloat16)
-        send_ref[ctx_index ^ place] = total[half:].astype(jnp.bfloat16)
-
-
-def routed_product(pieces, out_weight, homes, after=()):
+        for k in range(flight):
+            out_refs[k][ctx_index ^ place] = total[k * block : (k + 1) * block].astype(jnp.bfloat16)
+
+
+def routed_product(pieces, out_weight, homes):
     count = len(pieces)
-    cols = out_weight.shape[1]
-    shape = jax.ShapeDtypeStruct((count, homes * homes * CAP // 2, cols), jnp.bfloat16)
+    shape = jax.ShapeDtypeStruct((count, homes * CAP, out_weight.shape[1]), jnp.bfloat16)
+    return Step(
+        functools.partial(routed_kernel, count=count, homes=homes),
+        (*pieces, out_weight),
+        (shape,) * homes,
+    )
+
+
+def routed_sum_kernel(*refs):
+    total = refs[0][...].astype(jnp.float32)
+    for ref in refs[1:-1]:
+        total = total + ref[...].astype(jnp.float32)
+    count, rows, cols = total.shape
+    refs[-1][...] = total.reshape(count * rows, cols).astype(jnp.bfloat16)
+
+
+def routed_sum(*blocks):
+    count, rows, cols = blocks[0].shape
     return pl.pallas_call(
-        functools.partial(routed_kernel, count=count, homes=homes, after=len(after)),
-        out_shape=(shape, shape),
-        in_specs=whole_vmem(count + 1) + anywhere(len(after)),
-        out_specs=tuple(whole_vmem(2)),
-        compiler_params=vmem(32),
-        cost_estimate=FREE,
-        name="routed_product",
-    )(*pieces, out_weight, *after)
-
-
-def add_middle_kernel(keep_ref, arrived_ref, *refs, last):
-    total = keep_ref[...].astype(jnp.float32) + arrived_ref[...].astype(jnp.float32)
-    count, rows, cols = total.shape
-    if last:
-        refs[0][...] = total.reshape(count * rows, cols).astype(refs[0].dtype)
-    else:
-        refs[0][...] = total[:, : rows // 2].astype(refs[0].dtype)
-        refs[1][...] = total[:, rows // 2 :].astype(refs[1].dtype)
-
-
-def add_middle(keep, arrived, last):
-    count, rows, cols = keep.shape
-    if last:
-        out = jax.ShapeDtypeStruct((count * rows, cols), jnp.bfloat16)
-    else:
-        out = (
-            jax.ShapeDtypeStruct((count, rows // 2, cols), jnp.float32),
-            jax.ShapeDtypeStruct((count, rows // 2, cols), jnp.bfloat16),
-        )
-    return pl.pallas_call(
-        functools.partial(add_middle_kernel, last=last),
-        out_shape=out,
-        in_specs=whole_vmem(2),
-        out_specs=whole_vmem(1)[0] if last else tuple(whole_vmem(2)),
-        compiler_params=vmem(16),
+        routed_sum_kernel,
+        out_shape=jax.ShapeDtypeStruct((count * rows, cols), jnp.bfloat16),
+        in_specs=whole_vmem(len(blocks)),
+        out_specs=pl.BlockSpec(memory_space=pltpu.VMEM),
+        compiler_params=vmem(24),
         cost_estimate=FREE,
         name="routed_sum",
-    )(keep, arrived)
-
-
-def project_kernel(*refs, count, homes, sub, upper, after):
+    )(*blocks)
+
+
+def project_kernel(*refs, count, homes, sub, upper):
     piece_refs = refs[:count]
     weight_ref = refs[count]
     out_ref = refs[-1]
@@ -340,21 +351,17 @@
                 out_ref[at : at + sub, :] = product[source : source + sub]
 
 
-def project(pieces, out_weight, homes, sub, upper, after=()):
+def project(pieces, out_weight, homes, sub, upper):
     count = len(pieces)
-    return pl.pallas_call(
-        functools.partial(
-            project_kernel, count=count, homes=homes, sub=sub, upper=upper, after=len(after)
+    return Step(
+        functools.partial(project_kernel, count=count, homes=homes, sub=sub, upper=upper),
+        (*pieces, out_weight),
+        (
+            jax.ShapeDtypeStruct(
+                (homes // 2 * count * sub, out_weight.shape[1]), jnp.bfloat16
+            ),
         ),
-        out_shape=jax.ShapeDtypeStruct(
-            (homes // 2 * count * sub, out_weight.shape[1]), jnp.bfloat16
-        ),
-        in_specs=whole_vmem(count + 1) + anywhere(len(after)),
-        out_specs=pl.BlockSpec(memory_space=pltpu.VMEM),
-        compiler_params=vmem(32),
-        cost_estimate=FREE,
-        name="project_leave" if upper else "project_stay",
-    )(*pieces, out_weight, *after)
+    )
 
 
 def add_kernel(keep_ref, arrived_ref, *refs):
@@ -429,21 +436,22 @@
             piece_refs[place][...], down_ref[0, pl.ds(at, units), :], preferred_element_type=jnp.float32
         )
         total = part if total is None else total + part
-    out_ref[...] = total.astype(jnp.bfloat16)
-
-
-def down_product(pieces, down_weight, after=()):
+    for home in range(out_ref.shape[0]):
+        out_ref[home] = total[home * CAP : (home + 1) * CAP].astype(jnp.bfloat16)
+
+
+def down_product(pieces, down_weight):
     count = len(pieces)
     rows = pieces[0].shape[0]
     return pl.pallas_call(
         functools.partial(down_kernel, count=count),
-        out_shape=jax.ShapeDtypeStruct((rows, down_weight.shape[2]), jnp.bfloat16),
-        in_specs=whole_vmem(count + 1) + anywhere(len(after)),
+        out_shape=jax.ShapeDtypeStruct((rows // CAP, CAP, down_weight.shape[2]), jnp.bfloat16),
+        in_specs=whole_vmem(count + 1),
         out_specs=pl.BlockSpec(memory_space=pltpu.VMEM),
         compiler_params=vmem(20),
         cost_estimate=FREE,
         name="down_product",
-    )(*pieces, down_weight, *after)
+    )(*pieces, down_weight)
 
 
 def attended_kernel(*refs, places):
@@ -470,9 +478,7 @@
     )(*pieces, residual)
 
 
-def combine_kernel(routes_ref, weights_ref, *refs, flight, count):
-    back_refs = refs[:count]
-    out_ref = refs[-1]
+def combine_kernel(routes_ref, weights_ref, back_ref, out_ref, *, flight, count):
     routes_t = routes_ref[...]
     scores = weights_ref[...]
     shares = scores / jnp.sum(scores, axis=0, keepdims=True)
@@ -483,14 +489,19 @@
         for r in range(CAP):
             lines.append(jnp.where(ranks[j : j + 1] == r, share, 0.0))
     lines = jnp.concatenate(lines, axis=0)
-    cols = back_refs[0].shape[1]
-    for place, ref in enumerate(back_refs):
-        out_ref[:, place * cols : (place + 1) * cols] = lax.dot_general(
-            lines,
-            ref[...].astype(jnp.float32),
-            (((0,), (0,)), ((), ())),
-            precision=lax.Precision.HIGHEST,
-            preferred_element_type=jnp.float32,
+    pieces = []
+    rest = lines
+    for _ in range(3):
+        piece = rest.astype(jnp.bfloat16)
+        pieces.append(piece.astype(jnp.float32))
+        rest = rest - pieces[-1]
+    pieces = jnp.concatenate(pieces, axis=0).T.astype(jnp.bfloat16)
+    cols = back_ref.shape[2]
+    for place in range(count):
+        rows = [back_ref[place * flight + j].astype(jnp.float32) for j in range(flight)]
+        rows = jnp.concatenate(rows * 3, axis=0).astype(jnp.bfloat16)
+        out_ref[:, place * cols : (place + 1) * cols] = jnp.dot(
+            pieces, rows, preferred_element_type=jnp.float32
         ).astype(jnp.bfloat16)
 
 
@@ -534,6 +545,13 @@
         return out
 
 
+    def steps(self, name, *steps):
+        operands = self.tie(*[x for step in steps for x in step.operands])
+        results = together(name, steps, *operands)
+        self.last = results[-1][-1]
+        return results
+
+
 class Gather:
     def __init__(self, sequence, x):
         self.sequence = sequence
@@ -547,6 +565,10 @@
             self.found[k ^ self.step] = swap(piece, "ctx", self.step)
         self.step //= 2
 
+    def wait(self, *others):
+        for k in self.found:
+            self.found[k] = after(self.found[k], *others)
+
     def hops_to(self, step):
         while self.step >= step:
             self.hop()
@@ -556,14 +578,14 @@
 
 
 class Halving:
-    def __init__(self, sequence, send, add_step):
+    def __init__(self, sequence, keep, send, add_step, step=1):
         self.sequence = sequence
-        self.keep = None
+        self.keep = keep
         self.result = None
-        self.step = 1
+        self.step = step
         self.add_step = add_step
         self.count = lax.axis_size("exp")
-        self.arrived = swap(send, "exp", 1)
+        self.arrived = swap(send, "exp", step)
 
     def advance(self, hold=False):
         self.step *= 2
@@ -575,6 +597,9 @@
             self.keep, self.send = out
             if not hold:
                 self.release()
+
+    def wait(self, *others):
+        self.arrived = after(self.arrived, *others)
 
     def release(self):
         (send,) = self.sequence.tie(self.send)
@@ -647,80 +672,83 @@
         far.append(Gather(sequence, rows))
 
     def leaving(blocks):
-        return sequence.run(lambda *xs: project(xs, out_weight, homes, sub, True), blocks)
+        return project(blocks, out_weight, homes, sub, True)
 
     def staying(blocks):
-        return sequence.run(lambda *xs: project(xs, out_weight, homes, sub, False), blocks)
+        return project(blocks, out_weight, homes, sub, False)
 
     names = [k for k in range(n_ctx) if k > 1]
     one = (jnp.bfloat16,)
     mine = tuple(heads_out)
     near = tuple(near)
-    own = Halving(sequence, leaving(mine), plain_add(one))
-    routed = sequence.run(lambda r: pick(r, routes_all, heads_out, sub), (residual_in,))
+    far[0].hops_to(2)
+    (own_send,), (routed,) = sequence.steps(
+        "leave_and_pick", leaving(mine), pick(residual_in, routes_all, heads_out, sub)
+    )
     routed_all = Gather(sequence, routed)
+    (near_send,), (own_keep,), (near_keep,) = sequence.steps(
+        "leave_and_stay", leaving(near), staying(mine), staying(near)
+    )
+    own = Halving(sequence, own_keep, own_send, plain_add(one))
+    beside = Halving(sequence, near_keep, near_send, plain_add(one))
+    own.advance()
     routed_all.hops_to(2)
-    beside = Halving(sequence, leaving(near), plain_add(one))
-    own.keep = staying(mine)
-    beside.keep = staying(near)
-    own.advance()
+    beside.advance()
     routed_all.hop()
-    for gather in far:
-        gather.found[0] = after(gather.found[0], routed_all.found[n_ctx // 2])
-        gather.hops_to(2)
-    keep, send = sequence.run(
-        lambda *xs: routed_product(xs, out_weight, homes), routed_all.pieces(range(n_ctx))
-    )
-    routed_sum = Halving(sequence, send, add_middle)
-    routed_sum.keep = keep
-    beside.advance()
+    far[0].wait(routed_all.found[n_ctx // 2])
+    far[0].hop()
     (own_sum,) = own.finish()
-    routed_sum.advance()
-    far[0].hop()
+    if halves > 1:
+        far[1].wait(routed_all.found[n_ctx // 2])
+        far[1].hops_to(2)
+    (blocks,) = sequence.steps(
+        "routed_product", routed_product(routed_all.pieces(range(n_ctx)), out_weight, homes)
+    )
+    blocks = [blocks[0]] + [swap(blocks[k], "exp", k) for k in range(1, homes)]
     first = far[0].pieces(names)
-    sums = [Halving(sequence, leaving(first), plain_add(one * len(names)))]
-    sums[0].keep = staying(first)
+    (send,), (keep,) = sequence.steps("far", leaving(first), staying(first))
+    sums = [Halving(sequence, keep, send, plain_add(one * len(names)))]
     (near_sum,) = beside.finish()
-    routed_sum.finish()
-    stream_rows = gather_direct(routed_sum.result, "ctx")
-    sums[0].advance()
+    stream = sequence.run(routed_sum, tuple(blocks))
+    stream_rows = gather_direct(stream, "ctx")
     if halves > 1:
         far[1].hop()
         second = far[1].pieces(names)
-        sums.append(Halving(sequence, leaving(second), plain_add(one * len(names))))
-        sums[1].keep = staying(second)
+        (send,), (keep,) = sequence.steps("far", leaving(second), staying(second))
+        sums.append(Halving(sequence, keep, send, plain_add(one * len(names))))
     hidden = sequence.run(
         lambda *xs: hidden_units(xs, norm_gain[None, :], gate_weight, up_weight), tuple(stream_rows)
     )
     hidden_pieces = gather_direct(hidden, "ctx")
-    sums[0].finish()
+    sums[0].advance()
     if halves > 1:
+        sums[1].wait(*hidden_pieces)
         sums[1].advance()
     produced = sequence.run(lambda *xs: down_product(xs, down_weight), tuple(hidden_pieces))
     back = lax.all_to_all(
-        produced.reshape(n_ctx * homes, CAP, cols),
+        produced,
         ("ctx", "exp"),
         split_axis=0,
         concat_axis=0,
         tiled=True,
-    ).reshape(n_ctx, flight * CAP, cols)
+    )
     for total in sums:
         total.finish()
     parts = [own_sum, swap(near_sum, "ctx", 1)]
     places = [(0, 0), (1, 0)]
 
-    def combine(*back):
+    def combine(back):
         return pl.pallas_call(
             functools.partial(combine_kernel, flight=flight, count=n_ctx),
             out_shape=jax.ShapeDtypeStruct((block_tokens, width), jnp.bfloat16),
-            in_specs=whole_vmem(2 + n_ctx),
+            in_specs=whole_vmem(3),
             out_specs=pl.BlockSpec(memory_space=pltpu.VMEM),
             compiler_params=vmem(20),
             cost_estimate=FREE,
             name="combine",
-        )(routes.T, route_weights.T, *back)
-
-    combined = sequence.run(combine, tuple(back[i] for i in range(n_ctx)))
+        )(routes.T, route_weights.T, back)
+
+    combined = sequence.run(combine, (back,))
     for half in range(halves):
         for k, piece in zip(names, sums[half].result):
             parts.append(swap(piece, "ctx", k))

time: 95.5 us -> 91.5 us (0.958)
  starting transfers between devices: 41.1 us -> 36.3 us
  waiting for transfers between devices: 29.7 us -> 32.4 us
    ppermute x33 -> x34, starting transfers between devices: 34.6 us -> 28.8 us  [swap(): return lax.ppermute(x, axis, [(i, i ^ mask) for i in range(count)])]
    ppermute x33 -> x34, waiting for transfers between devices: 27.1 us -> 32.4 us  [swap(): return lax.ppermute(x, axis, [(i, i ^ mask) for i in range(count)])]
    all_to_all x1, waiting for transfers between devices: 2.58 us -> 0.01 us  [shards(): lax.all_to_all(produced, ('ctx', 'exp'), split_axis=0, concat_axis=0, til...]
    pallas_call x12 -> x6, Pallas kernels: 8.63 us -> 7.79 us  [the longest x5 7.76 us: together(): pl.pallas_call(kernel, out_shape=shapes, in_specs=whole_vmem(total), out_...]
  transfers between devices with their start and end apart: 36 -> 37, of which waited for: 14 -> 16; matrix products, arithmetic and copies ran while one was open for 1% -> 0% of each run, Pallas kernels for 19% -> 17%
where the time goes in v4:
time: 91.5 us; the launch traced here: 91.3 us
  starting transfers between devices  36.3 us (40%)
  waiting for transfers between devices  32.4 us (35%)
  Pallas kernels  18.9 us (21%)
  local copies, waits for them, and re-layouts  2.81 us (3%)
  between operations  0.92 us (1%)
    ppermute x34, waiting for transfers between devices, swap(): return lax.ppermute(x, axis, [(i, i ^ mask) for i in range(count)])  32.4 us
    ppermute x34, starting transfers between devices, swap(): return lax.ppermute(x, axis, [(i, i ^ mask) for i in range(count)])  28.8 us
    pallas_call x5, Pallas kernels, together(): pl.pallas_call(kernel, out_shape=shapes, in_specs=whole_vmem(total), out_...  7.76 us
    pallas_call x2, Pallas kernels, attention(): pl.pallas_call(functools.partial(attention_kernel, heads=width // HD, hom...  5.27 us
    all_to_all x1, starting transfers between devices, shards(): lax.all_to_all(produced, ('ctx', 'exp'), split_axis=0, concat_axis=0, til...  4.44 us
    ppermute x2, starting transfers between devices, shift(): return lax.ppermute(x, axis, [(i, (i + by) % count) for i in range(count)])  3.01 us
    unnamed x20, local copies, waits for them, and re-layouts  1.92 us
  transfers between devices with their start and end apart: 37, of which 16 were waited for; matrix products, arithmetic and copies ran while one was open for 0% of the time, Pallas kernels for 17%

profile of v4, /device:TPU:0, one launch (start us, length us, event | category | flops | bytes accessed | tf_op | source)
XLA Modules:
  0.0 91.3 jit_solution(6435893812174540779)
XLA Ops:
  0.6 0.9 dynamic-slice_bitcast_fusion
  1.6 3.0 %collective-permute-start = (bf16[2,256,128]{2,1,0:T(8,128)(2,1)S(1)}, bf16[2,256,128]{2,1,0:T(8,128)(2,1)S(1)}, u32[]{:S(2)}, u32[]{:S(2)}) collective-permute-start(bf16[2,256,128]{2,1,0:T(8,128)(2,1)S(1)} %pad_maximum_fusion.kv_own_ref), channel_id=1, source_target_pairs={{0,8},{4,12},{8,0},{12,4},{1,9},{5,13},{9,1},{13,5},{2,10},{6,14},... | collective-permute-start | bytes 393224 | tf_op jit(solution)/shard_map/ppermute | solution.py:27
  4.6 1.6 %collective-permute-start.3 = (s32[8,64]{1,0:T(8,128)}, s32[8,64]{1,0:T(8,128)S(1)}, u32[]{:S(2)}, u32[]{:S(2)}) collective-permute-start(s32[8,64]{1,0:T(8,128)} %bitcast.8), channel_id=1, source_target_pairs={{0,1},{1,0},{2,3},{3,2},{4,5},{5,4},{6,7},{7,6},{8,9},{9,8},{10,11... | collective-permute-start | bytes 6152 | tf_op jit(solution)/shard_map/ppermute | solution.py:22
  6.2 2.6 %collective-permute-start.4 = (s32[8,64]{1,0:T(8,128)}, s32[8,64]{1,0:T(8,128)S(1)}, u32[]{:S(2)}, u32[]{:S(2)}) collective-permute-start(s32[8,64]{1,0:T(8,128)} %bitcast.9), channel_id=1, source_target_pairs={{0,2},{1,3},{2,0},{3,1},{4,6},{5,7},{6,4},{7,5},{8,10},{9,11},{10,... | collective-permute-start | bytes 6152 | tf_op jit(solution)/shard_map/ppermute | solution.py:22
  9.0 1.2 %copy-done.5 = bf16[256,2048]{1,0:T(8,128)(2,1)S(1)} copy-done((bf16[256,2048]{1,0:T(8,128)(2,1)S(1)}, bf16[256,2048]{1,0:T(8,128)(2,1)}, u32[]{:S(2)}) %copy-start.5) | copy-done | bytes 1048600
  10.8 0.9 ready.1
  11.7 2.6 %attention_0.1.refs_0_.refs_8_.refs_3_ = bf16[128,2048]{1,0:T(8,128)(2,1)S(1)} custom-call(bf16[256,2048]{1,0:T(8,128)(2,1)S(1)} %get-tuple-element.131.q_ref, f32[256,640]{1,0:T(8,128)S(1)} %get-tuple-element.124.bias_ref, bf16[2,256,128]{2,1,0:T(8,128)(2,1)S(1)} %collective-permute-done.kv_far_ref, ...), custom_call_target="tpu_custom_call" | custom-call | tf_op jit(solution)/shard_map/attention_0/pallas_call | solution.py:201
  14.4 2.6 %attention_1.1.refs_1_.refs_9_.refs_4_ = bf16[128,2048]{1,0:T(8,128)(2,1)S(1)} custom-call(bf16[256,2048]{1,0:T(8,128)(2,1)S(1)} %get-tuple-element.131.q_ref, f32[256,640]{1,0:T(8,128)S(1)} %get-tuple-element.124.bias_ref, bf16[2,256,128]{2,1,0:T(8,128)(2,1)S(1)} %collective-permute-done.kv_far_ref, ...), custom_call_target="tpu_custom_call" | custom-call | tf_op jit(solution)/shard_map/attention_1/pallas_call | solution.py:201
  17.6 0.9 %collective-permute-start.11 = (bf16[128,2048]{1,0:T(8,128)(2,1)S(1)}, bf16[128,2048]{1,0:T(8,128)(2,1)S(1)}, u32[]{:S(2)}, u32[]{:S(2)}) collective-permute-start(bf16[128,2048]{1,0:T(8,128)(2,1)S(1)} %attention_0.1.refs_0_.refs_8_.refs_3_), channel_id=1, source_target_pairs={{0,8},{4,12},{8,0},{12,4},{1,9},{5,13},{9,1},{13,5},{2,10},{6,14},... | collective-permute-start | bytes 1572872 | tf_op jit(solution)/shard_map/ppermute | solution.py:22
  18.5 2.4 %leave_and_pick.1 = (bf16[128,1024]{1,0:T(8,128)(2,1)S(1)}, bf16[48,2048]{1,0:T(8,128)(2,1)S(1)}) custom-call(bf16[128,2048]{1,0:T(8,128)(2,1)S(1)} %attention_0.1.refs_0_.refs_8_.refs_3_, bf16[128,2048]{1,0:T(8,128)(2,1)S(1)} %attention_1.1.refs_1_.refs_9_.refs_4_, bf16[2048,1024]{1,0:T(8,128)(2,1)S(1)} %copy-done, bf16[64,4096]{1,0:T(8,128)(2,1)S(1)} %copy-done.4, ...), custom_call_target="tpu_custom_call" | custom-call | tf_op jit(solution)/shard_map/leave_and_pick/pallas_call | solution.py:74
  21.0 0.7 collective-permute-start.7
  21.7 1.8 %leave_and_stay.1 = (bf16[128,1024]{1,0:T(8,128)(2,1)S(1)}, bf16[128,1024]{1,0:T(8,128)(2,1)S(1)}, bf16[128,1024]{1,0:T(8,128)(2,1)S(1)}) custom-call(bf16[128,2048]{1,0:T(8,128)(2,1)S(1)} %collective-permute-done.2.refs_0_.refs_6_, bf16[128,2048]{1,0:T(8,128)(2,1)S(1)} %collective-permute-done.6.refs_1_.refs_7_, bf16[2048,1024]{1,0:T(8,128)(2,1)S(1)} %copy-done, ...), custom_call_target="tpu_custom_call" | custom-call | tf_op jit(solution)/shard_map/leave_and_stay/pallas_call | solution.py:74
  23.5 1.4 %collective-permute-start.9 = (bf16[128,1024]{1,0:T(8,128)(2,1)S(1)}, bf16[128,1024]{1,0:T(8,128)(2,1)S(1)}, u32[]{:S(2)}, u32[]{:S(2)}) collective-permute-start(bf16[128,1024]{1,0:T(8,128)(2,1)S(1)} %get-tuple-element.160), channel_id=1, source_target_pairs={{0,1},{1,0},{2,3},{3,2},{4,5},{5,4},{6,7},{7,6},{8,9},{9,8},{10,11... | collective-permute-start | bytes 786440 | tf_op jit(solution)/shard_map/ppermute | solution.py:22
  25.0 5.2 %collective-permute-done.7.arrived_ref = bf16[128,1024]{1,0:T(8,128)(2,1)S(1)} collective-permute-done((bf16[128,1024]{1,0:T(8,128)(2,1)S(1)}, bf16[128,1024]{1,0:T(8,128)(2,1)S(1)}, u32[]{:S(2)}, u32[]{:S(2)}) %collective-permute-start.7) | collective-permute-done | bytes 262176 | tf_op jit(solution)/shard_map/ppermute | solution.py:22
  30.3 1.2 %collective-permute-start.12 = (bf16[48,2048]{1,0:T(8,128)(2,1)S(1)}, bf16[48,2048]{1,0:T(8,128)(2,1)S(1)}, u32[]{:S(2)}, u32[]{:S(2)}) collective-permute-start(bf16[48,2048]{1,0:T(8,128)(2,1)S(1)} %get-tuple-element.174.refs_0_), channel_id=1, source_target_pairs={{0,8},{4,12},{8,0},{12,4},{1,9},{5,13},{9,1},{13,5},{2,10},{6,14},... | collective-permute-start | bytes 589832 | tf_op jit(solution)/shard_map/ppermute | solution.py:22
  31.5 2.1 %collective-permute-start.8 = (bf16[64,1024]{1,0:T(8,128)(2,1)S(1)}, bf16[64,1024]{1,0:T(8,128)(2,1)S(1)}, u32[]{:S(2)}, u32[]{:S(2)}) collective-permute-start(bf16[64,1024]{1,0:T(8,128)(2,1)S(1)} %get-tuple-element.159), channel_id=1, source_target_pairs={{0,2},{1,3},{2,0},{3,1},{4,6},{5,7},{6,4},{7,5},{8,10},{9,11},{10,... | collective-permute-start | bytes 393224 | tf_op jit(solution)/shard_map/ppermute | solution.py:22
  33.6 2.4 %collective-permute-done.12.refs_2_ = bf16[48,2048]{1,0:T(8,128)(2,1)S(1)} collective-permute-done((bf16[48,2048]{1,0:T(8,128)(2,1)S(1)}, bf16[48,2048]{1,0:T(8,128)(2,1)S(1)}, u32[]{:S(2)}, u32[]{:S(2)}) %collective-permute-start.12) | collective-permute-done | bytes 196640 | tf_op jit(solution)/shard_map/ppermute | solution.py:22
  36.0 1.5 %collective-permute-done.9.arrived_ref = bf16[128,1024]{1,0:T(8,128)(2,1)S(1)} collective-permute-done((bf16[128,1024]{1,0:T(8,128)(2,1)S(1)}, bf16[128,1024]{1,0:T(8,128)(2,1)S(1)}, u32[]{:S(2)}, u32[]{:S(2)}) %collective-permute-start.9) | collective-permute-done | bytes 262176 | tf_op jit(solution)/shard_map/ppermute | solution.py:22
  37.6 2.5 %collective-permute-done.8.arrived_ref = bf16[64,1024]{1,0:T(8,128)(2,1)S(1)} collective-permute-done((bf16[64,1024]{1,0:T(8,128)(2,1)S(1)}, bf16[64,1024]{1,0:T(8,128)(2,1)S(1)}, u32[]{:S(2)}, u32[]{:S(2)}) %collective-permute-start.8) | collective-permute-done | bytes 131104 | tf_op jit(solution)/shard_map/ppermute | solution.py:22
  40.2 0.9 %collective-permute-start.24 = (bf16[128,2048]{1,0:T(8,128)(2,1)S(1)}, bf16[128,2048]{1,0:T(8,128)(2,1)S(1)}, u32[]{:S(2)}, u32[]{:S(2)}) collective-permute-start(bf16[128,2048]{1,0:T(8,128)(2,1)S(1)} %attention_1.1.refs_1_.refs_9_.refs_4_), channel_id=1, source_target_pairs={{0,8},{4,12},{8,0},{12,4},{1,9},{5,13},{9,1},{13,5},{2,10},{6,14},... | collective-permute-start | bytes 1572872 | tf_op jit(solution)/shard_map/ppermute | solution.py:22
  41.6 0.9 %collective-permute-done.14.refs_1_ = bf16[48,2048]{1,0:T(8,128)(2,1)S(1)} collective-permute-done((bf16[48,2048]{1,0:T(8,128)(2,1)S(1)}, bf16[48,2048]{1,0:T(8,128)(2,1)S(1)}, u32[]{:S(2)}, u32[]{:S(2)}) %collective-permute-start.14) | collective-permute-done | bytes 196640 | tf_op jit(solution)/shard_map/ppermute | solution.py:22
  42.8 0.8 routed_product.1
  43.6 1.7 %collective-permute-start.18 = (bf16[4,8,1024]{2,1,0:T(8,128)(2,1)S(1)}, bf16[4,8,1024]{2,1,0:T(8,128)(2,1)S(1)}, u32[]{:S(2)}, u32[]{:S(2)}) collective-permute-start(bf16[4,8,1024]{2,1,0:T(8,128)(2,1)S(1)} %get-tuple-element.191), channel_id=1, source_target_pairs={{0,1},{1,0},{2,3},{3,2},{4,5},{5,4},{6,7},{7,6},{8,9},{9,8},{10,11... | collective-permute-start | bytes 196616 | tf_op jit(solution)/shard_map/ppermute | solution.py:22
  45.4 1.2 %collective-permute-start.19 = (bf16[4,8,1024]{2,1,0:T(8,128)(2,1)S(1)}, bf16[4,8,1024]{2,1,0:T(8,128)(2,1)S(1)}, u32[]{:S(2)}, u32[]{:S(2)}) collective-permute-start(bf16[4,8,1024]{2,1,0:T(8,128)(2,1)S(1)} %get-tuple-element.192), channel_id=1, source_target_pairs={{0,2},{1,3},{2,0},{3,1},{4,6},{5,7},{6,4},{7,5},{8,10},{9,11},{10,... | collective-permute-start | bytes 196616 | tf_op jit(solution)/shard_map/ppermute | solution.py:22
  46.6 1.5 %collective-permute-start.20 = (bf16[4,8,1024]{2,1,0:T(8,128)(2,1)S(1)}, bf16[4,8,1024]{2,1,0:T(8,128)(2,1)S(1)}, u32[]{:S(2)}, u32[]{:S(2)}) collective-permute-start(bf16[4,8,1024]{2,1,0:T(8,128)(2,1)S(1)} %get-tuple-element.179), channel_id=1, source_target_pairs={{0,3},{1,2},{2,1},{3,0},{4,7},{5,6},{6,5},{7,4},{8,11},{9,10},{10,... | collective-permute-start | bytes 196616 | tf_op jit(solution)/shard_map/ppermute | solution.py:22
  48.1 1.3 %far.2 = (bf16[128,1024]{1,0:T(8,128)(2,1)S(1)}, bf16[128,1024]{1,0:T(8,128)(2,1)S(1)}) custom-call(bf16[128,2048]{1,0:T(8,128)(2,1)S(1)} %collective-permute-done.11.refs_0_.refs_3_, bf16[128,2048]{1,0:T(8,128)(2,1)S(1)} %collective-permute-done.13.refs_1_.refs_4_, bf16[2048,1024]{1,0:T(8,128)(2,1)S(1)} %copy-done, ...), custom_call_target="tpu_custom_call" | custom-call | tf_op jit(solution)/shard_map/far/pallas_call | solution.py:74
  49.4 4.0 %collective-permute-done.10.arrived_ref = bf16[64,1024]{1,0:T(8,128)(2,1)S(1)} collective-permute-done((bf16[64,1024]{1,0:T(8,128)(2,1)S(1)}, bf16[64,1024]{1,0:T(8,128)(2,1)S(1)}, u32[]{:S(2)}, u32[]{:S(2)}) %collective-permute-start.10) | collective-permute-done | bytes 131104 | tf_op jit(solution)/shard_map/ppermute | solution.py:22
  53.4 1.4 %collective-permute-done.19.refs_2_ = bf16[4,8,1024]{2,1,0:T(8,128)(2,1)S(1)} collective-permute-done((bf16[4,8,1024]{2,1,0:T(8,128)(2,1)S(1)}, bf16[4,8,1024]{2,1,0:T(8,128)(2,1)S(1)}, u32[]{:S(2)}, u32[]{:S(2)}) %collective-permute-start.19) | collective-permute-done | bytes 65568 | tf_op jit(solution)/shard_map/ppermute | solution.py:22
  54.9 1.9 %collective-permute-start.17 = (bf16[128,1024]{1,0:T(8,128)(2,1)S(1)}, bf16[128,1024]{1,0:T(8,128)(2,1)S(1)}, u32[]{:S(2)}, u32[]{:S(2)}) collective-permute-start(bf16[128,1024]{1,0:T(8,128)(2,1)S(1)} %get-tuple-element.189), channel_id=1, source_target_pairs={{0,1},{1,0},{2,3},{3,2},{4,5},{5,4},{6,7},{7,6},{8,9},{9,8},{10,11... | collective-permute-start | bytes 786440 | tf_op jit(solution)/shard_map/ppermute | solution.py:22
  56.8 1.5 %far.3 = (bf16[128,1024]{1,0:T(8,128)(2,1)S(1)}, bf16[128,1024]{1,0:T(8,128)(2,1)S(1)}) custom-call(bf16[128,2048]{1,0:T(8,128)(2,1)S(1)} %collective-permute-done.24.refs_0_.refs_3_, bf16[128,2048]{1,0:T(8,128)(2,1)S(1)} %collective-permute-done.25.refs_1_.refs_4_, bf16[2048,1024]{1,0:T(8,128)(2,1)S(1)} %copy-done, ...), custom_call_target="tpu_custom_call" | custom-call | tf_op jit(solution)/shard_map/far/pallas_call | solution.py:74
  58.3 1.9 %collective-permute-start.30 = (bf16[128,1024]{1,0:T(8,128)(2,1)S(1)}, bf16[128,1024]{1,0:T(8,128)(2,1)S(1)}, u32[]{:S(2)}, u32[]{:S(2)}) collective-permute-start(bf16[128,1024]{1,0:T(8,128)(2,1)S(1)} %get-tuple-element.216), channel_id=1, source_target_pairs={{0,1},{1,0},{2,3},{3,2},{4,5},{5,4},{6,7},{7,6},{8,9},{9,8},{10,11... | collective-permute-start | bytes 786440 | tf_op jit(solution)/shard_map/ppermute | solution.py:22
  60.2 1.1 %collective-permute-start.22 = (bf16[32,1024]{1,0:T(8,128)(2,1)S(1)}, bf16[32,1024]{1,0:T(8,128)(2,1)S(1)}, u32[]{:S(2)}, u32[]{:S(2)}) collective-permute-start(bf16[32,1024]{1,0:T(8,128)(2,1)S(1)} %routed_sum.1.refs_0_), channel_id=1, source_target_pairs={{0,8},{4,12},{8,0},{12,4},{1,9},{5,13},{9,1},{13,5},{2,10},{6,14},... | collective-permute-start | bytes 196616 | tf_op jit(solution)/shard_map/ppermute | solution.py:22
  61.3 0.8 collective-permute-start.23
  62.0 3.0 %collective-permute-done.22.refs_2_ = bf16[32,1024]{1,0:T(8,128)(2,1)S(1)} collective-permute-done((bf16[32,1024]{1,0:T(8,128)(2,1)S(1)}, bf16[32,1024]{1,0:T(8,128)(2,1)S(1)}, u32[]{:S(2)}, u32[]{:S(2)}) %collective-permute-start.22) | collective-permute-done | bytes 65568 | tf_op jit(solution)/shard_map/ppermute | solution.py:22
  65.7 1.1 %hidden_units.1.refs_0_ = bf16[32,384]{1,0:T(8,128)(2,1)S(1)} custom-call(bf16[32,1024]{1,0:T(8,128)(2,1)S(1)} %routed_sum.1.refs_0_, bf16[32,1024]{1,0:T(8,128)(2,1)S(1)} %collective-permute-done.21.refs_1_, bf16[32,1024]{1,0:T(8,128)(2,1)S(1)} %collective-permute-done.22.refs_2_, bf16[32,1024]{1,0:T(8,128)(2,1)S(1)} %collective-permute-done.23.refs_3_, ...), custom_call_target="tpu_custom_call" | custom-call | tf_op jit(solution)/shard_map/hidden_units/pallas_call | solution.py:415
  67.4 1.1 %collective-permute-start.28 = (bf16[32,384]{1,0:T(8,128)(2,1)S(1)}, bf16[32,384]{1,0:T(8,128)(2,1)S(1)}, u32[]{:S(2)}, u32[]{:S(2)}) collective-permute-start(bf16[32,384]{1,0:T(8,128)(2,1)S(1)} %hidden_units.1.refs_0_), channel_id=1, source_target_pairs={{0,8},{4,12},{8,0},{12,4},{1,9},{5,13},{9,1},{13,5},{2,10},{6,14},... | collective-permute-start | bytes 73736 | tf_op jit(solution)/shard_map/ppermute | solution.py:22
  69.3 1.9 %collective-permute-done.28.refs_2_ = bf16[32,384]{1,0:T(8,128)(2,1)S(1)} collective-permute-done((bf16[32,384]{1,0:T(8,128)(2,1)S(1)}, bf16[32,384]{1,0:T(8,128)(2,1)S(1)}, u32[]{:S(2)}, u32[]{:S(2)}) %collective-permute-start.28) | collective-permute-done | bytes 24608 | tf_op jit(solution)/shard_map/ppermute | solution.py:22
  71.2 0.8 collective-permute-done.29.refs_3_
  72.5 1.3 %down_product.1 = bf16[16,2,1024]{2,1,0:T(2,128)(2,1)} custom-call(bf16[32,384]{1,0:T(8,128)(2,1)S(1)} %hidden_units.1.refs_0_, bf16[32,384]{1,0:T(8,128)(2,1)S(1)} %collective-permute-done.27.refs_1_, bf16[32,384]{1,0:T(8,128)(2,1)S(1)} %collective-permute-done.28.refs_2_, bf16[32,384]{1,0:T(8,128)(2,1)S(1)} %collective-permute-done.29.refs_3_, ...), custom_call_target="tpu_custom_call" | custom-call | tf_op jit(solution)/shard_map/down_product/pallas_call | solution.py:446
  73.8 4.4 %all-to-all-start = ((bf16[16,2,1024]{2,1,0:T(2,128)(2,1)}), bf16[16,2,1024]{2,1,0:T(2,128)(2,1)S(1)}, u32[]{:S(2)}, u32[]{:S(2)}) async-start(bf16[16,2,1024]{2,1,0:T(2,128)(2,1)} %down_product.1), calls=%async_computation | async-start | bytes 131072 | tf_op jit(solution)/shard_map/all_to_all | solution.py:728
  78.2 3.1 %collective-permute-done.26.arrived_ref = bf16[64,1024]{1,0:T(8,128)(2,1)S(1)} collective-permute-done((bf16[64,1024]{1,0:T(8,128)(2,1)S(1)}, bf16[64,1024]{1,0:T(8,128)(2,1)S(1)}, u32[]{:S(2)}, u32[]{:S(2)}) %collective-permute-start.26) | collective-permute-done | bytes 131104 | tf_op jit(solution)/shard_map/ppermute | solution.py:22
  81.3 1.2 %collective-permute-start.31 = (bf16[32,1024]{1,0:T(8,128)(2,1)S(1)}, bf16[32,1024]{1,0:T(8,128)(2,1)S(1)}, u32[]{:S(2)}, u32[]{:S(2)}) collective-permute-start(bf16[32,1024]{1,0:T(8,128)(2,1)S(1)} %get-tuple-element.227), channel_id=1, source_target_pairs={{0,8},{4,12},{8,0},{12,4},{1,9},{5,13},{9,1},{13,5},{2,10},{6,14},... | collective-permute-start | bytes 196616 | tf_op jit(solution)/shard_map/ppermute | solution.py:22
  82.8 2.0 %collective-permute-done.33.arrived_ref = bf16[64,1024]{1,0:T(8,128)(2,1)S(1)} collective-permute-done((bf16[64,1024]{1,0:T(8,128)(2,1)S(1)}, bf16[64,1024]{1,0:T(8,128)(2,1)S(1)}, u32[]{:S(2)}, u32[]{:S(2)}) %collective-permute-start.33) | collective-permute-done | bytes 131104 | tf_op jit(solution)/shard_map/ppermute | solution.py:22
  84.8 1.2 %collective-permute-start.34 = (bf16[32,1024]{1,0:T(8,128)(2,1)S(1)}, bf16[32,1024]{1,0:T(8,128)(2,1)S(1)}, u32[]{:S(2)}, u32[]{:S(2)}) collective-permute-start(bf16[32,1024]{1,0:T(8,128)(2,1)S(1)} %get-tuple-element.233), channel_id=1, source_target_pairs={{0,8},{4,12},{8,0},{12,4},{1,9},{5,13},{9,1},{13,5},{2,10},{6,14},... | collective-permute-start | bytes 196616 | tf_op jit(solution)/shard_map/ppermute | solution.py:22
  86.3 1.3 %combine.1 = bf16[64,4096]{1,0:T(8,128)(2,1)} custom-call(s32[8,64]{1,0:T(8,128)S(1)} %bitcast.12, f32[8,64]{1,0:T(8,128)S(1)} %bitcast.13, bf16[16,2,1024]{2,1,0:T(2,128)(2,1)S(1)} %all-to-all-done.back_ref), custom_call_target="tpu_custom_call" | custom-call | tf_op jit(solution)/shard_map/combine/pallas_call | solution.py:741
  87.6 1.8 %collective-permute-done.34.refs_4_ = bf16[32,1024]{1,0:T(8,128)(2,1)S(1)} collective-permute-done((bf16[32,1024]{1,0:T(8,128)(2,1)S(1)}, bf16[32,1024]{1,0:T(8,128)(2,1)S(1)}, u32[]{:S(2)}, u32[]{:S(2)}) %collective-permute-start.34) | collective-permute-done | bytes 65568 | tf_op jit(solution)/shard_map/ppermute | solution.py:22
  89.4 0.9 %collective-permute-done.35.refs_5_ = bf16[32,1024]{1,0:T(8,128)(2,1)S(1)} collective-permute-done((bf16[32,1024]{1,0:T(8,128)(2,1)S(1)}, bf16[32,1024]{1,0:T(8,128)(2,1)S(1)}, u32[]{:S(2)}, u32[]{:S(2)}) %collective-permute-start.35) | collective-permute-done | bytes 65568 | tf_op jit(solution)/shard_map/ppermute | solution.py:22
  90.3 0.9 %attended_rows.1 = bf16[64,4096]{1,0:T(8,128)(2,1)} custom-call(bf16[64,1024]{1,0:T(8,128)(2,1)S(1)} %add.16.refs_0_, bf16[64,1024]{1,0:T(8,128)(2,1)S(1)} %collective-permute-done.16.refs_1_, bf16[32,1024]{1,0:T(8,128)(2,1)S(1)} %collective-permute-done.31.refs_2_, bf16[32,1024]{1,0:T(8,128)(2,1)S(1)} %collective-permute-done.32.refs_3_, ...), custom_call_target="tpu_custom_call" | custom-call | tf_op jit(solution)/shard_map/attended_rows/pallas_call | solution.py:470
  (69 shorter events, 5.8 us)
Async XLA Ops:
  1.6 10.2 %collective-permute-start = (bf16[2,256,128]{2,1,0:T(8,128)(2,1)S(1)}, bf16[2,256,128]{2,1,0:T(8,128)(2,1)S(1)}, u32[]{:S(2)}, u32[]{:S(2)}) collective-permute-start(bf16[2,256,128]{2,1,0:T(8,128)(2,1)S(1)} %pad_maximum_fusion.kv_own_ref), channel_id=1, source_target_pairs={{0,8},{4,12},{8,0},{12,4},{1,9},{5,13},{9,1},{13,5},{2,10},{6,14},... | collective-permute-start | bytes 393224 | tf_op jit(solution)/shard_map/ppermute | solution.py:27
  4.6 7.2 %collective-permute-start.1 = (bf16[2,256,128]{2,1,0:T(8,128)(2,1)S(1)}, bf16[2,256,128]{2,1,0:T(8,128)(2,1)S(1)}, u32[]{:S(2)}, u32[]{:S(2)}) collective-permute-start(bf16[2,256,128]{2,1,0:T(8,128)(2,1)S(1)} %pad_maximum_fusion.kv_own_ref), channel_id=1, source_target_pairs={{0,4},{4,8},{8,12},{12,0},{1,5},{5,9},{9,13},{13,1},{2,6},{6,10},{... | collective-permute-start | bytes 393224 | tf_op jit(solution)/shard_map/ppermute | solution.py:27
  4.6 14.0 %copy-start = (bf16[2048,1024]{1,0:T(8,128)(2,1)S(1)}, bf16[2048,1024]{1,0:T(8,128)(2,1)}, u32[]{:S(2)}) copy-start(bf16[2048,1024]{1,0:T(8,128)(2,1)} %refs_5_.3) | copy-start | bytes 12582916
  4.6 14.0 %copy-start.4 = (bf16[64,4096]{1,0:T(8,128)(2,1)S(1)}, bf16[64,4096]{1,0:T(8,128)(2,1)}, u32[]{:S(2)}) copy-start(bf16[64,4096]{1,0:T(8,128)(2,1)} %refs_6_.3) | copy-start | bytes 1572868
  4.6 9.8 %collective-permute-start.3 = (s32[8,64]{1,0:T(8,128)}, s32[8,64]{1,0:T(8,128)S(1)}, u32[]{:S(2)}, u32[]{:S(2)}) collective-permute-start(s32[8,64]{1,0:T(8,128)} %bitcast.8), channel_id=1, source_target_pairs={{0,1},{1,0},{2,3},{3,2},{4,5},{5,4},{6,7},{7,6},{8,9},{9,8},{10,11... | collective-permute-start | bytes 6152 | tf_op jit(solution)/shard_map/ppermute | solution.py:22
  6.2 8.2 %collective-permute-start.4 = (s32[8,64]{1,0:T(8,128)}, s32[8,64]{1,0:T(8,128)S(1)}, u32[]{:S(2)}, u32[]{:S(2)}) collective-permute-start(s32[8,64]{1,0:T(8,128)} %bitcast.9), channel_id=1, source_target_pairs={{0,2},{1,3},{2,0},{3,1},{4,6},{5,7},{6,4},{7,5},{8,10},{9,11},{10,... | collective-permute-start | bytes 6152 | tf_op jit(solution)/shard_map/ppermute | solution.py:22
  8.8 5.6 %collective-permute-start.5 = (s32[8,64]{1,0:T(8,128)}, s32[8,64]{1,0:T(8,128)S(1)}, u32[]{:S(2)}, u32[]{:S(2)}) collective-permute-start(s32[8,64]{1,0:T(8,128)} %bitcast.10), channel_id=1, source_target_pairs={{0,3},{1,2},{2,1},{3,0},{4,7},{5,6},{6,5},{7,4},{8,11},{9,10},{10,... | collective-permute-start | bytes 6152 | tf_op jit(solution)/shard_map/ppermute | solution.py:22
  9.0 1.2 %copy-start.5 = (bf16[256,2048]{1,0:T(8,128)(2,1)S(1)}, bf16[256,2048]{1,0:T(8,128)(2,1)}, u32[]{:S(2)}) copy-start(bf16[256,2048]{1,0:T(8,128)(2,1)} %q_hbm) | copy-start | bytes 3145732
  10.2 0.7 copy-start.9
  10.8 7.7 %copy-start.7 = (s32[64,8]{0,1:T(8,128)S(1)}, s32[64,8]{0,1:T(8,128)}, u32[]{:S(2)}) copy-start(s32[64,8]{0,1:T(8,128)} %param.19) | copy-start | bytes 6148
  17.0 4.6 %collective-permute-start.6 = (bf16[128,2048]{1,0:T(8,128)(2,1)S(1)}, bf16[128,2048]{1,0:T(8,128)(2,1)S(1)}, u32[]{:S(2)}, u32[]{:S(2)}) collective-permute-start(bf16[128,2048]{1,0:T(8,128)(2,1)S(1)} %attention_1.1.refs_1_.refs_9_.refs_4_), channel_id=1, source_target_pairs={{0,4},{4,0},{8,12},{12,8},{1,5},{5,1},{9,13},{13,9},{2,6},{6,2},{1... | collective-permute-start | bytes 1572872 | tf_op jit(solution)/shard_map/ppermute | solution.py:22
  17.1 4.6 %collective-permute-start.2 = (bf16[128,2048]{1,0:T(8,128)(2,1)S(1)}, bf16[128,2048]{1,0:T(8,128)(2,1)S(1)}, u32[]{:S(2)}, u32[]{:S(2)}) collective-permute-start(bf16[128,2048]{1,0:T(8,128)(2,1)S(1)} %attention_0.1.refs_0_.refs_8_.refs_3_), channel_id=1, source_target_pairs={{0,4},{4,0},{8,12},{12,8},{1,5},{5,1},{9,13},{13,9},{2,6},{6,2},{1... | collective-permute-start | bytes 1572872 | tf_op jit(solution)/shard_map/ppermute | solution.py:22
  17.6 16.0 %collective-permute-start.11 = (bf16[128,2048]{1,0:T(8,128)(2,1)S(1)}, bf16[128,2048]{1,0:T(8,128)(2,1)S(1)}, u32[]{:S(2)}, u32[]{:S(2)}) collective-permute-start(bf16[128,2048]{1,0:T(8,128)(2,1)S(1)} %attention_0.1.refs_0_.refs_8_.refs_3_), channel_id=1, source_target_pairs={{0,8},{4,12},{8,0},{12,4},{1,9},{5,13},{9,1},{13,5},{2,10},{6,14},... | collective-permute-start | bytes 1572872 | tf_op jit(solution)/shard_map/ppermute | solution.py:22
  21.0 9.2 %collective-permute-start.7 = (bf16[128,1024]{1,0:T(8,128)(2,1)S(1)}, bf16[128,1024]{1,0:T(8,128)(2,1)S(1)}, u32[]{:S(2)}, u32[]{:S(2)}) collective-permute-start(bf16[128,1024]{1,0:T(8,128)(2,1)S(1)} %get-tuple-element.153), channel_id=1, source_target_pairs={{0,1},{1,0},{2,3},{3,2},{4,5},{5,4},{6,7},{7,6},{8,9},{9,8},{10,11... | collective-permute-start | bytes 786440 | tf_op jit(solution)/shard_map/ppermute | solution.py:22
  23.5 14.0 %collective-permute-start.9 = (bf16[128,1024]{1,0:T(8,128)(2,1)S(1)}, bf16[128,1024]{1,0:T(8,128)(2,1)S(1)}, u32[]{:S(2)}, u32[]{:S(2)}) collective-permute-start(bf16[128,1024]{1,0:T(8,128)(2,1)S(1)} %get-tuple-element.160), channel_id=1, source_target_pairs={{0,1},{1,0},{2,3},{3,2},{4,5},{5,4},{6,7},{7,6},{8,9},{9,8},{10,11... | collective-permute-start | bytes 786440 | tf_op jit(solution)/shard_map/ppermute | solution.py:22
  30.3 5.7 %collective-permute-start.12 = (bf16[48,2048]{1,0:T(8,128)(2,1)S(1)}, bf16[48,2048]{1,0:T(8,128)(2,1)S(1)}, u32[]{:S(2)}, u32[]{:S(2)}) collective-permute-start(bf16[48,2048]{1,0:T(8,128)(2,1)S(1)} %get-tuple-element.174.refs_0_), channel_id=1, source_target_pairs={{0,8},{4,12},{8,0},{12,4},{1,9},{5,13},{9,1},{13,5},{2,10},{6,14},... | collective-permute-start | bytes 589832 | tf_op jit(solution)/shard_map/ppermute | solution.py:22
  31.5 8.7 %collective-permute-start.8 = (bf16[64,1024]{1,0:T(8,128)(2,1)S(1)}, bf16[64,1024]{1,0:T(8,128)(2,1)S(1)}, u32[]{:S(2)}, u32[]{:S(2)}) collective-permute-start(bf16[64,1024]{1,0:T(8,128)(2,1)S(1)} %get-tuple-element.159), channel_id=1, source_target_pairs={{0,2},{1,3},{2,0},{3,1},{4,6},{5,7},{6,4},{7,5},{8,10},{9,11},{10,... | collective-permute-start | bytes 393224 | tf_op jit(solution)/shard_map/ppermute | solution.py:22
  37.5 9.1 %collective-permute-start.13 = (bf16[128,2048]{1,0:T(8,128)(2,1)S(1)}, bf16[128,2048]{1,0:T(8,128)(2,1)S(1)}, u32[]{:S(2)}, u32[]{:S(2)}) collective-permute-start(bf16[128,2048]{1,0:T(8,128)(2,1)S(1)} %collective-permute-done.11.refs_0_.refs_3_), channel_id=1, source_target_pairs={{0,4},{4,0},{8,12},{12,8},{1,5},{5,1},{9,13},{13,9},{2,6},{6,2},{1... | collective-permute-start | bytes 1572872 | tf_op jit(solution)/shard_map/ppermute | solution.py:22
  40.2 14.6 %collective-permute-start.24 = (bf16[128,2048]{1,0:T(8,128)(2,1)S(1)}, bf16[128,2048]{1,0:T(8,128)(2,1)S(1)}, u32[]{:S(2)}, u32[]{:S(2)}) collective-permute-start(bf16[128,2048]{1,0:T(8,128)(2,1)S(1)} %attention_1.1.refs_1_.refs_9_.refs_4_), channel_id=1, source_target_pairs={{0,8},{4,12},{8,0},{12,4},{1,9},{5,13},{9,1},{13,5},{2,10},{6,14},... | collective-permute-start | bytes 1572872 | tf_op jit(solution)/shard_map/ppermute | solution.py:22
  41.1 1.4 %collective-permute-start.14 = (bf16[48,2048]{1,0:T(8,128)(2,1)S(1)}, bf16[48,2048]{1,0:T(8,128)(2,1)S(1)}, u32[]{:S(2)}, u32[]{:S(2)}) collective-permute-start(bf16[48,2048]{1,0:T(8,128)(2,1)S(1)} %get-tuple-element.174.refs_0_), channel_id=1, source_target_pairs={{0,4},{4,0},{8,12},{12,8},{1,5},{5,1},{9,13},{13,9},{2,6},{6,2},{1... | collective-permute-start | bytes 589832 | tf_op jit(solution)/shard_map/ppermute | solution.py:22
  41.1 1.7 %collective-permute-start.15 = (bf16[48,2048]{1,0:T(8,128)(2,1)S(1)}, bf16[48,2048]{1,0:T(8,128)(2,1)S(1)}, u32[]{:S(2)}, u32[]{:S(2)}) collective-permute-start(bf16[48,2048]{1,0:T(8,128)(2,1)S(1)} %collective-permute-done.12.refs_2_), channel_id=1, source_target_pairs={{0,4},{4,0},{8,12},{12,8},{1,5},{5,1},{9,13},{13,9},{2,6},{6,2},{1... | collective-permute-start | bytes 589832 | tf_op jit(solution)/shard_map/ppermute | solution.py:22
  41.6 11.7 %collective-permute-start.10 = (bf16[64,1024]{1,0:T(8,128)(2,1)S(1)}, bf16[64,1024]{1,0:T(8,128)(2,1)S(1)}, u32[]{:S(2)}, u32[]{:S(2)}) collective-permute-start(bf16[64,1024]{1,0:T(8,128)(2,1)S(1)} %get-tuple-element.167), channel_id=1, source_target_pairs={{0,2},{1,3},{2,0},{3,1},{4,6},{5,7},{6,4},{7,5},{8,10},{9,11},{10,... | collective-permute-start | bytes 393224 | tf_op jit(solution)/shard_map/ppermute | solution.py:22
  43.6 9.7 %collective-permute-start.18 = (bf16[4,8,1024]{2,1,0:T(8,128)(2,1)S(1)}, bf16[4,8,1024]{2,1,0:T(8,128)(2,1)S(1)}, u32[]{:S(2)}, u32[]{:S(2)}) collective-permute-start(bf16[4,8,1024]{2,1,0:T(8,128)(2,1)S(1)} %get-tuple-element.191), channel_id=1, source_target_pairs={{0,1},{1,0},{2,3},{3,2},{4,5},{5,4},{6,7},{7,6},{8,9},{9,8},{10,11... | collective-permute-start | bytes 196616 | tf_op jit(solution)/shard_map/ppermute | solution.py:22
  45.4 9.3 %collective-permute-start.19 = (bf16[4,8,1024]{2,1,0:T(8,128)(2,1)S(1)}, bf16[4,8,1024]{2,1,0:T(8,128)(2,1)S(1)}, u32[]{:S(2)}, u32[]{:S(2)}) collective-permute-start(bf16[4,8,1024]{2,1,0:T(8,128)(2,1)S(1)} %get-tuple-element.192), channel_id=1, source_target_pairs={{0,2},{1,3},{2,0},{3,1},{4,6},{5,7},{6,4},{7,5},{8,10},{9,11},{10,... | collective-permute-start | bytes 196616 | tf_op jit(solution)/shard_map/ppermute | solution.py:22
  46.6 8.1 %collective-permute-start.20 = (bf16[4,8,1024]{2,1,0:T(8,128)(2,1)S(1)}, bf16[4,8,1024]{2,1,0:T(8,128)(2,1)S(1)}, u32[]{:S(2)}, u32[]{:S(2)}) collective-permute-start(bf16[4,8,1024]{2,1,0:T(8,128)(2,1)S(1)} %get-tuple-element.179), channel_id=1, source_target_pairs={{0,3},{1,2},{2,1},{3,0},{4,7},{5,6},{6,5},{7,4},{8,11},{9,10},{10,... | collective-permute-start | bytes 196616 | tf_op jit(solution)/shard_map/ppermute | solution.py:22
  54.8 2.1 %collective-permute-start.25 = (bf16[128,2048]{1,0:T(8,128)(2,1)S(1)}, bf16[128,2048]{1,0:T(8,128)(2,1)S(1)}, u32[]{:S(2)}, u32[]{:S(2)}) collective-permute-start(bf16[128,2048]{1,0:T(8,128)(2,1)S(1)} %collective-permute-done.24.refs_0_.refs_3_), channel_id=1, source_target_pairs={{0,4},{4,0},{8,12},{12,8},{1,5},{5,1},{9,13},{13,9},{2,6},{6,2},{1... | collective-permute-start | bytes 1572872 | tf_op jit(solution)/shard_map/ppermute | solution.py:22
  54.9 10.8 %copy-start.1 = (bf16[1,4096,384]{2,1,0:T(8,128)(2,1)S(1)}, bf16[1,4096,384]{2,1,0:T(8,128)(2,1)}, u32[]{:S(2)}) copy-start(bf16[1,4096,384]{2,1,0:T(8,128)(2,1)} %refs_5_.4) | copy-start | bytes 9437188
  54.9 10.8 %copy-start.2 = (bf16[1,4096,384]{2,1,0:T(8,128)(2,1)S(1)}, bf16[1,4096,384]{2,1,0:T(8,128)(2,1)}, u32[]{:S(2)}) copy-start(bf16[1,4096,384]{2,1,0:T(8,128)(2,1)} %refs_6_.2) | copy-start | bytes 9437188
  54.9 10.8 %copy-start.6 = (f32[4096]{0:T(1024)S(1)}, f32[4096]{0:T(1024)}, u32[]{:S(2)}) copy-start(f32[4096]{0:T(1024)} %param.18) | copy-start | bytes 49156
  54.9 13.9 %collective-permute-start.17 = (bf16[128,1024]{1,0:T(8,128)(2,1)S(1)}, bf16[128,1024]{1,0:T(8,128)(2,1)S(1)}, u32[]{:S(2)}, u32[]{:S(2)}) collective-permute-start(bf16[128,1024]{1,0:T(8,128)(2,1)S(1)} %get-tuple-element.189), channel_id=1, source_target_pairs={{0,1},{1,0},{2,3},{3,2},{4,5},{5,4},{6,7},{7,6},{8,9},{9,8},{10,11... | collective-permute-start | bytes 786440 | tf_op jit(solution)/shard_map/ppermute | solution.py:22
  58.3 13.7 %collective-permute-start.30 = (bf16[128,1024]{1,0:T(8,128)(2,1)S(1)}, bf16[128,1024]{1,0:T(8,128)(2,1)S(1)}, u32[]{:S(2)}, u32[]{:S(2)}) collective-permute-start(bf16[128,1024]{1,0:T(8,128)(2,1)S(1)} %get-tuple-element.216), channel_id=1, source_target_pairs={{0,1},{1,0},{2,3},{3,2},{4,5},{5,4},{6,7},{7,6},{8,9},{9,8},{10,11... | collective-permute-start | bytes 786440 | tf_op jit(solution)/shard_map/ppermute | solution.py:22
  60.2 1.9 %collective-permute-start.21 = (bf16[32,1024]{1,0:T(8,128)(2,1)S(1)}, bf16[32,1024]{1,0:T(8,128)(2,1)S(1)}, u32[]{:S(2)}, u32[]{:S(2)}) collective-permute-start(bf16[32,1024]{1,0:T(8,128)(2,1)S(1)} %routed_sum.1.refs_0_), channel_id=1, source_target_pairs={{0,4},{4,0},{8,12},{12,8},{1,5},{5,1},{9,13},{13,9},{2,6},{6,2},{1... | collective-permute-start | bytes 196616 | tf_op jit(solution)/shard_map/ppermute | solution.py:22
  60.2 4.9 %collective-permute-start.22 = (bf16[32,1024]{1,0:T(8,128)(2,1)S(1)}, bf16[32,1024]{1,0:T(8,128)(2,1)S(1)}, u32[]{:S(2)}, u32[]{:S(2)}) collective-permute-start(bf16[32,1024]{1,0:T(8,128)(2,1)S(1)} %routed_sum.1.refs_0_), channel_id=1, source_target_pairs={{0,8},{4,12},{8,0},{12,4},{1,9},{5,13},{9,1},{13,5},{2,10},{6,14},... | collective-permute-start | bytes 196616 | tf_op jit(solution)/shard_map/ppermute | solution.py:22
  61.3 4.4 %collective-permute-start.23 = (bf16[32,1024]{1,0:T(8,128)(2,1)S(1)}, bf16[32,1024]{1,0:T(8,128)(2,1)S(1)}, u32[]{:S(2)}, u32[]{:S(2)}) collective-permute-start(bf16[32,1024]{1,0:T(8,128)(2,1)S(1)} %routed_sum.1.refs_0_), channel_id=1, source_target_pairs={{0,12},{4,8},{8,4},{12,0},{1,13},{5,9},{9,5},{13,1},{2,14},{6,10},... | collective-permute-start | bytes 196616 | tf_op jit(solution)/shard_map/ppermute | solution.py:22
  65.7 6.8 %copy-start.3 = (bf16[1,1536,1024]{2,1,0:T(8,128)(2,1)S(1)}, bf16[1,1536,1024]{2,1,0:T(8,128)(2,1)}, u32[]{:S(2)}) copy-start(bf16[1,1536,1024]{2,1,0:T(8,128)(2,1)} %refs_4_.2) | copy-start | bytes 9437188
  66.8 19.5 %copy-start.8 = (f32[64,8]{0,1:T(8,128)S(1)}, f32[64,8]{0,1:T(8,128)}, u32[]{:S(2)}) copy-start(f32[64,8]{0,1:T(8,128)} %param.20) | copy-start | bytes 6148
  66.8 2.5 %collective-permute-start.27 = (bf16[32,384]{1,0:T(8,128)(2,1)S(1)}, bf16[32,384]{1,0:T(8,128)(2,1)S(1)}, u32[]{:S(2)}, u32[]{:S(2)}) collective-permute-start(bf16[32,384]{1,0:T(8,128)(2,1)S(1)} %hidden_units.1.refs_0_), channel_id=1, source_target_pairs={{0,4},{4,0},{8,12},{12,8},{1,5},{5,1},{9,13},{13,9},{2,6},{6,2},{1... | collective-permute-start | bytes 73736 | tf_op jit(solution)/shard_map/ppermute | solution.py:22
  67.4 3.8 %collective-permute-start.28 = (bf16[32,384]{1,0:T(8,128)(2,1)S(1)}, bf16[32,384]{1,0:T(8,128)(2,1)S(1)}, u32[]{:S(2)}, u32[]{:S(2)}) collective-permute-start(bf16[32,384]{1,0:T(8,128)(2,1)S(1)} %hidden_units.1.refs_0_), channel_id=1, source_target_pairs={{0,8},{4,12},{8,0},{12,4},{1,9},{5,13},{9,1},{13,5},{2,10},{6,14},... | collective-permute-start | bytes 73736 | tf_op jit(solution)/shard_map/ppermute | solution.py:22
  68.5 3.5 %collective-permute-start.29 = (bf16[32,384]{1,0:T(8,128)(2,1)S(1)}, bf16[32,384]{1,0:T(8,128)(2,1)S(1)}, u32[]{:S(2)}, u32[]{:S(2)}) collective-permute-start(bf16[32,384]{1,0:T(8,128)(2,1)S(1)} %hidden_units.1.refs_0_), channel_id=1, source_target_pairs={{0,12},{4,8},{8,4},{12,0},{1,13},{5,9},{9,5},{13,1},{2,14},{6,10},... | collective-permute-start | bytes 73736 | tf_op jit(solution)/shard_map/ppermute | solution.py:22
  68.9 12.4 %collective-permute-start.26 = (bf16[64,1024]{1,0:T(8,128)(2,1)S(1)}, bf16[64,1024]{1,0:T(8,128)(2,1)S(1)}, u32[]{:S(2)}, u32[]{:S(2)}) collective-permute-start(bf16[64,1024]{1,0:T(8,128)(2,1)S(1)} %get-tuple-element.215), channel_id=1, source_target_pairs={{0,2},{1,3},{2,0},{3,1},{4,6},{5,7},{6,4},{7,5},{8,10},{9,11},{10,... | collective-permute-start | bytes 393224 | tf_op jit(solution)/shard_map/ppermute | solution.py:22
  72.1 12.8 %collective-permute-start.33 = (bf16[64,1024]{1,0:T(8,128)(2,1)S(1)}, bf16[64,1024]{1,0:T(8,128)(2,1)S(1)}, u32[]{:S(2)}, u32[]{:S(2)}) collective-permute-start(bf16[64,1024]{1,0:T(8,128)(2,1)S(1)} %get-tuple-element.230), channel_id=1, source_target_pairs={{0,2},{1,3},{2,0},{3,1},{4,6},{5,7},{6,4},{7,5},{8,10},{9,11},{10,... | collective-permute-start | bytes 393224 | tf_op jit(solution)/shard_map/ppermute | solution.py:22
  72.5 15.2 %collective-permute-start.16 = (bf16[64,1024]{1,0:T(8,128)(2,1)S(1)}, bf16[64,1024]{1,0:T(8,128)(2,1)S(1)}, u32[]{:S(2)}, u32[]{:S(2)}) collective-permute-start(bf16[64,1024]{1,0:T(8,128)(2,1)S(1)} %add.17), channel_id=1, source_target_pairs={{0,4},{4,0},{8,12},{12,8},{1,5},{5,1},{9,13},{13,9},{2,6},{6,2},{1... | collective-permute-start | bytes 393224 | tf_op jit(solution)/shard_map/ppermute | solution.py:22
  73.8 12.6 %all-to-all-start = ((bf16[16,2,1024]{2,1,0:T(2,128)(2,1)}), bf16[16,2,1024]{2,1,0:T(2,128)(2,1)S(1)}, u32[]{:S(2)}, u32[]{:S(2)}) async-start(bf16[16,2,1024]{2,1,0:T(2,128)(2,1)} %down_product.1), calls=%async_computation | async-start | bytes 131072 | tf_op jit(solution)/shard_map/all_to_all | solution.py:728
  81.3 6.3 %collective-permute-start.31 = (bf16[32,1024]{1,0:T(8,128)(2,1)S(1)}, bf16[32,1024]{1,0:T(8,128)(2,1)S(1)}, u32[]{:S(2)}, u32[]{:S(2)}) collective-permute-start(bf16[32,1024]{1,0:T(8,128)(2,1)S(1)} %get-tuple-element.227), channel_id=1, source_target_pairs={{0,8},{4,12},{8,0},{12,4},{1,9},{5,13},{9,1},{13,5},{2,10},{6,14},... | collective-permute-start | bytes 196616 | tf_op jit(solution)/shard_map/ppermute | solution.py:22
  82.5 5.2 %collective-permute-start.32 = (bf16[32,1024]{1,0:T(8,128)(2,1)S(1)}, bf16[32,1024]{1,0:T(8,128)(2,1)S(1)}, u32[]{:S(2)}, u32[]{:S(2)}) collective-permute-start(bf16[32,1024]{1,0:T(8,128)(2,1)S(1)} %get-tuple-element.228), channel_id=1, source_target_pairs={{0,12},{4,8},{8,4},{12,0},{1,13},{5,9},{9,5},{13,1},{2,14},{6,10},... | collective-permute-start | bytes 196616 | tf_op jit(solution)/shard_map/ppermute | solution.py:22
  84.8 4.6 %collective-permute-start.34 = (bf16[32,1024]{1,0:T(8,128)(2,1)S(1)}, bf16[32,1024]{1,0:T(8,128)(2,1)S(1)}, u32[]{:S(2)}, u32[]{:S(2)}) collective-permute-start(bf16[32,1024]{1,0:T(8,128)(2,1)S(1)} %get-tuple-element.233), channel_id=1, source_target_pairs={{0,8},{4,12},{8,0},{12,4},{1,9},{5,13},{9,1},{13,5},{2,10},{6,14},... | collective-permute-start | bytes 196616 | tf_op jit(solution)/shard_map/ppermute | solution.py:22
  86.0 4.3 %collective-permute-start.35 = (bf16[32,1024]{1,0:T(8,128)(2,1)S(1)}, bf16[32,1024]{1,0:T(8,128)(2,1)S(1)}, u32[]{:S(2)}, u32[]{:S(2)}) collective-permute-start(bf16[32,1024]{1,0:T(8,128)(2,1)S(1)} %get-tuple-element.234), channel_id=1, source_target_pairs={{0,12},{4,8},{8,4},{12,0},{1,13},{5,9},{9,5},{13,1},{2,14},{6,10},... | collective-permute-start | bytes 196616 | tf_op jit(solution)/shard_map/ppermute | solution.py:22

commit v5 on v4

--- a/solution.py
+++ b/solution.py
@@ -714,6 +714,7 @@
     if halves > 1:
         far[1].hop()
         second = far[1].pieces(names)
+        second = lax.optimization_barrier(second + tuple(stream_rows))[: len(second)]
         (send,), (keep,) = sequence.steps("far", leaving(second), staying(second))
         sums.append(Halving(sequence, keep, send, plain_add(one * len(names))))
     hidden = sequence.run(
@@ -721,10 +722,10 @@
     )
     hidden_pieces = gather_direct(hidden, "ctx")
     sums[0].advance()
+    produced = sequence.run(lambda *xs: down_product(xs, down_weight), tuple(hidden_pieces))
     if halves > 1:
-        sums[1].wait(*hidden_pieces)
         sums[1].advance()
-    produced = sequence.run(lambda *xs: down_product(xs, down_weight), tuple(hidden_pieces))
+    (produced,) = sequence.tie(produced)
     back = lax.all_to_all(
         produced,
         ("ctx", "exp"),

time: 91.5 us -> 89.8 us (0.981)
  waiting for transfers between devices: 32.4 us -> 31 us
    ppermute x34, waiting for transfers between devices: 32.4 us -> 30.3 us  [swap(): return lax.ppermute(x, axis, [(i, i ^ mask) for i in range(count)])]
  transfers between devices with their start and end apart: 37 -> 37, of which waited for: 16 -> 18; matrix products, arithmetic and copies ran while one was open for 0% -> 0% of each run, Pallas kernels for 17% -> 17%
where the time goes in v5:
time: 89.8 us; the launch traced here: 89.5 us
  starting transfers between devices  36 us (40%)
  waiting for transfers between devices  31 us (35%)
  Pallas kernels  18.8 us (21%)
  local copies, waits for them, and re-layouts  2.8 us (3%)
  between operations  0.9 us (1%)
    ppermute x34, waiting for transfers between devices, swap(): return lax.ppermute(x, axis, [(i, i ^ mask) for i in range(count)])  30.3 us
    ppermute x34, starting transfers between devices, swap(): return lax.ppermute(x, axis, [(i, i ^ mask) for i in range(count)])  28.7 us
    pallas_call x5, Pallas kernels, together(): pl.pallas_call(kernel, out_shape=shapes, in_specs=whole_vmem(total), out_...  7.75 us
    pallas_call x2, Pallas kernels, attention(): pl.pallas_call(functools.partial(attention_kernel, heads=width // HD, hom...  5.27 us
    all_to_all x1, starting transfers between devices, shards(): lax.all_to_all(produced, ('ctx', 'exp'), split_axis=0, concat_axis=0, til...  4.3 us
    ppermute x2, starting transfers between devices, shift(): return lax.ppermute(x, axis, [(i, (i + by) % count) for i in range(count)])  3.01 us
    unnamed x20, local copies, waits for them, and re-layouts  1.91 us
  transfers between devices with their start and end apart: 37, of which 18 were waited for; matrix products, arithmetic and copies ran while one was open for 0% of the time, Pallas kernels for 17%

profile of v5, /device:TPU:0, one launch (start us, length us, event | category | flops | bytes accessed | tf_op | source)
XLA Modules:
  0.0 89.5 jit_solution(15925700957009025700)
XLA Ops:
  0.6 0.9 dynamic-slice_bitcast_fusion
  1.6 3.0 %collective-permute-start = (bf16[2,256,128]{2,1,0:T(8,128)(2,1)S(1)}, bf16[2,256,128]{2,1,0:T(8,128)(2,1)S(1)}, u32[]{:S(2)}, u32[]{:S(2)}) collective-permute-start(bf16[2,256,128]{2,1,0:T(8,128)(2,1)S(1)} %pad_maximum_fusion.kv_own_ref), channel_id=1, source_target_pairs={{0,8},{4,12},{8,0},{12,4},{1,9},{5,13},{9,1},{13,5},{2,10},{6,14},... | collective-permute-start | bytes 393224 | tf_op jit(solution)/shard_map/ppermute | solution.py:27
  4.6 1.6 %collective-permute-start.3 = (s32[8,64]{1,0:T(8,128)}, s32[8,64]{1,0:T(8,128)S(1)}, u32[]{:S(2)}, u32[]{:S(2)}) collective-permute-start(s32[8,64]{1,0:T(8,128)} %bitcast.8), channel_id=1, source_target_pairs={{0,1},{1,0},{2,3},{3,2},{4,5},{5,4},{6,7},{7,6},{8,9},{9,8},{10,11... | collective-permute-start | bytes 6152 | tf_op jit(solution)/shard_map/ppermute | solution.py:22
  6.2 2.6 %collective-permute-start.4 = (s32[8,64]{1,0:T(8,128)}, s32[8,64]{1,0:T(8,128)S(1)}, u32[]{:S(2)}, u32[]{:S(2)}) collective-permute-start(s32[8,64]{1,0:T(8,128)} %bitcast.9), channel_id=1, source_target_pairs={{0,2},{1,3},{2,0},{3,1},{4,6},{5,7},{6,4},{7,5},{8,10},{9,11},{10,... | collective-permute-start | bytes 6152 | tf_op jit(solution)/shard_map/ppermute | solution.py:22
  9.0 1.2 %copy-done.5 = bf16[256,2048]{1,0:T(8,128)(2,1)S(1)} copy-done((bf16[256,2048]{1,0:T(8,128)(2,1)S(1)}, bf16[256,2048]{1,0:T(8,128)(2,1)}, u32[]{:S(2)}) %copy-start.5) | copy-done | bytes 1048600
  10.8 0.9 ready.1
  11.7 2.6 %attention_0.1.refs_0_.refs_8_.refs_3_ = bf16[128,2048]{1,0:T(8,128)(2,1)S(1)} custom-call(bf16[256,2048]{1,0:T(8,128)(2,1)S(1)} %get-tuple-element.133.q_ref, f32[256,640]{1,0:T(8,128)S(1)} %get-tuple-element.126.bias_ref, bf16[2,256,128]{2,1,0:T(8,128)(2,1)S(1)} %collective-permute-done.kv_far_ref, ...), custom_call_target="tpu_custom_call" | custom-call | tf_op jit(solution)/shard_map/attention_0/pallas_call | solution.py:201
  14.4 2.6 %attention_1.1.refs_1_.refs_9_.refs_4_ = bf16[128,2048]{1,0:T(8,128)(2,1)S(1)} custom-call(bf16[256,2048]{1,0:T(8,128)(2,1)S(1)} %get-tuple-element.133.q_ref, f32[256,640]{1,0:T(8,128)S(1)} %get-tuple-element.126.bias_ref, bf16[2,256,128]{2,1,0:T(8,128)(2,1)S(1)} %collective-permute-done.kv_far_ref, ...), custom_call_target="tpu_custom_call" | custom-call | tf_op jit(solution)/shard_map/attention_1/pallas_call | solution.py:201
  17.6 0.9 %collective-permute-start.11 = (bf16[128,2048]{1,0:T(8,128)(2,1)S(1)}, bf16[128,2048]{1,0:T(8,128)(2,1)S(1)}, u32[]{:S(2)}, u32[]{:S(2)}) collective-permute-start(bf16[128,2048]{1,0:T(8,128)(2,1)S(1)} %attention_0.1.refs_0_.refs_8_.refs_3_), channel_id=1, source_target_pairs={{0,8},{4,12},{8,0},{12,4},{1,9},{5,13},{9,1},{13,5},{2,10},{6,14},... | collective-permute-start | bytes 1572872 | tf_op jit(solution)/shard_map/ppermute | solution.py:22
  18.5 2.4 %leave_and_pick.1 = (bf16[128,1024]{1,0:T(8,128)(2,1)S(1)}, bf16[48,2048]{1,0:T(8,128)(2,1)S(1)}) custom-call(bf16[128,2048]{1,0:T(8,128)(2,1)S(1)} %attention_0.1.refs_0_.refs_8_.refs_3_, bf16[128,2048]{1,0:T(8,128)(2,1)S(1)} %attention_1.1.refs_1_.refs_9_.refs_4_, bf16[2048,1024]{1,0:T(8,128)(2,1)S(1)} %copy-done, bf16[64,4096]{1,0:T(8,128)(2,1)S(1)} %copy-done.4, ...), custom_call_target="tpu_custom_call" | custom-call | tf_op jit(solution)/shard_map/leave_and_pick/pallas_call | solution.py:74
  21.7 1.8 %leave_and_stay.1 = (bf16[128,1024]{1,0:T(8,128)(2,1)S(1)}, bf16[128,1024]{1,0:T(8,128)(2,1)S(1)}, bf16[128,1024]{1,0:T(8,128)(2,1)S(1)}) custom-call(bf16[128,2048]{1,0:T(8,128)(2,1)S(1)} %collective-permute-done.2.refs_0_.refs_6_, bf16[128,2048]{1,0:T(8,128)(2,1)S(1)} %collective-permute-done.6.refs_1_.refs_7_, bf16[2048,1024]{1,0:T(8,128)(2,1)S(1)} %copy-done, ...), custom_call_target="tpu_custom_call" | custom-call | tf_op jit(solution)/shard_map/leave_and_stay/pallas_call | solution.py:74
  23.5 1.4 %collective-permute-start.9 = (bf16[128,1024]{1,0:T(8,128)(2,1)S(1)}, bf16[128,1024]{1,0:T(8,128)(2,1)S(1)}, u32[]{:S(2)}, u32[]{:S(2)}) collective-permute-start(bf16[128,1024]{1,0:T(8,128)(2,1)S(1)} %get-tuple-element.162), channel_id=1, source_target_pairs={{0,1},{1,0},{2,3},{3,2},{4,5},{5,4},{6,7},{7,6},{8,9},{9,8},{10,11... | collective-permute-start | bytes 786440 | tf_op jit(solution)/shard_map/ppermute | solution.py:22
  25.0 5.2 %collective-permute-done.7.arrived_ref = bf16[128,1024]{1,0:T(8,128)(2,1)S(1)} collective-permute-done((bf16[128,1024]{1,0:T(8,128)(2,1)S(1)}, bf16[128,1024]{1,0:T(8,128)(2,1)S(1)}, u32[]{:S(2)}, u32[]{:S(2)}) %collective-permute-start.7) | collective-permute-done | bytes 262176 | tf_op jit(solution)/shard_map/ppermute | solution.py:22
  30.3 1.2 %collective-permute-start.12 = (bf16[48,2048]{1,0:T(8,128)(2,1)S(1)}, bf16[48,2048]{1,0:T(8,128)(2,1)S(1)}, u32[]{:S(2)}, u32[]{:S(2)}) collective-permute-start(bf16[48,2048]{1,0:T(8,128)(2,1)S(1)} %get-tuple-element.176.refs_0_), channel_id=1, source_target_pairs={{0,8},{4,12},{8,0},{12,4},{1,9},{5,13},{9,1},{13,5},{2,10},{6,14},... | collective-permute-start | bytes 589832 | tf_op jit(solution)/shard_map/ppermute | solution.py:22
  31.5 2.1 %collective-permute-start.8 = (bf16[64,1024]{1,0:T(8,128)(2,1)S(1)}, bf16[64,1024]{1,0:T(8,128)(2,1)S(1)}, u32[]{:S(2)}, u32[]{:S(2)}) collective-permute-start(bf16[64,1024]{1,0:T(8,128)(2,1)S(1)} %get-tuple-element.161), channel_id=1, source_target_pairs={{0,2},{1,3},{2,0},{3,1},{4,6},{5,7},{6,4},{7,5},{8,10},{9,11},{10,... | collective-permute-start | bytes 393224 | tf_op jit(solution)/shard_map/ppermute | solution.py:22
  33.6 2.4 %collective-permute-done.12.refs_2_ = bf16[48,2048]{1,0:T(8,128)(2,1)S(1)} collective-permute-done((bf16[48,2048]{1,0:T(8,128)(2,1)S(1)}, bf16[48,2048]{1,0:T(8,128)(2,1)S(1)}, u32[]{:S(2)}, u32[]{:S(2)}) %collective-permute-start.12) | collective-permute-done | bytes 196640 | tf_op jit(solution)/shard_map/ppermute | solution.py:22
  36.0 1.5 %collective-permute-done.9.arrived_ref = bf16[128,1024]{1,0:T(8,128)(2,1)S(1)} collective-permute-done((bf16[128,1024]{1,0:T(8,128)(2,1)S(1)}, bf16[128,1024]{1,0:T(8,128)(2,1)S(1)}, u32[]{:S(2)}, u32[]{:S(2)}) %collective-permute-start.9) | collective-permute-done | bytes 262176 | tf_op jit(solution)/shard_map/ppermute | solution.py:22
  37.6 2.5 %collective-permute-done.8.arrived_ref = bf16[64,1024]{1,0:T(8,128)(2,1)S(1)} collective-permute-done((bf16[64,1024]{1,0:T(8,128)(2,1)S(1)}, bf16[64,1024]{1,0:T(8,128)(2,1)S(1)}, u32[]{:S(2)}, u32[]{:S(2)}) %collective-permute-start.8) | collective-permute-done | bytes 131104 | tf_op jit(solution)/shard_map/ppermute | solution.py:22
  40.2 0.9 %collective-permute-start.24 = (bf16[128,2048]{1,0:T(8,128)(2,1)S(1)}, bf16[128,2048]{1,0:T(8,128)(2,1)S(1)}, u32[]{:S(2)}, u32[]{:S(2)}) collective-permute-start(bf16[128,2048]{1,0:T(8,128)(2,1)S(1)} %attention_1.1.refs_1_.refs_9_.refs_4_), channel_id=1, source_target_pairs={{0,8},{4,12},{8,0},{12,4},{1,9},{5,13},{9,1},{13,5},{2,10},{6,14},... | collective-permute-start | bytes 1572872 | tf_op jit(solution)/shard_map/ppermute | solution.py:22
  41.6 0.9 %collective-permute-done.14.refs_1_ = bf16[48,2048]{1,0:T(8,128)(2,1)S(1)} collective-permute-done((bf16[48,2048]{1,0:T(8,128)(2,1)S(1)}, bf16[48,2048]{1,0:T(8,128)(2,1)S(1)}, u32[]{:S(2)}, u32[]{:S(2)}) %collective-permute-start.14) | collective-permute-done | bytes 196640 | tf_op jit(solution)/shard_map/ppermute | solution.py:22
  42.8 0.8 routed_product.1
  43.6 1.7 %collective-permute-start.18 = (bf16[4,8,1024]{2,1,0:T(8,128)(2,1)S(1)}, bf16[4,8,1024]{2,1,0:T(8,128)(2,1)S(1)}, u32[]{:S(2)}, u32[]{:S(2)}) collective-permute-start(bf16[4,8,1024]{2,1,0:T(8,128)(2,1)S(1)} %get-tuple-element.193), channel_id=1, source_target_pairs={{0,1},{1,0},{2,3},{3,2},{4,5},{5,4},{6,7},{7,6},{8,9},{9,8},{10,11... | collective-permute-start | bytes 196616 | tf_op jit(solution)/shard_map/ppermute | solution.py:22
  45.4 1.2 %collective-permute-start.19 = (bf16[4,8,1024]{2,1,0:T(8,128)(2,1)S(1)}, bf16[4,8,1024]{2,1,0:T(8,128)(2,1)S(1)}, u32[]{:S(2)}, u32[]{:S(2)}) collective-permute-start(bf16[4,8,1024]{2,1,0:T(8,128)(2,1)S(1)} %get-tuple-element.194), channel_id=1, source_target_pairs={{0,2},{1,3},{2,0},{3,1},{4,6},{5,7},{6,4},{7,5},{8,10},{9,11},{10,... | collective-permute-start | bytes 196616 | tf_op jit(solution)/shard_map/ppermute | solution.py:22
  46.6 1.5 %collective-permute-start.20 = (bf16[4,8,1024]{2,1,0:T(8,128)(2,1)S(1)}, bf16[4,8,1024]{2,1,0:T(8,128)(2,1)S(1)}, u32[]{:S(2)}, u32[]{:S(2)}) collective-permute-start(bf16[4,8,1024]{2,1,0:T(8,128)(2,1)S(1)} %get-tuple-element.181), channel_id=1, source_target_pairs={{0,3},{1,2},{2,1},{3,0},{4,7},{5,6},{6,5},{7,4},{8,11},{9,10},{10,... | collective-permute-start | bytes 196616 | tf_op jit(solution)/shard_map/ppermute | solution.py:22
  48.1 1.3 %far.2 = (bf16[128,1024]{1,0:T(8,128)(2,1)S(1)}, bf16[128,1024]{1,0:T(8,128)(2,1)S(1)}) custom-call(bf16[128,2048]{1,0:T(8,128)(2,1)S(1)} %collective-permute-done.11.refs_0_.refs_3_, bf16[128,2048]{1,0:T(8,128)(2,1)S(1)} %collective-permute-done.13.refs_1_.refs_4_, bf16[2048,1024]{1,0:T(8,128)(2,1)S(1)} %copy-done, ...), custom_call_target="tpu_custom_call" | custom-call | tf_op jit(solution)/shard_map/far/pallas_call | solution.py:74
  49.4 4.0 %collective-permute-done.10.arrived_ref = bf16[64,1024]{1,0:T(8,128)(2,1)S(1)} collective-permute-done((bf16[64,1024]{1,0:T(8,128)(2,1)S(1)}, bf16[64,1024]{1,0:T(8,128)(2,1)S(1)}, u32[]{:S(2)}, u32[]{:S(2)}) %collective-permute-start.10) | collective-permute-done | bytes 131104 | tf_op jit(solution)/shard_map/ppermute | solution.py:22
  53.4 1.4 %collective-permute-done.19.refs_2_ = bf16[4,8,1024]{2,1,0:T(8,128)(2,1)S(1)} collective-permute-done((bf16[4,8,1024]{2,1,0:T(8,128)(2,1)S(1)}, bf16[4,8,1024]{2,1,0:T(8,128)(2,1)S(1)}, u32[]{:S(2)}, u32[]{:S(2)}) %collective-permute-start.19) | collective-permute-done | bytes 65568 | tf_op jit(solution)/shard_map/ppermute | solution.py:22
  55.3 1.1 %collective-permute-start.22 = (bf16[32,1024]{1,0:T(8,128)(2,1)S(1)}, bf16[32,1024]{1,0:T(8,128)(2,1)S(1)}, u32[]{:S(2)}, u32[]{:S(2)}) collective-permute-start(bf16[32,1024]{1,0:T(8,128)(2,1)S(1)} %routed_sum.1.refs_0_), channel_id=1, source_target_pairs={{0,8},{4,12},{8,0},{12,4},{1,9},{5,13},{9,1},{13,5},{2,10},{6,14},... | collective-permute-start | bytes 196616 | tf_op jit(solution)/shard_map/ppermute | solution.py:22
  56.8 1.9 %collective-permute-start.17 = (bf16[128,1024]{1,0:T(8,128)(2,1)S(1)}, bf16[128,1024]{1,0:T(8,128)(2,1)S(1)}, u32[]{:S(2)}, u32[]{:S(2)}) collective-permute-start(bf16[128,1024]{1,0:T(8,128)(2,1)S(1)} %get-tuple-element.191), channel_id=1, source_target_pairs={{0,1},{1,0},{2,3},{3,2},{4,5},{5,4},{6,7},{7,6},{8,9},{9,8},{10,11... | collective-permute-start | bytes 786440 | tf_op jit(solution)/shard_map/ppermute | solution.py:22
  58.7 1.2 %collective-permute-done.22.refs_2_ = bf16[32,1024]{1,0:T(8,128)(2,1)S(1)} collective-permute-done((bf16[32,1024]{1,0:T(8,128)(2,1)S(1)}, bf16[32,1024]{1,0:T(8,128)(2,1)S(1)}, u32[]{:S(2)}, u32[]{:S(2)}) %collective-permute-start.22) | collective-permute-done | bytes 65568 | tf_op jit(solution)/shard_map/ppermute | solution.py:22
  59.8 0.9 %collective-permute-done.23.refs_3_ = bf16[32,1024]{1,0:T(8,128)(2,1)S(1)} collective-permute-done((bf16[32,1024]{1,0:T(8,128)(2,1)S(1)}, bf16[32,1024]{1,0:T(8,128)(2,1)S(1)}, u32[]{:S(2)}, u32[]{:S(2)}) %collective-permute-start.23) | collective-permute-done | bytes 65568 | tf_op jit(solution)/shard_map/ppermute | solution.py:22
  60.8 1.5 %far.3 = (bf16[128,1024]{1,0:T(8,128)(2,1)S(1)}, bf16[128,1024]{1,0:T(8,128)(2,1)S(1)}) custom-call(bf16[128,2048]{1,0:T(8,128)(2,1)S(1)} %collective-permute-done.24.refs_0_.refs_3_, bf16[128,2048]{1,0:T(8,128)(2,1)S(1)} %collective-permute-done.25.refs_1_.refs_4_, bf16[2048,1024]{1,0:T(8,128)(2,1)S(1)} %copy-done, ...), custom_call_target="tpu_custom_call" | custom-call | tf_op jit(solution)/shard_map/far/pallas_call | solution.py:74
  62.3 1.9 %collective-permute-start.27 = (bf16[128,1024]{1,0:T(8,128)(2,1)S(1)}, bf16[128,1024]{1,0:T(8,128)(2,1)S(1)}, u32[]{:S(2)}, u32[]{:S(2)}) collective-permute-start(bf16[128,1024]{1,0:T(8,128)(2,1)S(1)} %get-tuple-element.220), channel_id=1, source_target_pairs={{0,1},{1,0},{2,3},{3,2},{4,5},{5,4},{6,7},{7,6},{8,9},{9,8},{10,11... | collective-permute-start | bytes 786440 | tf_op jit(solution)/shard_map/ppermute | solution.py:22
  64.2 1.1 %hidden_units.1.refs_0_ = bf16[32,384]{1,0:T(8,128)(2,1)S(1)} custom-call(bf16[32,1024]{1,0:T(8,128)(2,1)S(1)} %routed_sum.1.refs_0_, bf16[32,1024]{1,0:T(8,128)(2,1)S(1)} %collective-permute-done.21.refs_1_, bf16[32,1024]{1,0:T(8,128)(2,1)S(1)} %collective-permute-done.22.refs_2_, bf16[32,1024]{1,0:T(8,128)(2,1)S(1)} %collective-permute-done.23.refs_3_, ...), custom_call_target="tpu_custom_call" | custom-call | tf_op jit(solution)/shard_map/hidden_units/pallas_call | solution.py:415
  65.5 1.1 %collective-permute-start.29 = (bf16[32,384]{1,0:T(8,128)(2,1)S(1)}, bf16[32,384]{1,0:T(8,128)(2,1)S(1)}, u32[]{:S(2)}, u32[]{:S(2)}) collective-permute-start(bf16[32,384]{1,0:T(8,128)(2,1)S(1)} %hidden_units.1.refs_0_), channel_id=1, source_target_pairs={{0,8},{4,12},{8,0},{12,4},{1,9},{5,13},{9,1},{13,5},{2,10},{6,14},... | collective-permute-start | bytes 73736 | tf_op jit(solution)/shard_map/ppermute | solution.py:22
  67.3 0.7 collective-permute-start.26
  68.1 1.2 %collective-permute-done.29.refs_2_ = bf16[32,384]{1,0:T(8,128)(2,1)S(1)} collective-permute-done((bf16[32,384]{1,0:T(8,128)(2,1)S(1)}, bf16[32,384]{1,0:T(8,128)(2,1)S(1)}, u32[]{:S(2)}, u32[]{:S(2)}) %collective-permute-start.29) | collective-permute-done | bytes 24608 | tf_op jit(solution)/shard_map/ppermute | solution.py:22
  69.9 1.3 %down_product.1 = bf16[16,2,1024]{2,1,0:T(2,128)(2,1)} custom-call(bf16[32,384]{1,0:T(8,128)(2,1)S(1)} %hidden_units.1.refs_0_, bf16[32,384]{1,0:T(8,128)(2,1)S(1)} %collective-permute-done.28.refs_1_, bf16[32,384]{1,0:T(8,128)(2,1)S(1)} %collective-permute-done.29.refs_2_, bf16[32,384]{1,0:T(8,128)(2,1)S(1)} %collective-permute-done.30.refs_3_, ...), custom_call_target="tpu_custom_call" | custom-call | tf_op jit(solution)/shard_map/down_product/pallas_call | solution.py:446
  71.2 1.7 %collective-permute-done.27.arrived_ref = bf16[128,1024]{1,0:T(8,128)(2,1)S(1)} collective-permute-done((bf16[128,1024]{1,0:T(8,128)(2,1)S(1)}, bf16[128,1024]{1,0:T(8,128)(2,1)S(1)}, u32[]{:S(2)}, u32[]{:S(2)}) %collective-permute-start.27) | collective-permute-done | bytes 262176 | tf_op jit(solution)/shard_map/ppermute | solution.py:22
  72.9 0.8 collective-permute-start.33
  73.7 4.3 %all-to-all-start = ((bf16[16,2,1024]{2,1,0:T(2,128)(2,1)}), bf16[16,2,1024]{2,1,0:T(2,128)(2,1)S(1)}, u32[]{:S(2)}, u32[]{:S(2)}) async-start(bf16[16,2,1024]{2,1,0:T(2,128)(2,1)} %down_product.1), calls=%async_computation | async-start | bytes 131072 | tf_op jit(solution)/shard_map/all_to_all | solution.py:729
  78.0 2.3 %collective-permute-done.26.arrived_ref = bf16[64,1024]{1,0:T(8,128)(2,1)S(1)} collective-permute-done((bf16[64,1024]{1,0:T(8,128)(2,1)S(1)}, bf16[64,1024]{1,0:T(8,128)(2,1)S(1)}, u32[]{:S(2)}, u32[]{:S(2)}) %collective-permute-start.26) | collective-permute-done | bytes 131104 | tf_op jit(solution)/shard_map/ppermute | solution.py:22
  80.3 1.0 %collective-permute-start.31 = (bf16[32,1024]{1,0:T(8,128)(2,1)S(1)}, bf16[32,1024]{1,0:T(8,128)(2,1)S(1)}, u32[]{:S(2)}, u32[]{:S(2)}) collective-permute-start(bf16[32,1024]{1,0:T(8,128)(2,1)S(1)} %get-tuple-element.230), channel_id=1, source_target_pairs={{0,8},{4,12},{8,0},{12,4},{1,9},{5,13},{9,1},{13,5},{2,10},{6,14},... | collective-permute-start | bytes 196616 | tf_op jit(solution)/shard_map/ppermute | solution.py:22
  81.3 1.5 %collective-permute-done.33.arrived_ref = bf16[64,1024]{1,0:T(8,128)(2,1)S(1)} collective-permute-done((bf16[64,1024]{1,0:T(8,128)(2,1)S(1)}, bf16[64,1024]{1,0:T(8,128)(2,1)S(1)}, u32[]{:S(2)}, u32[]{:S(2)}) %collective-permute-start.33) | collective-permute-done | bytes 131104 | tf_op jit(solution)/shard_map/ppermute | solution.py:22
  82.9 1.0 %collective-permute-start.34 = (bf16[32,1024]{1,0:T(8,128)(2,1)S(1)}, bf16[32,1024]{1,0:T(8,128)(2,1)S(1)}, u32[]{:S(2)}, u32[]{:S(2)}) collective-permute-start(bf16[32,1024]{1,0:T(8,128)(2,1)S(1)} %get-tuple-element.236), channel_id=1, source_target_pairs={{0,8},{4,12},{8,0},{12,4},{1,9},{5,13},{9,1},{13,5},{2,10},{6,14},... | collective-permute-start | bytes 196616 | tf_op jit(solution)/shard_map/ppermute | solution.py:22
  84.6 1.3 %combine.1 = bf16[64,4096]{1,0:T(8,128)(2,1)} custom-call(s32[8,64]{1,0:T(8,128)S(1)} %bitcast.12, f32[8,64]{1,0:T(8,128)S(1)} %bitcast.13, bf16[16,2,1024]{2,1,0:T(2,128)(2,1)S(1)} %all-to-all-done.back_ref), custom_call_target="tpu_custom_call" | custom-call | tf_op jit(solution)/shard_map/combine/pallas_call | solution.py:742
  85.9 2.1 %collective-permute-done.34.refs_4_ = bf16[32,1024]{1,0:T(8,128)(2,1)S(1)} collective-permute-done((bf16[32,1024]{1,0:T(8,128)(2,1)S(1)}, bf16[32,1024]{1,0:T(8,128)(2,1)S(1)}, u32[]{:S(2)}, u32[]{:S(2)}) %collective-permute-start.34) | collective-permute-done | bytes 65568 | tf_op jit(solution)/shard_map/ppermute | solution.py:22
  88.6 0.9 %attended_rows.1 = bf16[64,4096]{1,0:T(8,128)(2,1)} custom-call(bf16[64,1024]{1,0:T(8,128)(2,1)S(1)} %add.16.refs_0_, bf16[64,1024]{1,0:T(8,128)(2,1)S(1)} %collective-permute-done.16.refs_1_, bf16[32,1024]{1,0:T(8,128)(2,1)S(1)} %collective-permute-done.31.refs_2_, bf16[32,1024]{1,0:T(8,128)(2,1)S(1)} %collective-permute-done.32.refs_3_, ...), custom_call_target="tpu_custom_call" | custom-call | tf_op jit(solution)/shard_map/attended_rows/pallas_call | solution.py:470
  (69 shorter events, 7.1 us)
Async XLA Ops:
  1.6 10.2 %collective-permute-start = (bf16[2,256,128]{2,1,0:T(8,128)(2,1)S(1)}, bf16[2,256,128]{2,1,0:T(8,128)(2,1)S(1)}, u32[]{:S(2)}, u32[]{:S(2)}) collective-permute-start(bf16[2,256,128]{2,1,0:T(8,128)(2,1)S(1)} %pad_maximum_fusion.kv_own_ref), channel_id=1, source_target_pairs={{0,8},{4,12},{8,0},{12,4},{1,9},{5,13},{9,1},{13,5},{2,10},{6,14},... | collective-permute-start | bytes 393224 | tf_op jit(solution)/shard_map/ppermute | solution.py:27
  4.6 7.2 %collective-permute-start.1 = (bf16[2,256,128]{2,1,0:T(8,128)(2,1)S(1)}, bf16[2,256,128]{2,1,0:T(8,128)(2,1)S(1)}, u32[]{:S(2)}, u32[]{:S(2)}) collective-permute-start(bf16[2,256,128]{2,1,0:T(8,128)(2,1)S(1)} %pad_maximum_fusion.kv_own_ref), channel_id=1, source_target_pairs={{0,4},{4,8},{8,12},{12,0},{1,5},{5,9},{9,13},{13,1},{2,6},{6,10},{... | collective-permute-start | bytes 393224 | tf_op jit(solution)/shard_map/ppermute | solution.py:27
  4.6 14.0 %copy-start = (bf16[2048,1024]{1,0:T(8,128)(2,1)S(1)}, bf16[2048,1024]{1,0:T(8,128)(2,1)}, u32[]{:S(2)}) copy-start(bf16[2048,1024]{1,0:T(8,128)(2,1)} %refs_5_.3) | copy-start | bytes 12582916
  4.6 14.0 %copy-start.4 = (bf16[64,4096]{1,0:T(8,128)(2,1)S(1)}, bf16[64,4096]{1,0:T(8,128)(2,1)}, u32[]{:S(2)}) copy-start(bf16[64,4096]{1,0:T(8,128)(2,1)} %refs_6_.3) | copy-start | bytes 1572868
  4.6 9.8 %collective-permute-start.3 = (s32[8,64]{1,0:T(8,128)}, s32[8,64]{1,0:T(8,128)S(1)}, u32[]{:S(2)}, u32[]{:S(2)}) collective-permute-start(s32[8,64]{1,0:T(8,128)} %bitcast.8), channel_id=1, source_target_pairs={{0,1},{1,0},{2,3},{3,2},{4,5},{5,4},{6,7},{7,6},{8,9},{9,8},{10,11... | collective-permute-start | bytes 6152 | tf_op jit(solution)/shard_map/ppermute | solution.py:22
  6.2 8.2 %collective-permute-start.4 = (s32[8,64]{1,0:T(8,128)}, s32[8,64]{1,0:T(8,128)S(1)}, u32[]{:S(2)}, u32[]{:S(2)}) collective-permute-start(s32[8,64]{1,0:T(8,128)} %bitcast.9), channel_id=1, source_target_pairs={{0,2},{1,3},{2,0},{3,1},{4,6},{5,7},{6,4},{7,5},{8,10},{9,11},{10,... | collective-permute-start | bytes 6152 | tf_op jit(solution)/shard_map/ppermute | solution.py:22
  8.8 5.6 %collective-permute-start.5 = (s32[8,64]{1,0:T(8,128)}, s32[8,64]{1,0:T(8,128)S(1)}, u32[]{:S(2)}, u32[]{:S(2)}) collective-permute-start(s32[8,64]{1,0:T(8,128)} %bitcast.10), channel_id=1, source_target_pairs={{0,3},{1,2},{2,1},{3,0},{4,7},{5,6},{6,5},{7,4},{8,11},{9,10},{10,... | collective-permute-start | bytes 6152 | tf_op jit(solution)/shard_map/ppermute | solution.py:22
  9.0 1.2 %copy-start.5 = (bf16[256,2048]{1,0:T(8,128)(2,1)S(1)}, bf16[256,2048]{1,0:T(8,128)(2,1)}, u32[]{:S(2)}) copy-start(bf16[256,2048]{1,0:T(8,128)(2,1)} %q_hbm) | copy-start | bytes 3145732
  10.2 0.7 copy-start.9
  10.8 7.7 %copy-start.7 = (s32[64,8]{0,1:T(8,128)S(1)}, s32[64,8]{0,1:T(8,128)}, u32[]{:S(2)}) copy-start(s32[64,8]{0,1:T(8,128)} %param.19) | copy-start | bytes 6148
  17.0 4.6 %collective-permute-start.6 = (bf16[128,2048]{1,0:T(8,128)(2,1)S(1)}, bf16[128,2048]{1,0:T(8,128)(2,1)S(1)}, u32[]{:S(2)}, u32[]{:S(2)}) collective-permute-start(bf16[128,2048]{1,0:T(8,128)(2,1)S(1)} %attention_1.1.refs_1_.refs_9_.refs_4_), channel_id=1, source_target_pairs={{0,4},{4,0},{8,12},{12,8},{1,5},{5,1},{9,13},{13,9},{2,6},{6,2},{1... | collective-permute-start | bytes 1572872 | tf_op jit(solution)/shard_map/ppermute | solution.py:22
  17.1 4.6 %collective-permute-start.2 = (bf16[128,2048]{1,0:T(8,128)(2,1)S(1)}, bf16[128,2048]{1,0:T(8,128)(2,1)S(1)}, u32[]{:S(2)}, u32[]{:S(2)}) collective-permute-start(bf16[128,2048]{1,0:T(8,128)(2,1)S(1)} %attention_0.1.refs_0_.refs_8_.refs_3_), channel_id=1, source_target_pairs={{0,4},{4,0},{8,12},{12,8},{1,5},{5,1},{9,13},{13,9},{2,6},{6,2},{1... | collective-permute-start | bytes 1572872 | tf_op jit(solution)/shard_map/ppermute | solution.py:22
  17.6 16.0 %collective-permute-start.11 = (bf16[128,2048]{1,0:T(8,128)(2,1)S(1)}, bf16[128,2048]{1,0:T(8,128)(2,1)S(1)}, u32[]{:S(2)}, u32[]{:S(2)}) collective-permute-start(bf16[128,2048]{1,0:T(8,128)(2,1)S(1)} %attention_0.1.refs_0_.refs_8_.refs_3_), channel_id=1, source_target_pairs={{0,8},{4,12},{8,0},{12,4},{1,9},{5,13},{9,1},{13,5},{2,10},{6,14},... | collective-permute-start | bytes 1572872 | tf_op jit(solution)/shard_map/ppermute | solution.py:22
  21.0 9.2 %collective-permute-start.7 = (bf16[128,1024]{1,0:T(8,128)(2,1)S(1)}, bf16[128,1024]{1,0:T(8,128)(2,1)S(1)}, u32[]{:S(2)}, u32[]{:S(2)}) collective-permute-start(bf16[128,1024]{1,0:T(8,128)(2,1)S(1)} %get-tuple-element.155), channel_id=1, source_target_pairs={{0,1},{1,0},{2,3},{3,2},{4,5},{5,4},{6,7},{7,6},{8,9},{9,8},{10,11... | collective-permute-start | bytes 786440 | tf_op jit(solution)/shard_map/ppermute | solution.py:22
  23.5 14.0 %collective-permute-start.9 = (bf16[128,1024]{1,0:T(8,128)(2,1)S(1)}, bf16[128,1024]{1,0:T(8,128)(2,1)S(1)}, u32[]{:S(2)}, u32[]{:S(2)}) collective-permute-start(bf16[128,1024]{1,0:T(8,128)(2,1)S(1)} %get-tuple-element.162), channel_id=1, source_target_pairs={{0,1},{1,0},{2,3},{3,2},{4,5},{5,4},{6,7},{7,6},{8,9},{9,8},{10,11... | collective-permute-start | bytes 786440 | tf_op jit(solution)/shard_map/ppermute | solution.py:22
  30.3 5.7 %collective-permute-start.12 = (bf16[48,2048]{1,0:T(8,128)(2,1)S(1)}, bf16[48,2048]{1,0:T(8,128)(2,1)S(1)}, u32[]{:S(2)}, u32[]{:S(2)}) collective-permute-start(bf16[48,2048]{1,0:T(8,128)(2,1)S(1)} %get-tuple-element.176.refs_0_), channel_id=1, source_target_pairs={{0,8},{4,12},{8,0},{12,4},{1,9},{5,13},{9,1},{13,5},{2,10},{6,14},... | collective-permute-start | bytes 589832 | tf_op jit(solution)/shard_map/ppermute | solution.py:22
  31.5 8.7 %collective-permute-start.8 = (bf16[64,1024]{1,0:T(8,128)(2,1)S(1)}, bf16[64,1024]{1,0:T(8,128)(2,1)S(1)}, u32[]{:S(2)}, u32[]{:S(2)}) collective-permute-start(bf16[64,1024]{1,0:T(8,128)(2,1)S(1)} %get-tuple-element.161), channel_id=1, source_target_pairs={{0,2},{1,3},{2,0},{3,1},{4,6},{5,7},{6,4},{7,5},{8,10},{9,11},{10,... | collective-permute-start | bytes 393224 | tf_op jit(solution)/shard_map/ppermute | solution.py:22
  37.5 9.1 %collective-permute-start.13 = (bf16[128,2048]{1,0:T(8,128)(2,1)S(1)}, bf16[128,2048]{1,0:T(8,128)(2,1)S(1)}, u32[]{:S(2)}, u32[]{:S(2)}) collective-permute-start(bf16[128,2048]{1,0:T(8,128)(2,1)S(1)} %collective-permute-done.11.refs_0_.refs_3_), channel_id=1, source_target_pairs={{0,4},{4,0},{8,12},{12,8},{1,5},{5,1},{9,13},{13,9},{2,6},{6,2},{1... | collective-permute-start | bytes 1572872 | tf_op jit(solution)/shard_map/ppermute | solution.py:22
  40.2 14.6 %collective-permute-start.24 = (bf16[128,2048]{1,0:T(8,128)(2,1)S(1)}, bf16[128,2048]{1,0:T(8,128)(2,1)S(1)}, u32[]{:S(2)}, u32[]{:S(2)}) collective-permute-start(bf16[128,2048]{1,0:T(8,128)(2,1)S(1)} %attention_1.1.refs_1_.refs_9_.refs_4_), channel_id=1, source_target_pairs={{0,8},{4,12},{8,0},{12,4},{1,9},{5,13},{9,1},{13,5},{2,10},{6,14},... | collective-permute-start | bytes 1572872 | tf_op jit(solution)/shard_map/ppermute | solution.py:22
  41.1 1.4 %collective-permute-start.14 = (bf16[48,2048]{1,0:T(8,128)(2,1)S(1)}, bf16[48,2048]{1,0:T(8,128)(2,1)S(1)}, u32[]{:S(2)}, u32[]{:S(2)}) collective-permute-start(bf16[48,2048]{1,0:T(8,128)(2,1)S(1)} %get-tuple-element.176.refs_0_), channel_id=1, source_target_pairs={{0,4},{4,0},{8,12},{12,8},{1,5},{5,1},{9,13},{13,9},{2,6},{6,2},{1... | collective-permute-start | bytes 589832 | tf_op jit(solution)/shard_map/ppermute | solution.py:22
  41.1 1.7 %collective-permute-start.15 = (bf16[48,2048]{1,0:T(8,128)(2,1)S(1)}, bf16[48,2048]{1,0:T(8,128)(2,1)S(1)}, u32[]{:S(2)}, u32[]{:S(2)}) collective-permute-start(bf16[48,2048]{1,0:T(8,128)(2,1)S(1)} %collective-permute-done.12.refs_2_), channel_id=1, source_target_pairs={{0,4},{4,0},{8,12},{12,8},{1,5},{5,1},{9,13},{13,9},{2,6},{6,2},{1... | collective-permute-start | bytes 589832 | tf_op jit(solution)/shard_map/ppermute | solution.py:22
  41.6 11.7 %collective-permute-start.10 = (bf16[64,1024]{1,0:T(8,128)(2,1)S(1)}, bf16[64,1024]{1,0:T(8,128)(2,1)S(1)}, u32[]{:S(2)}, u32[]{:S(2)}) collective-permute-start(bf16[64,1024]{1,0:T(8,128)(2,1)S(1)} %get-tuple-element.169), channel_id=1, source_target_pairs={{0,2},{1,3},{2,0},{3,1},{4,6},{5,7},{6,4},{7,5},{8,10},{9,11},{10,... | collective-permute-start | bytes 393224 | tf_op jit(solution)/shard_map/ppermute | solution.py:22
  43.6 9.7 %collective-permute-start.18 = (bf16[4,8,1024]{2,1,0:T(8,128)(2,1)S(1)}, bf16[4,8,1024]{2,1,0:T(8,128)(2,1)S(1)}, u32[]{:S(2)}, u32[]{:S(2)}) collective-permute-start(bf16[4,8,1024]{2,1,0:T(8,128)(2,1)S(1)} %get-tuple-element.193), channel_id=1, source_target_pairs={{0,1},{1,0},{2,3},{3,2},{4,5},{5,4},{6,7},{7,6},{8,9},{9,8},{10,11... | collective-permute-start | bytes 196616 | tf_op jit(solution)/shard_map/ppermute | solution.py:22
  45.4 9.3 %collective-permute-start.19 = (bf16[4,8,1024]{2,1,0:T(8,128)(2,1)S(1)}, bf16[4,8,1024]{2,1,0:T(8,128)(2,1)S(1)}, u32[]{:S(2)}, u32[]{:S(2)}) collective-permute-start(bf16[4,8,1024]{2,1,0:T(8,128)(2,1)S(1)} %get-tuple-element.194), channel_id=1, source_target_pairs={{0,2},{1,3},{2,0},{3,1},{4,6},{5,7},{6,4},{7,5},{8,10},{9,11},{10,... | collective-permute-start | bytes 196616 | tf_op jit(solution)/shard_map/ppermute | solution.py:22
  46.6 8.1 %collective-permute-start.20 = (bf16[4,8,1024]{2,1,0:T(8,128)(2,1)S(1)}, bf16[4,8,1024]{2,1,0:T(8,128)(2,1)S(1)}, u32[]{:S(2)}, u32[]{:S(2)}) collective-permute-start(bf16[4,8,1024]{2,1,0:T(8,128)(2,1)S(1)} %get-tuple-element.181), channel_id=1, source_target_pairs={{0,3},{1,2},{2,1},{3,0},{4,7},{5,6},{6,5},{7,4},{8,11},{9,10},{10,... | collective-permute-start | bytes 196616 | tf_op jit(solution)/shard_map/ppermute | solution.py:22
  54.8 6.0 %collective-permute-start.25 = (bf16[128,2048]{1,0:T(8,128)(2,1)S(1)}, bf16[128,2048]{1,0:T(8,128)(2,1)S(1)}, u32[]{:S(2)}, u32[]{:S(2)}) collective-permute-start(bf16[128,2048]{1,0:T(8,128)(2,1)S(1)} %collective-permute-done.24.refs_0_.refs_3_), channel_id=1, source_target_pairs={{0,4},{4,0},{8,12},{12,8},{1,5},{5,1},{9,13},{13,9},{2,6},{6,2},{1... | collective-permute-start | bytes 1572872 | tf_op jit(solution)/shard_map/ppermute | solution.py:22
  54.9 3.8 %collective-permute-start.21 = (bf16[32,1024]{1,0:T(8,128)(2,1)S(1)}, bf16[32,1024]{1,0:T(8,128)(2,1)S(1)}, u32[]{:S(2)}, u32[]{:S(2)}) collective-permute-start(bf16[32,1024]{1,0:T(8,128)(2,1)S(1)} %routed_sum.1.refs_0_), channel_id=1, source_target_pairs={{0,4},{4,0},{8,12},{12,8},{1,5},{5,1},{9,13},{13,9},{2,6},{6,2},{1... | collective-permute-start | bytes 196616 | tf_op jit(solution)/shard_map/ppermute | solution.py:22
  55.3 4.5 %collective-permute-start.22 = (bf16[32,1024]{1,0:T(8,128)(2,1)S(1)}, bf16[32,1024]{1,0:T(8,128)(2,1)S(1)}, u32[]{:S(2)}, u32[]{:S(2)}) collective-permute-start(bf16[32,1024]{1,0:T(8,128)(2,1)S(1)} %routed_sum.1.refs_0_), channel_id=1, source_target_pairs={{0,8},{4,12},{8,0},{12,4},{1,9},{5,13},{9,1},{13,5},{2,10},{6,14},... | collective-permute-start | bytes 196616 | tf_op jit(solution)/shard_map/ppermute | solution.py:22
  56.5 4.3 %collective-permute-start.23 = (bf16[32,1024]{1,0:T(8,128)(2,1)S(1)}, bf16[32,1024]{1,0:T(8,128)(2,1)S(1)}, u32[]{:S(2)}, u32[]{:S(2)}) collective-permute-start(bf16[32,1024]{1,0:T(8,128)(2,1)S(1)} %routed_sum.1.refs_0_), channel_id=1, source_target_pairs={{0,12},{4,8},{8,4},{12,0},{1,13},{5,9},{9,5},{13,1},{2,14},{6,10},... | collective-permute-start | bytes 196616 | tf_op jit(solution)/shard_map/ppermute | solution.py:22
  56.8 7.4 %copy-start.1 = (bf16[1,4096,384]{2,1,0:T(8,128)(2,1)S(1)}, bf16[1,4096,384]{2,1,0:T(8,128)(2,1)}, u32[]{:S(2)}) copy-start(bf16[1,4096,384]{2,1,0:T(8,128)(2,1)} %refs_5_.4) | copy-start | bytes 9437188
  56.8 7.4 %copy-start.2 = (bf16[1,4096,384]{2,1,0:T(8,128)(2,1)S(1)}, bf16[1,4096,384]{2,1,0:T(8,128)(2,1)}, u32[]{:S(2)}) copy-start(bf16[1,4096,384]{2,1,0:T(8,128)(2,1)} %refs_6_.2) | copy-start | bytes 9437188
  56.8 7.4 %copy-start.6 = (f32[4096]{0:T(1024)S(1)}, f32[4096]{0:T(1024)}, u32[]{:S(2)}) copy-start(f32[4096]{0:T(1024)} %param.18) | copy-start | bytes 49156
  56.8 10.5 %collective-permute-start.17 = (bf16[128,1024]{1,0:T(8,128)(2,1)S(1)}, bf16[128,1024]{1,0:T(8,128)(2,1)S(1)}, u32[]{:S(2)}, u32[]{:S(2)}) collective-permute-start(bf16[128,1024]{1,0:T(8,128)(2,1)S(1)} %get-tuple-element.191), channel_id=1, source_target_pairs={{0,1},{1,0},{2,3},{3,2},{4,5},{5,4},{6,7},{7,6},{8,9},{9,8},{10,11... | collective-permute-start | bytes 786440 | tf_op jit(solution)/shard_map/ppermute | solution.py:22
  62.3 10.6 %collective-permute-start.27 = (bf16[128,1024]{1,0:T(8,128)(2,1)S(1)}, bf16[128,1024]{1,0:T(8,128)(2,1)S(1)}, u32[]{:S(2)}, u32[]{:S(2)}) collective-permute-start(bf16[128,1024]{1,0:T(8,128)(2,1)S(1)} %get-tuple-element.220), channel_id=1, source_target_pairs={{0,1},{1,0},{2,3},{3,2},{4,5},{5,4},{6,7},{7,6},{8,9},{9,8},{10,11... | collective-permute-start | bytes 786440 | tf_op jit(solution)/shard_map/ppermute | solution.py:22
  64.2 5.7 %copy-start.3 = (bf16[1,1536,1024]{2,1,0:T(8,128)(2,1)S(1)}, bf16[1,1536,1024]{2,1,0:T(8,128)(2,1)}, u32[]{:S(2)}) copy-start(bf16[1,1536,1024]{2,1,0:T(8,128)(2,1)} %refs_4_.2) | copy-start | bytes 9437188
  65.3 19.3 %copy-start.8 = (f32[64,8]{0,1:T(8,128)S(1)}, f32[64,8]{0,1:T(8,128)}, u32[]{:S(2)}) copy-start(f32[64,8]{0,1:T(8,128)} %param.20) | copy-start | bytes 6148
  65.3 2.7 %collective-permute-start.28 = (bf16[32,384]{1,0:T(8,128)(2,1)S(1)}, bf16[32,384]{1,0:T(8,128)(2,1)S(1)}, u32[]{:S(2)}, u32[]{:S(2)}) collective-permute-start(bf16[32,384]{1,0:T(8,128)(2,1)S(1)} %hidden_units.1.refs_0_), channel_id=1, source_target_pairs={{0,4},{4,0},{8,12},{12,8},{1,5},{5,1},{9,13},{13,9},{2,6},{6,2},{1... | collective-permute-start | bytes 73736 | tf_op jit(solution)/shard_map/ppermute | solution.py:22
  65.5 3.8 %collective-permute-start.29 = (bf16[32,384]{1,0:T(8,128)(2,1)S(1)}, bf16[32,384]{1,0:T(8,128)(2,1)S(1)}, u32[]{:S(2)}, u32[]{:S(2)}) collective-permute-start(bf16[32,384]{1,0:T(8,128)(2,1)S(1)} %hidden_units.1.refs_0_), channel_id=1, source_target_pairs={{0,8},{4,12},{8,0},{12,4},{1,9},{5,13},{9,1},{13,5},{2,10},{6,14},... | collective-permute-start | bytes 73736 | tf_op jit(solution)/shard_map/ppermute | solution.py:22
  66.6 3.3 %collective-permute-start.30 = (bf16[32,384]{1,0:T(8,128)(2,1)S(1)}, bf16[32,384]{1,0:T(8,128)(2,1)S(1)}, u32[]{:S(2)}, u32[]{:S(2)}) collective-permute-start(bf16[32,384]{1,0:T(8,128)(2,1)S(1)} %hidden_units.1.refs_0_), channel_id=1, source_target_pairs={{0,12},{4,8},{8,4},{12,0},{1,13},{5,9},{9,5},{13,1},{2,14},{6,10},... | collective-permute-start | bytes 73736 | tf_op jit(solution)/shard_map/ppermute | solution.py:22
  67.3 12.9 %collective-permute-start.26 = (bf16[64,1024]{1,0:T(8,128)(2,1)S(1)}, bf16[64,1024]{1,0:T(8,128)(2,1)S(1)}, u32[]{:S(2)}, u32[]{:S(2)}) collective-permute-start(bf16[64,1024]{1,0:T(8,128)(2,1)S(1)} %get-tuple-element.219), channel_id=1, source_target_pairs={{0,2},{1,3},{2,0},{3,1},{4,6},{5,7},{6,4},{7,5},{8,10},{9,11},{10,... | collective-permute-start | bytes 393224 | tf_op jit(solution)/shard_map/ppermute | solution.py:22
  72.9 9.9 %collective-permute-start.33 = (bf16[64,1024]{1,0:T(8,128)(2,1)S(1)}, bf16[64,1024]{1,0:T(8,128)(2,1)S(1)}, u32[]{:S(2)}, u32[]{:S(2)}) collective-permute-start(bf16[64,1024]{1,0:T(8,128)(2,1)S(1)} %get-tuple-element.233), channel_id=1, source_target_pairs={{0,2},{1,3},{2,0},{3,1},{4,6},{5,7},{6,4},{7,5},{8,10},{9,11},{10,... | collective-permute-start | bytes 393224 | tf_op jit(solution)/shard_map/ppermute | solution.py:22
  73.7 12.2 %collective-permute-start.16 = (bf16[64,1024]{1,0:T(8,128)(2,1)S(1)}, bf16[64,1024]{1,0:T(8,128)(2,1)S(1)}, u32[]{:S(2)}, u32[]{:S(2)}) collective-permute-start(bf16[64,1024]{1,0:T(8,128)(2,1)S(1)} %add.17), channel_id=1, source_target_pairs={{0,4},{4,0},{8,12},{12,8},{1,5},{5,1},{9,13},{13,9},{2,6},{6,2},{1... | collective-permute-start | bytes 393224 | tf_op jit(solution)/shard_map/ppermute | solution.py:22
  73.7 10.9 %all-to-all-start = ((bf16[16,2,1024]{2,1,0:T(2,128)(2,1)}), bf16[16,2,1024]{2,1,0:T(2,128)(2,1)S(1)}, u32[]{:S(2)}, u32[]{:S(2)}) async-start(bf16[16,2,1024]{2,1,0:T(2,128)(2,1)} %down_product.1), calls=%async_computation | async-start | bytes 131072 | tf_op jit(solution)/shard_map/all_to_all | solution.py:729
  80.3 5.6 %collective-permute-start.31 = (bf16[32,1024]{1,0:T(8,128)(2,1)S(1)}, bf16[32,1024]{1,0:T(8,128)(2,1)S(1)}, u32[]{:S(2)}, u32[]{:S(2)}) collective-permute-start(bf16[32,1024]{1,0:T(8,128)(2,1)S(1)} %get-tuple-element.230), channel_id=1, source_target_pairs={{0,8},{4,12},{8,0},{12,4},{1,9},{5,13},{9,1},{13,5},{2,10},{6,14},... | collective-permute-start | bytes 196616 | tf_op jit(solution)/shard_map/ppermute | solution.py:22
  81.3 4.6 %collective-permute-start.32 = (bf16[32,1024]{1,0:T(8,128)(2,1)S(1)}, bf16[32,1024]{1,0:T(8,128)(2,1)S(1)}, u32[]{:S(2)}, u32[]{:S(2)}) collective-permute-start(bf16[32,1024]{1,0:T(8,128)(2,1)S(1)} %get-tuple-element.231), channel_id=1, source_target_pairs={{0,12},{4,8},{8,4},{12,0},{1,13},{5,9},{9,5},{13,1},{2,14},{6,10},... | collective-permute-start | bytes 196616 | tf_op jit(solution)/shard_map/ppermute | solution.py:22
  82.9 5.1 %collective-permute-start.34 = (bf16[32,1024]{1,0:T(8,128)(2,1)S(1)}, bf16[32,1024]{1,0:T(8,128)(2,1)S(1)}, u32[]{:S(2)}, u32[]{:S(2)}) collective-permute-start(bf16[32,1024]{1,0:T(8,128)(2,1)S(1)} %get-tuple-element.236), channel_id=1, source_target_pairs={{0,8},{4,12},{8,0},{12,4},{1,9},{5,13},{9,1},{13,5},{2,10},{6,14},... | collective-permute-start | bytes 196616 | tf_op jit(solution)/shard_map/ppermute | solution.py:22
  83.9 4.7 %collective-permute-start.35 = (bf16[32,1024]{1,0:T(8,128)(2,1)S(1)}, bf16[32,1024]{1,0:T(8,128)(2,1)S(1)}, u32[]{:S(2)}, u32[]{:S(2)}) collective-permute-start(bf16[32,1024]{1,0:T(8,128)(2,1)S(1)} %get-tuple-element.237), channel_id=1, source_target_pairs={{0,12},{4,8},{8,4},{12,0},{1,13},{5,9},{9,5},{13,1},{2,14},{6,10},... | collective-permute-start | bytes 196616 | tf_op jit(solution)/shard_map/ppermute | solution.py:22

commit v6 on v5

--- a/solution.py
+++ b/solution.py
@@ -682,9 +682,8 @@
     mine = tuple(heads_out)
     near = tuple(near)
     far[0].hops_to(2)
-    (own_send,), (routed,) = sequence.steps(
-        "leave_and_pick", leaving(mine), pick(residual_in, routes_all, heads_out, sub)
-    )
+    ((own_send,),) = sequence.steps("leave", leaving(mine))
+    ((routed,),) = sequence.steps("pick", pick(residual_in, routes_all, heads_out, sub))
     routed_all = Gather(sequence, routed)
     (near_send,), (own_keep,), (near_keep,) = sequence.steps(
         "leave_and_stay", leaving(near), staying(mine), staying(near)

time: 89.8 us -> 88.1 us (0.981)
  waiting for transfers between devices: 31 us -> 29.5 us
    ppermute x34, waiting for transfers between devices: 30.3 us -> 28.8 us  [swap(): return lax.ppermute(x, axis, [(i, i ^ mask) for i in range(count)])]
    pallas_call x5 -> x6, Pallas kernels: 7.75 us -> 7.9 us  [together(): pl.pallas_call(kernel, out_shape=shapes, in_specs=whole_vmem(total), out_...]
  transfers between devices with their start and end apart: 37 -> 37, of which waited for: 18 -> 18; matrix products, arithmetic and copies ran while one was open for 0% -> 0% of each run, Pallas kernels for 17% -> 18%
where the time goes in v6:
time: 88.1 us; the launch traced here: 87.8 us
  starting transfers between devices  35.6 us (40%)
  waiting for transfers between devices  29.5 us (33%)
  Pallas kernels  19 us (22%)
  local copies, waits for them, and re-layouts  2.8 us (3%)
  between operations  0.93 us (1%)
    ppermute x34, waiting for transfers between devices, swap(): return lax.ppermute(x, axis, [(i, i ^ mask) for i in range(count)])  28.8 us
    ppermute x34, starting transfers between devices, swap(): return lax.ppermute(x, axis, [(i, i ^ mask) for i in range(count)])  28.3 us
    pallas_call x6, Pallas kernels, together(): pl.pallas_call(kernel, out_shape=shapes, in_specs=whole_vmem(total), out_...  7.9 us
    pallas_call x2, Pallas kernels, attention(): pl.pallas_call(functools.partial(attention_kernel, heads=width // HD, hom...  5.26 us
    all_to_all x1, starting transfers between devices, shards(): lax.all_to_all(produced, ('ctx', 'exp'), split_axis=0, concat_axis=0, til...  4.29 us
    ppermute x2, starting transfers between devices, shift(): return lax.ppermute(x, axis, [(i, (i + by) % count) for i in range(count)])  3.01 us
    unnamed x20, local copies, waits for them, and re-layouts  1.92 us
  transfers between devices with their start and end apart: 37, of which 18 were waited for; matrix products, arithmetic and copies ran while one was open for 0% of the time, Pallas kernels for 18%

profile of v6, /device:TPU:0, one launch (start us, length us, event | category | flops | bytes accessed | tf_op | source)
XLA Modules:
  0.0 87.8 jit_solution(8648746932940943167)
XLA Ops:
  0.6 0.9 %dynamic-slice_bitcast_fusion = (bf16[1,256,128]{2,1,0:T(8,128)(2,1)S(1)}, bf16[1,256,128]{2,1,0:T(8,128)(2,1)S(1)}) fusion(bf16[256,512]{1,0:T(8,128)(2,1)} %param.14, s32[]{:T(128)S(6)} %select_n.10, bf16[256,512]{1,0:T(8,128)(2,1)} %param.13), kind=kLoop, calls=%fused_computation.1 | loop fusion | bytes 262148 | tf_op jit(solution)/shard_map/stack | solution.py:649
  1.6 3.0 %collective-permute-start = (bf16[2,256,128]{2,1,0:T(8,128)(2,1)S(1)}, bf16[2,256,128]{2,1,0:T(8,128)(2,1)S(1)}, u32[]{:S(2)}, u32[]{:S(2)}) collective-permute-start(bf16[2,256,128]{2,1,0:T(8,128)(2,1)S(1)} %pad_maximum_fusion.kv_own_ref), channel_id=1, source_target_pairs={{0,8},{4,12},{8,0},{12,4},{1,9},{5,13},{9,1},{13,5},{2,10},{6,14},... | collective-permute-start | bytes 393224 | tf_op jit(solution)/shard_map/ppermute | solution.py:27
  4.6 1.6 %collective-permute-start.3 = (s32[8,64]{1,0:T(8,128)}, s32[8,64]{1,0:T(8,128)S(1)}, u32[]{:S(2)}, u32[]{:S(2)}) collective-permute-start(s32[8,64]{1,0:T(8,128)} %bitcast.8), channel_id=1, source_target_pairs={{0,1},{1,0},{2,3},{3,2},{4,5},{5,4},{6,7},{7,6},{8,9},{9,8},{10,11... | collective-permute-start | bytes 6152 | tf_op jit(solution)/shard_map/ppermute | solution.py:22
  6.2 2.6 %collective-permute-start.4 = (s32[8,64]{1,0:T(8,128)}, s32[8,64]{1,0:T(8,128)S(1)}, u32[]{:S(2)}, u32[]{:S(2)}) collective-permute-start(s32[8,64]{1,0:T(8,128)} %bitcast.9), channel_id=1, source_target_pairs={{0,2},{1,3},{2,0},{3,1},{4,6},{5,7},{6,4},{7,5},{8,10},{9,11},{10,... | collective-permute-start | bytes 6152 | tf_op jit(solution)/shard_map/ppermute | solution.py:22
  9.0 1.2 %copy-done.5 = bf16[256,2048]{1,0:T(8,128)(2,1)S(1)} copy-done((bf16[256,2048]{1,0:T(8,128)(2,1)S(1)}, bf16[256,2048]{1,0:T(8,128)(2,1)}, u32[]{:S(2)}) %copy-start.5) | copy-done | bytes 1048600
  10.8 0.9 ready.1
  11.7 2.6 %attention_0.1.refs_0_.refs_5_.refs_3_ = bf16[128,2048]{1,0:T(8,128)(2,1)S(1)} custom-call(bf16[256,2048]{1,0:T(8,128)(2,1)S(1)} %get-tuple-element.131.q_ref, f32[256,640]{1,0:T(8,128)S(1)} %get-tuple-element.124.bias_ref, bf16[2,256,128]{2,1,0:T(8,128)(2,1)S(1)} %collective-permute-done.kv_far_ref, ...), custom_call_target="tpu_custom_call" | custom-call | tf_op jit(solution)/shard_map/attention_0/pallas_call | solution.py:201
  14.4 2.6 %attention_1.1.refs_1_.refs_6_.refs_4_ = bf16[128,2048]{1,0:T(8,128)(2,1)S(1)} custom-call(bf16[256,2048]{1,0:T(8,128)(2,1)S(1)} %get-tuple-element.131.q_ref, f32[256,640]{1,0:T(8,128)S(1)} %get-tuple-element.124.bias_ref, bf16[2,256,128]{2,1,0:T(8,128)(2,1)S(1)} %collective-permute-done.kv_far_ref, ...), custom_call_target="tpu_custom_call" | custom-call | tf_op jit(solution)/shard_map/attention_1/pallas_call | solution.py:201
  17.6 0.9 %collective-permute-start.11 = (bf16[128,2048]{1,0:T(8,128)(2,1)S(1)}, bf16[128,2048]{1,0:T(8,128)(2,1)S(1)}, u32[]{:S(2)}, u32[]{:S(2)}) collective-permute-start(bf16[128,2048]{1,0:T(8,128)(2,1)S(1)} %attention_0.1.refs_0_.refs_5_.refs_3_), channel_id=1, source_target_pairs={{0,8},{4,12},{8,0},{12,4},{1,9},{5,13},{9,1},{13,5},{2,10},{6,14},... | collective-permute-start | bytes 1572872 | tf_op jit(solution)/shard_map/ppermute | solution.py:22
  18.6 0.7 leave.1
  20.0 1.8 %pick.1.refs_0_ = bf16[48,2048]{1,0:T(8,128)(2,1)S(1)} custom-call(bf16[64,4096]{1,0:T(8,128)(2,1)S(1)} %copy-done.4, s32[8,64]{1,0:T(8,128)S(1)} %bitcast.11, s32[8,64]{1,0:T(8,128)S(1)} %collective-permute-done.3.refs_2_, s32[8,64]{1,0:T(8,128)S(1)} %collective-permute-done.4.refs_3_, s32[8,64]{1,0:T(8,128)S(1)} %collective-permute-done.5.refs_4_, ...), custom_call_target="tpu_custom_call" | custom-call | tf_op jit(solution)/shard_map/pick/pallas_call | solution.py:74
  21.8 1.8 %leave_and_stay.1 = (bf16[128,1024]{1,0:T(8,128)(2,1)S(1)}, bf16[128,1024]{1,0:T(8,128)(2,1)S(1)}, bf16[128,1024]{1,0:T(8,128)(2,1)S(1)}) custom-call(bf16[128,2048]{1,0:T(8,128)(2,1)S(1)} %collective-permute-done.2.refs_0_.refs_6_, bf16[128,2048]{1,0:T(8,128)(2,1)S(1)} %collective-permute-done.6.refs_1_.refs_7_, bf16[2048,1024]{1,0:T(8,128)(2,1)S(1)} %copy-done, ...), custom_call_target="tpu_custom_call" | custom-call | tf_op jit(solution)/shard_map/leave_and_stay/pallas_call | solution.py:74
  23.7 1.5 %collective-permute-start.9 = (bf16[128,1024]{1,0:T(8,128)(2,1)S(1)}, bf16[128,1024]{1,0:T(8,128)(2,1)S(1)}, u32[]{:S(2)}, u32[]{:S(2)}) collective-permute-start(bf16[128,1024]{1,0:T(8,128)(2,1)S(1)} %get-tuple-element.158), channel_id=1, source_target_pairs={{0,1},{1,0},{2,3},{3,2},{4,5},{5,4},{6,7},{7,6},{8,9},{9,8},{10,11... | collective-permute-start | bytes 786440 | tf_op jit(solution)/shard_map/ppermute | solution.py:22
  25.1 3.4 %collective-permute-done.7.arrived_ref = bf16[128,1024]{1,0:T(8,128)(2,1)S(1)} collective-permute-done((bf16[128,1024]{1,0:T(8,128)(2,1)S(1)}, bf16[128,1024]{1,0:T(8,128)(2,1)S(1)}, u32[]{:S(2)}, u32[]{:S(2)}) %collective-permute-start.7) | collective-permute-done | bytes 262176 | tf_op jit(solution)/shard_map/ppermute | solution.py:22
  28.6 1.2 %collective-permute-start.12 = (bf16[48,2048]{1,0:T(8,128)(2,1)S(1)}, bf16[48,2048]{1,0:T(8,128)(2,1)S(1)}, u32[]{:S(2)}, u32[]{:S(2)}) collective-permute-start(bf16[48,2048]{1,0:T(8,128)(2,1)S(1)} %pick.1.refs_0_), channel_id=1, source_target_pairs={{0,8},{4,12},{8,0},{12,4},{1,9},{5,13},{9,1},{13,5},{2,10},{6,14},... | collective-permute-start | bytes 589832 | tf_op jit(solution)/shard_map/ppermute | solution.py:22
  29.8 1.7 %collective-permute-start.8 = (bf16[64,1024]{1,0:T(8,128)(2,1)S(1)}, bf16[64,1024]{1,0:T(8,128)(2,1)S(1)}, u32[]{:S(2)}, u32[]{:S(2)}) collective-permute-start(bf16[64,1024]{1,0:T(8,128)(2,1)S(1)} %get-tuple-element.157), channel_id=1, source_target_pairs={{0,2},{1,3},{2,0},{3,1},{4,6},{5,7},{6,4},{7,5},{8,10},{9,11},{10,... | collective-permute-start | bytes 393224 | tf_op jit(solution)/shard_map/ppermute | solution.py:22
  31.5 0.9 %collective-permute-done.11.refs_0_.refs_3_ = bf16[128,2048]{1,0:T(8,128)(2,1)S(1)} collective-permute-done((bf16[128,2048]{1,0:T(8,128)(2,1)S(1)}, bf16[128,2048]{1,0:T(8,128)(2,1)S(1)}, u32[]{:S(2)}, u32[]{:S(2)}) %collective-permute-start.11) | collective-permute-done | bytes 524320 | tf_op jit(solution)/shard_map/ppermute | solution.py:22
  32.4 3.3 %collective-permute-done.12.refs_2_ = bf16[48,2048]{1,0:T(8,128)(2,1)S(1)} collective-permute-done((bf16[48,2048]{1,0:T(8,128)(2,1)S(1)}, bf16[48,2048]{1,0:T(8,128)(2,1)S(1)}, u32[]{:S(2)}, u32[]{:S(2)}) %collective-permute-start.12) | collective-permute-done | bytes 196640 | tf_op jit(solution)/shard_map/ppermute | solution.py:22
  35.9 2.6 %collective-permute-done.8.arrived_ref = bf16[64,1024]{1,0:T(8,128)(2,1)S(1)} collective-permute-done((bf16[64,1024]{1,0:T(8,128)(2,1)S(1)}, bf16[64,1024]{1,0:T(8,128)(2,1)S(1)}, u32[]{:S(2)}, u32[]{:S(2)}) %collective-permute-start.8) | collective-permute-done | bytes 131104 | tf_op jit(solution)/shard_map/ppermute | solution.py:22
  38.5 0.8 collective-permute-start.24
  39.8 0.9 %collective-permute-done.14.refs_1_ = bf16[48,2048]{1,0:T(8,128)(2,1)S(1)} collective-permute-done((bf16[48,2048]{1,0:T(8,128)(2,1)S(1)}, bf16[48,2048]{1,0:T(8,128)(2,1)S(1)}, u32[]{:S(2)}, u32[]{:S(2)}) %collective-permute-start.14) | collective-permute-done | bytes 196640 | tf_op jit(solution)/shard_map/ppermute | solution.py:22
  41.0 0.8 routed_product.1
  41.8 1.8 %collective-permute-start.18 = (bf16[4,8,1024]{2,1,0:T(8,128)(2,1)S(1)}, bf16[4,8,1024]{2,1,0:T(8,128)(2,1)S(1)}, u32[]{:S(2)}, u32[]{:S(2)}) collective-permute-start(bf16[4,8,1024]{2,1,0:T(8,128)(2,1)S(1)} %get-tuple-element.189), channel_id=1, source_target_pairs={{0,1},{1,0},{2,3},{3,2},{4,5},{5,4},{6,7},{7,6},{8,9},{9,8},{10,11... | collective-permute-start | bytes 196616 | tf_op jit(solution)/shard_map/ppermute | solution.py:22
  43.6 1.2 %collective-permute-start.19 = (bf16[4,8,1024]{2,1,0:T(8,128)(2,1)S(1)}, bf16[4,8,1024]{2,1,0:T(8,128)(2,1)S(1)}, u32[]{:S(2)}, u32[]{:S(2)}) collective-permute-start(bf16[4,8,1024]{2,1,0:T(8,128)(2,1)S(1)} %get-tuple-element.190), channel_id=1, source_target_pairs={{0,2},{1,3},{2,0},{3,1},{4,6},{5,7},{6,4},{7,5},{8,10},{9,11},{10,... | collective-permute-start | bytes 196616 | tf_op jit(solution)/shard_map/ppermute | solution.py:22
  44.9 1.4 %collective-permute-start.20 = (bf16[4,8,1024]{2,1,0:T(8,128)(2,1)S(1)}, bf16[4,8,1024]{2,1,0:T(8,128)(2,1)S(1)}, u32[]{:S(2)}, u32[]{:S(2)}) collective-permute-start(bf16[4,8,1024]{2,1,0:T(8,128)(2,1)S(1)} %get-tuple-element.177), channel_id=1, source_target_pairs={{0,3},{1,2},{2,1},{3,0},{4,7},{5,6},{6,5},{7,4},{8,11},{9,10},{10,... | collective-permute-start | bytes 196616 | tf_op jit(solution)/shard_map/ppermute | solution.py:22
  46.3 1.3 %far.2 = (bf16[128,1024]{1,0:T(8,128)(2,1)S(1)}, bf16[128,1024]{1,0:T(8,128)(2,1)S(1)}) custom-call(bf16[128,2048]{1,0:T(8,128)(2,1)S(1)} %collective-permute-done.11.refs_0_.refs_3_, bf16[128,2048]{1,0:T(8,128)(2,1)S(1)} %collective-permute-done.13.refs_1_.refs_4_, bf16[2048,1024]{1,0:T(8,128)(2,1)S(1)} %copy-done, ...), custom_call_target="tpu_custom_call" | custom-call | tf_op jit(solution)/shard_map/far/pallas_call | solution.py:74
  47.5 4.0 %collective-permute-done.10.arrived_ref = bf16[64,1024]{1,0:T(8,128)(2,1)S(1)} collective-permute-done((bf16[64,1024]{1,0:T(8,128)(2,1)S(1)}, bf16[64,1024]{1,0:T(8,128)(2,1)S(1)}, u32[]{:S(2)}, u32[]{:S(2)}) %collective-permute-start.10) | collective-permute-done | bytes 131104 | tf_op jit(solution)/shard_map/ppermute | solution.py:22
  51.6 1.4 %collective-permute-done.19.refs_2_ = bf16[4,8,1024]{2,1,0:T(8,128)(2,1)S(1)} collective-permute-done((bf16[4,8,1024]{2,1,0:T(8,128)(2,1)S(1)}, bf16[4,8,1024]{2,1,0:T(8,128)(2,1)S(1)}, u32[]{:S(2)}, u32[]{:S(2)}) %collective-permute-start.19) | collective-permute-done | bytes 65568 | tf_op jit(solution)/shard_map/ppermute | solution.py:22
  53.6 1.1 %collective-permute-start.22 = (bf16[32,1024]{1,0:T(8,128)(2,1)S(1)}, bf16[32,1024]{1,0:T(8,128)(2,1)S(1)}, u32[]{:S(2)}, u32[]{:S(2)}) collective-permute-start(bf16[32,1024]{1,0:T(8,128)(2,1)S(1)} %routed_sum.1.refs_0_), channel_id=1, source_target_pairs={{0,8},{4,12},{8,0},{12,4},{1,9},{5,13},{9,1},{13,5},{2,10},{6,14},... | collective-permute-start | bytes 196616 | tf_op jit(solution)/shard_map/ppermute | solution.py:22
  55.0 1.9 %collective-permute-start.17 = (bf16[128,1024]{1,0:T(8,128)(2,1)S(1)}, bf16[128,1024]{1,0:T(8,128)(2,1)S(1)}, u32[]{:S(2)}, u32[]{:S(2)}) collective-permute-start(bf16[128,1024]{1,0:T(8,128)(2,1)S(1)} %get-tuple-element.187), channel_id=1, source_target_pairs={{0,1},{1,0},{2,3},{3,2},{4,5},{5,4},{6,7},{7,6},{8,9},{9,8},{10,11... | collective-permute-start | bytes 786440 | tf_op jit(solution)/shard_map/ppermute | solution.py:22
  56.9 1.2 %collective-permute-done.22.refs_2_ = bf16[32,1024]{1,0:T(8,128)(2,1)S(1)} collective-permute-done((bf16[32,1024]{1,0:T(8,128)(2,1)S(1)}, bf16[32,1024]{1,0:T(8,128)(2,1)S(1)}, u32[]{:S(2)}, u32[]{:S(2)}) %collective-permute-start.22) | collective-permute-done | bytes 65568 | tf_op jit(solution)/shard_map/ppermute | solution.py:22
  58.1 1.0 %collective-permute-done.23.refs_3_ = bf16[32,1024]{1,0:T(8,128)(2,1)S(1)} collective-permute-done((bf16[32,1024]{1,0:T(8,128)(2,1)S(1)}, bf16[32,1024]{1,0:T(8,128)(2,1)S(1)}, u32[]{:S(2)}, u32[]{:S(2)}) %collective-permute-start.23) | collective-permute-done | bytes 65568 | tf_op jit(solution)/shard_map/ppermute | solution.py:22
  59.1 1.5 %far.3 = (bf16[128,1024]{1,0:T(8,128)(2,1)S(1)}, bf16[128,1024]{1,0:T(8,128)(2,1)S(1)}) custom-call(bf16[128,2048]{1,0:T(8,128)(2,1)S(1)} %collective-permute-done.24.refs_0_.refs_3_, bf16[128,2048]{1,0:T(8,128)(2,1)S(1)} %collective-permute-done.25.refs_1_.refs_4_, bf16[2048,1024]{1,0:T(8,128)(2,1)S(1)} %copy-done, ...), custom_call_target="tpu_custom_call" | custom-call | tf_op jit(solution)/shard_map/far/pallas_call | solution.py:74
  60.6 1.9 %collective-permute-start.27 = (bf16[128,1024]{1,0:T(8,128)(2,1)S(1)}, bf16[128,1024]{1,0:T(8,128)(2,1)S(1)}, u32[]{:S(2)}, u32[]{:S(2)}) collective-permute-start(bf16[128,1024]{1,0:T(8,128)(2,1)S(1)} %get-tuple-element.216), channel_id=1, source_target_pairs={{0,1},{1,0},{2,3},{3,2},{4,5},{5,4},{6,7},{7,6},{8,9},{9,8},{10,11... | collective-permute-start | bytes 786440 | tf_op jit(solution)/shard_map/ppermute | solution.py:22
  62.5 1.1 %hidden_units.1.refs_0_ = bf16[32,384]{1,0:T(8,128)(2,1)S(1)} custom-call(bf16[32,1024]{1,0:T(8,128)(2,1)S(1)} %routed_sum.1.refs_0_, bf16[32,1024]{1,0:T(8,128)(2,1)S(1)} %collective-permute-done.21.refs_1_, bf16[32,1024]{1,0:T(8,128)(2,1)S(1)} %collective-permute-done.22.refs_2_, bf16[32,1024]{1,0:T(8,128)(2,1)S(1)} %collective-permute-done.23.refs_3_, ...), custom_call_target="tpu_custom_call" | custom-call | tf_op jit(solution)/shard_map/hidden_units/pallas_call | solution.py:415
  63.7 1.1 %collective-permute-start.29 = (bf16[32,384]{1,0:T(8,128)(2,1)S(1)}, bf16[32,384]{1,0:T(8,128)(2,1)S(1)}, u32[]{:S(2)}, u32[]{:S(2)}) collective-permute-start(bf16[32,384]{1,0:T(8,128)(2,1)S(1)} %hidden_units.1.refs_0_), channel_id=1, source_target_pairs={{0,8},{4,12},{8,0},{12,4},{1,9},{5,13},{9,1},{13,5},{2,10},{6,14},... | collective-permute-start | bytes 73736 | tf_op jit(solution)/shard_map/ppermute | solution.py:22
  66.3 1.3 %collective-permute-done.29.refs_2_ = bf16[32,384]{1,0:T(8,128)(2,1)S(1)} collective-permute-done((bf16[32,384]{1,0:T(8,128)(2,1)S(1)}, bf16[32,384]{1,0:T(8,128)(2,1)S(1)}, u32[]{:S(2)}, u32[]{:S(2)}) %collective-permute-start.29) | collective-permute-done | bytes 24608 | tf_op jit(solution)/shard_map/ppermute | solution.py:22
  68.2 1.3 %down_product.1 = bf16[16,2,1024]{2,1,0:T(2,128)(2,1)} custom-call(bf16[32,384]{1,0:T(8,128)(2,1)S(1)} %hidden_units.1.refs_0_, bf16[32,384]{1,0:T(8,128)(2,1)S(1)} %collective-permute-done.28.refs_1_, bf16[32,384]{1,0:T(8,128)(2,1)S(1)} %collective-permute-done.29.refs_2_, bf16[32,384]{1,0:T(8,128)(2,1)S(1)} %collective-permute-done.30.refs_3_, ...), custom_call_target="tpu_custom_call" | custom-call | tf_op jit(solution)/shard_map/down_product/pallas_call | solution.py:446
  69.5 1.3 %collective-permute-done.27.arrived_ref = bf16[128,1024]{1,0:T(8,128)(2,1)S(1)} collective-permute-done((bf16[128,1024]{1,0:T(8,128)(2,1)S(1)}, bf16[128,1024]{1,0:T(8,128)(2,1)S(1)}, u32[]{:S(2)}, u32[]{:S(2)}) %collective-permute-start.27) | collective-permute-done | bytes 262176 | tf_op jit(solution)/shard_map/ppermute | solution.py:22
  70.9 1.1 %collective-permute-start.33 = (bf16[64,1024]{1,0:T(8,128)(2,1)S(1)}, bf16[64,1024]{1,0:T(8,128)(2,1)S(1)}, u32[]{:S(2)}, u32[]{:S(2)}) collective-permute-start(bf16[64,1024]{1,0:T(8,128)(2,1)S(1)} %get-tuple-element.229), channel_id=1, source_target_pairs={{0,2},{1,3},{2,0},{3,1},{4,6},{5,7},{6,4},{7,5},{8,10},{9,11},{10,... | collective-permute-start | bytes 393224 | tf_op jit(solution)/shard_map/ppermute | solution.py:22
  72.0 4.3 %all-to-all-start = ((bf16[16,2,1024]{2,1,0:T(2,128)(2,1)}), bf16[16,2,1024]{2,1,0:T(2,128)(2,1)S(1)}, u32[]{:S(2)}, u32[]{:S(2)}) async-start(bf16[16,2,1024]{2,1,0:T(2,128)(2,1)} %down_product.1), calls=%async_computation | async-start | bytes 131072 | tf_op jit(solution)/shard_map/all_to_all | solution.py:728
  76.3 2.3 %collective-permute-done.26.arrived_ref = bf16[64,1024]{1,0:T(8,128)(2,1)S(1)} collective-permute-done((bf16[64,1024]{1,0:T(8,128)(2,1)S(1)}, bf16[64,1024]{1,0:T(8,128)(2,1)S(1)}, u32[]{:S(2)}, u32[]{:S(2)}) %collective-permute-start.26) | collective-permute-done | bytes 131104 | tf_op jit(solution)/shard_map/ppermute | solution.py:22
  78.6 1.0 %collective-permute-start.31 = (bf16[32,1024]{1,0:T(8,128)(2,1)S(1)}, bf16[32,1024]{1,0:T(8,128)(2,1)S(1)}, u32[]{:S(2)}, u32[]{:S(2)}) collective-permute-start(bf16[32,1024]{1,0:T(8,128)(2,1)S(1)} %get-tuple-element.226), channel_id=1, source_target_pairs={{0,8},{4,12},{8,0},{12,4},{1,9},{5,13},{9,1},{13,5},{2,10},{6,14},... | collective-permute-start | bytes 196616 | tf_op jit(solution)/shard_map/ppermute | solution.py:22
  79.6 1.6 %collective-permute-done.33.arrived_ref = bf16[64,1024]{1,0:T(8,128)(2,1)S(1)} collective-permute-done((bf16[64,1024]{1,0:T(8,128)(2,1)S(1)}, bf16[64,1024]{1,0:T(8,128)(2,1)S(1)}, u32[]{:S(2)}, u32[]{:S(2)}) %collective-permute-start.33) | collective-permute-done | bytes 131104 | tf_op jit(solution)/shard_map/ppermute | solution.py:22
  81.2 1.0 %collective-permute-start.34 = (bf16[32,1024]{1,0:T(8,128)(2,1)S(1)}, bf16[32,1024]{1,0:T(8,128)(2,1)S(1)}, u32[]{:S(2)}, u32[]{:S(2)}) collective-permute-start(bf16[32,1024]{1,0:T(8,128)(2,1)S(1)} %get-tuple-element.232), channel_id=1, source_target_pairs={{0,8},{4,12},{8,0},{12,4},{1,9},{5,13},{9,1},{13,5},{2,10},{6,14},... | collective-permute-start | bytes 196616 | tf_op jit(solution)/shard_map/ppermute | solution.py:22
  82.9 1.3 %combine.1 = bf16[64,4096]{1,0:T(8,128)(2,1)} custom-call(s32[8,64]{1,0:T(8,128)S(1)} %bitcast.12, f32[8,64]{1,0:T(8,128)S(1)} %bitcast.13, bf16[16,2,1024]{2,1,0:T(2,128)(2,1)S(1)} %all-to-all-done.back_ref), custom_call_target="tpu_custom_call" | custom-call | tf_op jit(solution)/shard_map/combine/pallas_call | solution.py:741
  84.2 2.1 %collective-permute-done.34.refs_4_ = bf16[32,1024]{1,0:T(8,128)(2,1)S(1)} collective-permute-done((bf16[32,1024]{1,0:T(8,128)(2,1)S(1)}, bf16[32,1024]{1,0:T(8,128)(2,1)S(1)}, u32[]{:S(2)}, u32[]{:S(2)}) %collective-permute-start.34) | collective-permute-done | bytes 65568 | tf_op jit(solution)/shard_map/ppermute | solution.py:22
  86.9 0.9 %attended_rows.1 = bf16[64,4096]{1,0:T(8,128)(2,1)} custom-call(bf16[64,1024]{1,0:T(8,128)(2,1)S(1)} %add.16.refs_0_, bf16[64,1024]{1,0:T(8,128)(2,1)S(1)} %collective-permute-done.16.refs_1_, bf16[32,1024]{1,0:T(8,128)(2,1)S(1)} %collective-permute-done.31.refs_2_, bf16[32,1024]{1,0:T(8,128)(2,1)S(1)} %collective-permute-done.32.refs_3_, ...), custom_call_target="tpu_custom_call" | custom-call | tf_op jit(solution)/shard_map/attended_rows/pallas_call | solution.py:470
  (70 shorter events, 7.6 us)
Async XLA Ops:
  1.6 10.1 %collective-permute-start = (bf16[2,256,128]{2,1,0:T(8,128)(2,1)S(1)}, bf16[2,256,128]{2,1,0:T(8,128)(2,1)S(1)}, u32[]{:S(2)}, u32[]{:S(2)}) collective-permute-start(bf16[2,256,128]{2,1,0:T(8,128)(2,1)S(1)} %pad_maximum_fusion.kv_own_ref), channel_id=1, source_target_pairs={{0,8},{4,12},{8,0},{12,4},{1,9},{5,13},{9,1},{13,5},{2,10},{6,14},... | collective-permute-start | bytes 393224 | tf_op jit(solution)/shard_map/ppermute | solution.py:27
  4.6 7.2 %collective-permute-start.1 = (bf16[2,256,128]{2,1,0:T(8,128)(2,1)S(1)}, bf16[2,256,128]{2,1,0:T(8,128)(2,1)S(1)}, u32[]{:S(2)}, u32[]{:S(2)}) collective-permute-start(bf16[2,256,128]{2,1,0:T(8,128)(2,1)S(1)} %pad_maximum_fusion.kv_own_ref), channel_id=1, source_target_pairs={{0,4},{4,8},{8,12},{12,0},{1,5},{5,9},{9,13},{13,1},{2,6},{6,10},{... | collective-permute-start | bytes 393224 | tf_op jit(solution)/shard_map/ppermute | solution.py:27
  4.6 14.0 %copy-start = (bf16[2048,1024]{1,0:T(8,128)(2,1)S(1)}, bf16[2048,1024]{1,0:T(8,128)(2,1)}, u32[]{:S(2)}) copy-start(bf16[2048,1024]{1,0:T(8,128)(2,1)} %refs_5_.3) | copy-start | bytes 12582916
  4.6 9.8 %collective-permute-start.3 = (s32[8,64]{1,0:T(8,128)}, s32[8,64]{1,0:T(8,128)S(1)}, u32[]{:S(2)}, u32[]{:S(2)}) collective-permute-start(s32[8,64]{1,0:T(8,128)} %bitcast.8), channel_id=1, source_target_pairs={{0,1},{1,0},{2,3},{3,2},{4,5},{5,4},{6,7},{7,6},{8,9},{9,8},{10,11... | collective-permute-start | bytes 6152 | tf_op jit(solution)/shard_map/ppermute | solution.py:22
  6.2 8.2 %collective-permute-start.4 = (s32[8,64]{1,0:T(8,128)}, s32[8,64]{1,0:T(8,128)S(1)}, u32[]{:S(2)}, u32[]{:S(2)}) collective-permute-start(s32[8,64]{1,0:T(8,128)} %bitcast.9), channel_id=1, source_target_pairs={{0,2},{1,3},{2,0},{3,1},{4,6},{5,7},{6,4},{7,5},{8,10},{9,11},{10,... | collective-permute-start | bytes 6152 | tf_op jit(solution)/shard_map/ppermute | solution.py:22
  8.8 5.6 %collective-permute-start.5 = (s32[8,64]{1,0:T(8,128)}, s32[8,64]{1,0:T(8,128)S(1)}, u32[]{:S(2)}, u32[]{:S(2)}) collective-permute-start(s32[8,64]{1,0:T(8,128)} %bitcast.10), channel_id=1, source_target_pairs={{0,3},{1,2},{2,1},{3,0},{4,7},{5,6},{6,5},{7,4},{8,11},{9,10},{10,... | collective-permute-start | bytes 6152 | tf_op jit(solution)/shard_map/ppermute | solution.py:22
  9.0 1.2 %copy-start.5 = (bf16[256,2048]{1,0:T(8,128)(2,1)S(1)}, bf16[256,2048]{1,0:T(8,128)(2,1)}, u32[]{:S(2)}) copy-start(bf16[256,2048]{1,0:T(8,128)(2,1)} %q_hbm) | copy-start | bytes 3145732
  10.2 0.7 copy-start.9
  17.0 2.9 %copy-start.4 = (bf16[64,4096]{1,0:T(8,128)(2,1)S(1)}, bf16[64,4096]{1,0:T(8,128)(2,1)}, u32[]{:S(2)}) copy-start(bf16[64,4096]{1,0:T(8,128)(2,1)} %refs_6_.3) | copy-start | bytes 1572868
  17.0 2.9 %copy-start.7 = (s32[64,8]{0,1:T(8,128)S(1)}, s32[64,8]{0,1:T(8,128)}, u32[]{:S(2)}) copy-start(s32[64,8]{0,1:T(8,128)} %param.19) | copy-start | bytes 6148
  17.1 4.8 %collective-permute-start.6 = (bf16[128,2048]{1,0:T(8,128)(2,1)S(1)}, bf16[128,2048]{1,0:T(8,128)(2,1)S(1)}, u32[]{:S(2)}, u32[]{:S(2)}) collective-permute-start(bf16[128,2048]{1,0:T(8,128)(2,1)S(1)} %attention_1.1.refs_1_.refs_6_.refs_4_), channel_id=1, source_target_pairs={{0,4},{4,0},{8,12},{12,8},{1,5},{5,1},{9,13},{13,9},{2,6},{6,2},{1... | collective-permute-start | bytes 1572872 | tf_op jit(solution)/shard_map/ppermute | solution.py:22
  17.1 4.7 %collective-permute-start.2 = (bf16[128,2048]{1,0:T(8,128)(2,1)S(1)}, bf16[128,2048]{1,0:T(8,128)(2,1)S(1)}, u32[]{:S(2)}, u32[]{:S(2)}) collective-permute-start(bf16[128,2048]{1,0:T(8,128)(2,1)S(1)} %attention_0.1.refs_0_.refs_5_.refs_3_), channel_id=1, source_target_pairs={{0,4},{4,0},{8,12},{12,8},{1,5},{5,1},{9,13},{13,9},{2,6},{6,2},{1... | collective-permute-start | bytes 1572872 | tf_op jit(solution)/shard_map/ppermute | solution.py:22
  17.6 14.8 %collective-permute-start.11 = (bf16[128,2048]{1,0:T(8,128)(2,1)S(1)}, bf16[128,2048]{1,0:T(8,128)(2,1)S(1)}, u32[]{:S(2)}, u32[]{:S(2)}) collective-permute-start(bf16[128,2048]{1,0:T(8,128)(2,1)S(1)} %attention_0.1.refs_0_.refs_5_.refs_3_), channel_id=1, source_target_pairs={{0,8},{4,12},{8,0},{12,4},{1,9},{5,13},{9,1},{13,5},{2,10},{6,14},... | collective-permute-start | bytes 1572872 | tf_op jit(solution)/shard_map/ppermute | solution.py:22
  19.3 9.2 %collective-permute-start.7 = (bf16[128,1024]{1,0:T(8,128)(2,1)S(1)}, bf16[128,1024]{1,0:T(8,128)(2,1)S(1)}, u32[]{:S(2)}, u32[]{:S(2)}) collective-permute-start(bf16[128,1024]{1,0:T(8,128)(2,1)S(1)} %leave.1), channel_id=1, source_target_pairs={{0,1},{1,0},{2,3},{3,2},{4,5},{5,4},{6,7},{7,6},{8,9},{9,8},{10,11... | collective-permute-start | bytes 786440 | tf_op jit(solution)/shard_map/ppermute | solution.py:22
  23.7 12.1 %collective-permute-start.9 = (bf16[128,1024]{1,0:T(8,128)(2,1)S(1)}, bf16[128,1024]{1,0:T(8,128)(2,1)S(1)}, u32[]{:S(2)}, u32[]{:S(2)}) collective-permute-start(bf16[128,1024]{1,0:T(8,128)(2,1)S(1)} %get-tuple-element.158), channel_id=1, source_target_pairs={{0,1},{1,0},{2,3},{3,2},{4,5},{5,4},{6,7},{7,6},{8,9},{9,8},{10,11... | collective-permute-start | bytes 786440 | tf_op jit(solution)/shard_map/ppermute | solution.py:22
  28.6 7.2 %collective-permute-start.12 = (bf16[48,2048]{1,0:T(8,128)(2,1)S(1)}, bf16[48,2048]{1,0:T(8,128)(2,1)S(1)}, u32[]{:S(2)}, u32[]{:S(2)}) collective-permute-start(bf16[48,2048]{1,0:T(8,128)(2,1)S(1)} %pick.1.refs_0_), channel_id=1, source_target_pairs={{0,8},{4,12},{8,0},{12,4},{1,9},{5,13},{9,1},{13,5},{2,10},{6,14},... | collective-permute-start | bytes 589832 | tf_op jit(solution)/shard_map/ppermute | solution.py:22
  29.8 8.7 %collective-permute-start.8 = (bf16[64,1024]{1,0:T(8,128)(2,1)S(1)}, bf16[64,1024]{1,0:T(8,128)(2,1)S(1)}, u32[]{:S(2)}, u32[]{:S(2)}) collective-permute-start(bf16[64,1024]{1,0:T(8,128)(2,1)S(1)} %get-tuple-element.157), channel_id=1, source_target_pairs={{0,2},{1,3},{2,0},{3,1},{4,6},{5,7},{6,4},{7,5},{8,10},{9,11},{10,... | collective-permute-start | bytes 393224 | tf_op jit(solution)/shard_map/ppermute | solution.py:22
  35.8 9.0 %collective-permute-start.13 = (bf16[128,2048]{1,0:T(8,128)(2,1)S(1)}, bf16[128,2048]{1,0:T(8,128)(2,1)S(1)}, u32[]{:S(2)}, u32[]{:S(2)}) collective-permute-start(bf16[128,2048]{1,0:T(8,128)(2,1)S(1)} %collective-permute-done.11.refs_0_.refs_3_), channel_id=1, source_target_pairs={{0,4},{4,0},{8,12},{12,8},{1,5},{5,1},{9,13},{13,9},{2,6},{6,2},{1... | collective-permute-start | bytes 1572872 | tf_op jit(solution)/shard_map/ppermute | solution.py:22
  38.5 14.5 %collective-permute-start.24 = (bf16[128,2048]{1,0:T(8,128)(2,1)S(1)}, bf16[128,2048]{1,0:T(8,128)(2,1)S(1)}, u32[]{:S(2)}, u32[]{:S(2)}) collective-permute-start(bf16[128,2048]{1,0:T(8,128)(2,1)S(1)} %attention_1.1.refs_1_.refs_6_.refs_4_), channel_id=1, source_target_pairs={{0,8},{4,12},{8,0},{12,4},{1,9},{5,13},{9,1},{13,5},{2,10},{6,14},... | collective-permute-start | bytes 1572872 | tf_op jit(solution)/shard_map/ppermute | solution.py:22
  39.3 1.4 %collective-permute-start.14 = (bf16[48,2048]{1,0:T(8,128)(2,1)S(1)}, bf16[48,2048]{1,0:T(8,128)(2,1)S(1)}, u32[]{:S(2)}, u32[]{:S(2)}) collective-permute-start(bf16[48,2048]{1,0:T(8,128)(2,1)S(1)} %pick.1.refs_0_), channel_id=1, source_target_pairs={{0,4},{4,0},{8,12},{12,8},{1,5},{5,1},{9,13},{13,9},{2,6},{6,2},{1... | collective-permute-start | bytes 589832 | tf_op jit(solution)/shard_map/ppermute | solution.py:22
  39.3 1.7 %collective-permute-start.15 = (bf16[48,2048]{1,0:T(8,128)(2,1)S(1)}, bf16[48,2048]{1,0:T(8,128)(2,1)S(1)}, u32[]{:S(2)}, u32[]{:S(2)}) collective-permute-start(bf16[48,2048]{1,0:T(8,128)(2,1)S(1)} %collective-permute-done.12.refs_2_), channel_id=1, source_target_pairs={{0,4},{4,0},{8,12},{12,8},{1,5},{5,1},{9,13},{13,9},{2,6},{6,2},{1... | collective-permute-start | bytes 589832 | tf_op jit(solution)/shard_map/ppermute | solution.py:22
  39.8 11.8 %collective-permute-start.10 = (bf16[64,1024]{1,0:T(8,128)(2,1)S(1)}, bf16[64,1024]{1,0:T(8,128)(2,1)S(1)}, u32[]{:S(2)}, u32[]{:S(2)}) collective-permute-start(bf16[64,1024]{1,0:T(8,128)(2,1)S(1)} %get-tuple-element.165), channel_id=1, source_target_pairs={{0,2},{1,3},{2,0},{3,1},{4,6},{5,7},{6,4},{7,5},{8,10},{9,11},{10,... | collective-permute-start | bytes 393224 | tf_op jit(solution)/shard_map/ppermute | solution.py:22
  41.8 9.8 %collective-permute-start.18 = (bf16[4,8,1024]{2,1,0:T(8,128)(2,1)S(1)}, bf16[4,8,1024]{2,1,0:T(8,128)(2,1)S(1)}, u32[]{:S(2)}, u32[]{:S(2)}) collective-permute-start(bf16[4,8,1024]{2,1,0:T(8,128)(2,1)S(1)} %get-tuple-element.189), channel_id=1, source_target_pairs={{0,1},{1,0},{2,3},{3,2},{4,5},{5,4},{6,7},{7,6},{8,9},{9,8},{10,11... | collective-permute-start | bytes 196616 | tf_op jit(solution)/shard_map/ppermute | solution.py:22
  43.6 9.3 %collective-permute-start.19 = (bf16[4,8,1024]{2,1,0:T(8,128)(2,1)S(1)}, bf16[4,8,1024]{2,1,0:T(8,128)(2,1)S(1)}, u32[]{:S(2)}, u32[]{:S(2)}) collective-permute-start(bf16[4,8,1024]{2,1,0:T(8,128)(2,1)S(1)} %get-tuple-element.190), channel_id=1, source_target_pairs={{0,2},{1,3},{2,0},{3,1},{4,6},{5,7},{6,4},{7,5},{8,10},{9,11},{10,... | collective-permute-start | bytes 196616 | tf_op jit(solution)/shard_map/ppermute | solution.py:22
  44.9 8.1 %collective-permute-start.20 = (bf16[4,8,1024]{2,1,0:T(8,128)(2,1)S(1)}, bf16[4,8,1024]{2,1,0:T(8,128)(2,1)S(1)}, u32[]{:S(2)}, u32[]{:S(2)}) collective-permute-start(bf16[4,8,1024]{2,1,0:T(8,128)(2,1)S(1)} %get-tuple-element.177), channel_id=1, source_target_pairs={{0,3},{1,2},{2,1},{3,0},{4,7},{5,6},{6,5},{7,4},{8,11},{9,10},{10,... | collective-permute-start | bytes 196616 | tf_op jit(solution)/shard_map/ppermute | solution.py:22
  53.0 6.0 %collective-permute-start.25 = (bf16[128,2048]{1,0:T(8,128)(2,1)S(1)}, bf16[128,2048]{1,0:T(8,128)(2,1)S(1)}, u32[]{:S(2)}, u32[]{:S(2)}) collective-permute-start(bf16[128,2048]{1,0:T(8,128)(2,1)S(1)} %collective-permute-done.24.refs_0_.refs_3_), channel_id=1, source_target_pairs={{0,4},{4,0},{8,12},{12,8},{1,5},{5,1},{9,13},{13,9},{2,6},{6,2},{1... | collective-permute-start | bytes 1572872 | tf_op jit(solution)/shard_map/ppermute | solution.py:22
  53.1 3.8 %collective-permute-start.21 = (bf16[32,1024]{1,0:T(8,128)(2,1)S(1)}, bf16[32,1024]{1,0:T(8,128)(2,1)S(1)}, u32[]{:S(2)}, u32[]{:S(2)}) collective-permute-start(bf16[32,1024]{1,0:T(8,128)(2,1)S(1)} %routed_sum.1.refs_0_), channel_id=1, source_target_pairs={{0,4},{4,0},{8,12},{12,8},{1,5},{5,1},{9,13},{13,9},{2,6},{6,2},{1... | collective-permute-start | bytes 196616 | tf_op jit(solution)/shard_map/ppermute | solution.py:22
  53.6 4.5 %collective-permute-start.22 = (bf16[32,1024]{1,0:T(8,128)(2,1)S(1)}, bf16[32,1024]{1,0:T(8,128)(2,1)S(1)}, u32[]{:S(2)}, u32[]{:S(2)}) collective-permute-start(bf16[32,1024]{1,0:T(8,128)(2,1)S(1)} %routed_sum.1.refs_0_), channel_id=1, source_target_pairs={{0,8},{4,12},{8,0},{12,4},{1,9},{5,13},{9,1},{13,5},{2,10},{6,14},... | collective-permute-start | bytes 196616 | tf_op jit(solution)/shard_map/ppermute | solution.py:22
  54.7 4.3 %collective-permute-start.23 = (bf16[32,1024]{1,0:T(8,128)(2,1)S(1)}, bf16[32,1024]{1,0:T(8,128)(2,1)S(1)}, u32[]{:S(2)}, u32[]{:S(2)}) collective-permute-start(bf16[32,1024]{1,0:T(8,128)(2,1)S(1)} %routed_sum.1.refs_0_), channel_id=1, source_target_pairs={{0,12},{4,8},{8,4},{12,0},{1,13},{5,9},{9,5},{13,1},{2,14},{6,10},... | collective-permute-start | bytes 196616 | tf_op jit(solution)/shard_map/ppermute | solution.py:22
  55.0 7.5 %copy-start.1 = (bf16[1,4096,384]{2,1,0:T(8,128)(2,1)S(1)}, bf16[1,4096,384]{2,1,0:T(8,128)(2,1)}, u32[]{:S(2)}) copy-start(bf16[1,4096,384]{2,1,0:T(8,128)(2,1)} %refs_5_.4) | copy-start | bytes 9437188
  55.0 7.5 %copy-start.2 = (bf16[1,4096,384]{2,1,0:T(8,128)(2,1)S(1)}, bf16[1,4096,384]{2,1,0:T(8,128)(2,1)}, u32[]{:S(2)}) copy-start(bf16[1,4096,384]{2,1,0:T(8,128)(2,1)} %refs_6_.2) | copy-start | bytes 9437188
  55.0 7.5 %copy-start.6 = (f32[4096]{0:T(1024)S(1)}, f32[4096]{0:T(1024)}, u32[]{:S(2)}) copy-start(f32[4096]{0:T(1024)} %param.18) | copy-start | bytes 49156
  55.0 10.5 %collective-permute-start.17 = (bf16[128,1024]{1,0:T(8,128)(2,1)S(1)}, bf16[128,1024]{1,0:T(8,128)(2,1)S(1)}, u32[]{:S(2)}, u32[]{:S(2)}) collective-permute-start(bf16[128,1024]{1,0:T(8,128)(2,1)S(1)} %get-tuple-element.187), channel_id=1, source_target_pairs={{0,1},{1,0},{2,3},{3,2},{4,5},{5,4},{6,7},{7,6},{8,9},{9,8},{10,11... | collective-permute-start | bytes 786440 | tf_op jit(solution)/shard_map/ppermute | solution.py:22
  60.6 10.3 %collective-permute-start.27 = (bf16[128,1024]{1,0:T(8,128)(2,1)S(1)}, bf16[128,1024]{1,0:T(8,128)(2,1)S(1)}, u32[]{:S(2)}, u32[]{:S(2)}) collective-permute-start(bf16[128,1024]{1,0:T(8,128)(2,1)S(1)} %get-tuple-element.216), channel_id=1, source_target_pairs={{0,1},{1,0},{2,3},{3,2},{4,5},{5,4},{6,7},{7,6},{8,9},{9,8},{10,11... | collective-permute-start | bytes 786440 | tf_op jit(solution)/shard_map/ppermute | solution.py:22
  62.5 5.7 %copy-start.3 = (bf16[1,1536,1024]{2,1,0:T(8,128)(2,1)S(1)}, bf16[1,1536,1024]{2,1,0:T(8,128)(2,1)}, u32[]{:S(2)}) copy-start(bf16[1,1536,1024]{2,1,0:T(8,128)(2,1)} %refs_4_.2) | copy-start | bytes 9437188
  63.6 19.3 %copy-start.8 = (f32[64,8]{0,1:T(8,128)S(1)}, f32[64,8]{0,1:T(8,128)}, u32[]{:S(2)}) copy-start(f32[64,8]{0,1:T(8,128)} %param.20) | copy-start | bytes 6148
  63.6 2.6 %collective-permute-start.28 = (bf16[32,384]{1,0:T(8,128)(2,1)S(1)}, bf16[32,384]{1,0:T(8,128)(2,1)S(1)}, u32[]{:S(2)}, u32[]{:S(2)}) collective-permute-start(bf16[32,384]{1,0:T(8,128)(2,1)S(1)} %hidden_units.1.refs_0_), channel_id=1, source_target_pairs={{0,4},{4,0},{8,12},{12,8},{1,5},{5,1},{9,13},{13,9},{2,6},{6,2},{1... | collective-permute-start | bytes 73736 | tf_op jit(solution)/shard_map/ppermute | solution.py:22
  63.7 3.9 %collective-permute-start.29 = (bf16[32,384]{1,0:T(8,128)(2,1)S(1)}, bf16[32,384]{1,0:T(8,128)(2,1)S(1)}, u32[]{:S(2)}, u32[]{:S(2)}) collective-permute-start(bf16[32,384]{1,0:T(8,128)(2,1)S(1)} %hidden_units.1.refs_0_), channel_id=1, source_target_pairs={{0,8},{4,12},{8,0},{12,4},{1,9},{5,13},{9,1},{13,5},{2,10},{6,14},... | collective-permute-start | bytes 73736 | tf_op jit(solution)/shard_map/ppermute | solution.py:22
  64.9 3.3 %collective-permute-start.30 = (bf16[32,384]{1,0:T(8,128)(2,1)S(1)}, bf16[32,384]{1,0:T(8,128)(2,1)S(1)}, u32[]{:S(2)}, u32[]{:S(2)}) collective-permute-start(bf16[32,384]{1,0:T(8,128)(2,1)S(1)} %hidden_units.1.refs_0_), channel_id=1, source_target_pairs={{0,12},{4,8},{8,4},{12,0},{1,13},{5,9},{9,5},{13,1},{2,14},{6,10},... | collective-permute-start | bytes 73736 | tf_op jit(solution)/shard_map/ppermute | solution.py:22
  65.6 12.9 %collective-permute-start.26 = (bf16[64,1024]{1,0:T(8,128)(2,1)S(1)}, bf16[64,1024]{1,0:T(8,128)(2,1)S(1)}, u32[]{:S(2)}, u32[]{:S(2)}) collective-permute-start(bf16[64,1024]{1,0:T(8,128)(2,1)S(1)} %get-tuple-element.215), channel_id=1, source_target_pairs={{0,2},{1,3},{2,0},{3,1},{4,6},{5,7},{6,4},{7,5},{8,10},{9,11},{10,... | collective-permute-start | bytes 393224 | tf_op jit(solution)/shard_map/ppermute | solution.py:22
  70.9 10.3 %collective-permute-start.33 = (bf16[64,1024]{1,0:T(8,128)(2,1)S(1)}, bf16[64,1024]{1,0:T(8,128)(2,1)S(1)}, u32[]{:S(2)}, u32[]{:S(2)}) collective-permute-start(bf16[64,1024]{1,0:T(8,128)(2,1)S(1)} %get-tuple-element.229), channel_id=1, source_target_pairs={{0,2},{1,3},{2,0},{3,1},{4,6},{5,7},{6,4},{7,5},{8,10},{9,11},{10,... | collective-permute-start | bytes 393224 | tf_op jit(solution)/shard_map/ppermute | solution.py:22
  72.0 12.2 %collective-permute-start.16 = (bf16[64,1024]{1,0:T(8,128)(2,1)S(1)}, bf16[64,1024]{1,0:T(8,128)(2,1)S(1)}, u32[]{:S(2)}, u32[]{:S(2)}) collective-permute-start(bf16[64,1024]{1,0:T(8,128)(2,1)S(1)} %add.17), channel_id=1, source_target_pairs={{0,4},{4,0},{8,12},{12,8},{1,5},{5,1},{9,13},{13,9},{2,6},{6,2},{1... | collective-permute-start | bytes 393224 | tf_op jit(solution)/shard_map/ppermute | solution.py:22
  72.0 10.9 %all-to-all-start = ((bf16[16,2,1024]{2,1,0:T(2,128)(2,1)}), bf16[16,2,1024]{2,1,0:T(2,128)(2,1)S(1)}, u32[]{:S(2)}, u32[]{:S(2)}) async-start(bf16[16,2,1024]{2,1,0:T(2,128)(2,1)} %down_product.1), calls=%async_computation | async-start | bytes 131072 | tf_op jit(solution)/shard_map/all_to_all | solution.py:728
  78.6 5.6 %collective-permute-start.31 = (bf16[32,1024]{1,0:T(8,128)(2,1)S(1)}, bf16[32,1024]{1,0:T(8,128)(2,1)S(1)}, u32[]{:S(2)}, u32[]{:S(2)}) collective-permute-start(bf16[32,1024]{1,0:T(8,128)(2,1)S(1)} %get-tuple-element.226), channel_id=1, source_target_pairs={{0,8},{4,12},{8,0},{12,4},{1,9},{5,13},{9,1},{13,5},{2,10},{6,14},... | collective-permute-start | bytes 196616 | tf_op jit(solution)/shard_map/ppermute | solution.py:22
  79.6 4.6 %collective-permute-start.32 = (bf16[32,1024]{1,0:T(8,128)(2,1)S(1)}, bf16[32,1024]{1,0:T(8,128)(2,1)S(1)}, u32[]{:S(2)}, u32[]{:S(2)}) collective-permute-start(bf16[32,1024]{1,0:T(8,128)(2,1)S(1)} %get-tuple-element.227), channel_id=1, source_target_pairs={{0,12},{4,8},{8,4},{12,0},{1,13},{5,9},{9,5},{13,1},{2,14},{6,10},... | collective-permute-start | bytes 196616 | tf_op jit(solution)/shard_map/ppermute | solution.py:22
  81.2 5.2 %collective-permute-start.34 = (bf16[32,1024]{1,0:T(8,128)(2,1)S(1)}, bf16[32,1024]{1,0:T(8,128)(2,1)S(1)}, u32[]{:S(2)}, u32[]{:S(2)}) collective-permute-start(bf16[32,1024]{1,0:T(8,128)(2,1)S(1)} %get-tuple-element.232), channel_id=1, source_target_pairs={{0,8},{4,12},{8,0},{12,4},{1,9},{5,13},{9,1},{13,5},{2,10},{6,14},... | collective-permute-start | bytes 196616 | tf_op jit(solution)/shard_map/ppermute | solution.py:22
  82.2 4.7 %collective-permute-start.35 = (bf16[32,1024]{1,0:T(8,128)(2,1)S(1)}, bf16[32,1024]{1,0:T(8,128)(2,1)S(1)}, u32[]{:S(2)}, u32[]{:S(2)}) collective-permute-start(bf16[32,1024]{1,0:T(8,128)(2,1)S(1)} %get-tuple-element.233), channel_id=1, source_target_pairs={{0,12},{4,8},{8,4},{12,0},{1,13},{5,9},{9,5},{13,1},{2,14},{6,10},... | collective-permute-start | bytes 196616 | tf_op jit(solution)/shard_map/ppermute | solution.py:22

commit v7 on v6

--- a/solution.py
+++ b/solution.py
@@ -282,19 +282,20 @@
     slots = flight * CAP
     block = homes * CAP
     lines = flight * block
-    line = lax.broadcasted_iota(jnp.int32, (lines, slots), 0)
+    first_col = ctx_index * cols
+    column = pl.multiple_of(first_col % depth, HD)
+    held = piece_refs[0].shape[0] - lines
+    line = lax.broadcasted_iota(jnp.int32, (lines, held), 0)
     expert = line // block ^ exp_index
-    source = jnp.where(line // CAP % homes == exp_index, expert * CAP + line % CAP, -1)
-    onehot = (source == lax.broadcasted_iota(jnp.int32, (lines, slots), 1)).astype(jnp.bfloat16)
+    row = first_col // depth * slots + expert * CAP + line % CAP
+    source = jnp.where(line // CAP % homes == exp_index, row, -1)
+    onehot = (source == lax.broadcasted_iota(jnp.int32, (lines, held), 1)).astype(jnp.bfloat16)
     heads = jnp.concatenate([ref[:lines, :] for ref in piece_refs], axis=0)
     product = jnp.dot(heads, weight_ref[...], preferred_element_type=jnp.float32)
-    first_col = ctx_index * cols
-    column = pl.multiple_of(first_col % depth, HD)
-    row = pl.multiple_of(lines + first_col // depth * slots, slots)
     for place in range(count):
         extra = jnp.dot(
             onehot,
-            piece_refs[place][pl.ds(row, slots), pl.ds(column, cols)],
+            piece_refs[place][lines:, pl.ds(column, cols)],
             preferred_element_type=jnp.float32,
         )
         total = product[place * lines : (place + 1) * lines] + extra

time: 88.1 us -> 88.1 us (level)
  no operation moved by 1% of the time
where the time goes in v7:
time: 88.1 us; the launch traced here: 87.8 us
  starting transfers between devices  35.6 us (40%)
  waiting for transfers between devices  29.5 us (33%)
  Pallas kernels  19 us (22%)
  local copies, waits for them, and re-layouts  2.8 us (3%)
  between operations  0.93 us (1%)
    ppermute x34, waiting for transfers between devices, swap(): return lax.ppermute(x, axis, [(i, i ^ mask) for i in range(count)])  28.8 us
    ppermute x34, starting transfers between devices, swap(): return lax.ppermute(x, axis, [(i, i ^ mask) for i in range(count)])  28.3 us
    pallas_call x6, Pallas kernels, together(): pl.pallas_call(kernel, out_shape=shapes, in_specs=whole_vmem(total), out_...  7.89 us
    pallas_call x2, Pallas kernels, attention(): pl.pallas_call(functools.partial(attention_kernel, heads=width // HD, hom...  5.26 us
    all_to_all x1, starting transfers between devices, shards(): lax.all_to_all(produced, ('ctx', 'exp'), split_axis=0, concat_axis=0, til...  4.29 us
    ppermute x2, starting transfers between devices, shift(): return lax.ppermute(x, axis, [(i, (i + by) % count) for i in range(count)])  3.01 us
    unnamed x20, local copies, waits for them, and re-layouts  1.92 us
  transfers between devices with their start and end apart: 37, of which 18 were waited for; matrix products, arithmetic and copies ran while one was open for 0% of the time, Pallas kernels for 18%

profile of v7, /device:TPU:0, one launch (start us, length us, event | category | flops | bytes accessed | tf_op | source)
XLA Modules:
  0.0 87.8 jit_solution(17444152275087418928)
XLA Ops:
  0.6 0.9 %dynamic-slice_bitcast_fusion = (bf16[1,256,128]{2,1,0:T(8,128)(2,1)S(1)}, bf16[1,256,128]{2,1,0:T(8,128)(2,1)S(1)}) fusion(bf16[256,512]{1,0:T(8,128)(2,1)} %param.14, s32[]{:T(128)S(6)} %select_n.10, bf16[256,512]{1,0:T(8,128)(2,1)} %param.13), kind=kLoop, calls=%fused_computation.1 | loop fusion | bytes 262148 | tf_op jit(solution)/shard_map/stack | solution.py:650
  1.6 3.0 %collective-permute-start = (bf16[2,256,128]{2,1,0:T(8,128)(2,1)S(1)}, bf16[2,256,128]{2,1,0:T(8,128)(2,1)S(1)}, u32[]{:S(2)}, u32[]{:S(2)}) collective-permute-start(bf16[2,256,128]{2,1,0:T(8,128)(2,1)S(1)} %pad_maximum_fusion.kv_own_ref), channel_id=1, source_target_pairs={{0,8},{4,12},{8,0},{12,4},{1,9},{5,13},{9,1},{13,5},{2,10},{6,14},... | collective-permute-start | bytes 393224 | tf_op jit(solution)/shard_map/ppermute | solution.py:27
  4.6 1.6 %collective-permute-start.3 = (s32[8,64]{1,0:T(8,128)}, s32[8,64]{1,0:T(8,128)S(1)}, u32[]{:S(2)}, u32[]{:S(2)}) collective-permute-start(s32[8,64]{1,0:T(8,128)} %bitcast.8), channel_id=1, source_target_pairs={{0,1},{1,0},{2,3},{3,2},{4,5},{5,4},{6,7},{7,6},{8,9},{9,8},{10,11... | collective-permute-start | bytes 6152 | tf_op jit(solution)/shard_map/ppermute | solution.py:22
  6.2 2.6 %collective-permute-start.4 = (s32[8,64]{1,0:T(8,128)}, s32[8,64]{1,0:T(8,128)S(1)}, u32[]{:S(2)}, u32[]{:S(2)}) collective-permute-start(s32[8,64]{1,0:T(8,128)} %bitcast.9), channel_id=1, source_target_pairs={{0,2},{1,3},{2,0},{3,1},{4,6},{5,7},{6,4},{7,5},{8,10},{9,11},{10,... | collective-permute-start | bytes 6152 | tf_op jit(solution)/shard_map/ppermute | solution.py:22
  9.0 1.2 %copy-done.5 = bf16[256,2048]{1,0:T(8,128)(2,1)S(1)} copy-done((bf16[256,2048]{1,0:T(8,128)(2,1)S(1)}, bf16[256,2048]{1,0:T(8,128)(2,1)}, u32[]{:S(2)}) %copy-start.5) | copy-done | bytes 1048600
  10.8 0.9 ready.1
  11.7 2.6 %attention_0.1.refs_0_.refs_5_.refs_3_ = bf16[128,2048]{1,0:T(8,128)(2,1)S(1)} custom-call(bf16[256,2048]{1,0:T(8,128)(2,1)S(1)} %get-tuple-element.131.q_ref, f32[256,640]{1,0:T(8,128)S(1)} %get-tuple-element.124.bias_ref, bf16[2,256,128]{2,1,0:T(8,128)(2,1)S(1)} %collective-permute-done.kv_far_ref, ...), custom_call_target="tpu_custom_call" | custom-call | tf_op jit(solution)/shard_map/attention_0/pallas_call | solution.py:201
  14.4 2.6 %attention_1.1.refs_1_.refs_6_.refs_4_ = bf16[128,2048]{1,0:T(8,128)(2,1)S(1)} custom-call(bf16[256,2048]{1,0:T(8,128)(2,1)S(1)} %get-tuple-element.131.q_ref, f32[256,640]{1,0:T(8,128)S(1)} %get-tuple-element.124.bias_ref, bf16[2,256,128]{2,1,0:T(8,128)(2,1)S(1)} %collective-permute-done.kv_far_ref, ...), custom_call_target="tpu_custom_call" | custom-call | tf_op jit(solution)/shard_map/attention_1/pallas_call | solution.py:201
  17.6 0.9 %collective-permute-start.11 = (bf16[128,2048]{1,0:T(8,128)(2,1)S(1)}, bf16[128,2048]{1,0:T(8,128)(2,1)S(1)}, u32[]{:S(2)}, u32[]{:S(2)}) collective-permute-start(bf16[128,2048]{1,0:T(8,128)(2,1)S(1)} %attention_0.1.refs_0_.refs_5_.refs_3_), channel_id=1, source_target_pairs={{0,8},{4,12},{8,0},{12,4},{1,9},{5,13},{9,1},{13,5},{2,10},{6,14},... | collective-permute-start | bytes 1572872 | tf_op jit(solution)/shard_map/ppermute | solution.py:22
  18.6 0.7 leave.1
  20.0 1.8 %pick.1.refs_0_ = bf16[48,2048]{1,0:T(8,128)(2,1)S(1)} custom-call(bf16[64,4096]{1,0:T(8,128)(2,1)S(1)} %copy-done.4, s32[8,64]{1,0:T(8,128)S(1)} %bitcast.11, s32[8,64]{1,0:T(8,128)S(1)} %collective-permute-done.3.refs_2_, s32[8,64]{1,0:T(8,128)S(1)} %collective-permute-done.4.refs_3_, s32[8,64]{1,0:T(8,128)S(1)} %collective-permute-done.5.refs_4_, ...), custom_call_target="tpu_custom_call" | custom-call | tf_op jit(solution)/shard_map/pick/pallas_call | solution.py:74
  21.8 1.8 %leave_and_stay.1 = (bf16[128,1024]{1,0:T(8,128)(2,1)S(1)}, bf16[128,1024]{1,0:T(8,128)(2,1)S(1)}, bf16[128,1024]{1,0:T(8,128)(2,1)S(1)}) custom-call(bf16[128,2048]{1,0:T(8,128)(2,1)S(1)} %collective-permute-done.2.refs_0_.refs_6_, bf16[128,2048]{1,0:T(8,128)(2,1)S(1)} %collective-permute-done.6.refs_1_.refs_7_, bf16[2048,1024]{1,0:T(8,128)(2,1)S(1)} %copy-done, ...), custom_call_target="tpu_custom_call" | custom-call | tf_op jit(solution)/shard_map/leave_and_stay/pallas_call | solution.py:74
  23.7 1.5 %collective-permute-start.9 = (bf16[128,1024]{1,0:T(8,128)(2,1)S(1)}, bf16[128,1024]{1,0:T(8,128)(2,1)S(1)}, u32[]{:S(2)}, u32[]{:S(2)}) collective-permute-start(bf16[128,1024]{1,0:T(8,128)(2,1)S(1)} %get-tuple-element.158), channel_id=1, source_target_pairs={{0,1},{1,0},{2,3},{3,2},{4,5},{5,4},{6,7},{7,6},{8,9},{9,8},{10,11... | collective-permute-start | bytes 786440 | tf_op jit(solution)/shard_map/ppermute | solution.py:22
  25.1 3.4 %collective-permute-done.7.arrived_ref = bf16[128,1024]{1,0:T(8,128)(2,1)S(1)} collective-permute-done((bf16[128,1024]{1,0:T(8,128)(2,1)S(1)}, bf16[128,1024]{1,0:T(8,128)(2,1)S(1)}, u32[]{:S(2)}, u32[]{:S(2)}) %collective-permute-start.7) | collective-permute-done | bytes 262176 | tf_op jit(solution)/shard_map/ppermute | solution.py:22
  28.6 1.2 %collective-permute-start.12 = (bf16[48,2048]{1,0:T(8,128)(2,1)S(1)}, bf16[48,2048]{1,0:T(8,128)(2,1)S(1)}, u32[]{:S(2)}, u32[]{:S(2)}) collective-permute-start(bf16[48,2048]{1,0:T(8,128)(2,1)S(1)} %pick.1.refs_0_), channel_id=1, source_target_pairs={{0,8},{4,12},{8,0},{12,4},{1,9},{5,13},{9,1},{13,5},{2,10},{6,14},... | collective-permute-start | bytes 589832 | tf_op jit(solution)/shard_map/ppermute | solution.py:22
  29.8 1.7 %collective-permute-start.8 = (bf16[64,1024]{1,0:T(8,128)(2,1)S(1)}, bf16[64,1024]{1,0:T(8,128)(2,1)S(1)}, u32[]{:S(2)}, u32[]{:S(2)}) collective-permute-start(bf16[64,1024]{1,0:T(8,128)(2,1)S(1)} %get-tuple-element.157), channel_id=1, source_target_pairs={{0,2},{1,3},{2,0},{3,1},{4,6},{5,7},{6,4},{7,5},{8,10},{9,11},{10,... | collective-permute-start | bytes 393224 | tf_op jit(solution)/shard_map/ppermute | solution.py:22
  31.5 0.9 %collective-permute-done.11.refs_0_.refs_3_ = bf16[128,2048]{1,0:T(8,128)(2,1)S(1)} collective-permute-done((bf16[128,2048]{1,0:T(8,128)(2,1)S(1)}, bf16[128,2048]{1,0:T(8,128)(2,1)S(1)}, u32[]{:S(2)}, u32[]{:S(2)}) %collective-permute-start.11) | collective-permute-done | bytes 524320 | tf_op jit(solution)/shard_map/ppermute | solution.py:22
  32.4 3.3 %collective-permute-done.12.refs_2_ = bf16[48,2048]{1,0:T(8,128)(2,1)S(1)} collective-permute-done((bf16[48,2048]{1,0:T(8,128)(2,1)S(1)}, bf16[48,2048]{1,0:T(8,128)(2,1)S(1)}, u32[]{:S(2)}, u32[]{:S(2)}) %collective-permute-start.12) | collective-permute-done | bytes 196640 | tf_op jit(solution)/shard_map/ppermute | solution.py:22
  35.9 2.6 %collective-permute-done.8.arrived_ref = bf16[64,1024]{1,0:T(8,128)(2,1)S(1)} collective-permute-done((bf16[64,1024]{1,0:T(8,128)(2,1)S(1)}, bf16[64,1024]{1,0:T(8,128)(2,1)S(1)}, u32[]{:S(2)}, u32[]{:S(2)}) %collective-permute-start.8) | collective-permute-done | bytes 131104 | tf_op jit(solution)/shard_map/ppermute | solution.py:22
  38.5 0.8 collective-permute-start.24
  39.8 0.9 %collective-permute-done.14.refs_1_ = bf16[48,2048]{1,0:T(8,128)(2,1)S(1)} collective-permute-done((bf16[48,2048]{1,0:T(8,128)(2,1)S(1)}, bf16[48,2048]{1,0:T(8,128)(2,1)S(1)}, u32[]{:S(2)}, u32[]{:S(2)}) %collective-permute-start.14) | collective-permute-done | bytes 196640 | tf_op jit(solution)/shard_map/ppermute | solution.py:22
  41.0 0.8 routed_product.1
  41.8 1.8 %collective-permute-start.18 = (bf16[4,8,1024]{2,1,0:T(8,128)(2,1)S(1)}, bf16[4,8,1024]{2,1,0:T(8,128)(2,1)S(1)}, u32[]{:S(2)}, u32[]{:S(2)}) collective-permute-start(bf16[4,8,1024]{2,1,0:T(8,128)(2,1)S(1)} %get-tuple-element.189), channel_id=1, source_target_pairs={{0,1},{1,0},{2,3},{3,2},{4,5},{5,4},{6,7},{7,6},{8,9},{9,8},{10,11... | collective-permute-start | bytes 196616 | tf_op jit(solution)/shard_map/ppermute | solution.py:22
  43.6 1.2 %collective-permute-start.19 = (bf16[4,8,1024]{2,1,0:T(8,128)(2,1)S(1)}, bf16[4,8,1024]{2,1,0:T(8,128)(2,1)S(1)}, u32[]{:S(2)}, u32[]{:S(2)}) collective-permute-start(bf16[4,8,1024]{2,1,0:T(8,128)(2,1)S(1)} %get-tuple-element.190), channel_id=1, source_target_pairs={{0,2},{1,3},{2,0},{3,1},{4,6},{5,7},{6,4},{7,5},{8,10},{9,11},{10,... | collective-permute-start | bytes 196616 | tf_op jit(solution)/shard_map/ppermute | solution.py:22
  44.9 1.4 %collective-permute-start.20 = (bf16[4,8,1024]{2,1,0:T(8,128)(2,1)S(1)}, bf16[4,8,1024]{2,1,0:T(8,128)(2,1)S(1)}, u32[]{:S(2)}, u32[]{:S(2)}) collective-permute-start(bf16[4,8,1024]{2,1,0:T(8,128)(2,1)S(1)} %get-tuple-element.177), channel_id=1, source_target_pairs={{0,3},{1,2},{2,1},{3,0},{4,7},{5,6},{6,5},{7,4},{8,11},{9,10},{10,... | collective-permute-start | bytes 196616 | tf_op jit(solution)/shard_map/ppermute | solution.py:22
  46.3 1.3 %far.2 = (bf16[128,1024]{1,0:T(8,128)(2,1)S(1)}, bf16[128,1024]{1,0:T(8,128)(2,1)S(1)}) custom-call(bf16[128,2048]{1,0:T(8,128)(2,1)S(1)} %collective-permute-done.11.refs_0_.refs_3_, bf16[128,2048]{1,0:T(8,128)(2,1)S(1)} %collective-permute-done.13.refs_1_.refs_4_, bf16[2048,1024]{1,0:T(8,128)(2,1)S(1)} %copy-done, ...), custom_call_target="tpu_custom_call" | custom-call | tf_op jit(solution)/shard_map/far/pallas_call | solution.py:74
  47.5 4.0 %collective-permute-done.10.arrived_ref = bf16[64,1024]{1,0:T(8,128)(2,1)S(1)} collective-permute-done((bf16[64,1024]{1,0:T(8,128)(2,1)S(1)}, bf16[64,1024]{1,0:T(8,128)(2,1)S(1)}, u32[]{:S(2)}, u32[]{:S(2)}) %collective-permute-start.10) | collective-permute-done | bytes 131104 | tf_op jit(solution)/shard_map/ppermute | solution.py:22
  51.6 1.4 %collective-permute-done.19.refs_2_ = bf16[4,8,1024]{2,1,0:T(8,128)(2,1)S(1)} collective-permute-done((bf16[4,8,1024]{2,1,0:T(8,128)(2,1)S(1)}, bf16[4,8,1024]{2,1,0:T(8,128)(2,1)S(1)}, u32[]{:S(2)}, u32[]{:S(2)}) %collective-permute-start.19) | collective-permute-done | bytes 65568 | tf_op jit(solution)/shard_map/ppermute | solution.py:22
  53.6 1.1 %collective-permute-start.22 = (bf16[32,1024]{1,0:T(8,128)(2,1)S(1)}, bf16[32,1024]{1,0:T(8,128)(2,1)S(1)}, u32[]{:S(2)}, u32[]{:S(2)}) collective-permute-start(bf16[32,1024]{1,0:T(8,128)(2,1)S(1)} %routed_sum.1.refs_0_), channel_id=1, source_target_pairs={{0,8},{4,12},{8,0},{12,4},{1,9},{5,13},{9,1},{13,5},{2,10},{6,14},... | collective-permute-start | bytes 196616 | tf_op jit(solution)/shard_map/ppermute | solution.py:22
  55.0 1.9 %collective-permute-start.17 = (bf16[128,1024]{1,0:T(8,128)(2,1)S(1)}, bf16[128,1024]{1,0:T(8,128)(2,1)S(1)}, u32[]{:S(2)}, u32[]{:S(2)}) collective-permute-start(bf16[128,1024]{1,0:T(8,128)(2,1)S(1)} %get-tuple-element.187), channel_id=1, source_target_pairs={{0,1},{1,0},{2,3},{3,2},{4,5},{5,4},{6,7},{7,6},{8,9},{9,8},{10,11... | collective-permute-start | bytes 786440 | tf_op jit(solution)/shard_map/ppermute | solution.py:22
  56.9 1.2 %collective-permute-done.22.refs_2_ = bf16[32,1024]{1,0:T(8,128)(2,1)S(1)} collective-permute-done((bf16[32,1024]{1,0:T(8,128)(2,1)S(1)}, bf16[32,1024]{1,0:T(8,128)(2,1)S(1)}, u32[]{:S(2)}, u32[]{:S(2)}) %collective-permute-start.22) | collective-permute-done | bytes 65568 | tf_op jit(solution)/shard_map/ppermute | solution.py:22
  58.1 1.0 %collective-permute-done.23.refs_3_ = bf16[32,1024]{1,0:T(8,128)(2,1)S(1)} collective-permute-done((bf16[32,1024]{1,0:T(8,128)(2,1)S(1)}, bf16[32,1024]{1,0:T(8,128)(2,1)S(1)}, u32[]{:S(2)}, u32[]{:S(2)}) %collective-permute-start.23) | collective-permute-done | bytes 65568 | tf_op jit(solution)/shard_map/ppermute | solution.py:22
  59.1 1.5 %far.3 = (bf16[128,1024]{1,0:T(8,128)(2,1)S(1)}, bf16[128,1024]{1,0:T(8,128)(2,1)S(1)}) custom-call(bf16[128,2048]{1,0:T(8,128)(2,1)S(1)} %collective-permute-done.24.refs_0_.refs_3_, bf16[128,2048]{1,0:T(8,128)(2,1)S(1)} %collective-permute-done.25.refs_1_.refs_4_, bf16[2048,1024]{1,0:T(8,128)(2,1)S(1)} %copy-done, ...), custom_call_target="tpu_custom_call" | custom-call | tf_op jit(solution)/shard_map/far/pallas_call | solution.py:74
  60.6 1.9 %collective-permute-start.27 = (bf16[128,1024]{1,0:T(8,128)(2,1)S(1)}, bf16[128,1024]{1,0:T(8,128)(2,1)S(1)}, u32[]{:S(2)}, u32[]{:S(2)}) collective-permute-start(bf16[128,1024]{1,0:T(8,128)(2,1)S(1)} %get-tuple-element.216), channel_id=1, source_target_pairs={{0,1},{1,0},{2,3},{3,2},{4,5},{5,4},{6,7},{7,6},{8,9},{9,8},{10,11... | collective-permute-start | bytes 786440 | tf_op jit(solution)/shard_map/ppermute | solution.py:22
  62.5 1.1 %hidden_units.1.refs_0_ = bf16[32,384]{1,0:T(8,128)(2,1)S(1)} custom-call(bf16[32,1024]{1,0:T(8,128)(2,1)S(1)} %routed_sum.1.refs_0_, bf16[32,1024]{1,0:T(8,128)(2,1)S(1)} %collective-permute-done.21.refs_1_, bf16[32,1024]{1,0:T(8,128)(2,1)S(1)} %collective-permute-done.22.refs_2_, bf16[32,1024]{1,0:T(8,128)(2,1)S(1)} %collective-permute-done.23.refs_3_, ...), custom_call_target="tpu_custom_call" | custom-call | tf_op jit(solution)/shard_map/hidden_units/pallas_call | solution.py:416
  63.7 1.1 %collective-permute-start.29 = (bf16[32,384]{1,0:T(8,128)(2,1)S(1)}, bf16[32,384]{1,0:T(8,128)(2,1)S(1)}, u32[]{:S(2)}, u32[]{:S(2)}) collective-permute-start(bf16[32,384]{1,0:T(8,128)(2,1)S(1)} %hidden_units.1.refs_0_), channel_id=1, source_target_pairs={{0,8},{4,12},{8,0},{12,4},{1,9},{5,13},{9,1},{13,5},{2,10},{6,14},... | collective-permute-start | bytes 73736 | tf_op jit(solution)/shard_map/ppermute | solution.py:22
  66.3 1.3 %collective-permute-done.29.refs_2_ = bf16[32,384]{1,0:T(8,128)(2,1)S(1)} collective-permute-done((bf16[32,384]{1,0:T(8,128)(2,1)S(1)}, bf16[32,384]{1,0:T(8,128)(2,1)S(1)}, u32[]{:S(2)}, u32[]{:S(2)}) %collective-permute-start.29) | collective-permute-done | bytes 24608 | tf_op jit(solution)/shard_map/ppermute | solution.py:22
  68.2 1.3 %down_product.1 = bf16[16,2,1024]{2,1,0:T(2,128)(2,1)} custom-call(bf16[32,384]{1,0:T(8,128)(2,1)S(1)} %hidden_units.1.refs_0_, bf16[32,384]{1,0:T(8,128)(2,1)S(1)} %collective-permute-done.28.refs_1_, bf16[32,384]{1,0:T(8,128)(2,1)S(1)} %collective-permute-done.29.refs_2_, bf16[32,384]{1,0:T(8,128)(2,1)S(1)} %collective-permute-done.30.refs_3_, ...), custom_call_target="tpu_custom_call" | custom-call | tf_op jit(solution)/shard_map/down_product/pallas_call | solution.py:447
  69.5 1.4 %collective-permute-done.27.arrived_ref = bf16[128,1024]{1,0:T(8,128)(2,1)S(1)} collective-permute-done((bf16[128,1024]{1,0:T(8,128)(2,1)S(1)}, bf16[128,1024]{1,0:T(8,128)(2,1)S(1)}, u32[]{:S(2)}, u32[]{:S(2)}) %collective-permute-start.27) | collective-permute-done | bytes 262176 | tf_op jit(solution)/shard_map/ppermute | solution.py:22
  70.9 1.1 %collective-permute-start.33 = (bf16[64,1024]{1,0:T(8,128)(2,1)S(1)}, bf16[64,1024]{1,0:T(8,128)(2,1)S(1)}, u32[]{:S(2)}, u32[]{:S(2)}) collective-permute-start(bf16[64,1024]{1,0:T(8,128)(2,1)S(1)} %get-tuple-element.229), channel_id=1, source_target_pairs={{0,2},{1,3},{2,0},{3,1},{4,6},{5,7},{6,4},{7,5},{8,10},{9,11},{10,... | collective-permute-start | bytes 393224 | tf_op jit(solution)/shard_map/ppermute | solution.py:22
  72.0 4.3 %all-to-all-start = ((bf16[16,2,1024]{2,1,0:T(2,128)(2,1)}), bf16[16,2,1024]{2,1,0:T(2,128)(2,1)S(1)}, u32[]{:S(2)}, u32[]{:S(2)}) async-start(bf16[16,2,1024]{2,1,0:T(2,128)(2,1)} %down_product.1), calls=%async_computation | async-start | bytes 131072 | tf_op jit(solution)/shard_map/all_to_all | solution.py:729
  76.3 2.3 %collective-permute-done.26.arrived_ref = bf16[64,1024]{1,0:T(8,128)(2,1)S(1)} collective-permute-done((bf16[64,1024]{1,0:T(8,128)(2,1)S(1)}, bf16[64,1024]{1,0:T(8,128)(2,1)S(1)}, u32[]{:S(2)}, u32[]{:S(2)}) %collective-permute-start.26) | collective-permute-done | bytes 131104 | tf_op jit(solution)/shard_map/ppermute | solution.py:22
  78.6 1.0 %collective-permute-start.31 = (bf16[32,1024]{1,0:T(8,128)(2,1)S(1)}, bf16[32,1024]{1,0:T(8,128)(2,1)S(1)}, u32[]{:S(2)}, u32[]{:S(2)}) collective-permute-start(bf16[32,1024]{1,0:T(8,128)(2,1)S(1)} %get-tuple-element.226), channel_id=1, source_target_pairs={{0,8},{4,12},{8,0},{12,4},{1,9},{5,13},{9,1},{13,5},{2,10},{6,14},... | collective-permute-start | bytes 196616 | tf_op jit(solution)/shard_map/ppermute | solution.py:22
  79.6 1.6 %collective-permute-done.33.arrived_ref = bf16[64,1024]{1,0:T(8,128)(2,1)S(1)} collective-permute-done((bf16[64,1024]{1,0:T(8,128)(2,1)S(1)}, bf16[64,1024]{1,0:T(8,128)(2,1)S(1)}, u32[]{:S(2)}, u32[]{:S(2)}) %collective-permute-start.33) | collective-permute-done | bytes 131104 | tf_op jit(solution)/shard_map/ppermute | solution.py:22
  81.2 1.0 %collective-permute-start.34 = (bf16[32,1024]{1,0:T(8,128)(2,1)S(1)}, bf16[32,1024]{1,0:T(8,128)(2,1)S(1)}, u32[]{:S(2)}, u32[]{:S(2)}) collective-permute-start(bf16[32,1024]{1,0:T(8,128)(2,1)S(1)} %get-tuple-element.232), channel_id=1, source_target_pairs={{0,8},{4,12},{8,0},{12,4},{1,9},{5,13},{9,1},{13,5},{2,10},{6,14},... | collective-permute-start | bytes 196616 | tf_op jit(solution)/shard_map/ppermute | solution.py:22
  82.9 1.3 %combine.1 = bf16[64,4096]{1,0:T(8,128)(2,1)} custom-call(s32[8,64]{1,0:T(8,128)S(1)} %bitcast.12, f32[8,64]{1,0:T(8,128)S(1)} %bitcast.13, bf16[16,2,1024]{2,1,0:T(2,128)(2,1)S(1)} %all-to-all-done.back_ref), custom_call_target="tpu_custom_call" | custom-call | tf_op jit(solution)/shard_map/combine/pallas_call | solution.py:742
  84.2 2.1 %collective-permute-done.34.refs_4_ = bf16[32,1024]{1,0:T(8,128)(2,1)S(1)} collective-permute-done((bf16[32,1024]{1,0:T(8,128)(2,1)S(1)}, bf16[32,1024]{1,0:T(8,128)(2,1)S(1)}, u32[]{:S(2)}, u32[]{:S(2)}) %collective-permute-start.34) | collective-permute-done | bytes 65568 | tf_op jit(solution)/shard_map/ppermute | solution.py:22
  86.9 0.9 %attended_rows.1 = bf16[64,4096]{1,0:T(8,128)(2,1)} custom-call(bf16[64,1024]{1,0:T(8,128)(2,1)S(1)} %add.16.refs_0_, bf16[64,1024]{1,0:T(8,128)(2,1)S(1)} %collective-permute-done.16.refs_1_, bf16[32,1024]{1,0:T(8,128)(2,1)S(1)} %collective-permute-done.31.refs_2_, bf16[32,1024]{1,0:T(8,128)(2,1)S(1)} %collective-permute-done.32.refs_3_, ...), custom_call_target="tpu_custom_call" | custom-call | tf_op jit(solution)/shard_map/attended_rows/pallas_call | solution.py:471
  (70 shorter events, 7.6 us)
Async XLA Ops:
  1.6 10.1 %collective-permute-start = (bf16[2,256,128]{2,1,0:T(8,128)(2,1)S(1)}, bf16[2,256,128]{2,1,0:T(8,128)(2,1)S(1)}, u32[]{:S(2)}, u32[]{:S(2)}) collective-permute-start(bf16[2,256,128]{2,1,0:T(8,128)(2,1)S(1)} %pad_maximum_fusion.kv_own_ref), channel_id=1, source_target_pairs={{0,8},{4,12},{8,0},{12,4},{1,9},{5,13},{9,1},{13,5},{2,10},{6,14},... | collective-permute-start | bytes 393224 | tf_op jit(solution)/shard_map/ppermute | solution.py:27
  4.6 7.2 %collective-permute-start.1 = (bf16[2,256,128]{2,1,0:T(8,128)(2,1)S(1)}, bf16[2,256,128]{2,1,0:T(8,128)(2,1)S(1)}, u32[]{:S(2)}, u32[]{:S(2)}) collective-permute-start(bf16[2,256,128]{2,1,0:T(8,128)(2,1)S(1)} %pad_maximum_fusion.kv_own_ref), channel_id=1, source_target_pairs={{0,4},{4,8},{8,12},{12,0},{1,5},{5,9},{9,13},{13,1},{2,6},{6,10},{... | collective-permute-start | bytes 393224 | tf_op jit(solution)/shard_map/ppermute | solution.py:27
  4.6 14.0 %copy-start = (bf16[2048,1024]{1,0:T(8,128)(2,1)S(1)}, bf16[2048,1024]{1,0:T(8,128)(2,1)}, u32[]{:S(2)}) copy-start(bf16[2048,1024]{1,0:T(8,128)(2,1)} %refs_5_.3) | copy-start | bytes 12582916
  4.6 9.8 %collective-permute-start.3 = (s32[8,64]{1,0:T(8,128)}, s32[8,64]{1,0:T(8,128)S(1)}, u32[]{:S(2)}, u32[]{:S(2)}) collective-permute-start(s32[8,64]{1,0:T(8,128)} %bitcast.8), channel_id=1, source_target_pairs={{0,1},{1,0},{2,3},{3,2},{4,5},{5,4},{6,7},{7,6},{8,9},{9,8},{10,11... | collective-permute-start | bytes 6152 | tf_op jit(solution)/shard_map/ppermute | solution.py:22
  6.2 8.2 %collective-permute-start.4 = (s32[8,64]{1,0:T(8,128)}, s32[8,64]{1,0:T(8,128)S(1)}, u32[]{:S(2)}, u32[]{:S(2)}) collective-permute-start(s32[8,64]{1,0:T(8,128)} %bitcast.9), channel_id=1, source_target_pairs={{0,2},{1,3},{2,0},{3,1},{4,6},{5,7},{6,4},{7,5},{8,10},{9,11},{10,... | collective-permute-start | bytes 6152 | tf_op jit(solution)/shard_map/ppermute | solution.py:22
  8.8 5.6 %collective-permute-start.5 = (s32[8,64]{1,0:T(8,128)}, s32[8,64]{1,0:T(8,128)S(1)}, u32[]{:S(2)}, u32[]{:S(2)}) collective-permute-start(s32[8,64]{1,0:T(8,128)} %bitcast.10), channel_id=1, source_target_pairs={{0,3},{1,2},{2,1},{3,0},{4,7},{5,6},{6,5},{7,4},{8,11},{9,10},{10,... | collective-permute-start | bytes 6152 | tf_op jit(solution)/shard_map/ppermute | solution.py:22
  9.0 1.2 %copy-start.5 = (bf16[256,2048]{1,0:T(8,128)(2,1)S(1)}, bf16[256,2048]{1,0:T(8,128)(2,1)}, u32[]{:S(2)}) copy-start(bf16[256,2048]{1,0:T(8,128)(2,1)} %q_hbm) | copy-start | bytes 3145732
  10.2 0.7 copy-start.9
  17.0 2.9 %copy-start.4 = (bf16[64,4096]{1,0:T(8,128)(2,1)S(1)}, bf16[64,4096]{1,0:T(8,128)(2,1)}, u32[]{:S(2)}) copy-start(bf16[64,4096]{1,0:T(8,128)(2,1)} %refs_6_.3) | copy-start | bytes 1572868
  17.0 2.9 %copy-start.7 = (s32[64,8]{0,1:T(8,128)S(1)}, s32[64,8]{0,1:T(8,128)}, u32[]{:S(2)}) copy-start(s32[64,8]{0,1:T(8,128)} %param.19) | copy-start | bytes 6148
  17.1 4.8 %collective-permute-start.6 = (bf16[128,2048]{1,0:T(8,128)(2,1)S(1)}, bf16[128,2048]{1,0:T(8,128)(2,1)S(1)}, u32[]{:S(2)}, u32[]{:S(2)}) collective-permute-start(bf16[128,2048]{1,0:T(8,128)(2,1)S(1)} %attention_1.1.refs_1_.refs_6_.refs_4_), channel_id=1, source_target_pairs={{0,4},{4,0},{8,12},{12,8},{1,5},{5,1},{9,13},{13,9},{2,6},{6,2},{1... | collective-permute-start | bytes 1572872 | tf_op jit(solution)/shard_map/ppermute | solution.py:22
  17.1 4.7 %collective-permute-start.2 = (bf16[128,2048]{1,0:T(8,128)(2,1)S(1)}, bf16[128,2048]{1,0:T(8,128)(2,1)S(1)}, u32[]{:S(2)}, u32[]{:S(2)}) collective-permute-start(bf16[128,2048]{1,0:T(8,128)(2,1)S(1)} %attention_0.1.refs_0_.refs_5_.refs_3_), channel_id=1, source_target_pairs={{0,4},{4,0},{8,12},{12,8},{1,5},{5,1},{9,13},{13,9},{2,6},{6,2},{1... | collective-permute-start | bytes 1572872 | tf_op jit(solution)/shard_map/ppermute | solution.py:22
  17.6 14.8 %collective-permute-start.11 = (bf16[128,2048]{1,0:T(8,128)(2,1)S(1)}, bf16[128,2048]{1,0:T(8,128)(2,1)S(1)}, u32[]{:S(2)}, u32[]{:S(2)}) collective-permute-start(bf16[128,2048]{1,0:T(8,128)(2,1)S(1)} %attention_0.1.refs_0_.refs_5_.refs_3_), channel_id=1, source_target_pairs={{0,8},{4,12},{8,0},{12,4},{1,9},{5,13},{9,1},{13,5},{2,10},{6,14},... | collective-permute-start | bytes 1572872 | tf_op jit(solution)/shard_map/ppermute | solution.py:22
  19.3 9.2 %collective-permute-start.7 = (bf16[128,1024]{1,0:T(8,128)(2,1)S(1)}, bf16[128,1024]{1,0:T(8,128)(2,1)S(1)}, u32[]{:S(2)}, u32[]{:S(2)}) collective-permute-start(bf16[128,1024]{1,0:T(8,128)(2,1)S(1)} %leave.1), channel_id=1, source_target_pairs={{0,1},{1,0},{2,3},{3,2},{4,5},{5,4},{6,7},{7,6},{8,9},{9,8},{10,11... | collective-permute-start | bytes 786440 | tf_op jit(solution)/shard_map/ppermute | solution.py:22
  23.7 12.1 %collective-permute-start.9 = (bf16[128,1024]{1,0:T(8,128)(2,1)S(1)}, bf16[128,1024]{1,0:T(8,128)(2,1)S(1)}, u32[]{:S(2)}, u32[]{:S(2)}) collective-permute-start(bf16[128,1024]{1,0:T(8,128)(2,1)S(1)} %get-tuple-element.158), channel_id=1, source_target_pairs={{0,1},{1,0},{2,3},{3,2},{4,5},{5,4},{6,7},{7,6},{8,9},{9,8},{10,11... | collective-permute-start | bytes 786440 | tf_op jit(solution)/shard_map/ppermute | solution.py:22
  28.6 7.2 %collective-permute-start.12 = (bf16[48,2048]{1,0:T(8,128)(2,1)S(1)}, bf16[48,2048]{1,0:T(8,128)(2,1)S(1)}, u32[]{:S(2)}, u32[]{:S(2)}) collective-permute-start(bf16[48,2048]{1,0:T(8,128)(2,1)S(1)} %pick.1.refs_0_), channel_id=1, source_target_pairs={{0,8},{4,12},{8,0},{12,4},{1,9},{5,13},{9,1},{13,5},{2,10},{6,14},... | collective-permute-start | bytes 589832 | tf_op jit(solution)/shard_map/ppermute | solution.py:22
  29.8 8.7 %collective-permute-start.8 = (bf16[64,1024]{1,0:T(8,128)(2,1)S(1)}, bf16[64,1024]{1,0:T(8,128)(2,1)S(1)}, u32[]{:S(2)}, u32[]{:S(2)}) collective-permute-start(bf16[64,1024]{1,0:T(8,128)(2,1)S(1)} %get-tuple-element.157), channel_id=1, source_target_pairs={{0,2},{1,3},{2,0},{3,1},{4,6},{5,7},{6,4},{7,5},{8,10},{9,11},{10,... | collective-permute-start | bytes 393224 | tf_op jit(solution)/shard_map/ppermute | solution.py:22
  35.8 9.0 %collective-permute-start.13 = (bf16[128,2048]{1,0:T(8,128)(2,1)S(1)}, bf16[128,2048]{1,0:T(8,128)(2,1)S(1)}, u32[]{:S(2)}, u32[]{:S(2)}) collective-permute-start(bf16[128,2048]{1,0:T(8,128)(2,1)S(1)} %collective-permute-done.11.refs_0_.refs_3_), channel_id=1, source_target_pairs={{0,4},{4,0},{8,12},{12,8},{1,5},{5,1},{9,13},{13,9},{2,6},{6,2},{1... | collective-permute-start | bytes 1572872 | tf_op jit(solution)/shard_map/ppermute | solution.py:22
  38.5 14.5 %collective-permute-start.24 = (bf16[128,2048]{1,0:T(8,128)(2,1)S(1)}, bf16[128,2048]{1,0:T(8,128)(2,1)S(1)}, u32[]{:S(2)}, u32[]{:S(2)}) collective-permute-start(bf16[128,2048]{1,0:T(8,128)(2,1)S(1)} %attention_1.1.refs_1_.refs_6_.refs_4_), channel_id=1, source_target_pairs={{0,8},{4,12},{8,0},{12,4},{1,9},{5,13},{9,1},{13,5},{2,10},{6,14},... | collective-permute-start | bytes 1572872 | tf_op jit(solution)/shard_map/ppermute | solution.py:22
  39.3 1.4 %collective-permute-start.14 = (bf16[48,2048]{1,0:T(8,128)(2,1)S(1)}, bf16[48,2048]{1,0:T(8,128)(2,1)S(1)}, u32[]{:S(2)}, u32[]{:S(2)}) collective-permute-start(bf16[48,2048]{1,0:T(8,128)(2,1)S(1)} %pick.1.refs_0_), channel_id=1, source_target_pairs={{0,4},{4,0},{8,12},{12,8},{1,5},{5,1},{9,13},{13,9},{2,6},{6,2},{1... | collective-permute-start | bytes 589832 | tf_op jit(solution)/shard_map/ppermute | solution.py:22
  39.3 1.7 %collective-permute-start.15 = (bf16[48,2048]{1,0:T(8,128)(2,1)S(1)}, bf16[48,2048]{1,0:T(8,128)(2,1)S(1)}, u32[]{:S(2)}, u32[]{:S(2)}) collective-permute-start(bf16[48,2048]{1,0:T(8,128)(2,1)S(1)} %collective-permute-done.12.refs_2_), channel_id=1, source_target_pairs={{0,4},{4,0},{8,12},{12,8},{1,5},{5,1},{9,13},{13,9},{2,6},{6,2},{1... | collective-permute-start | bytes 589832 | tf_op jit(solution)/shard_map/ppermute | solution.py:22
  39.8 11.8 %collective-permute-start.10 = (bf16[64,1024]{1,0:T(8,128)(2,1)S(1)}, bf16[64,1024]{1,0:T(8,128)(2,1)S(1)}, u32[]{:S(2)}, u32[]{:S(2)}) collective-permute-start(bf16[64,1024]{1,0:T(8,128)(2,1)S(1)} %get-tuple-element.165), channel_id=1, source_target_pairs={{0,2},{1,3},{2,0},{3,1},{4,6},{5,7},{6,4},{7,5},{8,10},{9,11},{10,... | collective-permute-start | bytes 393224 | tf_op jit(solution)/shard_map/ppermute | solution.py:22
  41.8 9.8 %collective-permute-start.18 = (bf16[4,8,1024]{2,1,0:T(8,128)(2,1)S(1)}, bf16[4,8,1024]{2,1,0:T(8,128)(2,1)S(1)}, u32[]{:S(2)}, u32[]{:S(2)}) collective-permute-start(bf16[4,8,1024]{2,1,0:T(8,128)(2,1)S(1)} %get-tuple-element.189), channel_id=1, source_target_pairs={{0,1},{1,0},{2,3},{3,2},{4,5},{5,4},{6,7},{7,6},{8,9},{9,8},{10,11... | collective-permute-start | bytes 196616 | tf_op jit(solution)/shard_map/ppermute | solution.py:22
  43.6 9.3 %collective-permute-start.19 = (bf16[4,8,1024]{2,1,0:T(8,128)(2,1)S(1)}, bf16[4,8,1024]{2,1,0:T(8,128)(2,1)S(1)}, u32[]{:S(2)}, u32[]{:S(2)}) collective-permute-start(bf16[4,8,1024]{2,1,0:T(8,128)(2,1)S(1)} %get-tuple-element.190), channel_id=1, source_target_pairs={{0,2},{1,3},{2,0},{3,1},{4,6},{5,7},{6,4},{7,5},{8,10},{9,11},{10,... | collective-permute-start | bytes 196616 | tf_op jit(solution)/shard_map/ppermute | solution.py:22
  44.9 8.1 %collective-permute-start.20 = (bf16[4,8,1024]{2,1,0:T(8,128)(2,1)S(1)}, bf16[4,8,1024]{2,1,0:T(8,128)(2,1)S(1)}, u32[]{:S(2)}, u32[]{:S(2)}) collective-permute-start(bf16[4,8,1024]{2,1,0:T(8,128)(2,1)S(1)} %get-tuple-element.177), channel_id=1, source_target_pairs={{0,3},{1,2},{2,1},{3,0},{4,7},{5,6},{6,5},{7,4},{8,11},{9,10},{10,... | collective-permute-start | bytes 196616 | tf_op jit(solution)/shard_map/ppermute | solution.py:22
  53.0 6.0 %collective-permute-start.25 = (bf16[128,2048]{1,0:T(8,128)(2,1)S(1)}, bf16[128,2048]{1,0:T(8,128)(2,1)S(1)}, u32[]{:S(2)}, u32[]{:S(2)}) collective-permute-start(bf16[128,2048]{1,0:T(8,128)(2,1)S(1)} %collective-permute-done.24.refs_0_.refs_3_), channel_id=1, source_target_pairs={{0,4},{4,0},{8,12},{12,8},{1,5},{5,1},{9,13},{13,9},{2,6},{6,2},{1... | collective-permute-start | bytes 1572872 | tf_op jit(solution)/shard_map/ppermute | solution.py:22
  53.1 3.8 %collective-permute-start.21 = (bf16[32,1024]{1,0:T(8,128)(2,1)S(1)}, bf16[32,1024]{1,0:T(8,128)(2,1)S(1)}, u32[]{:S(2)}, u32[]{:S(2)}) collective-permute-start(bf16[32,1024]{1,0:T(8,128)(2,1)S(1)} %routed_sum.1.refs_0_), channel_id=1, source_target_pairs={{0,4},{4,0},{8,12},{12,8},{1,5},{5,1},{9,13},{13,9},{2,6},{6,2},{1... | collective-permute-start | bytes 196616 | tf_op jit(solution)/shard_map/ppermute | solution.py:22
  53.6 4.5 %collective-permute-start.22 = (bf16[32,1024]{1,0:T(8,128)(2,1)S(1)}, bf16[32,1024]{1,0:T(8,128)(2,1)S(1)}, u32[]{:S(2)}, u32[]{:S(2)}) collective-permute-start(bf16[32,1024]{1,0:T(8,128)(2,1)S(1)} %routed_sum.1.refs_0_), channel_id=1, source_target_pairs={{0,8},{4,12},{8,0},{12,4},{1,9},{5,13},{9,1},{13,5},{2,10},{6,14},... | collective-permute-start | bytes 196616 | tf_op jit(solution)/shard_map/ppermute | solution.py:22
  54.7 4.3 %collective-permute-start.23 = (bf16[32,1024]{1,0:T(8,128)(2,1)S(1)}, bf16[32,1024]{1,0:T(8,128)(2,1)S(1)}, u32[]{:S(2)}, u32[]{:S(2)}) collective-permute-start(bf16[32,1024]{1,0:T(8,128)(2,1)S(1)} %routed_sum.1.refs_0_), channel_id=1, source_target_pairs={{0,12},{4,8},{8,4},{12,0},{1,13},{5,9},{9,5},{13,1},{2,14},{6,10},... | collective-permute-start | bytes 196616 | tf_op jit(solution)/shard_map/ppermute | solution.py:22
  55.0 7.5 %copy-start.1 = (bf16[1,4096,384]{2,1,0:T(8,128)(2,1)S(1)}, bf16[1,4096,384]{2,1,0:T(8,128)(2,1)}, u32[]{:S(2)}) copy-start(bf16[1,4096,384]{2,1,0:T(8,128)(2,1)} %refs_5_.4) | copy-start | bytes 9437188
  55.0 7.5 %copy-start.2 = (bf16[1,4096,384]{2,1,0:T(8,128)(2,1)S(1)}, bf16[1,4096,384]{2,1,0:T(8,128)(2,1)}, u32[]{:S(2)}) copy-start(bf16[1,4096,384]{2,1,0:T(8,128)(2,1)} %refs_6_.2) | copy-start | bytes 9437188
  55.0 7.5 %copy-start.6 = (f32[4096]{0:T(1024)S(1)}, f32[4096]{0:T(1024)}, u32[]{:S(2)}) copy-start(f32[4096]{0:T(1024)} %param.18) | copy-start | bytes 49156
  55.0 10.5 %collective-permute-start.17 = (bf16[128,1024]{1,0:T(8,128)(2,1)S(1)}, bf16[128,1024]{1,0:T(8,128)(2,1)S(1)}, u32[]{:S(2)}, u32[]{:S(2)}) collective-permute-start(bf16[128,1024]{1,0:T(8,128)(2,1)S(1)} %get-tuple-element.187), channel_id=1, source_target_pairs={{0,1},{1,0},{2,3},{3,2},{4,5},{5,4},{6,7},{7,6},{8,9},{9,8},{10,11... | collective-permute-start | bytes 786440 | tf_op jit(solution)/shard_map/ppermute | solution.py:22
  60.6 10.3 %collective-permute-start.27 = (bf16[128,1024]{1,0:T(8,128)(2,1)S(1)}, bf16[128,1024]{1,0:T(8,128)(2,1)S(1)}, u32[]{:S(2)}, u32[]{:S(2)}) collective-permute-start(bf16[128,1024]{1,0:T(8,128)(2,1)S(1)} %get-tuple-element.216), channel_id=1, source_target_pairs={{0,1},{1,0},{2,3},{3,2},{4,5},{5,4},{6,7},{7,6},{8,9},{9,8},{10,11... | collective-permute-start | bytes 786440 | tf_op jit(solution)/shard_map/ppermute | solution.py:22
  62.5 5.7 %copy-start.3 = (bf16[1,1536,1024]{2,1,0:T(8,128)(2,1)S(1)}, bf16[1,1536,1024]{2,1,0:T(8,128)(2,1)}, u32[]{:S(2)}) copy-start(bf16[1,1536,1024]{2,1,0:T(8,128)(2,1)} %refs_4_.2) | copy-start | bytes 9437188
  63.6 19.3 %copy-start.8 = (f32[64,8]{0,1:T(8,128)S(1)}, f32[64,8]{0,1:T(8,128)}, u32[]{:S(2)}) copy-start(f32[64,8]{0,1:T(8,128)} %param.20) | copy-start | bytes 6148
  63.6 2.6 %collective-permute-start.28 = (bf16[32,384]{1,0:T(8,128)(2,1)S(1)}, bf16[32,384]{1,0:T(8,128)(2,1)S(1)}, u32[]{:S(2)}, u32[]{:S(2)}) collective-permute-start(bf16[32,384]{1,0:T(8,128)(2,1)S(1)} %hidden_units.1.refs_0_), channel_id=1, source_target_pairs={{0,4},{4,0},{8,12},{12,8},{1,5},{5,1},{9,13},{13,9},{2,6},{6,2},{1... | collective-permute-start | bytes 73736 | tf_op jit(solution)/shard_map/ppermute | solution.py:22
  63.7 3.9 %collective-permute-start.29 = (bf16[32,384]{1,0:T(8,128)(2,1)S(1)}, bf16[32,384]{1,0:T(8,128)(2,1)S(1)}, u32[]{:S(2)}, u32[]{:S(2)}) collective-permute-start(bf16[32,384]{1,0:T(8,128)(2,1)S(1)} %hidden_units.1.refs_0_), channel_id=1, source_target_pairs={{0,8},{4,12},{8,0},{12,4},{1,9},{5,13},{9,1},{13,5},{2,10},{6,14},... | collective-permute-start | bytes 73736 | tf_op jit(solution)/shard_map/ppermute | solution.py:22
  64.9 3.3 %collective-permute-start.30 = (bf16[32,384]{1,0:T(8,128)(2,1)S(1)}, bf16[32,384]{1,0:T(8,128)(2,1)S(1)}, u32[]{:S(2)}, u32[]{:S(2)}) collective-permute-start(bf16[32,384]{1,0:T(8,128)(2,1)S(1)} %hidden_units.1.refs_0_), channel_id=1, source_target_pairs={{0,12},{4,8},{8,4},{12,0},{1,13},{5,9},{9,5},{13,1},{2,14},{6,10},... | collective-permute-start | bytes 73736 | tf_op jit(solution)/shard_map/ppermute | solution.py:22
  65.6 12.9 %collective-permute-start.26 = (bf16[64,1024]{1,0:T(8,128)(2,1)S(1)}, bf16[64,1024]{1,0:T(8,128)(2,1)S(1)}, u32[]{:S(2)}, u32[]{:S(2)}) collective-permute-start(bf16[64,1024]{1,0:T(8,128)(2,1)S(1)} %get-tuple-element.215), channel_id=1, source_target_pairs={{0,2},{1,3},{2,0},{3,1},{4,6},{5,7},{6,4},{7,5},{8,10},{9,11},{10,... | collective-permute-start | bytes 393224 | tf_op jit(solution)/shard_map/ppermute | solution.py:22
  70.9 10.2 %collective-permute-start.33 = (bf16[64,1024]{1,0:T(8,128)(2,1)S(1)}, bf16[64,1024]{1,0:T(8,128)(2,1)S(1)}, u32[]{:S(2)}, u32[]{:S(2)}) collective-permute-start(bf16[64,1024]{1,0:T(8,128)(2,1)S(1)} %get-tuple-element.229), channel_id=1, source_target_pairs={{0,2},{1,3},{2,0},{3,1},{4,6},{5,7},{6,4},{7,5},{8,10},{9,11},{10,... | collective-permute-start | bytes 393224 | tf_op jit(solution)/shard_map/ppermute | solution.py:22
  72.0 12.2 %collective-permute-start.16 = (bf16[64,1024]{1,0:T(8,128)(2,1)S(1)}, bf16[64,1024]{1,0:T(8,128)(2,1)S(1)}, u32[]{:S(2)}, u32[]{:S(2)}) collective-permute-start(bf16[64,1024]{1,0:T(8,128)(2,1)S(1)} %add.17), channel_id=1, source_target_pairs={{0,4},{4,0},{8,12},{12,8},{1,5},{5,1},{9,13},{13,9},{2,6},{6,2},{1... | collective-permute-start | bytes 393224 | tf_op jit(solution)/shard_map/ppermute | solution.py:22
  72.0 10.9 %all-to-all-start = ((bf16[16,2,1024]{2,1,0:T(2,128)(2,1)}), bf16[16,2,1024]{2,1,0:T(2,128)(2,1)S(1)}, u32[]{:S(2)}, u32[]{:S(2)}) async-start(bf16[16,2,1024]{2,1,0:T(2,128)(2,1)} %down_product.1), calls=%async_computation | async-start | bytes 131072 | tf_op jit(solution)/shard_map/all_to_all | solution.py:729
  78.6 5.6 %collective-permute-start.31 = (bf16[32,1024]{1,0:T(8,128)(2,1)S(1)}, bf16[32,1024]{1,0:T(8,128)(2,1)S(1)}, u32[]{:S(2)}, u32[]{:S(2)}) collective-permute-start(bf16[32,1024]{1,0:T(8,128)(2,1)S(1)} %get-tuple-element.226), channel_id=1, source_target_pairs={{0,8},{4,12},{8,0},{12,4},{1,9},{5,13},{9,1},{13,5},{2,10},{6,14},... | collective-permute-start | bytes 196616 | tf_op jit(solution)/shard_map/ppermute | solution.py:22
  79.6 4.6 %collective-permute-start.32 = (bf16[32,1024]{1,0:T(8,128)(2,1)S(1)}, bf16[32,1024]{1,0:T(8,128)(2,1)S(1)}, u32[]{:S(2)}, u32[]{:S(2)}) collective-permute-start(bf16[32,1024]{1,0:T(8,128)(2,1)S(1)} %get-tuple-element.227), channel_id=1, source_target_pairs={{0,12},{4,8},{8,4},{12,0},{1,13},{5,9},{9,5},{13,1},{2,14},{6,10},... | collective-permute-start | bytes 196616 | tf_op jit(solution)/shard_map/ppermute | solution.py:22
  81.2 5.2 %collective-permute-start.34 = (bf16[32,1024]{1,0:T(8,128)(2,1)S(1)}, bf16[32,1024]{1,0:T(8,128)(2,1)S(1)}, u32[]{:S(2)}, u32[]{:S(2)}) collective-permute-start(bf16[32,1024]{1,0:T(8,128)(2,1)S(1)} %get-tuple-element.232), channel_id=1, source_target_pairs={{0,8},{4,12},{8,0},{12,4},{1,9},{5,13},{9,1},{13,5},{2,10},{6,14},... | collective-permute-start | bytes 196616 | tf_op jit(solution)/shard_map/ppermute | solution.py:22
  82.2 4.7 %collective-permute-start.35 = (bf16[32,1024]{1,0:T(8,128)(2,1)S(1)}, bf16[32,1024]{1,0:T(8,128)(2,1)S(1)}, u32[]{:S(2)}, u32[]{:S(2)}) collective-permute-start(bf16[32,1024]{1,0:T(8,128)(2,1)S(1)} %get-tuple-element.233), channel_id=1, source_target_pairs={{0,12},{4,8},{8,4},{12,0},{1,13},{5,9},{9,5},{13,1},{2,14},{6,10},... | collective-permute-start | bytes 196616 | tf_op jit(solution)/shard_map/ppermute | solution.py:22
